TPU v7x, 256 devices: a whole 4x4x8 slice. The times are simulated.
256 devices in a mesh: row: 32 (over y_lo, z, core), col: 8 (over y_hi, x).
Axes of the slice: x: 4, y: 4 (y_hi: 2, y_lo: 2; y = y_hi * 2 + y_lo), z: 8, core: 2. Of those that a mesh axis runs over, the one named last changes fastest.
Arguments:
- pair_matrix: bfloat16 [64, 16, 3072], P('row', None, 'col'), may hold values from -0.109375 to 0.109375
- screened: bfloat16 [64, 3072, 3072], P('row', 'col'), may hold values from -6 to 6
- coulomb: float32 [3072], P('col'), may hold values from 0.2 to 2
- q_index: int32 [64, 64], replicated, may hold values from 0 to 63, as said below
Outputs:
- kernel: float32 [1024, 1024], P('row', 'col')
Inputs may be any that keep to these rules, and one draw needn't show every extreme that they name: q_index[k, k'] = (m(k) - m(k')) mod 64 for a permutation m of the panel's k-points, so every row and every column holds each q exactly once.
All inputs are finite; a program needn't handle non-finite values.
Results may differ from a plain program's by a relative error of at most 0.0095.
Values may be sent and summed in bfloat16 or wider, within the bound.
No kernel may reach another device: no remote copies, remote signals or barrier semaphores. Data moves between devices by JAX's collectives and lax.ppermute only.
A program may use at most 128 MiB of HBM per device.

v0:
```python
import jax
import jax.numpy as jnp
from jax import lax
from jax.sharding import PartitionSpec as P


def select_rows(blocks, indices):
    return jnp.take(blocks, indices, axis=0)


def local(pair_matrix, screened, coulomb, q_index):
    mine = pair_matrix.shape[0]
    bands = pair_matrix.shape[1]
    share = pair_matrix.shape[2]
    panel = lax.all_gather(pair_matrix, "row", axis=0, tiled=True)
    total = panel.shape[0]
    row_place = lax.axis_index("row")
    positions = lax.iota(jnp.int32, total)
    flat = panel.reshape(total * bands, share)
    blocks = []
    for slot in range(mine):
        w_block = screened[slot]
        q_value = row_place * mine + slot
        partner = jnp.sum(jnp.where(q_index == q_value, positions[None, :], 0), axis=1)

        def project(offset, length, w_block=w_block):
            return lax.dot_general(
                w_block, flat, (((0,), (1,)), ((), ())), preferred_element_type=jnp.float32
            )

        image = lax.psum_scatter(
            project(jnp.int32(0), lax.axis_size("col") * share),
            "col",
            scatter_dimension=0,
            tiled=True,
        )
        chosen = jnp.take(panel, partner, axis=0)
        rounded = image.astype(jnp.bfloat16).reshape(image.shape[0], total, bands)
        blocks.append(
            jnp.einsum("gkb,kcg->kbc", rounded, chosen, preferred_element_type=jnp.float32)
        )
    direct = jnp.stack(blocks, axis=1)
    my_q = lax.dynamic_slice_in_dim(q_index, row_place * mine, mine, 0)
    weighted = (pair_matrix.astype(jnp.float32) * coulomb).astype(jnp.bfloat16)
    bare = jnp.einsum("kbg,jcg->kjbc", weighted, panel, preferred_element_type=jnp.float32)
    picker = jax.vmap(select_rows)
    arrived = lax.all_to_all(direct, "row", split_axis=0, concat_axis=1, tiled=True)
    placed = picker(arrived, my_q)
    summed = lax.psum_scatter(2.0 * bare - placed, "col", scatter_dimension=1, tiled=True)
    return jnp.transpose(summed, (0, 2, 1, 3)).reshape(mine * bands, -1)


def solution(mesh):
    placed = (P("row", None, "col"), P("row", "col", None), P("col"), P())
    return jax.shard_map(
        local, mesh=mesh, in_specs=placed, out_specs=P("row", "col"), check_vma=False
    )
```

profile of v0, /device:TPU:1, one launch (start us, length us, event | category | flops | bytes accessed | tf_op | source)
XLA Modules:
  0.0 476.7 jit_solution(12999826723010227293)
XLA Ops:
  6.5 40.9 %all_gather.3 = bf16[64,16,384]{2,1,0:T(8,128)(2,1)S(1)} all-gather(bf16[2,16,384]{2,1,0:T(8,128)(2,1)} %param.6), channel_id=1, replica_groups=mesh['row'=32,'col'=8] {'row'}, dimensions={0}, use_global_device_ids=true | all-gather | bytes 811008 | tf_op jit(solution)/shard_map/all_gather | solution.py:15
  47.4 8.1 %fusion = f32[3072,1024]{1,0:T(8,128)} fusion(bf16[1024,384]{1,0:T(8,128)(2,1)S(1)} %bitcast.41, bf16[2,384,3072]{2,1,0:T(8,128)(2,1)} %param.7), kind=kOutput, calls=%fused_computation.3 | convolution fusion | flops 2415919104 | bytes 15728640 | tf_op jit(solution)/shard_map/dot_general | solution.py:27
  55.6 8.3 %fusion.2 = f32[3072,1024]{1,0:T(8,128)} fusion(bf16[1024,384]{1,0:T(8,128)(2,1)S(1)} %bitcast.42, bf16[2,384,3072]{2,1,0:T(8,128)(2,1)} %param.7), kind=kOutput, calls=%fused_computation.5 | convolution fusion | flops 2415919104 | bytes 15728640 | tf_op jit(solution)/shard_map/dot_general | solution.py:27
  63.9 0.7 copy-done.1
  64.8 0.7 gather_fusion.2
  65.5 0.7 gather_fusion.1
  66.3 141.5 %reduce-scatter.6.cloned.1.call-done = f32[384,1024]{1,0:T(8,128)} async-done(((f32[3072,1024]{1,0:T(8,128)}), f32[384,1024]{1,0:T(8,128)}) %reduce-scatter.6.cloned.1.call-update) | async-done | bytes 1572880 | tf_op jit(solution)/shard_map/reduce_scatter | solution.py:31
  207.8 1.5 convert_element_type.15
  209.3 1.2 copy.33
  210.5 157.0 %reduce-scatter.4.cloned.1.call-done = f32[384,1024]{1,0:T(8,128)} async-done(((f32[3072,1024]{1,0:T(8,128)}), f32[384,1024]{1,0:T(8,128)}) %reduce-scatter.4.cloned.1.call-update) | async-done | bytes 1572880 | tf_op jit(solution)/shard_map/reduce_scatter | solution.py:31
  367.5 1.5 convert_element_type.14
  369.1 1.2 copy.32
  370.2 1.7 convolution_bitcast_fusion
  371.9 1.7 convolution_bitcast_fusion.1
  373.9 1.0 reshape.62
  374.9 8.4 %all-to-all-start = ((f32[32,1,1024]{2,1,0:T(1,128)}), f32[32,1,1024]{2,1,0:T(1,128)S(1)}, u32[]{:S(2)}, u32[]{:S(2)}) async-start(f32[32,1,1024]{2,1,0:T(1,128)} %reshape.62), calls=%async_computation.2 | async-start | bytes 262144 | tf_op jit(solution)/shard_map/all_to_all | solution.py:47
  383.5 8.9 %all-to-all-done = f32[32,1,1024]{2,1,0:T(1,128)S(1)} async-done(((f32[32,1,1024]{2,1,0:T(1,128)}), f32[32,1,1024]{2,1,0:T(1,128)S(1)}, u32[]{:S(2)}, u32[]{:S(2)}) %all-to-all-start) | async-done | bytes 131104 | tf_op jit(solution)/shard_map/all_to_all | solution.py:47
  393.0 1.0 reduce
  394.4 1.0 gather_fusion
  396.0 0.6 fusion.7
  396.6 1.8 copy.38
  398.4 70.1 %reduce-scatter.8.cloned.1.call-done = f32[2,8,16,16]{3,2,0,1:T(8,128)} async-done(((f32[2,64,16,16]{3,2,0,1:T(8,128)}), f32[2,8,16,16]{3,2,0,1:T(8,128)}) %reduce-scatter.8.cloned.1.call-update) | async-done | bytes 16400 | tf_op jit(solution)/shard_map/reduce_scatter | solution.py:49
  468.5 1.0 copy.39
  469.5 0.7 reshape.26
  (25 shorter events, 2.1 us)
Async XLA Ops:
  6.5 201.2 %reduce-scatter.6.cloned.1.call-start = ((), (), s32[]{:S(2)}) async-start(), calls=%async_computation.5 | async-start | bytes 14155776 | tf_op jit(solution)/shard_map/reduce_scatter | solution.py:31
  55.6 312.0 %reduce-scatter.4.cloned.1.call-start = ((), (), s32[]{:S(2)}) async-start(), calls=%async_computation.4 | async-start | bytes 14155776 | tf_op jit(solution)/shard_map/reduce_scatter | solution.py:31
  63.9 0.8 copy-start.1
  373.9 22.1 %copy-start = (bf16[2,16,384]{2,1,0:T(8,128)(2,1)S(1)}, bf16[2,16,384]{2,1,0:T(8,128)(2,1)}, u32[]{:S(2)}) copy-start(bf16[2,16,384]{2,1,0:T(8,128)(2,1)} %param.6) | copy-start | bytes 73732
  373.9 22.1 %copy-start.2 = (f32[384]{0:T(512)S(1)}, f32[384]{0:T(512)}, u32[]{:S(2)}) copy-start(f32[384]{0:T(512)} %param.8) | copy-start | bytes 4612
  374.9 17.5 %all-to-all-start = ((f32[32,1,1024]{2,1,0:T(1,128)}), f32[32,1,1024]{2,1,0:T(1,128)S(1)}, u32[]{:S(2)}, u32[]{:S(2)}) async-start(f32[32,1,1024]{2,1,0:T(1,128)} %reshape.62), calls=%async_computation.2 | async-start | bytes 262144 | tf_op jit(solution)/shard_map/all_to_all | solution.py:47
  383.4 85.1 %reduce-scatter.8.cloned.1.call-start = ((), (), s32[]{:S(2)}) async-start(), calls=%async_computation.6 | async-start | bytes 1179648 | tf_op jit(solution)/shard_map/reduce_scatter | solution.py:49
Sparse Core Ops, SparseCore 0:
  55.7 152.0 reduce-scatter.5
  212.6 154.9 reduce-scatter.3
  398.5 69.9 reduce-scatter.7
where the time goes:
time: 478 us; the launch traced here: 477 us
  waiting for transfers between devices  378 us (79%)
  blocking collectives  40.9 us (9%)
  matrix products  20.4 us (4%)
  between operations  13.3 us (3%)
  local copies, waits for them, and re-layouts  11.8 us (2%)
  starting transfers between devices  8.51 us (2%)
    reduce_scatter x2, waiting for transfers between devices, local(): lax.psum_scatter(project(jnp.int32(0), lax.axis_size('col') * share), 'co...  299 us
    reduce_scatter x1, waiting for transfers between devices, local(): lax.psum_scatter(2.0 * bare - placed, 'col', scatter_dimension=1, tiled=T...  70.1 us
    all_gather x1, blocking collectives, local(): panel = lax.all_gather(pair_matrix, 'row', axis=0, tiled=True)  40.9 us
    dot_general x2, matrix products, project(): lax.dot_general(w_block, flat, (((0,), (1,)), ((), ())), preferred_elemen...  16.4 us
  transfers between devices with their start and end apart: 4, of which 4 were waited for; matrix products, arithmetic and copies ran while one was open for 3% of the time, Pallas kernels for 0%

commit v1 on v0

v1 whole, which is shorter than its diff:
```python
import jax
import jax.numpy as jnp
from jax import lax
from jax.experimental import pallas as pl
from jax.experimental.pallas import tpu as pltpu
from jax.sharding import PartitionSpec as P

AXES = ("row", "col")
NX, NY, NZ, NCORE = 4, 4, 8, 2
SHIFTS = (0, 2, 1, -1)
ZSHIFTS = (0, 2, -2, 4)
VMEM = 48 * 1024 * 1024


def device_index(x, y, z, c):
    y_hi, y_lo = divmod(y % NY, 2)
    row = (y_lo * NZ + z % NZ) * NCORE + c
    return row * 8 + y_hi * NX + x % NX


def pairs(move):
    found = []
    for x in range(NX):
        for y in range(NY):
            for z in range(NZ):
                for c in range(NCORE):
                    found.append((device_index(x, y, z, c), device_index(*move(x, y, z, c))))
    return found


SWAP = pairs(lambda x, y, z, c: (x, y, z, 1 - c))
ZPAIR = pairs(lambda x, y, z, c: (x, y, z ^ 1, c))


def along_z(s):
    return pairs(lambda x, y, z, c: (x, y, z + s, c))


def first_plane(s):
    return pairs(lambda x, y, z, c: (x + s, y, z, c) if c == 0 else (x, y + s, z, c))


def second_plane(s):
    return pairs(lambda x, y, z, c: (x, y + s, z, c) if c == 0 else (x + s, y, z, c))


def send(value, perm):
    return lax.ppermute(value, AXES, perm)


def contract(a, b):
    return lax.dot_general(a, b, (((1,), (1,)), ((), ())), preferred_element_type=jnp.float32)


def project_kernel(cols, lows, p0, p1, p2, p3, mine, coulomb, w_own, w_other, out, total):
    share = p0.shape[2]

    def run(w):
        total[...] = jnp.zeros_like(total)
        for k, panel in enumerate((p0, p1, p2, p3)):
            for half in range(2):
                at = 4 * k + 2 * half
                left = jnp.concatenate([panel[2 * half], panel[2 * half + 1]], axis=1)
                right = jnp.concatenate(
                    [
                        w[0, :, pl.ds(pl.multiple_of(cols[at + i] * share, share), share)]
                        for i in range(2)
                    ],
                    axis=1,
                )
                total[lows[at]] += contract(left, right)
        for low in range(2):
            bare = (2.0 * coulomb[...]) * mine[low].astype(jnp.float32)
            out[0, low] = (bare - total[low]).astype(out.dtype)

    @pl.when(pl.program_id(0) < 2)
    def _():
        run(w_own)

    @pl.when(pl.program_id(0) >= 2)
    def _():
        run(w_other)


def project(cols, lows, panels, mine, coulomb, w_own, w_other):
    rows, share = panels[0].shape[1:]
    whole = w_own.shape[2]
    fixed = lambda shape: pl.BlockSpec(shape, lambda q, *_: (0,) * len(shape))
    return pl.pallas_call(
        project_kernel,
        grid_spec=pltpu.PrefetchScalarGridSpec(
            num_scalar_prefetch=2,
            grid=(4,),
            in_specs=[fixed((4, rows, share))] * 4
            + [
                fixed((2, rows, share)),
                fixed((1, share)),
                pl.BlockSpec((1, share, whole), lambda q, *_: (jnp.minimum(q, 1), 0, 0)),
                pl.BlockSpec((1, share, whole), lambda q, *_: (jnp.maximum(q - 2, 0), 0, 0)),
            ],
            out_specs=pl.BlockSpec((1, 2, rows, share), lambda q, *_: (q, 0, 0, 0)),
            scratch_shapes=[pltpu.VMEM((2, rows, share), jnp.float32)],
        ),
        out_shape=jax.ShapeDtypeStruct((4, 2, rows, share), jnp.bfloat16),
        compiler_params=pltpu.CompilerParams(vmem_limit_bytes=VMEM),
        cost_estimate=pl.CostEstimate(
            flops=2 * 4 * 2 * rows * share * whole, bytes_accessed=15 << 20, transcendentals=0
        ),
        name="project",
    )(cols, lows, *panels, mine, coulomb, w_own, w_other)


def meet_kernel(starts, places, u, mine, other, out, left_rows):
    rows = mine.shape[1]
    for low in range(2):
        left_rows[pl.ds(low * rows, rows), :] = mine[low]
        left_rows[pl.ds((2 + low) * rows, rows), :] = other[low]
    lane = lax.broadcasted_iota(jnp.int32, (16, 128), 1) // 16
    for target in range(8):
        for two in range(2):
            left, right = [], []
            for q in (2 * two, 2 * two + 1):
                for i in range(4):
                    start = pl.multiple_of(starts[(q * 8 + target) * 4 + i], 16)
                    left.append(left_rows[pl.ds(start, 16), :])
                for i in range(2):
                    place = pl.multiple_of(places[(2 * target + i) % NZ] * 32, 32)
                    right.append(u[q, target // 4, pl.ds(place, 32), :])
            product = contract(jnp.concatenate(left, axis=0), jnp.concatenate(right, axis=0))
            block = jnp.zeros((16, 128), jnp.float32)
            for i in range(8):
                block = jnp.where(lane == i, product[16 * i : 16 * i + 16], block)
            out[target, two] = block


def meet(starts, places, u, mine, other):
    rows, share = mine.shape[1:]
    smem = pl.BlockSpec(memory_space=pltpu.SMEM)
    vmem = pl.BlockSpec(memory_space=pltpu.VMEM)
    return pl.pallas_call(
        meet_kernel,
        in_specs=[smem, smem, vmem, vmem, vmem],
        out_specs=vmem,
        out_shape=jax.ShapeDtypeStruct((8, 2, 16, 128), jnp.float32),
        scratch_shapes=[pltpu.VMEM((4 * rows, share), jnp.bfloat16)],
        compiler_params=pltpu.CompilerParams(vmem_limit_bytes=VMEM),
        name="meet",
    )(starts, places, u, mine, other)


def spread_kernel(mask, terms, out):
    lane = lax.broadcasted_iota(jnp.int32, (16, 128), 1)
    blocks = []
    for two in range(2):
        full = terms[0, two]
        for j in range(1, 8):
            full = full + terms[j, two]
        turned = pltpu.roll(full, 64, 1)
        blocks.append(jnp.where(lane < 64, full, turned))
        blocks.append(jnp.where(lane < 64, turned, full))
    for target in range(out.shape[0]):
        block = jnp.zeros((16, 128), jnp.float32)
        for q in range(4):
            block = jnp.where(mask[target, q : q + 1, :] > 0, blocks[q], block)
        out[target] = block.astype(out.dtype)


def spread(mask, terms):
    vmem = pl.BlockSpec(memory_space=pltpu.VMEM)
    return pl.pallas_call(
        spread_kernel,
        in_specs=[vmem, vmem],
        out_specs=vmem,
        out_shape=jax.ShapeDtypeStruct((32, 16, 128), jnp.float32),
        name="spread",
    )(mask, terms)


def settle_kernel(arrived, out):
    lane = lax.broadcasted_iota(jnp.int32, (16, 128), 1) // 32
    sums = []
    for c in range(2):
        full = arrived[c].astype(jnp.float32)
        for r in range(2 + c, arrived.shape[0], 2):
            full = full + arrived[r].astype(jnp.float32)
        sums.append(full)
    for k in range(2):
        block = jnp.zeros((16, 128), jnp.float32)
        for z in range(2):
            for c in range(2):
                move = (z * 64 + c * 32 - k * 64 - z * 32) % 128
                turned = pltpu.roll(sums[c], move, 1) if move else sums[c]
                block = jnp.where(lane == 2 * z + c, turned, block)
        out[16 * k : 16 * k + 16, :] = block


def settle(arrived):
    vmem = pl.BlockSpec(memory_space=pltpu.VMEM)
    return pl.pallas_call(
        settle_kernel,
        in_specs=[vmem],
        out_specs=vmem,
        out_shape=jax.ShapeDtypeStruct((32, 128), jnp.float32),
        name="settle",
    )(arrived)


def local(pair_matrix, screened, coulomb, q_index):
    bands, share = pair_matrix.shape[1:]
    r, j = lax.axis_index("row"), lax.axis_index("col")
    c, z, y_lo = r % 2, (r // 2) % NZ, r // 16
    x, y = j % NX, 2 * (j // NX) + y_lo

    shifts = jnp.array(SHIFTS, jnp.int32)
    first, second = shifts[None, :], shifts[:, None]
    xs = jnp.mod(x - jnp.where(c == 0, first, second), NX)
    ys = jnp.mod(y - jnp.where(c == 0, second, first), NY)
    cols = ((ys // 2) * NX + xs).reshape(-1).astype(jnp.int32)
    lows = jnp.broadcast_to(ys % 2, (4, 4)).reshape(-1).astype(jnp.int32)

    z_from = jnp.mod(
        jnp.stack([z, z ^ 1])[:, None] - jnp.array(ZSHIFTS, jnp.int32)[None, :], NZ
    ).reshape(-1)
    order = lax.iota(jnp.int32, NZ)
    places = jnp.sum(jnp.where(z_from[None, :] == order[:, None], order[None, :], 0), axis=1)

    q_mine = jnp.stack([2 * r, 2 * r + 1, 2 * (r ^ 1), 2 * (r ^ 1) + 1])
    slot = lax.iota(jnp.int32, 4)
    k_cols = 2 * (4 * lax.iota(jnp.int32, 8)[:, None] + 2 * (slot // 2) + c) + slot % 2
    chosen = jnp.take(q_index, k_cols.reshape(-1), axis=1)
    ks = lax.iota(jnp.int32, q_index.shape[0])
    partner = jnp.sum(
        jnp.where(chosen[None] == q_mine[:, None, None], ks[None, :, None], 0), axis=1
    )
    k_row = partner // 2
    z_place = jnp.sum(
        jnp.where((k_row // 2 % NZ)[..., None] == order, places, 0), axis=-1
    )
    starts = (
        (((k_row % 2) ^ c) * 2 + k_row // 16) * (NZ * 32) + z_place * 32 + (partner % 2) * 16
    )
    starts = starts.reshape(-1).astype(jnp.int32)

    my_cols = 2 * (4 * j + 2 * (slot // 2) + c) + slot % 2
    seen = jnp.take(q_index, my_cols, axis=1).reshape(32, 2, 4)
    mask = (seen[:, None] == q_mine[None, :, None, None]).astype(jnp.int32)
    mask = jnp.broadcast_to(mask[..., None], (32, 4, 2, 4, 16)).reshape(32, 4, 128)

    w_other = send(screened, SWAP)
    own = pair_matrix.reshape(1, 2 * bands, share)
    even = jnp.concatenate([own] + [send(own, along_z(s)) for s in ZSHIFTS[1:]], axis=0)
    stack = jnp.concatenate([even, send(even, ZPAIR)], axis=0).reshape(1, NZ * 32, share)
    parts = [send(stack, first_plane(s)) for s in SHIFTS[1:]]
    panel = jnp.concatenate([stack] + parts, axis=0)
    panels = [panel] + [send(panel, second_plane(s)) for s in SHIFTS[1:]]

    up = jnp.where(c == 0, panels[3][0], parts[2][0])
    down = jnp.where(c == 0, panels[2][0], parts[1][0])
    across = jnp.where(y_lo == 0, up, down)
    mine = jnp.stack(
        [jnp.where(y_lo == 0, stack[0], across), jnp.where(y_lo == 0, across, stack[0])]
    )
    other = send(mine, SWAP)

    u = project(cols, lows, panels, mine, coulomb.reshape(1, share), screened, w_other)
    terms = meet(starts, places.astype(jnp.int32), u, mine, other)
    terms = lax.all_to_all(terms, "col", split_axis=0, concat_axis=0, tiled=True)
    placed = spread(mask, terms)
    arrived = lax.all_to_all(placed, "row", split_axis=0, concat_axis=0, tiled=True)
    return settle(arrived)


def solution(mesh):
    placed = (P("row", None, "col"), P("row", "col", None), P("col"), P())
    return jax.shard_map(
        local, mesh=mesh, in_specs=placed, out_specs=P("row", "col"), check_vma=False
    )
```

time: 478 us -> 105 us (0.22)
  waiting for transfers between devices: 378 us -> 31.2 us
  blocking collectives: 40.9 us -> 17.9 us
  matrix products: 20.4 us -> 0 us
  starting transfers between devices: 8.51 us -> 28.8 us
  Pallas kernels: 0 us -> 17.1 us
  between operations: 13.3 us -> 0.13 us
  local copies, waits for them, and re-layouts: 11.8 us -> 5.61 us
    reduce_scatter x3 -> x0, waiting for transfers between devices: 369 us -> none  [the longest x2 299 us: local(): lax.psum_scatter(project(jnp.int32(0), lax.axis_size('col') * share), 'co...]
    all_gather x1 -> x0, blocking collectives: 40.9 us -> none  [local(): panel = lax.all_gather(pair_matrix, 'row', axis=0, tiled=True)]
    ppermute x0 -> x12, waiting for transfers between devices: none -> 25.1 us  [send(): return lax.ppermute(value, AXES, perm)]
    ppermute x0 -> x12, starting transfers between devices: none -> 22.5 us  [send(): return lax.ppermute(value, AXES, perm)]
    dot_general x5 -> x0, matrix products: 20.4 us -> none  [the longest x2 16.4 us: project(): lax.dot_general(w_block, flat, (((0,), (1,)), ((), ())), preferred_elemen...]
    all_to_all x0 -> x1, blocking collectives: none -> 17.9 us  [local(): lax.all_to_all(placed, 'row', split_axis=0, concat_axis=0, tiled=True)]
    pallas_call x0 -> x4, Pallas kernels: none -> 17.1 us  [the longest x1 11.6 us: project(): pl.pallas_call(project_kernel, grid_spec=pltpu.PrefetchScalarGridSpec(num...]
  transfers between devices with their start and end apart: 4 -> 13, of which waited for: 4 -> 8; matrix products, arithmetic and copies ran while one was open for 3% -> 8% of each run, Pallas kernels for 0% -> 11%
where the time goes in v1:
time: 105 us; the launch traced here: 104 us
  waiting for transfers between devices  31.2 us (30%)
  starting transfers between devices  28.8 us (27%)
  blocking collectives  17.9 us (17%)
  Pallas kernels  17.1 us (16%)
  local copies, waits for them, and re-layouts  5.61 us (5%)
  other arithmetic  3.52 us (3%)
    ppermute x12, waiting for transfers between devices, send(): return lax.ppermute(value, AXES, perm)  25.1 us
    ppermute x12, starting transfers between devices, send(): return lax.ppermute(value, AXES, perm)  22.5 us
    all_to_all x1, blocking collectives, local(): lax.all_to_all(placed, 'row', split_axis=0, concat_axis=0, tiled=True)  17.9 us
    pallas_call x1, Pallas kernels, project(): pl.pallas_call(project_kernel, grid_spec=pltpu.PrefetchScalarGridSpec(num...  11.6 us
    all_to_all x1, starting transfers between devices, local(): lax.all_to_all(terms, 'col', split_axis=0, concat_axis=0, tiled=True)  6.36 us
    all_to_all x1, waiting for transfers between devices, local(): lax.all_to_all(terms, 'col', split_axis=0, concat_axis=0, tiled=True)  6.11 us
    unnamed x7, local copies, waits for them, and re-layouts  2.26 us
  transfers between devices with their start and end apart: 13, of which 8 were waited for; matrix products, arithmetic and copies ran while one was open for 8% of the time, Pallas kernels for 11%

profile of v1, /device:TPU:1, one launch (start us, length us, event | category | flops | bytes accessed | tf_op | source)
XLA Modules:
  0.0 104.3 jit_solution(6578950423310230906)
XLA Ops:
  0.0 3.8 %collective-permute-start = (bf16[1,32,384]{2,1,0:T(8,128)(2,1)}, bf16[1,32,384]{2,1,0:T(8,128)(2,1)S(1)}, u32[]{:S(2)}, u32[]{:S(2)}) collective-permute-start(bf16[1,32,384]{2,1,0:T(8,128)(2,1)} %bitcast.32), channel_id=1, source_target_pairs={{0,32},{8,40},{16,48},{24,56},{32,64},{40,72},{48,80},{56,88},{64,... | collective-permute-start | bytes 73736 | tf_op jit(solution)/shard_map/ppermute | solution.py:48
  3.8 3.0 %collective-permute-start.1 = (bf16[1,32,384]{2,1,0:T(8,128)(2,1)}, bf16[1,32,384]{2,1,0:T(8,128)(2,1)S(1)}, u32[]{:S(2)}, u32[]{:S(2)}) collective-permute-start(bf16[1,32,384]{2,1,0:T(8,128)(2,1)} %bitcast.33), channel_id=1, source_target_pairs={{0,96},{8,104},{16,112},{24,120},{32,0},{40,8},{48,16},{56,24},{64... | collective-permute-start | bytes 73736 | tf_op jit(solution)/shard_map/ppermute | solution.py:48
  6.9 4.5 %collective-permute-start.2 = (bf16[1,32,384]{2,1,0:T(8,128)(2,1)}, bf16[1,32,384]{2,1,0:T(8,128)(2,1)S(1)}, u32[]{:S(2)}, u32[]{:S(2)}) collective-permute-start(bf16[1,32,384]{2,1,0:T(8,128)(2,1)} %bitcast.34), channel_id=1, source_target_pairs={{0,64},{8,72},{16,80},{24,88},{32,96},{40,104},{48,112},{56,120},{... | collective-permute-start | bytes 73736 | tf_op jit(solution)/shard_map/ppermute | solution.py:48
  11.3 1.5 %collective-permute-start.10 = (bf16[2,384,3072]{2,1,0:T(8,128)(2,1)}, bf16[2,384,3072]{2,1,0:T(8,128)(2,1)}, u32[]{:S(2)}, u32[]{:S(2)}) collective-permute-start(bf16[2,384,3072]{2,1,0:T(8,128)(2,1)} %w_own.1), channel_id=1, source_target_pairs={{0,8},{8,0},{16,24},{24,16},{32,40},{40,32},{48,56},{56,48},{64,72... | collective-permute-start | bytes 14155784 | tf_op jit(solution)/shard_map/ppermute | solution.py:48
  20.3 3.7 %collective-permute-done.3 = bf16[4,32,384]{2,1,0:T(8,128)(2,1)S(1)} collective-permute-done((bf16[4,32,384]{2,1,0:T(8,128)(2,1)S(1)}, bf16[4,32,384]{2,1,0:T(8,128)(2,1)S(1)}, u32[]{:S(2)}, u32[]{:S(2)}) %collective-permute-start.3) | collective-permute-done | bytes 98336 | tf_op jit(solution)/shard_map/ppermute | solution.py:48
  23.9 1.4 %collective-permute-start.5 = (bf16[1,256,384]{2,1,0:T(8,128)(2,1)S(1)}, bf16[1,256,384]{2,1,0:T(8,128)(2,1)S(1)}, u32[]{:S(2)}, u32[]{:S(2)}) collective-permute-start(bf16[1,256,384]{2,1,0:T(8,128)(2,1)S(1)} %bitcast.23), channel_id=1, source_target_pairs={{0,1},{8,136},{16,17},{24,152},{32,33},{40,168},{48,49},{56,184},{... | collective-permute-start | bytes 589832 | tf_op jit(solution)/shard_map/ppermute | solution.py:48
  25.3 1.5 %collective-permute-start.6 = (bf16[1,256,384]{2,1,0:T(8,128)(2,1)S(1)}, bf16[1,256,384]{2,1,0:T(8,128)(2,1)S(1)}, u32[]{:S(2)}, u32[]{:S(2)}) collective-permute-start(bf16[1,256,384]{2,1,0:T(8,128)(2,1)S(1)} %bitcast.24), channel_id=1, source_target_pairs={{0,3},{8,140},{16,19},{24,156},{32,35},{40,172},{48,51},{56,188},{... | collective-permute-start | bytes 589832 | tf_op jit(solution)/shard_map/ppermute | solution.py:48
  26.8 1.6 %collective-permute-start.4 = (bf16[1,256,384]{2,1,0:T(8,128)(2,1)S(1)}, bf16[1,256,384]{2,1,0:T(8,128)(2,1)S(1)}, u32[]{:S(2)}, u32[]{:S(2)}) collective-permute-start(bf16[1,256,384]{2,1,0:T(8,128)(2,1)S(1)} %bitcast.25), channel_id=1, source_target_pairs={{0,2},{8,12},{16,18},{24,28},{32,34},{40,44},{48,50},{56,60},{64,6... | collective-permute-start | bytes 589832 | tf_op jit(solution)/shard_map/ppermute | solution.py:48
  29.1 1.0 collective-permute-done.5
  30.1 1.5 %collective-permute-done.6 = bf16[1,256,384]{2,1,0:T(8,128)(2,1)S(1)} collective-permute-done((bf16[1,256,384]{2,1,0:T(8,128)(2,1)S(1)}, bf16[1,256,384]{2,1,0:T(8,128)(2,1)S(1)}, u32[]{:S(2)}, u32[]{:S(2)}) %collective-permute-start.6) | collective-permute-done | bytes 196640 | tf_op jit(solution)/shard_map/ppermute | solution.py:48
  31.6 1.8 %collective-permute-done.4 = bf16[1,256,384]{2,1,0:T(8,128)(2,1)S(1)} collective-permute-done((bf16[1,256,384]{2,1,0:T(8,128)(2,1)S(1)}, bf16[1,256,384]{2,1,0:T(8,128)(2,1)S(1)}, u32[]{:S(2)}, u32[]{:S(2)}) %collective-permute-start.4) | collective-permute-done | bytes 196640 | tf_op jit(solution)/shard_map/ppermute | solution.py:48
  33.5 1.0 collective-permute-start.8
  34.5 1.8 %collective-permute-start.9 = (bf16[4,256,384]{2,1,0:T(8,128)(2,1)S(1)}, bf16[4,256,384]{2,1,0:T(8,128)(2,1)S(1)}, u32[]{:S(2)}, u32[]{:S(2)}) collective-permute-start(bf16[4,256,384]{2,1,0:T(8,128)(2,1)S(1)} %pad_maximum_fusion.p0), channel_id=1, source_target_pairs={{0,132},{8,11},{16,148},{24,27},{32,164},{40,43},{48,180},{56,59},... | collective-permute-start | bytes 2359304 | tf_op jit(solution)/shard_map/ppermute | solution.py:48
  36.4 1.3 %collective-permute-start.7 = (bf16[4,256,384]{2,1,0:T(8,128)(2,1)S(1)}, bf16[4,256,384]{2,1,0:T(8,128)(2,1)S(1)}, u32[]{:S(2)}, u32[]{:S(2)}) collective-permute-start(bf16[4,256,384]{2,1,0:T(8,128)(2,1)S(1)} %pad_maximum_fusion.p0), channel_id=1, source_target_pairs={{0,4},{8,10},{16,20},{24,26},{32,36},{40,42},{48,52},{56,58},{64,6... | collective-permute-start | bytes 2359304 | tf_op jit(solution)/shard_map/ppermute | solution.py:48
  37.8 8.2 %collective-permute-done.8.p2 = bf16[4,256,384]{2,1,0:T(8,128)(2,1)S(1)} collective-permute-done((bf16[4,256,384]{2,1,0:T(8,128)(2,1)S(1)}, bf16[4,256,384]{2,1,0:T(8,128)(2,1)S(1)}, u32[]{:S(2)}, u32[]{:S(2)}) %collective-permute-start.8) | collective-permute-done | bytes 786464 | tf_op jit(solution)/shard_map/ppermute | solution.py:48
  45.9 7.7 %collective-permute-done.9.p3 = bf16[4,256,384]{2,1,0:T(8,128)(2,1)S(1)} collective-permute-done((bf16[4,256,384]{2,1,0:T(8,128)(2,1)S(1)}, bf16[4,256,384]{2,1,0:T(8,128)(2,1)S(1)}, u32[]{:S(2)}, u32[]{:S(2)}) %collective-permute-start.9) | collective-permute-done | bytes 786464 | tf_op jit(solution)/shard_map/ppermute | solution.py:48
  54.0 1.3 %collective-permute-done.7.p1 = bf16[4,256,384]{2,1,0:T(8,128)(2,1)S(1)} collective-permute-done((bf16[4,256,384]{2,1,0:T(8,128)(2,1)S(1)}, bf16[4,256,384]{2,1,0:T(8,128)(2,1)S(1)}, u32[]{:S(2)}, u32[]{:S(2)}) %collective-permute-start.7) | collective-permute-done | bytes 786464 | tf_op jit(solution)/shard_map/ppermute | solution.py:48
  55.3 11.6 %project.1.u = bf16[4,2,256,384]{3,2,1,0:T(8,128)(2,1)S(1)} custom-call(s32[16]{0:T(128)S(1)} %fusion.7.cols, s32[16]{0:T(128)S(1)} %get-tuple-element.7.lows, bf16[4,256,384]{2,1,0:T(8,128)(2,1)S(1)} %pad_maximum_fusion.p0, bf16[4,256,384]{2,1,0:T(8,128)(2,1)S(1)} %collective-permute-done.7.p1, bf16[4,256,384]{2,1,0:T(8,128)(2,1)S(1)} %collective-permute-done.8.p2, ...), custom_call_target="tpu_custom_call" | custom-call | flops 4831838208 | bytes 15728640 | tf_op jit(solution)/shard_map/project/pallas_call | solution.py:89
  66.9 2.0 %meet.1 = f32[8,2,16,128]{3,2,1,0:T(8,128)} custom-call(s32[128]{0:T(128)S(1)} %fusion.15.starts, s32[8]{0:T(128)S(1)} %select_reduce_fusion.2.places, bf16[4,2,256,384]{3,2,1,0:T(8,128)(2,1)S(1)} %project.1.u, bf16[2,256,384]{2,1,0:T(8,128)(2,1)S(1)} %pad_maximum_fusion.1.mine, bf16[2,256,384]{2,1,0:T(8,128)(2,1)S(1)} %collective-permute-done.11.other), custom_call_target="tpu_custom_call" | custom-call | tf_op jit(solution)/shard_map/meet/pallas_call | solution.py:140
  69.0 6.4 %all-to-all-start = ((f32[8,2,16,128]{3,2,1,0:T(8,128)}), f32[8,2,16,128]{3,2,1,0:T(8,128)S(1)}, u32[]{:S(2)}, u32[]{:S(2)}) async-start(f32[8,2,16,128]{3,2,1,0:T(8,128)} %meet.1), calls=%async_computation | async-start | bytes 262144 | tf_op jit(solution)/shard_map/all_to_all | solution.py:267
  76.2 6.1 %all-to-all-done.terms = f32[8,2,16,128]{3,2,1,0:T(8,128)S(1)} async-done(((f32[8,2,16,128]{3,2,1,0:T(8,128)}), f32[8,2,16,128]{3,2,1,0:T(8,128)S(1)}, u32[]{:S(2)}, u32[]{:S(2)}) %all-to-all-start) | async-done | bytes 131104 | tf_op jit(solution)/shard_map/all_to_all | solution.py:267
  82.9 1.8 %spread.1 = f32[32,16,128]{2,1,0:T(8,128)} custom-call(s32[32,4,128]{2,1,0:T(4,128)} %copy.21.mask, f32[8,2,16,128]{3,2,1,0:T(8,128)} %copy-done), custom_call_target="tpu_custom_call" | custom-call | tf_op jit(solution)/shard_map/spread/pallas_call | solution.py:170
  84.7 17.9 %all_to_all.10.arrived = f32[32,16,128]{2,1,0:T(8,128)} all-to-all(f32[32,16,128]{2,1,0:T(8,128)} %spread.1), channel_id=1, replica_groups=mesh['row'=32,'col'=8] {'row'}, dimensions={0} | all-to-all | bytes 524288 | tf_op jit(solution)/shard_map/all_to_all | solution.py:269
  102.7 1.7 %settle.1 = f32[32,128]{1,0:T(8,128)} custom-call(f32[32,16,128]{2,1,0:T(8,128)} %all_to_all.10.arrived), custom_call_target="tpu_custom_call" | custom-call | tf_op jit(solution)/shard_map/settle/pallas_call | solution.py:199
  (59 shorter events, 10.2 us)
Async XLA Ops:
  0.0 18.6 %collective-permute-start = (bf16[1,32,384]{2,1,0:T(8,128)(2,1)}, bf16[1,32,384]{2,1,0:T(8,128)(2,1)S(1)}, u32[]{:S(2)}, u32[]{:S(2)}) collective-permute-start(bf16[1,32,384]{2,1,0:T(8,128)(2,1)} %bitcast.32), channel_id=1, source_target_pairs={{0,32},{8,40},{16,48},{24,56},{32,64},{40,72},{48,80},{56,88},{64,... | collective-permute-start | bytes 73736 | tf_op jit(solution)/shard_map/ppermute | solution.py:48
  3.8 14.8 %collective-permute-start.1 = (bf16[1,32,384]{2,1,0:T(8,128)(2,1)}, bf16[1,32,384]{2,1,0:T(8,128)(2,1)S(1)}, u32[]{:S(2)}, u32[]{:S(2)}) collective-permute-start(bf16[1,32,384]{2,1,0:T(8,128)(2,1)} %bitcast.33), channel_id=1, source_target_pairs={{0,96},{8,104},{16,112},{24,120},{32,0},{40,8},{48,16},{56,24},{64... | collective-permute-start | bytes 73736 | tf_op jit(solution)/shard_map/ppermute | solution.py:48
  6.9 11.8 %collective-permute-start.2 = (bf16[1,32,384]{2,1,0:T(8,128)(2,1)}, bf16[1,32,384]{2,1,0:T(8,128)(2,1)S(1)}, u32[]{:S(2)}, u32[]{:S(2)}) collective-permute-start(bf16[1,32,384]{2,1,0:T(8,128)(2,1)} %bitcast.34), channel_id=1, source_target_pairs={{0,64},{8,72},{16,80},{24,88},{32,96},{40,104},{48,112},{56,120},{... | collective-permute-start | bytes 73736 | tf_op jit(solution)/shard_map/ppermute | solution.py:48
  11.3 44.0 %collective-permute-start.10 = (bf16[2,384,3072]{2,1,0:T(8,128)(2,1)}, bf16[2,384,3072]{2,1,0:T(8,128)(2,1)}, u32[]{:S(2)}, u32[]{:S(2)}) collective-permute-start(bf16[2,384,3072]{2,1,0:T(8,128)(2,1)} %w_own.1), channel_id=1, source_target_pairs={{0,8},{8,0},{16,24},{24,16},{32,40},{40,32},{48,56},{56,48},{64,72... | collective-permute-start | bytes 14155784 | tf_op jit(solution)/shard_map/ppermute | solution.py:48
  19.4 4.5 %collective-permute-start.3 = (bf16[4,32,384]{2,1,0:T(8,128)(2,1)S(1)}, bf16[4,32,384]{2,1,0:T(8,128)(2,1)S(1)}, u32[]{:S(2)}, u32[]{:S(2)}) collective-permute-start(bf16[4,32,384]{2,1,0:T(8,128)(2,1)S(1)} %pad_maximum_fusion.2), channel_id=1, source_target_pairs={{0,16},{8,24},{16,0},{24,8},{32,48},{40,56},{48,32},{56,40},{64,80... | collective-permute-start | bytes 294920 | tf_op jit(solution)/shard_map/ppermute | solution.py:48
  23.9 6.2 %collective-permute-start.5 = (bf16[1,256,384]{2,1,0:T(8,128)(2,1)S(1)}, bf16[1,256,384]{2,1,0:T(8,128)(2,1)S(1)}, u32[]{:S(2)}, u32[]{:S(2)}) collective-permute-start(bf16[1,256,384]{2,1,0:T(8,128)(2,1)S(1)} %bitcast.23), channel_id=1, source_target_pairs={{0,1},{8,136},{16,17},{24,152},{32,33},{40,168},{48,49},{56,184},{... | collective-permute-start | bytes 589832 | tf_op jit(solution)/shard_map/ppermute | solution.py:48
  25.3 6.3 %collective-permute-start.6 = (bf16[1,256,384]{2,1,0:T(8,128)(2,1)S(1)}, bf16[1,256,384]{2,1,0:T(8,128)(2,1)S(1)}, u32[]{:S(2)}, u32[]{:S(2)}) collective-permute-start(bf16[1,256,384]{2,1,0:T(8,128)(2,1)S(1)} %bitcast.24), channel_id=1, source_target_pairs={{0,3},{8,140},{16,19},{24,156},{32,35},{40,172},{48,51},{56,188},{... | collective-permute-start | bytes 589832 | tf_op jit(solution)/shard_map/ppermute | solution.py:48
  26.8 6.5 %collective-permute-start.4 = (bf16[1,256,384]{2,1,0:T(8,128)(2,1)S(1)}, bf16[1,256,384]{2,1,0:T(8,128)(2,1)S(1)}, u32[]{:S(2)}, u32[]{:S(2)}) collective-permute-start(bf16[1,256,384]{2,1,0:T(8,128)(2,1)S(1)} %bitcast.25), channel_id=1, source_target_pairs={{0,2},{8,12},{16,18},{24,28},{32,34},{40,44},{48,50},{56,60},{64,6... | collective-permute-start | bytes 589832 | tf_op jit(solution)/shard_map/ppermute | solution.py:48
  33.5 12.4 %collective-permute-start.8 = (bf16[4,256,384]{2,1,0:T(8,128)(2,1)S(1)}, bf16[4,256,384]{2,1,0:T(8,128)(2,1)S(1)}, u32[]{:S(2)}, u32[]{:S(2)}) collective-permute-start(bf16[4,256,384]{2,1,0:T(8,128)(2,1)S(1)} %pad_maximum_fusion.p0), channel_id=1, source_target_pairs={{0,128},{8,9},{16,144},{24,25},{32,160},{40,41},{48,176},{56,57},{... | collective-permute-start | bytes 2359304 | tf_op jit(solution)/shard_map/ppermute | solution.py:48
  34.5 19.1 %collective-permute-start.9 = (bf16[4,256,384]{2,1,0:T(8,128)(2,1)S(1)}, bf16[4,256,384]{2,1,0:T(8,128)(2,1)S(1)}, u32[]{:S(2)}, u32[]{:S(2)}) collective-permute-start(bf16[4,256,384]{2,1,0:T(8,128)(2,1)S(1)} %pad_maximum_fusion.p0), channel_id=1, source_target_pairs={{0,132},{8,11},{16,148},{24,27},{32,164},{40,43},{48,180},{56,59},... | collective-permute-start | bytes 2359304 | tf_op jit(solution)/shard_map/ppermute | solution.py:48
  36.4 18.9 %collective-permute-start.7 = (bf16[4,256,384]{2,1,0:T(8,128)(2,1)S(1)}, bf16[4,256,384]{2,1,0:T(8,128)(2,1)S(1)}, u32[]{:S(2)}, u32[]{:S(2)}) collective-permute-start(bf16[4,256,384]{2,1,0:T(8,128)(2,1)S(1)} %pad_maximum_fusion.p0), channel_id=1, source_target_pairs={{0,4},{8,10},{16,20},{24,26},{32,36},{40,42},{48,52},{56,58},{64,6... | collective-permute-start | bytes 2359304 | tf_op jit(solution)/shard_map/ppermute | solution.py:48
  53.8 13.2 %collective-permute-start.11 = (bf16[2,256,384]{2,1,0:T(8,128)(2,1)S(1)}, bf16[2,256,384]{2,1,0:T(8,128)(2,1)S(1)}, u32[]{:S(2)}, u32[]{:S(2)}) collective-permute-start(bf16[2,256,384]{2,1,0:T(8,128)(2,1)S(1)} %pad_maximum_fusion.1.mine), channel_id=1, source_target_pairs={{0,8},{8,0},{16,24},{24,16},{32,40},{40,32},{48,56},{56,48},{64,72... | collective-permute-start | bytes 1179656 | tf_op jit(solution)/shard_map/ppermute | solution.py:48
  69.0 13.3 %all-to-all-start = ((f32[8,2,16,128]{3,2,1,0:T(8,128)}), f32[8,2,16,128]{3,2,1,0:T(8,128)S(1)}, u32[]{:S(2)}, u32[]{:S(2)}) async-start(f32[8,2,16,128]{3,2,1,0:T(8,128)} %meet.1), calls=%async_computation | async-start | bytes 262144 | tf_op jit(solution)/shard_map/all_to_all | solution.py:267
  82.3 0.7 copy-start

commit v2 on v1

--- a/solution.py
+++ b/solution.py
@@ -9,7 +9,7 @@
 NX, NY, NZ, NCORE = 4, 4, 8, 2
 SHIFTS = (0, 2, 1, -1)
 ZSHIFTS = (0, 2, -2, 4)
-VMEM = 48 * 1024 * 1024
+VMEM = 32 * 1024 * 1024
 
 
 def device_index(x, y, z, c):
@@ -52,26 +52,24 @@
     return lax.dot_general(a, b, (((1,), (1,)), ((), ())), preferred_element_type=jnp.float32)
 
 
-def project_kernel(cols, lows, p0, p1, p2, p3, mine, coulomb, w_own, w_other, out, total):
-    share = p0.shape[2]
+def product(panel, half, w, spots):
+    left = jnp.concatenate([panel[2 * half], panel[2 * half + 1]], axis=1)
+    return contract(left, jnp.concatenate([w(spots[0]), w(spots[1])], axis=1))
+
+
+def begin_kernel(cols, lows, panel, w_own, w_other, out, kept):
+    share = panel.shape[2]
 
     def run(w):
-        total[...] = jnp.zeros_like(total)
-        for k, panel in enumerate((p0, p1, p2, p3)):
-            for half in range(2):
-                at = 4 * k + 2 * half
-                left = jnp.concatenate([panel[2 * half], panel[2 * half + 1]], axis=1)
-                right = jnp.concatenate(
-                    [
-                        w[0, :, pl.ds(pl.multiple_of(cols[at + i] * share, share), share)]
-                        for i in range(2)
-                    ],
-                    axis=1,
-                )
-                total[lows[at]] += contract(left, right)
-        for low in range(2):
-            bare = (2.0 * coulomb[...]) * mine[low].astype(jnp.float32)
-            out[0, low] = (bare - total[low]).astype(out.dtype)
+        def block(at):
+            return w[0, :, pl.ds(pl.multiple_of(cols[at] * share, share), share)]
+
+        out[...] = jnp.zeros_like(out)
+        for half in range(2):
+            at = 2 * half
+            out[0, lows[at]] -= product(panel, half, block, (at, at + 1))
+        for i in range(4):
+            kept[0, :, i * share : (i + 1) * share] = block(4 + i)
 
     @pl.when(pl.program_id(0) < 2)
     def _():
@@ -82,39 +80,107 @@
         run(w_other)
 
 
-def project(cols, lows, panels, mine, coulomb, w_own, w_other):
-    rows, share = panels[0].shape[1:]
+def more_kernel(cols, lows, p2, p3, before, mine, coulomb, w_own, w_other, out):
+    share = p2.shape[2]
+
+    def run(w):
+        def block(at):
+            return w[0, :, pl.ds(pl.multiple_of(cols[at] * share, share), share)]
+
+        for low in range(2):
+            bare = (2.0 * coulomb[...]) * mine[low].astype(jnp.float32)
+            out[0, low] = before[0, low] + bare
+        for k, panel in ((2, p2), (3, p3)):
+            for half in range(2):
+                at = 4 * k + 2 * half
+                out[0, lows[at]] -= product(panel, half, block, (at, at + 1))
+
+    @pl.when(pl.program_id(0) < 2)
+    def _():
+        run(w_own)
+
+    @pl.when(pl.program_id(0) >= 2)
+    def _():
+        run(w_other)
+
+
+def fixed(shape):
+    return pl.BlockSpec(shape, lambda q, *_: (0,) * len(shape))
+
+
+def transfer_specs(share, whole):
+    return [
+        pl.BlockSpec((1, share, whole), lambda q, *_: (jnp.minimum(q, 1), 0, 0)),
+        pl.BlockSpec((1, share, whole), lambda q, *_: (jnp.maximum(q - 2, 0), 0, 0)),
+    ]
+
+
+def begin(cols, lows, panel, w_own, w_other):
+    rows, share = panel.shape[1:]
     whole = w_own.shape[2]
-    fixed = lambda shape: pl.BlockSpec(shape, lambda q, *_: (0,) * len(shape))
-    return pl.pallas_call(
-        project_kernel,
+    return pl.pallas_call(
+        begin_kernel,
         grid_spec=pltpu.PrefetchScalarGridSpec(
             num_scalar_prefetch=2,
             grid=(4,),
-            in_specs=[fixed((4, rows, share))] * 4
-            + [
+            in_specs=[fixed((4, rows, share))] + transfer_specs(share, whole),
+            out_specs=[
+                pl.BlockSpec((1, 2, rows, share), lambda q, *_: (q, 0, 0, 0)),
+                pl.BlockSpec((1, share, 4 * share), lambda q, *_: (q, 0, 0)),
+            ],
+        ),
+        out_shape=[
+            jax.ShapeDtypeStruct((4, 2, rows, share), jnp.float32),
+            jax.ShapeDtypeStruct((4, share, 4 * share), jnp.bfloat16),
+        ],
+        compiler_params=pltpu.CompilerParams(vmem_limit_bytes=VMEM),
+        cost_estimate=pl.CostEstimate(
+            flops=2 * 4 * 4 * rows * share * share, bytes_accessed=17 << 20, transcendentals=0
+        ),
+        name="begin",
+    )(cols, lows, panel, w_own, w_other)
+
+
+def more(cols, lows, p2, p3, before, mine, coulomb, w_own, w_other):
+    rows, share = p2.shape[1:]
+    whole = w_own.shape[2]
+    total = pl.BlockSpec((1, 2, rows, share), lambda q, *_: (q, 0, 0, 0))
+    return pl.pallas_call(
+        more_kernel,
+        grid_spec=pltpu.PrefetchScalarGridSpec(
+            num_scalar_prefetch=2,
+            grid=(4,),
+            in_specs=[
+                fixed((4, rows, share)),
+                fixed((4, rows, share)),
+                total,
                 fixed((2, rows, share)),
                 fixed((1, share)),
-                pl.BlockSpec((1, share, whole), lambda q, *_: (jnp.minimum(q, 1), 0, 0)),
-                pl.BlockSpec((1, share, whole), lambda q, *_: (jnp.maximum(q - 2, 0), 0, 0)),
-            ],
-            out_specs=pl.BlockSpec((1, 2, rows, share), lambda q, *_: (q, 0, 0, 0)),
-            scratch_shapes=[pltpu.VMEM((2, rows, share), jnp.float32)],
-        ),
-        out_shape=jax.ShapeDtypeStruct((4, 2, rows, share), jnp.bfloat16),
+            ]
+            + transfer_specs(share, whole),
+            out_specs=total,
+        ),
+        out_shape=jax.ShapeDtypeStruct((4, 2, rows, share), jnp.float32),
         compiler_params=pltpu.CompilerParams(vmem_limit_bytes=VMEM),
         cost_estimate=pl.CostEstimate(
-            flops=2 * 4 * 2 * rows * share * whole, bytes_accessed=15 << 20, transcendentals=0
-        ),
-        name="project",
-    )(cols, lows, *panels, mine, coulomb, w_own, w_other)
-
-
-def meet_kernel(starts, places, u, mine, other, out, left_rows):
-    rows = mine.shape[1]
+            flops=2 * 4 * 8 * rows * share * share, bytes_accessed=17 << 20, transcendentals=0
+        ),
+        name="more",
+    )(cols, lows, p2, p3, before, mine, coulomb, w_own, w_other)
+
+
+def finish_kernel(starts, places, lows, panel, before, kept, mine, other, out, left_rows, total, u):
+    rows, share = mine.shape[1:]
     for low in range(2):
         left_rows[pl.ds(low * rows, rows), :] = mine[low]
         left_rows[pl.ds((2 + low) * rows, rows), :] = other[low]
+    for q in range(4):
+        total[...] = before[q]
+        for half in range(2):
+            left = jnp.concatenate([panel[2 * half], panel[2 * half + 1]], axis=1)
+            right = kept[q, :, 2 * half * share : (2 * half + 2) * share]
+            total[lows[4 + 2 * half]] -= contract(left, right)
+        u[q] = total[...].astype(u.dtype)
     lane = lax.broadcasted_iota(jnp.int32, (16, 128), 1) // 16
     for target in range(8):
         for two in range(2):
@@ -126,26 +192,33 @@
                 for i in range(2):
                     place = pl.multiple_of(places[(2 * target + i) % NZ] * 32, 32)
                     right.append(u[q, target // 4, pl.ds(place, 32), :])
-            product = contract(jnp.concatenate(left, axis=0), jnp.concatenate(right, axis=0))
+            met = contract(jnp.concatenate(left, axis=0), jnp.concatenate(right, axis=0))
             block = jnp.zeros((16, 128), jnp.float32)
             for i in range(8):
-                block = jnp.where(lane == i, product[16 * i : 16 * i + 16], block)
+                block = jnp.where(lane == i, met[16 * i : 16 * i + 16], block)
             out[target, two] = block
 
 
-def meet(starts, places, u, mine, other):
+def finish(starts, places, lows, panel, before, kept, mine, other):
     rows, share = mine.shape[1:]
     smem = pl.BlockSpec(memory_space=pltpu.SMEM)
     vmem = pl.BlockSpec(memory_space=pltpu.VMEM)
     return pl.pallas_call(
-        meet_kernel,
-        in_specs=[smem, smem, vmem, vmem, vmem],
+        finish_kernel,
+        in_specs=[smem] * 3 + [vmem] * 5,
         out_specs=vmem,
         out_shape=jax.ShapeDtypeStruct((8, 2, 16, 128), jnp.float32),
-        scratch_shapes=[pltpu.VMEM((4 * rows, share), jnp.bfloat16)],
+        scratch_shapes=[
+            pltpu.VMEM((4 * rows, share), jnp.bfloat16),
+            pltpu.VMEM((2, rows, share), jnp.float32),
+            pltpu.VMEM((4, 2, rows, share), jnp.bfloat16),
+        ],
         compiler_params=pltpu.CompilerParams(vmem_limit_bytes=VMEM),
-        name="meet",
-    )(starts, places, u, mine, other)
+        cost_estimate=pl.CostEstimate(
+            flops=2 * 4 * 4 * rows * share * share, bytes_accessed=9 << 20, transcendentals=0
+        ),
+        name="finish",
+    )(starts, places, lows, panel, before, kept, mine, other)
 
 
 def spread_kernel(mask, terms, out):
@@ -208,6 +281,12 @@
 def local(pair_matrix, screened, coulomb, q_index):
     bands, share = pair_matrix.shape[1:]
     r, j = lax.axis_index("row"), lax.axis_index("col")
+    w_other = send(screened, SWAP)
+    own = pair_matrix.reshape(1, 2 * bands, share)
+    even = jnp.concatenate([own] + [send(own, along_z(s)) for s in ZSHIFTS[1:]], axis=0)
+    stack = jnp.concatenate([even, send(even, ZPAIR)], axis=0).reshape(1, NZ * 32, share)
+    parts = [send(stack, first_plane(s)) for s in SHIFTS[1:]]
+    r, j, q_index, _ = lax.optimization_barrier((r, j, q_index, stack))
     c, z, y_lo = r % 2, (r // 2) % NZ, r // 16
     x, y = j % NX, 2 * (j // NX) + y_lo
 
@@ -246,11 +325,6 @@
     mask = (seen[:, None] == q_mine[None, :, None, None]).astype(jnp.int32)
     mask = jnp.broadcast_to(mask[..., None], (32, 4, 2, 4, 16)).reshape(32, 4, 128)
 
-    w_other = send(screened, SWAP)
-    own = pair_matrix.reshape(1, 2 * bands, share)
-    even = jnp.concatenate([own] + [send(own, along_z(s)) for s in ZSHIFTS[1:]], axis=0)
-    stack = jnp.concatenate([even, send(even, ZPAIR)], axis=0).reshape(1, NZ * 32, share)
-    parts = [send(stack, first_plane(s)) for s in SHIFTS[1:]]
     panel = jnp.concatenate([stack] + parts, axis=0)
     panels = [panel] + [send(panel, second_plane(s)) for s in SHIFTS[1:]]
 
@@ -262,8 +336,13 @@
     )
     other = send(mine, SWAP)
 
-    u = project(cols, lows, panels, mine, coulomb.reshape(1, share), screened, w_other)
-    terms = meet(starts, places.astype(jnp.int32), u, mine, other)
+    total, kept = begin(cols, lows, panel, screened, w_other)
+    total = more(
+        cols, lows, panels[2], panels[3], total, mine, coulomb.reshape(1, share), screened, w_other
+    )
+    terms = finish(
+        starts, places.astype(jnp.int32), lows, panels[1], total, kept, mine, other
+    )
     terms = lax.all_to_all(terms, "col", split_axis=0, concat_axis=0, tiled=True)
     placed = spread(mask, terms)
     arrived = lax.all_to_all(placed, "row", split_axis=0, concat_axis=0, tiled=True)

time: 105 us -> 114 us (1.086)
  waiting for transfers between devices: 31.2 us -> 24.3 us
  Pallas kernels: 17.1 us -> 22 us
  starting transfers between devices: 28.8 us -> 33.4 us
  blocking collectives: 17.9 us -> 21.9 us
  local copies, waits for them, and re-layouts: 5.61 us -> 7.96 us
    ppermute x12, waiting for transfers between devices: 25.1 us -> 18.2 us  [send(): return lax.ppermute(value, AXES, perm)]
    pallas_call x2 -> x3, Pallas kernels: 13.6 us -> 18.6 us  [the longest x1 7.37 us: more(): pl.pallas_call(more_kernel, grid_spec=pltpu.PrefetchScalarGridSpec(num_sc...]
    all_to_all x1, starting transfers between devices: 6.36 us -> 10.7 us  [local(): lax.all_to_all(terms, 'col', split_axis=0, concat_axis=0, tiled=True)]
    all_to_all x1, blocking collectives: 17.9 us -> 21.9 us  [local(): lax.all_to_all(placed, 'row', split_axis=0, concat_axis=0, tiled=True)]
    unnamed x7 -> x12, local copies, waits for them, and re-layouts: 2.26 us -> 3.77 us
  transfers between devices with their start and end apart: 13 -> 13, of which waited for: 8 -> 5; matrix products, arithmetic and copies ran while one was open for 8% -> 7% of each run, Pallas kernels for 11% -> 12%
where the time goes in v2:
time: 114 us; the launch traced here: 113 us
  starting transfers between devices  33.4 us (29%)
  waiting for transfers between devices  24.3 us (21%)
  Pallas kernels  22 us (19%)
  blocking collectives  21.9 us (19%)
  local copies, waits for them, and re-layouts  7.96 us (7%)
  other arithmetic  3.51 us (3%)
    ppermute x12, starting transfers between devices, send(): return lax.ppermute(value, AXES, perm)  22.8 us
    all_to_all x1, blocking collectives, local(): lax.all_to_all(placed, 'row', split_axis=0, concat_axis=0, tiled=True)  21.9 us
    ppermute x12, waiting for transfers between devices, send(): return lax.ppermute(value, AXES, perm)  18.2 us
    all_to_all x1, starting transfers between devices, local(): lax.all_to_all(terms, 'col', split_axis=0, concat_axis=0, tiled=True)  10.7 us
    pallas_call x1, Pallas kernels, more(): pl.pallas_call(more_kernel, grid_spec=pltpu.PrefetchScalarGridSpec(num_sc...  7.37 us
    pallas_call x1, Pallas kernels, begin(): pl.pallas_call(begin_kernel, grid_spec=pltpu.PrefetchScalarGridSpec(num_s...  6.25 us
    all_to_all x1, waiting for transfers between devices, local(): lax.all_to_all(terms, 'col', split_axis=0, concat_axis=0, tiled=True)  6.11 us
    pallas_call x1, Pallas kernels, finish(): pl.pallas_call(finish_kernel, in_specs=[smem] * 3 + [vmem] * 5, out_specs...  4.96 us
  transfers between devices with their start and end apart: 13, of which 5 were waited for; matrix products, arithmetic and copies ran while one was open for 7% of the time, Pallas kernels for 12%

profile of v2, /device:TPU:1, one launch (start us, length us, event | category | flops | bytes accessed | tf_op | source)
XLA Modules:
  0.0 113.3 jit_solution(4503765670272386481)
XLA Ops:
  0.0 3.8 %collective-permute-start = (bf16[1,32,384]{2,1,0:T(8,128)(2,1)}, bf16[1,32,384]{2,1,0:T(8,128)(2,1)S(1)}, u32[]{:S(2)}, u32[]{:S(2)}) collective-permute-start(bf16[1,32,384]{2,1,0:T(8,128)(2,1)} %bitcast.34), channel_id=1, source_target_pairs={{0,32},{8,40},{16,48},{24,56},{32,64},{40,72},{48,80},{56,88},{64,... | collective-permute-start | bytes 73736 | tf_op jit(solution)/shard_map/ppermute | solution.py:48
  3.8 3.0 %collective-permute-start.1 = (bf16[1,32,384]{2,1,0:T(8,128)(2,1)}, bf16[1,32,384]{2,1,0:T(8,128)(2,1)S(1)}, u32[]{:S(2)}, u32[]{:S(2)}) collective-permute-start(bf16[1,32,384]{2,1,0:T(8,128)(2,1)} %bitcast.35), channel_id=1, source_target_pairs={{0,96},{8,104},{16,112},{24,120},{32,0},{40,8},{48,16},{56,24},{64... | collective-permute-start | bytes 73736 | tf_op jit(solution)/shard_map/ppermute | solution.py:48
  6.9 4.5 %collective-permute-start.2 = (bf16[1,32,384]{2,1,0:T(8,128)(2,1)}, bf16[1,32,384]{2,1,0:T(8,128)(2,1)S(1)}, u32[]{:S(2)}, u32[]{:S(2)}) collective-permute-start(bf16[1,32,384]{2,1,0:T(8,128)(2,1)} %bitcast.36), channel_id=1, source_target_pairs={{0,64},{8,72},{16,80},{24,88},{32,96},{40,104},{48,112},{56,120},{... | collective-permute-start | bytes 73736 | tf_op jit(solution)/shard_map/ppermute | solution.py:48
  11.3 1.5 %collective-permute-start.10 = (bf16[2,384,3072]{2,1,0:T(8,128)(2,1)}, bf16[2,384,3072]{2,1,0:T(8,128)(2,1)}, u32[]{:S(2)}, u32[]{:S(2)}) collective-permute-start(bf16[2,384,3072]{2,1,0:T(8,128)(2,1)} %w_own.3), channel_id=1, source_target_pairs={{0,8},{8,0},{16,24},{24,16},{32,40},{40,32},{48,56},{56,48},{64,72... | collective-permute-start | bytes 14155784 | tf_op jit(solution)/shard_map/ppermute | solution.py:48
  15.0 0.8 collective-permute-start.3
  15.9 2.7 %collective-permute-done.3 = bf16[4,32,384]{2,1,0:T(8,128)(2,1)S(1)} collective-permute-done((bf16[4,32,384]{2,1,0:T(8,128)(2,1)S(1)}, bf16[4,32,384]{2,1,0:T(8,128)(2,1)S(1)}, u32[]{:S(2)}, u32[]{:S(2)}) %collective-permute-start.3) | collective-permute-done | bytes 98336 | tf_op jit(solution)/shard_map/ppermute | solution.py:48
  18.6 1.4 %collective-permute-start.5 = (bf16[1,256,384]{2,1,0:T(8,128)(2,1)S(1)}, bf16[1,256,384]{2,1,0:T(8,128)(2,1)S(1)}, u32[]{:S(2)}, u32[]{:S(2)}) collective-permute-start(bf16[1,256,384]{2,1,0:T(8,128)(2,1)S(1)} %bitcast.25), channel_id=1, source_target_pairs={{0,1},{8,136},{16,17},{24,152},{32,33},{40,168},{48,49},{56,184},{... | collective-permute-start | bytes 589832 | tf_op jit(solution)/shard_map/ppermute | solution.py:48
  20.0 1.5 %collective-permute-start.6 = (bf16[1,256,384]{2,1,0:T(8,128)(2,1)S(1)}, bf16[1,256,384]{2,1,0:T(8,128)(2,1)S(1)}, u32[]{:S(2)}, u32[]{:S(2)}) collective-permute-start(bf16[1,256,384]{2,1,0:T(8,128)(2,1)S(1)} %bitcast.26), channel_id=1, source_target_pairs={{0,3},{8,140},{16,19},{24,156},{32,35},{40,172},{48,51},{56,188},{... | collective-permute-start | bytes 589832 | tf_op jit(solution)/shard_map/ppermute | solution.py:48
  21.5 1.6 %collective-permute-start.4 = (bf16[1,256,384]{2,1,0:T(8,128)(2,1)S(1)}, bf16[1,256,384]{2,1,0:T(8,128)(2,1)S(1)}, u32[]{:S(2)}, u32[]{:S(2)}) collective-permute-start(bf16[1,256,384]{2,1,0:T(8,128)(2,1)S(1)} %bitcast.27), channel_id=1, source_target_pairs={{0,2},{8,12},{16,18},{24,28},{32,34},{40,44},{48,50},{56,60},{64,6... | collective-permute-start | bytes 589832 | tf_op jit(solution)/shard_map/ppermute | solution.py:48
  23.3 0.8 copy.17
  27.9 1.3 %collective-permute-start.8 = (bf16[4,256,384]{2,1,0:T(8,128)(2,1)S(1)}, bf16[4,256,384]{2,1,0:T(8,128)(2,1)S(1)}, u32[]{:S(2)}, u32[]{:S(2)}) collective-permute-start(bf16[4,256,384]{2,1,0:T(8,128)(2,1)S(1)} %pad_maximum_fusion.panel), channel_id=1, source_target_pairs={{0,128},{8,9},{16,144},{24,25},{32,160},{40,41},{48,176},{56,57},{... | collective-permute-start | bytes 2359304 | tf_op jit(solution)/shard_map/ppermute | solution.py:48
  29.2 1.7 %collective-permute-start.9 = (bf16[4,256,384]{2,1,0:T(8,128)(2,1)S(1)}, bf16[4,256,384]{2,1,0:T(8,128)(2,1)S(1)}, u32[]{:S(2)}, u32[]{:S(2)}) collective-permute-start(bf16[4,256,384]{2,1,0:T(8,128)(2,1)S(1)} %pad_maximum_fusion.panel), channel_id=1, source_target_pairs={{0,132},{8,11},{16,148},{24,27},{32,164},{40,43},{48,180},{56,59},... | collective-permute-start | bytes 2359304 | tf_op jit(solution)/shard_map/ppermute | solution.py:48
  31.8 1.4 %collective-permute-start.7 = (bf16[4,256,384]{2,1,0:T(8,128)(2,1)S(1)}, bf16[4,256,384]{2,1,0:T(8,128)(2,1)}, u32[]{:S(2)}, u32[]{:S(2)}) collective-permute-start(bf16[4,256,384]{2,1,0:T(8,128)(2,1)S(1)} %pad_maximum_fusion.panel), channel_id=1, source_target_pairs={{0,4},{8,10},{16,20},{24,26},{32,36},{40,42},{48,52},{56,58},{64,6... | collective-permute-start | bytes 2359304 | tf_op jit(solution)/shard_map/ppermute | solution.py:48
  33.3 7.2 %collective-permute-done.8.p2 = bf16[4,256,384]{2,1,0:T(8,128)(2,1)S(1)} collective-permute-done((bf16[4,256,384]{2,1,0:T(8,128)(2,1)S(1)}, bf16[4,256,384]{2,1,0:T(8,128)(2,1)S(1)}, u32[]{:S(2)}, u32[]{:S(2)}) %collective-permute-start.8) | collective-permute-done | bytes 786464 | tf_op jit(solution)/shard_map/ppermute | solution.py:48
  40.4 7.8 %collective-permute-done.9.p3 = bf16[4,256,384]{2,1,0:T(8,128)(2,1)S(1)} collective-permute-done((bf16[4,256,384]{2,1,0:T(8,128)(2,1)S(1)}, bf16[4,256,384]{2,1,0:T(8,128)(2,1)S(1)}, u32[]{:S(2)}, u32[]{:S(2)}) %collective-permute-start.9) | collective-permute-done | bytes 786464 | tf_op jit(solution)/shard_map/ppermute | solution.py:48
  48.8 2.3 %copy-done = bf16[2,384,3072]{2,1,0:T(8,128)(2,1)S(1)} copy-done((bf16[2,384,3072]{2,1,0:T(8,128)(2,1)S(1)}, bf16[2,384,3072]{2,1,0:T(8,128)(2,1)}, u32[]{:S(2)}) %copy-start) | copy-done | bytes 4718616
  51.1 6.3 %begin.1 = (f32[4,2,256,384]{3,2,1,0:T(8,128)S(1)}, bf16[4,384,1536]{2,1,0:T(8,128)(2,1)S(1)}) custom-call(s32[16]{0:T(128)S(1)} %get-tuple-element.17.cols, s32[16]{0:T(128)S(1)} %and_select_fusion.2.lows, bf16[4,256,384]{2,1,0:T(8,128)(2,1)S(1)} %pad_maximum_fusion.panel, bf16[2,384,3072]{2,1,0:T(8,128)(2,1)S(1)} %copy-done, ...), custom_call_target="tpu_custom_call" | custom-call | flops 1207959552 | bytes 17825792 | tf_op jit(solution)/shard_map/begin/pallas_call | solution.py:121
  57.4 7.4 %more.1.before = f32[4,2,256,384]{3,2,1,0:T(8,128)S(1)} custom-call(s32[16]{0:T(128)S(1)} %get-tuple-element.17.cols, s32[16]{0:T(128)S(1)} %and_select_fusion.2.lows, bf16[4,256,384]{2,1,0:T(8,128)(2,1)S(1)} %collective-permute-done.8.p2, bf16[4,256,384]{2,1,0:T(8,128)(2,1)S(1)} %collective-permute-done.9.p3, ...), custom_call_target="tpu_custom_call" | custom-call | flops 2415919104 | bytes 17825792 | tf_op jit(solution)/shard_map/more/pallas_call | solution.py:148
  64.8 5.0 %finish.1 = f32[8,2,16,128]{3,2,1,0:T(8,128)} custom-call(s32[128]{0:T(128)S(1)} %fusion.15.starts, s32[8]{0:T(128)S(1)} %select_reduce_fusion.2.places, s32[16]{0:T(128)S(1)} %and_select_fusion.2.lows, bf16[4,256,384]{2,1,0:T(8,128)(2,1)} %collective-permute-done.7.panel, f32[4,2,256,384]{3,2,1,0:T(8,128)S(1)} %more.1.before, ...), custom_call_target="tpu_custom_call" | custom-call | flops 1207959552 | bytes 9437184 | tf_op jit(solution)/shard_map/finish/pallas_call | solution.py:206
  69.8 10.7 %all-to-all-start = ((f32[8,2,16,128]{3,2,1,0:T(8,128)}), f32[8,2,16,128]{3,2,1,0:T(8,128)S(1)}, u32[]{:S(2)}, u32[]{:S(2)}) async-start(f32[8,2,16,128]{3,2,1,0:T(8,128)} %finish.1), calls=%async_computation | async-start | bytes 262144 | tf_op jit(solution)/shard_map/all_to_all | solution.py:346
  81.3 6.1 %all-to-all-done.terms = f32[8,2,16,128]{3,2,1,0:T(8,128)S(1)} async-done(((f32[8,2,16,128]{3,2,1,0:T(8,128)}), f32[8,2,16,128]{3,2,1,0:T(8,128)S(1)}, u32[]{:S(2)}, u32[]{:S(2)}) %all-to-all-start) | async-done | bytes 131104 | tf_op jit(solution)/shard_map/all_to_all | solution.py:346
  88.0 1.8 %spread.1 = f32[32,16,128]{2,1,0:T(8,128)} custom-call(s32[32,4,128]{2,1,0:T(4,128)} %copy.21.mask, f32[8,2,16,128]{3,2,1,0:T(8,128)} %copy-done.1), custom_call_target="tpu_custom_call" | custom-call | tf_op jit(solution)/shard_map/spread/pallas_call | solution.py:243
  89.8 21.9 %all_to_all.10.arrived = f32[32,16,128]{2,1,0:T(8,128)} all-to-all(f32[32,16,128]{2,1,0:T(8,128)} %spread.1), channel_id=1, replica_groups=mesh['row'=32,'col'=8] {'row'}, dimensions={0} | all-to-all | bytes 524288 | tf_op jit(solution)/shard_map/all_to_all | solution.py:348
  111.7 1.7 %settle.1 = f32[32,128]{1,0:T(8,128)} custom-call(f32[32,16,128]{2,1,0:T(8,128)} %all_to_all.10.arrived), custom_call_target="tpu_custom_call" | custom-call | tf_op jit(solution)/shard_map/settle/pallas_call | solution.py:272
  (67 shorter events, 9.2 us)
Async XLA Ops:
  0.0 14.3 %collective-permute-start = (bf16[1,32,384]{2,1,0:T(8,128)(2,1)}, bf16[1,32,384]{2,1,0:T(8,128)(2,1)S(1)}, u32[]{:S(2)}, u32[]{:S(2)}) collective-permute-start(bf16[1,32,384]{2,1,0:T(8,128)(2,1)} %bitcast.34), channel_id=1, source_target_pairs={{0,32},{8,40},{16,48},{24,56},{32,64},{40,72},{48,80},{56,88},{64,... | collective-permute-start | bytes 73736 | tf_op jit(solution)/shard_map/ppermute | solution.py:48
  3.8 10.4 %collective-permute-start.1 = (bf16[1,32,384]{2,1,0:T(8,128)(2,1)}, bf16[1,32,384]{2,1,0:T(8,128)(2,1)S(1)}, u32[]{:S(2)}, u32[]{:S(2)}) collective-permute-start(bf16[1,32,384]{2,1,0:T(8,128)(2,1)} %bitcast.35), channel_id=1, source_target_pairs={{0,96},{8,104},{16,112},{24,120},{32,0},{40,8},{48,16},{56,24},{64... | collective-permute-start | bytes 73736 | tf_op jit(solution)/shard_map/ppermute | solution.py:48
  6.9 7.4 %collective-permute-start.2 = (bf16[1,32,384]{2,1,0:T(8,128)(2,1)}, bf16[1,32,384]{2,1,0:T(8,128)(2,1)S(1)}, u32[]{:S(2)}, u32[]{:S(2)}) collective-permute-start(bf16[1,32,384]{2,1,0:T(8,128)(2,1)} %bitcast.36), channel_id=1, source_target_pairs={{0,64},{8,72},{16,80},{24,88},{32,96},{40,104},{48,112},{56,120},{... | collective-permute-start | bytes 73736 | tf_op jit(solution)/shard_map/ppermute | solution.py:48
  11.3 37.4 %collective-permute-start.10 = (bf16[2,384,3072]{2,1,0:T(8,128)(2,1)}, bf16[2,384,3072]{2,1,0:T(8,128)(2,1)}, u32[]{:S(2)}, u32[]{:S(2)}) collective-permute-start(bf16[2,384,3072]{2,1,0:T(8,128)(2,1)} %w_own.3), channel_id=1, source_target_pairs={{0,8},{8,0},{16,24},{24,16},{32,40},{40,32},{48,56},{56,48},{64,72... | collective-permute-start | bytes 14155784 | tf_op jit(solution)/shard_map/ppermute | solution.py:48
  15.0 3.6 %collective-permute-start.3 = (bf16[4,32,384]{2,1,0:T(8,128)(2,1)S(1)}, bf16[4,32,384]{2,1,0:T(8,128)(2,1)S(1)}, u32[]{:S(2)}, u32[]{:S(2)}) collective-permute-start(bf16[4,32,384]{2,1,0:T(8,128)(2,1)S(1)} %pad_maximum_fusion.2), channel_id=1, source_target_pairs={{0,16},{8,24},{16,0},{24,8},{32,48},{40,56},{48,32},{56,40},{64,80... | collective-permute-start | bytes 294920 | tf_op jit(solution)/shard_map/ppermute | solution.py:48
  18.6 8.6 %collective-permute-start.5 = (bf16[1,256,384]{2,1,0:T(8,128)(2,1)S(1)}, bf16[1,256,384]{2,1,0:T(8,128)(2,1)S(1)}, u32[]{:S(2)}, u32[]{:S(2)}) collective-permute-start(bf16[1,256,384]{2,1,0:T(8,128)(2,1)S(1)} %bitcast.25), channel_id=1, source_target_pairs={{0,1},{8,136},{16,17},{24,152},{32,33},{40,168},{48,49},{56,184},{... | collective-permute-start | bytes 589832 | tf_op jit(solution)/shard_map/ppermute | solution.py:48
  20.0 7.2 %collective-permute-start.6 = (bf16[1,256,384]{2,1,0:T(8,128)(2,1)S(1)}, bf16[1,256,384]{2,1,0:T(8,128)(2,1)S(1)}, u32[]{:S(2)}, u32[]{:S(2)}) collective-permute-start(bf16[1,256,384]{2,1,0:T(8,128)(2,1)S(1)} %bitcast.26), channel_id=1, source_target_pairs={{0,3},{8,140},{16,19},{24,156},{32,35},{40,172},{48,51},{56,188},{... | collective-permute-start | bytes 589832 | tf_op jit(solution)/shard_map/ppermute | solution.py:48
  21.5 6.3 %collective-permute-start.4 = (bf16[1,256,384]{2,1,0:T(8,128)(2,1)S(1)}, bf16[1,256,384]{2,1,0:T(8,128)(2,1)S(1)}, u32[]{:S(2)}, u32[]{:S(2)}) collective-permute-start(bf16[1,256,384]{2,1,0:T(8,128)(2,1)S(1)} %bitcast.27), channel_id=1, source_target_pairs={{0,2},{8,12},{16,18},{24,28},{32,34},{40,44},{48,50},{56,60},{64,6... | collective-permute-start | bytes 589832 | tf_op jit(solution)/shard_map/ppermute | solution.py:48
  27.9 12.5 %collective-permute-start.8 = (bf16[4,256,384]{2,1,0:T(8,128)(2,1)S(1)}, bf16[4,256,384]{2,1,0:T(8,128)(2,1)S(1)}, u32[]{:S(2)}, u32[]{:S(2)}) collective-permute-start(bf16[4,256,384]{2,1,0:T(8,128)(2,1)S(1)} %pad_maximum_fusion.panel), channel_id=1, source_target_pairs={{0,128},{8,9},{16,144},{24,25},{32,160},{40,41},{48,176},{56,57},{... | collective-permute-start | bytes 2359304 | tf_op jit(solution)/shard_map/ppermute | solution.py:48
  29.2 19.0 %collective-permute-start.9 = (bf16[4,256,384]{2,1,0:T(8,128)(2,1)S(1)}, bf16[4,256,384]{2,1,0:T(8,128)(2,1)S(1)}, u32[]{:S(2)}, u32[]{:S(2)}) collective-permute-start(bf16[4,256,384]{2,1,0:T(8,128)(2,1)S(1)} %pad_maximum_fusion.panel), channel_id=1, source_target_pairs={{0,132},{8,11},{16,148},{24,27},{32,164},{40,43},{48,180},{56,59},... | collective-permute-start | bytes 2359304 | tf_op jit(solution)/shard_map/ppermute | solution.py:48
  31.8 32.9 %collective-permute-start.7 = (bf16[4,256,384]{2,1,0:T(8,128)(2,1)S(1)}, bf16[4,256,384]{2,1,0:T(8,128)(2,1)}, u32[]{:S(2)}, u32[]{:S(2)}) collective-permute-start(bf16[4,256,384]{2,1,0:T(8,128)(2,1)S(1)} %pad_maximum_fusion.panel), channel_id=1, source_target_pairs={{0,4},{8,10},{16,20},{24,26},{32,36},{40,42},{48,52},{56,58},{64,6... | collective-permute-start | bytes 2359304 | tf_op jit(solution)/shard_map/ppermute | solution.py:48
  48.3 9.1 %slice-start = ((s8[4718592]{0:T(1024)(128)(4,1)}), s8[524288]{0:T(1024)(128)(4,1)S(1)}, s32[]{:S(2)}) async-start(s8[4718592]{0:T(1024)(128)(4,1)} %bitcast.23), calls=%async_computation.2 | async-start | bytes 1048576
  48.4 16.4 %collective-permute-start.11 = (bf16[2,256,384]{2,1,0:T(8,128)(2,1)S(1)}, bf16[2,256,384]{2,1,0:T(8,128)(2,1)}, u32[]{:S(2)}, u32[]{:S(2)}) collective-permute-start(bf16[2,256,384]{2,1,0:T(8,128)(2,1)S(1)} %pad_maximum_fusion.1.mine), channel_id=1, source_target_pairs={{0,8},{8,0},{16,24},{24,16},{32,40},{40,32},{48,56},{56,48},{64,72... | collective-permute-start | bytes 1179656 | tf_op jit(solution)/shard_map/ppermute | solution.py:48
  48.8 2.3 %copy-start = (bf16[2,384,3072]{2,1,0:T(8,128)(2,1)S(1)}, bf16[2,384,3072]{2,1,0:T(8,128)(2,1)}, u32[]{:S(2)}) copy-start(bf16[2,384,3072]{2,1,0:T(8,128)(2,1)} %w_own.3) | copy-start | bytes 14155780
  51.1 6.3 %slice-start.1 = ((s8[4718592]{0:T(1024)(128)(4,1)}), s8[4194304]{0:T(1024)(128)(4,1)S(1)}, s32[]{:S(2)}) async-start(s8[4718592]{0:T(1024)(128)(4,1)} %bitcast.23), calls=%async_computation.3 | async-start | bytes 8388608
  69.8 17.6 %all-to-all-start = ((f32[8,2,16,128]{3,2,1,0:T(8,128)}), f32[8,2,16,128]{3,2,1,0:T(8,128)S(1)}, u32[]{:S(2)}, u32[]{:S(2)}) async-start(f32[8,2,16,128]{3,2,1,0:T(8,128)} %finish.1), calls=%async_computation | async-start | bytes 262144 | tf_op jit(solution)/shard_map/all_to_all | solution.py:346
  87.4 0.7 copy-start.1

commit v3 on v2

--- a/solution.py
+++ b/solution.py
@@ -328,6 +328,8 @@
     panel = jnp.concatenate([stack] + parts, axis=0)
     panels = [panel] + [send(panel, second_plane(s)) for s in SHIFTS[1:]]
 
+    total, kept = begin(cols, lows, panel, screened, w_other)
+    total, panels[2], panels[3] = lax.optimization_barrier((total, panels[2], panels[3]))
     up = jnp.where(c == 0, panels[3][0], parts[2][0])
     down = jnp.where(c == 0, panels[2][0], parts[1][0])
     across = jnp.where(y_lo == 0, up, down)
@@ -336,7 +338,6 @@
     )
     other = send(mine, SWAP)
 
-    total, kept = begin(cols, lows, panel, screened, w_other)
     total = more(
         cols, lows, panels[2], panels[3], total, mine, coulomb.reshape(1, share), screened, w_other
     )

time: 114 us -> 107 us (0.939)
  waiting for transfers between devices: 24.3 us -> 16.8 us
  local copies, waits for them, and re-layouts: 7.96 us -> 12.9 us
  starting transfers between devices: 33.4 us -> 30.8 us
  blocking collectives: 21.9 us -> 19.8 us
    ppermute x12, waiting for transfers between devices: 18.2 us -> 10.7 us  [send(): return lax.ppermute(value, AXES, perm)]
    all_to_all x1, starting transfers between devices: 10.7 us -> 3.37 us  [local(): lax.all_to_all(terms, 'col', split_axis=0, concat_axis=0, tiled=True)]
    ppermute x12, starting transfers between devices: 22.8 us -> 27.4 us  [send(): return lax.ppermute(value, AXES, perm)]
    unnamed x12 -> x20, local copies, waits for them, and re-layouts: 3.77 us -> 7.27 us
    all_to_all x1, blocking collectives: 21.9 us -> 19.8 us  [local(): lax.all_to_all(placed, 'row', split_axis=0, concat_axis=0, tiled=True)]
  transfers between devices with their start and end apart: 13 -> 13, of which waited for: 5 -> 4; matrix products, arithmetic and copies ran while one was open for 7% -> 10% of each run, Pallas kernels for 12% -> 13%
where the time goes in v3:
time: 107 us; the launch traced here: 106 us
  starting transfers between devices  30.8 us (29%)
  Pallas kernels  21.4 us (20%)
  blocking collectives  19.8 us (19%)
  waiting for transfers between devices  16.8 us (16%)
  local copies, waits for them, and re-layouts  12.9 us (12%)
  other arithmetic  4.11 us (4%)
    ppermute x12, starting transfers between devices, send(): return lax.ppermute(value, AXES, perm)  27.4 us
    all_to_all x1, blocking collectives, local(): lax.all_to_all(placed, 'row', split_axis=0, concat_axis=0, tiled=True)  19.8 us
    ppermute x12, waiting for transfers between devices, send(): return lax.ppermute(value, AXES, perm)  10.7 us
    pallas_call x1, Pallas kernels, more(): pl.pallas_call(more_kernel, grid_spec=pltpu.PrefetchScalarGridSpec(num_sc...  7.37 us
    unnamed x20, local copies, waits for them, and re-layouts  7.27 us
    pallas_call x1, Pallas kernels, begin(): pl.pallas_call(begin_kernel, grid_spec=pltpu.PrefetchScalarGridSpec(num_s...  6.25 us
    all_to_all x1, waiting for transfers between devices, local(): lax.all_to_all(terms, 'col', split_axis=0, concat_axis=0, tiled=True)  6.06 us
    pallas_call x1, Pallas kernels, finish(): pl.pallas_call(finish_kernel, in_specs=[smem] * 3 + [vmem] * 5, out_specs...  4.32 us
  transfers between devices with their start and end apart: 13, of which 4 were waited for; matrix products, arithmetic and copies ran while one was open for 10% of the time, Pallas kernels for 13%

profile of v3, /device:TPU:1, one launch (start us, length us, event | category | flops | bytes accessed | tf_op | source)
XLA Modules:
  0.0 106.1 jit_solution(3654860580032790956)
XLA Ops:
  0.0 3.8 %collective-permute-start = (bf16[1,32,384]{2,1,0:T(8,128)(2,1)}, bf16[1,32,384]{2,1,0:T(8,128)(2,1)S(1)}, u32[]{:S(2)}, u32[]{:S(2)}) collective-permute-start(bf16[1,32,384]{2,1,0:T(8,128)(2,1)} %bitcast.34), channel_id=1, source_target_pairs={{0,32},{8,40},{16,48},{24,56},{32,64},{40,72},{48,80},{56,88},{64,... | collective-permute-start | bytes 73736 | tf_op jit(solution)/shard_map/ppermute | solution.py:48
  3.8 3.0 %collective-permute-start.1 = (bf16[1,32,384]{2,1,0:T(8,128)(2,1)}, bf16[1,32,384]{2,1,0:T(8,128)(2,1)S(1)}, u32[]{:S(2)}, u32[]{:S(2)}) collective-permute-start(bf16[1,32,384]{2,1,0:T(8,128)(2,1)} %bitcast.35), channel_id=1, source_target_pairs={{0,96},{8,104},{16,112},{24,120},{32,0},{40,8},{48,16},{56,24},{64... | collective-permute-start | bytes 73736 | tf_op jit(solution)/shard_map/ppermute | solution.py:48
  6.9 4.5 %collective-permute-start.2 = (bf16[1,32,384]{2,1,0:T(8,128)(2,1)}, bf16[1,32,384]{2,1,0:T(8,128)(2,1)S(1)}, u32[]{:S(2)}, u32[]{:S(2)}) collective-permute-start(bf16[1,32,384]{2,1,0:T(8,128)(2,1)} %bitcast.36), channel_id=1, source_target_pairs={{0,64},{8,72},{16,80},{24,88},{32,96},{40,104},{48,112},{56,120},{... | collective-permute-start | bytes 73736 | tf_op jit(solution)/shard_map/ppermute | solution.py:48
  11.3 1.5 %collective-permute-start.8 = (bf16[2,384,3072]{2,1,0:T(8,128)(2,1)}, bf16[2,384,3072]{2,1,0:T(8,128)(2,1)}, u32[]{:S(2)}, u32[]{:S(2)}) collective-permute-start(bf16[2,384,3072]{2,1,0:T(8,128)(2,1)} %w_own.3), channel_id=1, source_target_pairs={{0,8},{8,0},{16,24},{24,16},{32,40},{40,32},{48,56},{56,48},{64,72... | collective-permute-start | bytes 14155784 | tf_op jit(solution)/shard_map/ppermute | solution.py:48
  15.9 2.7 %collective-permute-done.3 = bf16[4,32,384]{2,1,0:T(8,128)(2,1)S(1)} collective-permute-done((bf16[4,32,384]{2,1,0:T(8,128)(2,1)S(1)}, bf16[4,32,384]{2,1,0:T(8,128)(2,1)S(1)}, u32[]{:S(2)}, u32[]{:S(2)}) %collective-permute-start.3) | collective-permute-done | bytes 98336 | tf_op jit(solution)/shard_map/ppermute | solution.py:48
  18.6 1.4 %collective-permute-start.5 = (bf16[1,256,384]{2,1,0:T(8,128)(2,1)S(1)}, bf16[1,256,384]{2,1,0:T(8,128)(2,1)S(1)}, u32[]{:S(2)}, u32[]{:S(2)}) collective-permute-start(bf16[1,256,384]{2,1,0:T(8,128)(2,1)S(1)} %bitcast.25), channel_id=1, source_target_pairs={{0,1},{8,136},{16,17},{24,152},{32,33},{40,168},{48,49},{56,184},{... | collective-permute-start | bytes 589832 | tf_op jit(solution)/shard_map/ppermute | solution.py:48
  20.0 1.5 %collective-permute-start.6 = (bf16[1,256,384]{2,1,0:T(8,128)(2,1)S(1)}, bf16[1,256,384]{2,1,0:T(8,128)(2,1)S(1)}, u32[]{:S(2)}, u32[]{:S(2)}) collective-permute-start(bf16[1,256,384]{2,1,0:T(8,128)(2,1)S(1)} %bitcast.26), channel_id=1, source_target_pairs={{0,3},{8,140},{16,19},{24,156},{32,35},{40,172},{48,51},{56,188},{... | collective-permute-start | bytes 589832 | tf_op jit(solution)/shard_map/ppermute | solution.py:48
  21.5 1.6 %collective-permute-start.4 = (bf16[1,256,384]{2,1,0:T(8,128)(2,1)S(1)}, bf16[1,256,384]{2,1,0:T(8,128)(2,1)S(1)}, u32[]{:S(2)}, u32[]{:S(2)}) collective-permute-start(bf16[1,256,384]{2,1,0:T(8,128)(2,1)S(1)} %bitcast.27), channel_id=1, source_target_pairs={{0,2},{8,12},{16,18},{24,28},{32,34},{40,44},{48,50},{56,60},{64,6... | collective-permute-start | bytes 589832 | tf_op jit(solution)/shard_map/ppermute | solution.py:48
  29.8 2.6 %collective-permute-start.10 = (bf16[4,256,384]{2,1,0:T(8,128)(2,1)S(1)}, bf16[4,256,384]{2,1,0:T(8,128)(2,1)S(1)}, u32[]{:S(2)}, u32[]{:S(2)}) collective-permute-start(bf16[4,256,384]{2,1,0:T(8,128)(2,1)S(1)} %pad_maximum_fusion.panel), channel_id=1, source_target_pairs={{0,132},{8,11},{16,148},{24,27},{32,164},{40,43},{48,180},{56,59},... | collective-permute-start | bytes 2359304 | tf_op jit(solution)/shard_map/ppermute | solution.py:48
  33.0 1.8 %collective-permute-start.7 = (bf16[4,256,384]{2,1,0:T(8,128)(2,1)S(1)}, bf16[4,256,384]{2,1,0:T(8,128)(2,1)S(1)}, u32[]{:S(2)}, u32[]{:S(2)}) collective-permute-start(bf16[4,256,384]{2,1,0:T(8,128)(2,1)S(1)} %pad_maximum_fusion.panel), channel_id=1, source_target_pairs={{0,4},{8,10},{16,20},{24,26},{32,36},{40,42},{48,52},{56,58},{64,6... | collective-permute-start | bytes 2359304 | tf_op jit(solution)/shard_map/ppermute | solution.py:48
  34.9 2.3 %copy-done = bf16[2,384,3072]{2,1,0:T(8,128)(2,1)S(1)} copy-done((bf16[2,384,3072]{2,1,0:T(8,128)(2,1)S(1)}, bf16[2,384,3072]{2,1,0:T(8,128)(2,1)}, u32[]{:S(2)}) %copy-start) | copy-done | bytes 4718616
  37.2 6.2 %begin.1 = (f32[4,2,256,384]{3,2,1,0:T(8,128)S(1)}, bf16[4,384,1536]{2,1,0:T(8,128)(2,1)S(1)}) custom-call(s32[16]{0:T(128)S(1)} %get-tuple-element.23.cols, s32[16]{0:T(128)S(1)} %and_select_fusion.2.lows, bf16[4,256,384]{2,1,0:T(8,128)(2,1)S(1)} %pad_maximum_fusion.panel, bf16[2,384,3072]{2,1,0:T(8,128)(2,1)S(1)} %copy-done, ...), custom_call_target="tpu_custom_call" | custom-call | flops 1207959552 | bytes 17825792 | tf_op jit(solution)/shard_map/begin/pallas_call | solution.py:121
  43.5 1.6 %copy-done.1 = f32[4,2,256,384]{3,2,1,0:T(8,128)} copy-done((f32[4,2,256,384]{3,2,1,0:T(8,128)}, f32[4,2,256,384]{3,2,1,0:T(8,128)S(1)}, u32[]{:S(2)}) %copy-start.1) | copy-done | bytes 3145752
  45.1 4.6 %collective-permute-done.10.p3 = bf16[4,256,384]{2,1,0:T(8,128)(2,1)S(1)} collective-permute-done((bf16[4,256,384]{2,1,0:T(8,128)(2,1)S(1)}, bf16[4,256,384]{2,1,0:T(8,128)(2,1)S(1)}, u32[]{:S(2)}, u32[]{:S(2)}) %collective-permute-start.10) | collective-permute-done | bytes 786464 | tf_op jit(solution)/shard_map/ppermute | solution.py:48
  49.7 3.4 %collective-permute-done.9.p2 = bf16[4,256,384]{2,1,0:T(8,128)(2,1)S(1)} collective-permute-done((bf16[4,256,384]{2,1,0:T(8,128)(2,1)S(1)}, bf16[4,256,384]{2,1,0:T(8,128)(2,1)S(1)}, u32[]{:S(2)}, u32[]{:S(2)}) %collective-permute-start.9) | collective-permute-done | bytes 786464 | tf_op jit(solution)/shard_map/ppermute | solution.py:48
  53.3 5.0 %collective-permute-start.11 = (bf16[2,256,384]{2,1,0:T(8,128)(2,1)S(1)}, bf16[2,256,384]{2,1,0:T(8,128)(2,1)S(1)}, u32[]{:S(2)}, u32[]{:S(2)}) collective-permute-start(bf16[2,256,384]{2,1,0:T(8,128)(2,1)S(1)} %pad_maximum_fusion.1.mine), channel_id=1, source_target_pairs={{0,8},{8,0},{16,24},{24,16},{32,40},{40,32},{48,56},{56,48},{64,72... | collective-permute-start | bytes 1179656 | tf_op jit(solution)/shard_map/ppermute | solution.py:48
  58.3 1.9 %copy-done.2 = f32[4,2,256,384]{3,2,1,0:T(8,128)S(1)} copy-done((f32[4,2,256,384]{3,2,1,0:T(8,128)S(1)}, f32[4,2,256,384]{3,2,1,0:T(8,128)}, u32[]{:S(2)}) %copy-start.2) | copy-done | bytes 3145752
  60.2 7.4 %more.1.before = f32[4,2,256,384]{3,2,1,0:T(8,128)S(1)} custom-call(s32[16]{0:T(128)S(1)} %get-tuple-element.23.cols, s32[16]{0:T(128)S(1)} %and_select_fusion.2.lows, bf16[4,256,384]{2,1,0:T(8,128)(2,1)S(1)} %collective-permute-done.9.p2, bf16[4,256,384]{2,1,0:T(8,128)(2,1)S(1)} %collective-permute-done.10.p3, f32[4,2,256,384]{3,2,1,0:T(8,128)S(1)} %copy-done.2, ...), custom_call_target="tpu_custom_call" | custom-call | flops 2415919104 | bytes 17825792 | tf_op jit(solution)/shard_map/more/pallas_call | solution.py:148
  67.6 4.3 %finish.1 = f32[8,2,16,128]{3,2,1,0:T(8,128)} custom-call(s32[128]{0:T(128)S(1)} %fusion.14.starts, s32[8]{0:T(128)S(1)} %select_reduce_fusion.2.places, s32[16]{0:T(128)S(1)} %and_select_fusion.2.lows, bf16[4,256,384]{2,1,0:T(8,128)(2,1)S(1)} %collective-permute-done.7.panel, f32[4,2,256,384]{3,2,1,0:T(8,128)S(1)} %more.1.before, ...), custom_call_target="tpu_custom_call" | custom-call | flops 1207959552 | bytes 9437184 | tf_op jit(solution)/shard_map/finish/pallas_call | solution.py:206
  71.9 3.4 %all-to-all-start = ((f32[8,2,16,128]{3,2,1,0:T(8,128)}), f32[8,2,16,128]{3,2,1,0:T(8,128)S(1)}, u32[]{:S(2)}, u32[]{:S(2)}) async-start(f32[8,2,16,128]{3,2,1,0:T(8,128)} %finish.1), calls=%async_computation | async-start | bytes 262144 | tf_op jit(solution)/shard_map/all_to_all | solution.py:347
  76.1 6.1 %all-to-all-done.terms = f32[8,2,16,128]{3,2,1,0:T(8,128)S(1)} async-done(((f32[8,2,16,128]{3,2,1,0:T(8,128)}), f32[8,2,16,128]{3,2,1,0:T(8,128)S(1)}, u32[]{:S(2)}, u32[]{:S(2)}) %all-to-all-start) | async-done | bytes 131104 | tf_op jit(solution)/shard_map/all_to_all | solution.py:347
  82.8 1.8 %spread.1 = f32[32,16,128]{2,1,0:T(8,128)} custom-call(s32[32,4,128]{2,1,0:T(4,128)} %copy.21.mask, f32[8,2,16,128]{3,2,1,0:T(8,128)} %copy-done.3), custom_call_target="tpu_custom_call" | custom-call | tf_op jit(solution)/shard_map/spread/pallas_call | solution.py:243
  84.6 19.8 %all_to_all.10.arrived = f32[32,16,128]{2,1,0:T(8,128)} all-to-all(f32[32,16,128]{2,1,0:T(8,128)} %spread.1), channel_id=1, replica_groups=mesh['row'=32,'col'=8] {'row'}, dimensions={0} | all-to-all | bytes 524288 | tf_op jit(solution)/shard_map/all_to_all | solution.py:349
  104.4 1.7 %settle.1 = f32[32,128]{1,0:T(8,128)} custom-call(f32[32,16,128]{2,1,0:T(8,128)} %all_to_all.10.arrived), custom_call_target="tpu_custom_call" | custom-call | tf_op jit(solution)/shard_map/settle/pallas_call | solution.py:272
  (75 shorter events, 12.1 us)
Async XLA Ops:
  0.0 14.3 %collective-permute-start = (bf16[1,32,384]{2,1,0:T(8,128)(2,1)}, bf16[1,32,384]{2,1,0:T(8,128)(2,1)S(1)}, u32[]{:S(2)}, u32[]{:S(2)}) collective-permute-start(bf16[1,32,384]{2,1,0:T(8,128)(2,1)} %bitcast.34), channel_id=1, source_target_pairs={{0,32},{8,40},{16,48},{24,56},{32,64},{40,72},{48,80},{56,88},{64,... | collective-permute-start | bytes 73736 | tf_op jit(solution)/shard_map/ppermute | solution.py:48
  3.8 10.4 %collective-permute-start.1 = (bf16[1,32,384]{2,1,0:T(8,128)(2,1)}, bf16[1,32,384]{2,1,0:T(8,128)(2,1)S(1)}, u32[]{:S(2)}, u32[]{:S(2)}) collective-permute-start(bf16[1,32,384]{2,1,0:T(8,128)(2,1)} %bitcast.35), channel_id=1, source_target_pairs={{0,96},{8,104},{16,112},{24,120},{32,0},{40,8},{48,16},{56,24},{64... | collective-permute-start | bytes 73736 | tf_op jit(solution)/shard_map/ppermute | solution.py:48
  6.9 7.4 %collective-permute-start.2 = (bf16[1,32,384]{2,1,0:T(8,128)(2,1)}, bf16[1,32,384]{2,1,0:T(8,128)(2,1)S(1)}, u32[]{:S(2)}, u32[]{:S(2)}) collective-permute-start(bf16[1,32,384]{2,1,0:T(8,128)(2,1)} %bitcast.36), channel_id=1, source_target_pairs={{0,64},{8,72},{16,80},{24,88},{32,96},{40,104},{48,112},{56,120},{... | collective-permute-start | bytes 73736 | tf_op jit(solution)/shard_map/ppermute | solution.py:48
  11.3 23.5 %collective-permute-start.8 = (bf16[2,384,3072]{2,1,0:T(8,128)(2,1)}, bf16[2,384,3072]{2,1,0:T(8,128)(2,1)}, u32[]{:S(2)}, u32[]{:S(2)}) collective-permute-start(bf16[2,384,3072]{2,1,0:T(8,128)(2,1)} %w_own.3), channel_id=1, source_target_pairs={{0,8},{8,0},{16,24},{24,16},{32,40},{40,32},{48,56},{56,48},{64,72... | collective-permute-start | bytes 14155784 | tf_op jit(solution)/shard_map/ppermute | solution.py:48
  15.0 3.6 %collective-permute-start.3 = (bf16[4,32,384]{2,1,0:T(8,128)(2,1)S(1)}, bf16[4,32,384]{2,1,0:T(8,128)(2,1)S(1)}, u32[]{:S(2)}, u32[]{:S(2)}) collective-permute-start(bf16[4,32,384]{2,1,0:T(8,128)(2,1)S(1)} %pad_maximum_fusion.2), channel_id=1, source_target_pairs={{0,16},{8,24},{16,0},{24,8},{32,48},{40,56},{48,32},{56,40},{64,80... | collective-permute-start | bytes 294920 | tf_op jit(solution)/shard_map/ppermute | solution.py:48
  18.6 11.0 %collective-permute-start.5 = (bf16[1,256,384]{2,1,0:T(8,128)(2,1)S(1)}, bf16[1,256,384]{2,1,0:T(8,128)(2,1)S(1)}, u32[]{:S(2)}, u32[]{:S(2)}) collective-permute-start(bf16[1,256,384]{2,1,0:T(8,128)(2,1)S(1)} %bitcast.25), channel_id=1, source_target_pairs={{0,1},{8,136},{16,17},{24,152},{32,33},{40,168},{48,49},{56,184},{... | collective-permute-start | bytes 589832 | tf_op jit(solution)/shard_map/ppermute | solution.py:48
  20.0 9.6 %collective-permute-start.6 = (bf16[1,256,384]{2,1,0:T(8,128)(2,1)S(1)}, bf16[1,256,384]{2,1,0:T(8,128)(2,1)S(1)}, u32[]{:S(2)}, u32[]{:S(2)}) collective-permute-start(bf16[1,256,384]{2,1,0:T(8,128)(2,1)S(1)} %bitcast.26), channel_id=1, source_target_pairs={{0,3},{8,140},{16,19},{24,156},{32,35},{40,172},{48,51},{56,188},{... | collective-permute-start | bytes 589832 | tf_op jit(solution)/shard_map/ppermute | solution.py:48
  21.5 8.1 %collective-permute-start.4 = (bf16[1,256,384]{2,1,0:T(8,128)(2,1)S(1)}, bf16[1,256,384]{2,1,0:T(8,128)(2,1)S(1)}, u32[]{:S(2)}, u32[]{:S(2)}) collective-permute-start(bf16[1,256,384]{2,1,0:T(8,128)(2,1)S(1)} %bitcast.27), channel_id=1, source_target_pairs={{0,2},{8,12},{16,18},{24,28},{32,34},{40,44},{48,50},{56,60},{64,6... | collective-permute-start | bytes 589832 | tf_op jit(solution)/shard_map/ppermute | solution.py:48
  29.6 28.6 %slice-start = ((s8[4718592]{0:T(1024)(128)(4,1)}), s8[524288]{0:T(1024)(128)(4,1)S(1)}, s32[]{:S(2)}) async-start(s8[4718592]{0:T(1024)(128)(4,1)} %bitcast.23), calls=%async_computation.2 | async-start | bytes 1048576
  29.8 19.9 %collective-permute-start.10 = (bf16[4,256,384]{2,1,0:T(8,128)(2,1)S(1)}, bf16[4,256,384]{2,1,0:T(8,128)(2,1)S(1)}, u32[]{:S(2)}, u32[]{:S(2)}) collective-permute-start(bf16[4,256,384]{2,1,0:T(8,128)(2,1)S(1)} %pad_maximum_fusion.panel), channel_id=1, source_target_pairs={{0,132},{8,11},{16,148},{24,27},{32,164},{40,43},{48,180},{56,59},... | collective-permute-start | bytes 2359304 | tf_op jit(solution)/shard_map/ppermute | solution.py:48
  32.3 20.8 %collective-permute-start.9 = (bf16[4,256,384]{2,1,0:T(8,128)(2,1)S(1)}, bf16[4,256,384]{2,1,0:T(8,128)(2,1)S(1)}, u32[]{:S(2)}, u32[]{:S(2)}) collective-permute-start(bf16[4,256,384]{2,1,0:T(8,128)(2,1)S(1)} %pad_maximum_fusion.panel), channel_id=1, source_target_pairs={{0,128},{8,9},{16,144},{24,25},{32,160},{40,41},{48,176},{56,57},{... | collective-permute-start | bytes 2359304 | tf_op jit(solution)/shard_map/ppermute | solution.py:48
  33.0 34.5 %collective-permute-start.7 = (bf16[4,256,384]{2,1,0:T(8,128)(2,1)S(1)}, bf16[4,256,384]{2,1,0:T(8,128)(2,1)S(1)}, u32[]{:S(2)}, u32[]{:S(2)}) collective-permute-start(bf16[4,256,384]{2,1,0:T(8,128)(2,1)S(1)} %pad_maximum_fusion.panel), channel_id=1, source_target_pairs={{0,4},{8,10},{16,20},{24,26},{32,36},{40,42},{48,52},{56,58},{64,6... | collective-permute-start | bytes 2359304 | tf_op jit(solution)/shard_map/ppermute | solution.py:48
  34.9 2.3 %copy-start = (bf16[2,384,3072]{2,1,0:T(8,128)(2,1)S(1)}, bf16[2,384,3072]{2,1,0:T(8,128)(2,1)}, u32[]{:S(2)}) copy-start(bf16[2,384,3072]{2,1,0:T(8,128)(2,1)} %w_own.3) | copy-start | bytes 14155780
  37.2 21.0 %copy-start.4 = (s32[128]{0:T(128)S(1)}, s32[128]{0:T(128)}, u32[]{:S(2)}) copy-start(s32[128]{0:T(128)} %reduce_sum.30) | copy-start | bytes 1540
  37.2 21.0 %copy-start.5 = (s32[128]{0:T(128)S(1)}, s32[128]{0:T(128)}, u32[]{:S(2)}) copy-start(s32[128]{0:T(128)} %mul.121) | copy-start | bytes 1540
  37.2 21.0 %slice-start.1 = ((s8[4718592]{0:T(1024)(128)(4,1)}), s8[4194304]{0:T(1024)(128)(4,1)S(1)}, s32[]{:S(2)}) async-start(s8[4718592]{0:T(1024)(128)(4,1)} %bitcast.23), calls=%async_computation.3 | async-start | bytes 8388608
  43.5 1.6 %copy-start.1 = (f32[4,2,256,384]{3,2,1,0:T(8,128)}, f32[4,2,256,384]{3,2,1,0:T(8,128)S(1)}, u32[]{:S(2)}) copy-start(f32[4,2,256,384]{3,2,1,0:T(8,128)S(1)} %get-tuple-element.19.before) | copy-start | bytes 9437188
  53.3 14.3 %collective-permute-start.11 = (bf16[2,256,384]{2,1,0:T(8,128)(2,1)S(1)}, bf16[2,256,384]{2,1,0:T(8,128)(2,1)S(1)}, u32[]{:S(2)}, u32[]{:S(2)}) collective-permute-start(bf16[2,256,384]{2,1,0:T(8,128)(2,1)S(1)} %pad_maximum_fusion.1.mine), channel_id=1, source_target_pairs={{0,8},{8,0},{16,24},{24,16},{32,40},{40,32},{48,56},{56,48},{64,72... | collective-permute-start | bytes 1179656 | tf_op jit(solution)/shard_map/ppermute | solution.py:48
  58.3 1.9 %copy-start.2 = (f32[4,2,256,384]{3,2,1,0:T(8,128)S(1)}, f32[4,2,256,384]{3,2,1,0:T(8,128)}, u32[]{:S(2)}) copy-start(f32[4,2,256,384]{3,2,1,0:T(8,128)} %copy-done.1) | copy-start | bytes 9437188
  71.9 10.3 %all-to-all-start = ((f32[8,2,16,128]{3,2,1,0:T(8,128)}), f32[8,2,16,128]{3,2,1,0:T(8,128)S(1)}, u32[]{:S(2)}, u32[]{:S(2)}) async-start(f32[8,2,16,128]{3,2,1,0:T(8,128)} %finish.1), calls=%async_computation | async-start | bytes 262144 | tf_op jit(solution)/shard_map/all_to_all | solution.py:347
  82.1 0.6 copy-start.3

commit v4 on v2

v4 whole, which is shorter than its diff:
```python
import jax
import jax.numpy as jnp
from jax import lax
from jax.experimental import pallas as pl
from jax.experimental.pallas import tpu as pltpu
from jax.sharding import PartitionSpec as P

AXES = ("row", "col")
NX, NY, NZ, NCORE = 4, 4, 8, 2
SHIFTS = (0, 2, 1, -1)
ZSHIFTS = (0, 2, 4, -2)
VMEM = 48 * 1024 * 1024


def device_index(x, y, z, c):
    y_hi, y_lo = divmod(y % NY, 2)
    row = (y_lo * NZ + z % NZ) * NCORE + c
    return row * 8 + y_hi * NX + x % NX


def pairs(move):
    found = []
    for x in range(NX):
        for y in range(NY):
            for z in range(NZ):
                for c in range(NCORE):
                    found.append((device_index(x, y, z, c), device_index(*move(x, y, z, c))))
    return found


SWAP = pairs(lambda x, y, z, c: (x, y, z, 1 - c))
ZPAIR = pairs(lambda x, y, z, c: (x, y, z ^ 1, c))


def along_z(s):
    return pairs(lambda x, y, z, c: (x, y, z + s, c))


def first_plane(s):
    return pairs(lambda x, y, z, c: (x + s, y, z, c) if c == 0 else (x, y + s, z, c))


def second_plane(s):
    return pairs(lambda x, y, z, c: (x, y + s, z, c) if c == 0 else (x + s, y, z, c))


def send(value, perm):
    return lax.ppermute(value, AXES, perm)


def contract(a, b):
    return lax.dot_general(a, b, (((1,), (1,)), ((), ())), preferred_element_type=jnp.float32)


def where_am_i():
    r, j = lax.axis_index("row"), lax.axis_index("col")
    return r, j, r & 1, (r >> 1) & 7, r >> 4


def spot(k, i):
    r, j, c, _, y_lo = where_am_i()
    first, second = SHIFTS[i], SHIFTS[k]
    x = ((j & 3) - first - c * (second - first)) & 3
    y = (2 * (j >> 2) + y_lo - second - c * (first - second)) & 3
    return (y >> 1) * NX + x, y & 1


def place_of(z_wanted):
    z = where_am_i()[3]
    side = (z ^ z_wanted) & 1
    return side * 4 + ((((z ^ side) - z_wanted) & 7) >> 1)


def product(pieces, w, share, k, pair):
    right = []
    for i in (2 * pair, 2 * pair + 1):
        start = pl.multiple_of(spot(k, i)[0] * share, share)
        right.append(w[0, :, pl.ds(start, share)])
    left = jnp.concatenate([pieces[0], pieces[1]], axis=1)
    return spot(k, 2 * pair)[1], contract(left, jnp.concatenate(right, axis=1))


def for_each_w(run, w_own, w_other):
    @pl.when(pl.program_id(0) < 2)
    def _():
        run(w_own)

    @pl.when(pl.program_id(0) >= 2)
    def _():
        run(w_other)


def begin_kernel(p01, p23, w_own, w_other, out, kept):
    share = p01.shape[2]

    def run(w):
        out[...] = jnp.zeros_like(out)
        for pair, pieces in enumerate((p01, p23)):
            low, term = product(pieces, w, share, 0, pair)
            out[0, low] -= term
        for i in range(4):
            start = pl.multiple_of(spot(1, i)[0] * share, share)
            kept[0, :, i * share : (i + 1) * share] = w[0, :, pl.ds(start, share)]

    for_each_w(run, w_own, w_other)


def more_kernel(f0, f1, g0, g1, before, mine, coulomb, w_own, w_other, out):
    share = f0.shape[2]

    def run(w):
        for low in range(2):
            bare = (2.0 * coulomb[...]) * mine[low].astype(jnp.float32)
            out[0, low] = before[0, low] + bare
        for k, pair, pieces in ((2, 0, f0), (2, 1, f1), (3, 0, g0), (3, 1, g1)):
            low, term = product(pieces, w, share, k, pair)
            out[0, low] -= term

    for_each_w(run, w_own, w_other)


def fixed(shape):
    return pl.BlockSpec(shape, lambda q: (0,) * len(shape))


def w_specs(share, whole):
    return [
        pl.BlockSpec((1, share, whole), lambda q: (jnp.minimum(q, 1), 0, 0)),
        pl.BlockSpec((1, share, whole), lambda q: (jnp.maximum(q - 2, 0), 0, 0)),
    ]


def cost(pieces, rows, share, reads):
    return pl.CostEstimate(
        flops=2 * 4 * pieces * rows * share * share, bytes_accessed=reads << 20, transcendentals=0
    )


def begin(p01, p23, w_own, w_other):
    rows, share = p01.shape[1:]
    return pl.pallas_call(
        begin_kernel,
        grid=(4,),
        in_specs=[fixed((2, rows, share))] * 2 + w_specs(share, w_own.shape[2]),
        out_specs=[
            pl.BlockSpec((1, 2, rows, share), lambda q: (q, 0, 0, 0)),
            pl.BlockSpec((1, share, 4 * share), lambda q: (q, 0, 0)),
        ],
        out_shape=[
            jax.ShapeDtypeStruct((4, 2, rows, share), jnp.float32),
            jax.ShapeDtypeStruct((4, share, 4 * share), jnp.bfloat16),
        ],
        compiler_params=pltpu.CompilerParams(vmem_limit_bytes=VMEM),
        cost_estimate=cost(4, rows, share, 17),
        name="begin",
    )(p01, p23, w_own, w_other)


def more(f0, f1, g0, g1, before, mine, coulomb, w_own, w_other):
    rows, share = f0.shape[1:]
    total = pl.BlockSpec((1, 2, rows, share), lambda q: (q, 0, 0, 0))
    return pl.pallas_call(
        more_kernel,
        grid=(4,),
        in_specs=[fixed((2, rows, share))] * 4
        + [total, fixed((2, rows, share)), fixed((1, share))]
        + w_specs(share, w_own.shape[2]),
        out_specs=total,
        out_shape=jax.ShapeDtypeStruct((4, 2, rows, share), jnp.float32),
        compiler_params=pltpu.CompilerParams(vmem_limit_bytes=VMEM),
        cost_estimate=cost(8, rows, share, 17),
        name="more",
    )(f0, f1, g0, g1, before, mine, coulomb, w_own, w_other)


def finish_kernel(partner, p01, p23, before, kept, mine, other, out, left_rows, total, u):
    rows, share = mine.shape[1:]
    c = where_am_i()[2]
    for low in range(2):
        left_rows[pl.ds(low * rows, rows), :] = mine[low]
        left_rows[pl.ds((2 + low) * rows, rows), :] = other[low]
    for q in range(4):
        total[...] = before[q]
        for pair, pieces in enumerate((p01, p23)):
            left = jnp.concatenate([pieces[0], pieces[1]], axis=1)
            right = kept[q, :, 2 * pair * share : (2 * pair + 2) * share]
            total[spot(1, 2 * pair)[1]] -= contract(left, right)
        u[q] = total[...].astype(u.dtype)
    lane = lax.broadcasted_iota(jnp.int32, (16, 128), 1) // 16
    for target in range(8):
        places = [place_of((2 * target + i) % NZ) for i in range(2)]
        for two in range(2):
            left, right = [], []
            for q in (2 * two, 2 * two + 1):
                for i in range(4):
                    k = partner[q, 8 * target + 4 * (i // 2) + 2 * c + i % 2]
                    block = ((((k >> 1) & 1) ^ c) * 2 + (k >> 5)) * NZ + place_of((k >> 2) & 7)
                    start = pl.multiple_of(block * 32 + (k & 1) * 16, 16)
                    left.append(left_rows[pl.ds(start, 16), :])
                for place in places:
                    right.append(u[q, target // 4, pl.ds(pl.multiple_of(place * 32, 32), 32), :])
            met = contract(jnp.concatenate(left, axis=0), jnp.concatenate(right, axis=0))
            block = jnp.zeros((16, 128), jnp.float32)
            for i in range(8):
                block = jnp.where(lane == i, met[16 * i : 16 * i + 16], block)
            out[target, two] = block


def finish(partner, p01, p23, before, kept, mine, other):
    rows, share = mine.shape[1:]
    vmem = pl.BlockSpec(memory_space=pltpu.VMEM)
    return pl.pallas_call(
        finish_kernel,
        in_specs=[pl.BlockSpec(memory_space=pltpu.SMEM)] + [vmem] * 6,
        out_specs=vmem,
        out_shape=jax.ShapeDtypeStruct((8, 2, 16, 128), jnp.float32),
        scratch_shapes=[
            pltpu.VMEM((4 * rows, share), jnp.bfloat16),
            pltpu.VMEM((2, rows, share), jnp.float32),
            pltpu.VMEM((4, 2, rows, share), jnp.bfloat16),
        ],
        compiler_params=pltpu.CompilerParams(vmem_limit_bytes=VMEM),
        cost_estimate=cost(4, rows, share, 9),
        name="finish",
    )(partner, p01, p23, before, kept, mine, other)


def spread_kernel(q_index, terms, out):
    r, j, c, _, _ = where_am_i()
    ks = q_index.shape[0]
    row = lax.broadcasted_iota(jnp.int32, (ks, 128), 0)
    col = lax.broadcasted_iota(jnp.int32, (ks, 128), 1)
    slot = (col & 63) >> 4
    hit = row == 8 * j + 4 * (slot >> 1) + 2 * c + (slot & 1)
    seen = jnp.zeros((ks // 2, 128), jnp.float32)
    for k in range(2):
        rows = q_index[pl.ds(k, ks // 2, stride=2), :].astype(jnp.float32).astype(jnp.bfloat16)
        pick = jnp.where(hit & (col >> 6 == k), 1.0, 0.0).astype(jnp.bfloat16)
        seen = seen + jnp.dot(rows, pick, preferred_element_type=jnp.float32)
    seen = seen.astype(jnp.int32)
    lane = lax.broadcasted_iota(jnp.int32, (16, 128), 1)
    blocks = []
    for two in range(2):
        full = terms[0, two]
        for i in range(1, 8):
            full = full + terms[i, two]
        turned = pltpu.roll(full, 64, 1)
        blocks.append(jnp.where(lane < 64, full, turned))
        blocks.append(jnp.where(lane < 64, turned, full))
    mine = (2 * r, 2 * r + 1, 2 * (r ^ 1), 2 * (r ^ 1) + 1)
    for target in range(out.shape[0]):
        wanted = jnp.broadcast_to(seen[target : target + 1, :], (16, 128))
        block = jnp.zeros((16, 128), jnp.float32)
        for q in range(4):
            block = jnp.where(wanted == mine[q], blocks[q], block)
        out[target] = block.astype(out.dtype)


def spread(q_index, terms):
    vmem = pl.BlockSpec(memory_space=pltpu.VMEM)
    return pl.pallas_call(
        spread_kernel,
        in_specs=[vmem, vmem],
        out_specs=vmem,
        out_shape=jax.ShapeDtypeStruct((32, 16, 128), jnp.float32),
        name="spread",
    )(q_index, terms)


def settle_kernel(arrived, out):
    lane = lax.broadcasted_iota(jnp.int32, (16, 128), 1) // 32
    sums = []
    for c in range(2):
        full = arrived[c].astype(jnp.float32)
        for r in range(2 + c, arrived.shape[0], 2):
            full = full + arrived[r].astype(jnp.float32)
        sums.append(full)
    for k in range(2):
        block = jnp.zeros((16, 128), jnp.float32)
        for z in range(2):
            for c in range(2):
                move = (z * 64 + c * 32 - k * 64 - z * 32) % 128
                turned = pltpu.roll(sums[c], move, 1) if move else sums[c]
                block = jnp.where(lane == 2 * z + c, turned, block)
        out[16 * k : 16 * k + 16, :] = block


def settle(arrived):
    vmem = pl.BlockSpec(memory_space=pltpu.VMEM)
    return pl.pallas_call(
        settle_kernel,
        in_specs=[vmem],
        out_specs=vmem,
        out_shape=jax.ShapeDtypeStruct((32, 128), jnp.float32),
        name="settle",
    )(arrived)


def local(pair_matrix, screened, coulomb, q_index):
    bands, share = pair_matrix.shape[1:]
    r, _, c, _, y_lo = where_am_i()
    w_other = send(screened, SWAP)
    own = pair_matrix.reshape(1, 2 * bands, share)
    even = jnp.concatenate([own] + [send(own, along_z(s)) for s in ZSHIFTS[1:]], axis=0)
    stack = jnp.concatenate([even, send(even, ZPAIR)], axis=0).reshape(1, NZ * 32, share)
    parts = [send(stack, first_plane(s)) for s in SHIFTS[1:]]
    p01 = jnp.concatenate([stack, parts[0]], axis=0)
    p23 = jnp.concatenate([parts[1], parts[2]], axis=0)

    f0 = send(p01, second_plane(1))
    g1 = send(p23, second_plane(-1))
    f1 = send(p23, second_plane(1))
    g0 = send(p01, second_plane(-1))
    ff0 = send(f0, second_plane(1))
    gg1 = send(g1, second_plane(-1))

    q_mine = jnp.stack([2 * r, 2 * r + 1, 2 * (r ^ 1), 2 * (r ^ 1) + 1])
    ks = lax.iota(jnp.int32, q_index.shape[0])
    partner = jnp.sum(
        jnp.where(q_index[None] == q_mine[:, None, None], ks[None, :, None], 0), axis=1
    )

    total, kept = begin(p01, p23, screened, w_other)
    total, f1, g0 = lax.optimization_barrier((total, f1, g0))
    up = jnp.where(c == 0, g0[0], parts[2][0])
    down = jnp.where(c == 0, f0[0], parts[1][0])
    across = jnp.where(y_lo == 0, up, down)
    mine = jnp.stack(
        [jnp.where(y_lo == 0, stack[0], across), jnp.where(y_lo == 0, across, stack[0])]
    )
    other = send(mine, SWAP)

    total = more(f0, f1, g0, g1, total, mine, coulomb.reshape(1, share), screened, w_other)
    terms = finish(partner.astype(jnp.int32), ff0, gg1, total, kept, mine, other)
    terms = lax.all_to_all(terms, "col", split_axis=0, concat_axis=0, tiled=True)
    placed = spread(q_index, terms)
    arrived = lax.all_to_all(placed, "row", split_axis=0, concat_axis=0, tiled=True)
    return settle(arrived)


def solution(mesh):
    placed = (P("row", None, "col"), P("row", "col", None), P("col"), P())
    return jax.shard_map(
        local, mesh=mesh, in_specs=placed, out_specs=P("row", "col"), check_vma=False
    )
```

time: 114 us -> 102 us (0.89)
  waiting for transfers between devices: 24.3 us -> 10.1 us
  blocking collectives: 21.9 us -> 33.7 us
  local copies, waits for them, and re-layouts: 7.96 us -> 2.54 us
  starting transfers between devices: 33.4 us -> 29.1 us
  Pallas kernels: 22 us -> 25.3 us
  other arithmetic: 3.51 us -> 1.12 us
    all_to_all x0 -> x1, blocking collectives: none -> 13.2 us  [local(): lax.all_to_all(terms, 'col', split_axis=0, concat_axis=0, tiled=True)]
    all_to_all x1 -> x0, starting transfers between devices: 10.7 us -> none  [local(): lax.all_to_all(terms, 'col', split_axis=0, concat_axis=0, tiled=True)]
    ppermute x12 -> x15, waiting for transfers between devices: 18.2 us -> 10.1 us  [send(): return lax.ppermute(value, AXES, perm)]
    ppermute x12 -> x15, starting transfers between devices: 22.8 us -> 29.1 us  [send(): return lax.ppermute(value, AXES, perm)]
    all_to_all x1 -> x0, waiting for transfers between devices: 6.11 us -> none  [local(): lax.all_to_all(terms, 'col', split_axis=0, concat_axis=0, tiled=True)]
    pallas_call x3, Pallas kernels: 18.6 us -> 21.8 us  [the longest x1 8.03 us: begin(): pl.pallas_call(begin_kernel, grid=(4,), in_specs=[fixed((2, rows, share))...]
    sub x2 -> x0, other arithmetic: 1.54 us -> none  [the longest x1 0.8 us: local(): ys = jnp.mod(y - jnp.where(c == 0, second, first), NY)]
    all_to_all x1, blocking collectives: 21.9 us -> 20.5 us  [local(): lax.all_to_all(placed, 'row', split_axis=0, concat_axis=0, tiled=True)]
  transfers between devices with their start and end apart: 13 -> 15, of which waited for: 5 -> 6; matrix products, arithmetic and copies ran while one was open for 7% -> 2% of each run, Pallas kernels for 12% -> 16%
where the time goes in v4:
time: 102 us
  blocking collectives  33.7 us (33%)
  starting transfers between devices  29.1 us (29%)
  Pallas kernels  25.3 us (25%)
  waiting for transfers between devices  10.1 us (10%)
  local copies, waits for them, and re-layouts  2.54 us (2%)
  other arithmetic  1.12 us (1%)
    ppermute x15, starting transfers between devices, send(): return lax.ppermute(value, AXES, perm)  29.1 us
    all_to_all x1, blocking collectives, local(): lax.all_to_all(placed, 'row', split_axis=0, concat_axis=0, tiled=True)  20.5 us
    all_to_all x1, blocking collectives, local(): lax.all_to_all(terms, 'col', split_axis=0, concat_axis=0, tiled=True)  13.2 us
    ppermute x15, waiting for transfers between devices, send(): return lax.ppermute(value, AXES, perm)  10.1 us
    pallas_call x1, Pallas kernels, begin(): pl.pallas_call(begin_kernel, grid=(4,), in_specs=[fixed((2, rows, share))...  8.03 us
    pallas_call x1, Pallas kernels, more(): pl.pallas_call(more_kernel, grid=(4,), in_specs=[fixed((2, rows, share))]...  7.99 us
    pallas_call x1, Pallas kernels, finish(): pl.pallas_call(finish_kernel, in_specs=[pl.BlockSpec(memory_space=pltpu.S...  5.81 us
    unnamed x11, local copies, waits for them, and re-layouts  2.49 us
  transfers between devices with their start and end apart: 15, of which 6 were waited for; matrix products, arithmetic and copies ran while one was open for 2% of the time, Pallas kernels for 16%

profile of v4, /device:TPU:1, one launch (start us, length us, event | category | flops | bytes accessed | tf_op | source)
XLA Modules:
  0.0 101.9 jit_solution(9433744102249746173)
XLA Ops:
  0.0 3.2 %collective-permute-start.11 = (bf16[2,384,3072]{2,1,0:T(8,128)(2,1)}, bf16[2,384,3072]{2,1,0:T(8,128)(2,1)}, u32[]{:S(2)}, u32[]{:S(2)}) collective-permute-start(bf16[2,384,3072]{2,1,0:T(8,128)(2,1)} %w_own.3), channel_id=1, source_target_pairs={{0,8},{8,0},{16,24},{24,16},{32,40},{40,32},{48,56},{56,48},{64,72... | collective-permute-start | bytes 14155784 | tf_op jit(solution)/shard_map/ppermute | solution.py:48
  3.2 1.3 %collective-permute-start = (bf16[1,32,384]{2,1,0:T(8,128)(2,1)}, bf16[1,32,384]{2,1,0:T(8,128)(2,1)S(1)}, u32[]{:S(2)}, u32[]{:S(2)}) collective-permute-start(bf16[1,32,384]{2,1,0:T(8,128)(2,1)} %bitcast.18), channel_id=1, source_target_pairs={{0,32},{8,40},{16,48},{24,56},{32,64},{40,72},{48,80},{56,88},{64,... | collective-permute-start | bytes 73736 | tf_op jit(solution)/shard_map/ppermute | solution.py:48
  4.5 5.1 %collective-permute-start.1 = (bf16[1,32,384]{2,1,0:T(8,128)(2,1)}, bf16[1,32,384]{2,1,0:T(8,128)(2,1)S(1)}, u32[]{:S(2)}, u32[]{:S(2)}) collective-permute-start(bf16[1,32,384]{2,1,0:T(8,128)(2,1)} %bitcast.19), channel_id=1, source_target_pairs={{0,64},{8,72},{16,80},{24,88},{32,96},{40,104},{48,112},{56,120},{... | collective-permute-start | bytes 73736 | tf_op jit(solution)/shard_map/ppermute | solution.py:48
  9.6 2.4 %collective-permute-start.2 = (bf16[1,32,384]{2,1,0:T(8,128)(2,1)}, bf16[1,32,384]{2,1,0:T(8,128)(2,1)S(1)}, u32[]{:S(2)}, u32[]{:S(2)}) collective-permute-start(bf16[1,32,384]{2,1,0:T(8,128)(2,1)} %bitcast.20), channel_id=1, source_target_pairs={{0,96},{8,104},{16,112},{24,120},{32,0},{40,8},{48,16},{56,24},{64... | collective-permute-start | bytes 73736 | tf_op jit(solution)/shard_map/ppermute | solution.py:48
  15.0 3.2 %collective-permute-done.3 = bf16[4,32,384]{2,1,0:T(8,128)(2,1)S(1)} collective-permute-done((bf16[4,32,384]{2,1,0:T(8,128)(2,1)S(1)}, bf16[4,32,384]{2,1,0:T(8,128)(2,1)S(1)}, u32[]{:S(2)}, u32[]{:S(2)}) %collective-permute-start.3) | collective-permute-done | bytes 98336 | tf_op jit(solution)/shard_map/ppermute | solution.py:48
  18.2 1.4 %collective-permute-start.7 = (bf16[1,256,384]{2,1,0:T(8,128)(2,1)S(1)}, bf16[1,256,384]{2,1,0:T(8,128)(2,1)S(1)}, u32[]{:S(2)}, u32[]{:S(2)}) collective-permute-start(bf16[1,256,384]{2,1,0:T(8,128)(2,1)S(1)} %bitcast.12), channel_id=1, source_target_pairs={{0,1},{8,136},{16,17},{24,152},{32,33},{40,168},{48,49},{56,184},{... | collective-permute-start | bytes 589832 | tf_op jit(solution)/shard_map/ppermute | solution.py:48
  19.6 1.5 %collective-permute-start.8 = (bf16[1,256,384]{2,1,0:T(8,128)(2,1)S(1)}, bf16[1,256,384]{2,1,0:T(8,128)(2,1)S(1)}, u32[]{:S(2)}, u32[]{:S(2)}) collective-permute-start(bf16[1,256,384]{2,1,0:T(8,128)(2,1)S(1)} %bitcast.13), channel_id=1, source_target_pairs={{0,3},{8,140},{16,19},{24,156},{32,35},{40,172},{48,51},{56,188},{... | collective-permute-start | bytes 589832 | tf_op jit(solution)/shard_map/ppermute | solution.py:48
  21.2 1.6 %collective-permute-start.4 = (bf16[1,256,384]{2,1,0:T(8,128)(2,1)S(1)}, bf16[1,256,384]{2,1,0:T(8,128)(2,1)S(1)}, u32[]{:S(2)}, u32[]{:S(2)}) collective-permute-start(bf16[1,256,384]{2,1,0:T(8,128)(2,1)S(1)} %bitcast.14), channel_id=1, source_target_pairs={{0,2},{8,12},{16,18},{24,28},{32,34},{40,44},{48,50},{56,60},{64,6... | collective-permute-start | bytes 589832 | tf_op jit(solution)/shard_map/ppermute | solution.py:48
  22.7 1.4 %collective-permute-done.7 = bf16[1,256,384]{2,1,0:T(8,128)(2,1)S(1)} collective-permute-done((bf16[1,256,384]{2,1,0:T(8,128)(2,1)S(1)}, bf16[1,256,384]{2,1,0:T(8,128)(2,1)S(1)}, u32[]{:S(2)}, u32[]{:S(2)}) %collective-permute-start.7) | collective-permute-done | bytes 196640 | tf_op jit(solution)/shard_map/ppermute | solution.py:48
  24.1 1.7 %collective-permute-done.8 = bf16[1,256,384]{2,1,0:T(8,128)(2,1)S(1)} collective-permute-done((bf16[1,256,384]{2,1,0:T(8,128)(2,1)S(1)}, bf16[1,256,384]{2,1,0:T(8,128)(2,1)S(1)}, u32[]{:S(2)}, u32[]{:S(2)}) %collective-permute-start.8) | collective-permute-done | bytes 196640 | tf_op jit(solution)/shard_map/ppermute | solution.py:48
  25.9 2.6 %collective-permute-start.9 = (bf16[2,256,384]{2,1,0:T(8,128)(2,1)S(1)}, bf16[2,256,384]{2,1,0:T(8,128)(2,1)S(1)}, u32[]{:S(2)}, u32[]{:S(2)}) collective-permute-start(bf16[2,256,384]{2,1,0:T(8,128)(2,1)S(1)} %constant_dynamic-update-slice_fusion.5.p23), channel_id=1, source_target_pairs={{0,132},{8,11},{16,148},{24,27},{32,164},{40,43},{48,180},{56,59},... | collective-permute-start | bytes 1179656 | tf_op jit(solution)/shard_map/ppermute | solution.py:48
  28.7 1.2 %collective-permute-start.12 = (bf16[2,256,384]{2,1,0:T(8,128)(2,1)S(1)}, bf16[2,256,384]{2,1,0:T(8,128)(2,1)S(1)}, u32[]{:S(2)}, u32[]{:S(2)}) collective-permute-start(bf16[2,256,384]{2,1,0:T(8,128)(2,1)S(1)} %constant_dynamic-update-slice_fusion.5.p23), channel_id=1, source_target_pairs={{0,128},{8,9},{16,144},{24,25},{32,160},{40,41},{48,176},{56,57},{... | collective-permute-start | bytes 1179656 | tf_op jit(solution)/shard_map/ppermute | solution.py:48
  30.0 1.5 %collective-permute-start.13 = (bf16[2,256,384]{2,1,0:T(8,128)(2,1)S(1)}, bf16[2,256,384]{2,1,0:T(8,128)(2,1)S(1)}, u32[]{:S(2)}, u32[]{:S(2)}) collective-permute-start(bf16[2,256,384]{2,1,0:T(8,128)(2,1)S(1)} %pad_maximum_fusion.p01), channel_id=1, source_target_pairs={{0,132},{8,11},{16,148},{24,27},{32,164},{40,43},{48,180},{56,59},... | collective-permute-start | bytes 1179656 | tf_op jit(solution)/shard_map/ppermute | solution.py:48
  31.4 2.4 %collective-permute-done.9.g1 = bf16[2,256,384]{2,1,0:T(8,128)(2,1)S(1)} collective-permute-done((bf16[2,256,384]{2,1,0:T(8,128)(2,1)S(1)}, bf16[2,256,384]{2,1,0:T(8,128)(2,1)S(1)}, u32[]{:S(2)}, u32[]{:S(2)}) %collective-permute-start.9) | collective-permute-done | bytes 393248 | tf_op jit(solution)/shard_map/ppermute | solution.py:48
  33.8 2.7 %collective-permute-start.10 = (bf16[2,256,384]{2,1,0:T(8,128)(2,1)S(1)}, bf16[2,256,384]{2,1,0:T(8,128)(2,1)S(1)}, u32[]{:S(2)}, u32[]{:S(2)}) collective-permute-start(bf16[2,256,384]{2,1,0:T(8,128)(2,1)S(1)} %collective-permute-done.9.g1), channel_id=1, source_target_pairs={{0,132},{8,11},{16,148},{24,27},{32,164},{40,43},{48,180},{56,59},... | collective-permute-start | bytes 1179656 | tf_op jit(solution)/shard_map/ppermute | solution.py:48
  36.7 8.0 %begin.1 = (f32[4,2,256,384]{3,2,1,0:T(8,128)S(1)}, bf16[4,384,1536]{2,1,0:T(8,128)(2,1)}) custom-call(bf16[2,256,384]{2,1,0:T(8,128)(2,1)S(1)} %pad_maximum_fusion.p01, bf16[2,256,384]{2,1,0:T(8,128)(2,1)S(1)} %constant_dynamic-update-slice_fusion.5.p23, bf16[2,384,3072]{2,1,0:T(8,128)(2,1)} %w_own.3, bf16[2,384,3072]{2,1,0:T(8,128)(2,1)} %collective-permute-done.11.w_other), custom_call_target="tpu_custom_call" | custom-call | flops 1207959552 | bytes 17825792 | tf_op jit(solution)/shard_map/begin/pallas_call | solution.py:141
  44.8 1.7 %copy-done = f32[4,2,256,384]{3,2,1,0:T(8,128)} copy-done((f32[4,2,256,384]{3,2,1,0:T(8,128)}, f32[4,2,256,384]{3,2,1,0:T(8,128)S(1)}, u32[]{:S(2)}) %copy-start) | copy-done | bytes 3145752
  46.6 4.1 %collective-permute-start.14 = (bf16[2,256,384]{2,1,0:T(8,128)(2,1)S(1)}, bf16[2,256,384]{2,1,0:T(8,128)(2,1)S(1)}, u32[]{:S(2)}, u32[]{:S(2)}) collective-permute-start(bf16[2,256,384]{2,1,0:T(8,128)(2,1)S(1)} %pad_maximum_fusion.1.mine), channel_id=1, source_target_pairs={{0,8},{8,0},{16,24},{24,16},{32,40},{40,32},{48,56},{56,48},{64,72... | collective-permute-start | bytes 1179656 | tf_op jit(solution)/shard_map/ppermute | solution.py:48
  50.9 8.0 %more.1.before = f32[4,2,256,384]{3,2,1,0:T(8,128)S(1)} custom-call(bf16[2,256,384]{2,1,0:T(8,128)(2,1)S(1)} %collective-permute-done.5.f0, bf16[2,256,384]{2,1,0:T(8,128)(2,1)S(1)} %collective-permute-done.12.f1, bf16[2,256,384]{2,1,0:T(8,128)(2,1)S(1)} %collective-permute-done.13.g0, bf16[2,256,384]{2,1,0:T(8,128)(2,1)S(1)} %collective-permute-done.9.g1, ...), custom_call_target="tpu_custom_call" | custom-call | flops 2415919104 | bytes 17825792 | tf_op jit(solution)/shard_map/more/pallas_call | solution.py:162
  58.9 5.8 %finish.1 = f32[8,2,16,128]{3,2,1,0:T(8,128)S(1)} custom-call(s32[4,64]{1,0:T(4,128)S(1)} %select_reduce_fusion.partner, bf16[2,256,384]{2,1,0:T(8,128)(2,1)S(1)} %collective-permute-done.6.p01, bf16[2,256,384]{2,1,0:T(8,128)(2,1)S(1)} %collective-permute-done.10.p23, f32[4,2,256,384]{3,2,1,0:T(8,128)S(1)} %more.1.before, ...), custom_call_target="tpu_custom_call" | custom-call | flops 1207959552 | bytes 9437184 | tf_op jit(solution)/shard_map/finish/pallas_call | solution.py:212
  64.7 13.2 %all_to_all.10.terms = f32[8,2,16,128]{3,2,1,0:T(8,128)} all-to-all(f32[8,2,16,128]{3,2,1,0:T(8,128)S(1)} %finish.1), channel_id=1, replica_groups=mesh['row'=32,'col'=8] {'col'}, dimensions={0} | all-to-all | bytes 262144 | tf_op jit(solution)/shard_map/all_to_all | solution.py:335
  78.0 1.8 %spread.1 = f32[32,16,128]{2,1,0:T(8,128)} custom-call(s32[64,64]{1,0:T(8,128)} %q_index.1, f32[8,2,16,128]{3,2,1,0:T(8,128)} %all_to_all.10.terms), custom_call_target="tpu_custom_call" | custom-call | tf_op jit(solution)/shard_map/spread/pallas_call | solution.py:261
  79.8 20.5 %all_to_all.11.arrived = f32[32,16,128]{2,1,0:T(8,128)} all-to-all(f32[32,16,128]{2,1,0:T(8,128)} %spread.1), channel_id=1, replica_groups=mesh['row'=32,'col'=8] {'row'}, dimensions={0} | all-to-all | bytes 524288 | tf_op jit(solution)/shard_map/all_to_all | solution.py:337
  100.3 1.7 %settle.1 = f32[32,128]{1,0:T(8,128)} custom-call(f32[32,16,128]{2,1,0:T(8,128)} %all_to_all.11.arrived), custom_call_target="tpu_custom_call" | custom-call | tf_op jit(solution)/shard_map/settle/pallas_call | solution.py:290
  (34 shorter events, 3.9 us)
Async XLA Ops:
  0.0 36.7 %collective-permute-start.11 = (bf16[2,384,3072]{2,1,0:T(8,128)(2,1)}, bf16[2,384,3072]{2,1,0:T(8,128)(2,1)}, u32[]{:S(2)}, u32[]{:S(2)}) collective-permute-start(bf16[2,384,3072]{2,1,0:T(8,128)(2,1)} %w_own.3), channel_id=1, source_target_pairs={{0,8},{8,0},{16,24},{24,16},{32,40},{40,32},{48,56},{56,48},{64,72... | collective-permute-start | bytes 14155784 | tf_op jit(solution)/shard_map/ppermute | solution.py:48
  3.2 9.5 %collective-permute-start = (bf16[1,32,384]{2,1,0:T(8,128)(2,1)}, bf16[1,32,384]{2,1,0:T(8,128)(2,1)S(1)}, u32[]{:S(2)}, u32[]{:S(2)}) collective-permute-start(bf16[1,32,384]{2,1,0:T(8,128)(2,1)} %bitcast.18), channel_id=1, source_target_pairs={{0,32},{8,40},{16,48},{24,56},{32,64},{40,72},{48,80},{56,88},{64,... | collective-permute-start | bytes 73736 | tf_op jit(solution)/shard_map/ppermute | solution.py:48
  4.5 8.3 %collective-permute-start.1 = (bf16[1,32,384]{2,1,0:T(8,128)(2,1)}, bf16[1,32,384]{2,1,0:T(8,128)(2,1)S(1)}, u32[]{:S(2)}, u32[]{:S(2)}) collective-permute-start(bf16[1,32,384]{2,1,0:T(8,128)(2,1)} %bitcast.19), channel_id=1, source_target_pairs={{0,64},{8,72},{16,80},{24,88},{32,96},{40,104},{48,112},{56,120},{... | collective-permute-start | bytes 73736 | tf_op jit(solution)/shard_map/ppermute | solution.py:48
  9.6 4.3 %collective-permute-start.2 = (bf16[1,32,384]{2,1,0:T(8,128)(2,1)}, bf16[1,32,384]{2,1,0:T(8,128)(2,1)S(1)}, u32[]{:S(2)}, u32[]{:S(2)}) collective-permute-start(bf16[1,32,384]{2,1,0:T(8,128)(2,1)} %bitcast.20), channel_id=1, source_target_pairs={{0,96},{8,104},{16,112},{24,120},{32,0},{40,8},{48,16},{56,24},{64... | collective-permute-start | bytes 73736 | tf_op jit(solution)/shard_map/ppermute | solution.py:48
  14.7 3.6 %collective-permute-start.3 = (bf16[4,32,384]{2,1,0:T(8,128)(2,1)S(1)}, bf16[4,32,384]{2,1,0:T(8,128)(2,1)S(1)}, u32[]{:S(2)}, u32[]{:S(2)}) collective-permute-start(bf16[4,32,384]{2,1,0:T(8,128)(2,1)S(1)} %pad_maximum_fusion.2), channel_id=1, source_target_pairs={{0,16},{8,24},{16,0},{24,8},{32,48},{40,56},{48,32},{56,40},{64,80... | collective-permute-start | bytes 294920 | tf_op jit(solution)/shard_map/ppermute | solution.py:48
  18.2 5.9 %collective-permute-start.7 = (bf16[1,256,384]{2,1,0:T(8,128)(2,1)S(1)}, bf16[1,256,384]{2,1,0:T(8,128)(2,1)S(1)}, u32[]{:S(2)}, u32[]{:S(2)}) collective-permute-start(bf16[1,256,384]{2,1,0:T(8,128)(2,1)S(1)} %bitcast.12), channel_id=1, source_target_pairs={{0,1},{8,136},{16,17},{24,152},{32,33},{40,168},{48,49},{56,184},{... | collective-permute-start | bytes 589832 | tf_op jit(solution)/shard_map/ppermute | solution.py:48
  19.6 6.3 %collective-permute-start.8 = (bf16[1,256,384]{2,1,0:T(8,128)(2,1)S(1)}, bf16[1,256,384]{2,1,0:T(8,128)(2,1)S(1)}, u32[]{:S(2)}, u32[]{:S(2)}) collective-permute-start(bf16[1,256,384]{2,1,0:T(8,128)(2,1)S(1)} %bitcast.13), channel_id=1, source_target_pairs={{0,3},{8,140},{16,19},{24,156},{32,35},{40,172},{48,51},{56,188},{... | collective-permute-start | bytes 589832 | tf_op jit(solution)/shard_map/ppermute | solution.py:48
  21.2 7.3 %collective-permute-start.4 = (bf16[1,256,384]{2,1,0:T(8,128)(2,1)S(1)}, bf16[1,256,384]{2,1,0:T(8,128)(2,1)S(1)}, u32[]{:S(2)}, u32[]{:S(2)}) collective-permute-start(bf16[1,256,384]{2,1,0:T(8,128)(2,1)S(1)} %bitcast.14), channel_id=1, source_target_pairs={{0,2},{8,12},{16,18},{24,28},{32,34},{40,44},{48,50},{56,60},{64,6... | collective-permute-start | bytes 589832 | tf_op jit(solution)/shard_map/ppermute | solution.py:48
  25.9 7.9 %collective-permute-start.9 = (bf16[2,256,384]{2,1,0:T(8,128)(2,1)S(1)}, bf16[2,256,384]{2,1,0:T(8,128)(2,1)S(1)}, u32[]{:S(2)}, u32[]{:S(2)}) collective-permute-start(bf16[2,256,384]{2,1,0:T(8,128)(2,1)S(1)} %constant_dynamic-update-slice_fusion.5.p23), channel_id=1, source_target_pairs={{0,132},{8,11},{16,148},{24,27},{32,164},{40,43},{48,180},{56,59},... | collective-permute-start | bytes 1179656 | tf_op jit(solution)/shard_map/ppermute | solution.py:48
  28.5 8.2 %collective-permute-start.5 = (bf16[2,256,384]{2,1,0:T(8,128)(2,1)S(1)}, bf16[2,256,384]{2,1,0:T(8,128)(2,1)S(1)}, u32[]{:S(2)}, u32[]{:S(2)}) collective-permute-start(bf16[2,256,384]{2,1,0:T(8,128)(2,1)S(1)} %pad_maximum_fusion.p01), channel_id=1, source_target_pairs={{0,128},{8,9},{16,144},{24,25},{32,160},{40,41},{48,176},{56,57},{... | collective-permute-start | bytes 1179656 | tf_op jit(solution)/shard_map/ppermute | solution.py:48
  28.7 17.7 %collective-permute-start.12 = (bf16[2,256,384]{2,1,0:T(8,128)(2,1)S(1)}, bf16[2,256,384]{2,1,0:T(8,128)(2,1)S(1)}, u32[]{:S(2)}, u32[]{:S(2)}) collective-permute-start(bf16[2,256,384]{2,1,0:T(8,128)(2,1)S(1)} %constant_dynamic-update-slice_fusion.5.p23), channel_id=1, source_target_pairs={{0,128},{8,9},{16,144},{24,25},{32,160},{40,41},{48,176},{56,57},{... | collective-permute-start | bytes 1179656 | tf_op jit(solution)/shard_map/ppermute | solution.py:48
  30.0 16.5 %collective-permute-start.13 = (bf16[2,256,384]{2,1,0:T(8,128)(2,1)S(1)}, bf16[2,256,384]{2,1,0:T(8,128)(2,1)S(1)}, u32[]{:S(2)}, u32[]{:S(2)}) collective-permute-start(bf16[2,256,384]{2,1,0:T(8,128)(2,1)S(1)} %pad_maximum_fusion.p01), channel_id=1, source_target_pairs={{0,132},{8,11},{16,148},{24,27},{32,164},{40,43},{48,180},{56,59},... | collective-permute-start | bytes 1179656 | tf_op jit(solution)/shard_map/ppermute | solution.py:48
  31.4 19.3 %copy-start.2 = (f32[384]{0:T(512)S(1)}, f32[384]{0:T(512)}, u32[]{:S(2)}) copy-start(f32[384]{0:T(512)} %param.6) | copy-start | bytes 4612
  31.4 19.3 %copy-start.1 = (s32[64,64]{1,0:T(8,128)S(1)}, s32[64,64]{1,0:T(8,128)}, u32[]{:S(2)}) copy-start(s32[64,64]{1,0:T(8,128)} %q_index.1) | copy-start | bytes 49156
  33.8 25.1 %collective-permute-start.10 = (bf16[2,256,384]{2,1,0:T(8,128)(2,1)S(1)}, bf16[2,256,384]{2,1,0:T(8,128)(2,1)S(1)}, u32[]{:S(2)}, u32[]{:S(2)}) collective-permute-start(bf16[2,256,384]{2,1,0:T(8,128)(2,1)S(1)} %collective-permute-done.9.g1), channel_id=1, source_target_pairs={{0,132},{8,11},{16,148},{24,27},{32,164},{40,43},{48,180},{56,59},... | collective-permute-start | bytes 1179656 | tf_op jit(solution)/shard_map/ppermute | solution.py:48
  36.7 22.2 %collective-permute-start.6 = (bf16[2,256,384]{2,1,0:T(8,128)(2,1)S(1)}, bf16[2,256,384]{2,1,0:T(8,128)(2,1)S(1)}, u32[]{:S(2)}, u32[]{:S(2)}) collective-permute-start(bf16[2,256,384]{2,1,0:T(8,128)(2,1)S(1)} %collective-permute-done.5.f0), channel_id=1, source_target_pairs={{0,128},{8,9},{16,144},{24,25},{32,160},{40,41},{48,176},{56,57},{... | collective-permute-start | bytes 1179656 | tf_op jit(solution)/shard_map/ppermute | solution.py:48
  44.8 1.7 %copy-start = (f32[4,2,256,384]{3,2,1,0:T(8,128)}, f32[4,2,256,384]{3,2,1,0:T(8,128)S(1)}, u32[]{:S(2)}) copy-start(f32[4,2,256,384]{3,2,1,0:T(8,128)S(1)} %get-tuple-element.13.before) | copy-start | bytes 9437188
  46.6 12.3 %collective-permute-start.14 = (bf16[2,256,384]{2,1,0:T(8,128)(2,1)S(1)}, bf16[2,256,384]{2,1,0:T(8,128)(2,1)S(1)}, u32[]{:S(2)}, u32[]{:S(2)}) collective-permute-start(bf16[2,256,384]{2,1,0:T(8,128)(2,1)S(1)} %pad_maximum_fusion.1.mine), channel_id=1, source_target_pairs={{0,8},{8,0},{16,24},{24,16},{32,40},{40,32},{48,56},{56,48},{64,72... | collective-permute-start | bytes 1179656 | tf_op jit(solution)/shard_map/ppermute | solution.py:48

commit v5 on v4

v5 whole, which is shorter than its diff:
```python
import jax
import jax.numpy as jnp
from jax import lax
from jax.experimental import pallas as pl
from jax.experimental.pallas import tpu as pltpu
from jax.sharding import PartitionSpec as P

AXES = ("row", "col")
NX, NY, NZ, NCORE = 4, 4, 8, 2
SHIFTS = (0, 2, 1, -1)
ZSHIFTS = (0, 2, 4, -2)
VMEM = 24 * 1024 * 1024


def device_index(x, y, z, c):
    y_hi, y_lo = divmod(y % NY, 2)
    row = (y_lo * NZ + z % NZ) * NCORE + c
    return row * 8 + y_hi * NX + x % NX


def pairs(move):
    found = []
    for x in range(NX):
        for y in range(NY):
            for z in range(NZ):
                for c in range(NCORE):
                    found.append((device_index(x, y, z, c), device_index(*move(x, y, z, c))))
    return found


SWAP = pairs(lambda x, y, z, c: (x, y, z, 1 - c))
ZPAIR = pairs(lambda x, y, z, c: (x, y, z ^ 1, c))


def along_z(s):
    return pairs(lambda x, y, z, c: (x, y, z + s, c))


def first_plane(s):
    return pairs(lambda x, y, z, c: (x + s, y, z, c) if c == 0 else (x, y + s, z, c))


def second_plane(s):
    return pairs(lambda x, y, z, c: (x, y + s, z, c) if c == 0 else (x + s, y, z, c))


def send(value, perm):
    return lax.ppermute(value, AXES, perm)


def contract(a, b):
    return lax.dot_general(a, b, (((1,), (1,)), ((), ())), preferred_element_type=jnp.float32)


def where_am_i():
    r, j = lax.axis_index("row"), lax.axis_index("col")
    return r, j, r & 1, (r >> 1) & 7, r >> 4


def spot(k, i):
    r, j, c, _, y_lo = where_am_i()
    first, second = SHIFTS[i], SHIFTS[k]
    x = ((j & 3) - first - c * (second - first)) & 3
    y = (2 * (j >> 2) + y_lo - second - c * (first - second)) & 3
    return (y >> 1) * NX + x, y & 1


def place_of(z_wanted):
    z = where_am_i()[3]
    side = (z ^ z_wanted) & 1
    return side * 4 + ((((z ^ side) - z_wanted) & 7) >> 1)


def load_kernel(own, other, out, sems):
    copies = [
        pltpu.make_async_copy(own, out.at[pl.ds(0, 2)], sems.at[0]),
        pltpu.make_async_copy(other, out.at[pl.ds(2, 2)], sems.at[1]),
    ]
    for copy in copies:
        copy.start()
    for copy in copies:
        copy.wait()


def load(own, other):
    _, share, whole = own.shape
    return pl.pallas_call(
        load_kernel,
        in_specs=[pl.BlockSpec(memory_space=pl.ANY)] * 2,
        out_specs=pl.BlockSpec(memory_space=pltpu.VMEM),
        out_shape=jax.ShapeDtypeStruct((4, share, whole), own.dtype),
        scratch_shapes=[pltpu.SemaphoreType.DMA((2,))],
        compiler_params=pltpu.CompilerParams(vmem_limit_bytes=VMEM),
        cost_estimate=pl.CostEstimate(
            flops=0, bytes_accessed=8 * share * whole * 2, transcendentals=0
        ),
        name="load",
    )(own, other)


def solve_kernel(
    partner, coulomb, w, p01, p23, f0, f1, g0, g1, ff0, gg1, other, out, panel, left_rows, image
):
    rows, share = p01.shape[1:]
    r, j, c, _, _ = where_am_i()
    starts = [pl.multiple_of(place_of(z) * 32, 32) for z in range(NZ)]
    arrays = ((p01, p23), (ff0, gg1), (f0, f1), (g0, g1))
    for k in range(4):
        for i in range(4):
            col, low = spot(k, i)
            for z in range(NZ):
                to = pl.multiple_of(low * rows + z * 32, 32)
                piece = arrays[k][i // 2][i % 2, pl.ds(starts[z], 32), :]
                panel[pl.ds(to, 32), pl.ds(pl.multiple_of(col * share, share), share)] = piece
    left_rows[: 2 * rows, :] = panel[:, pl.ds(pl.multiple_of(j * share, share), share)]
    for low in range(2):
        for z in range(NZ):
            to = (2 + low) * rows + z * 32
            left_rows[to : to + 32, :] = other[low, pl.ds(starts[z], 32), :]
    for q in range(4):
        image[q] = contract(w[q], panel[...]).astype(image.dtype)

    lane = lax.broadcasted_iota(jnp.int32, (16, 128), 1)
    twice = 2.0 * coulomb[...]
    for pair in range(4):
        columns = left_rows[128 * pair : 128 * pair + 128, :]
        blocks = []
        for q in range(4):
            left = []
            for i in range(8):
                k = partner[q, 16 * pair + 8 * (i // 4) + 4 * (i // 2 % 2) + 2 * c + i % 2]
                block = ((((k >> 1) & 1) ^ c) * 2 + (k >> 5)) * NZ + ((k >> 2) & 7)
                start = pl.multiple_of(block * 32 + (k & 1) * 16, 16)
                left.append(left_rows[pl.ds(start, 16), :])
            left = jnp.concatenate(left, axis=0)
            weighted = (left.astype(jnp.float32) * twice).astype(left.dtype)
            met = contract(weighted, columns) - jnp.dot(
                left,
                image[q, :, 128 * pair : 128 * pair + 128],
                preferred_element_type=jnp.float32,
            )
            block = jnp.zeros((16, 128), jnp.float32)
            for i in range(8):
                block = jnp.where(lane // 16 == i, met[16 * i : 16 * i + 16], block)
            blocks.append(block)
        for two in range(2):
            even, odd = blocks[2 * two], blocks[2 * two + 1]
            out[2 * pair, two] = jnp.where(lane < 64, even, pltpu.roll(odd, 64, 1))
            out[2 * pair + 1, two] = jnp.where(lane < 64, pltpu.roll(even, 64, 1), odd)


def solve(partner, coulomb, w, panels, other):
    rows, share = panels[0].shape[1:]
    whole = w.shape[2]
    vmem = pl.BlockSpec(memory_space=pltpu.VMEM)
    return pl.pallas_call(
        solve_kernel,
        in_specs=[pl.BlockSpec(memory_space=pltpu.SMEM)] + [vmem] * 11,
        out_specs=vmem,
        out_shape=jax.ShapeDtypeStruct((8, 2, 16, 128), jnp.float32),
        scratch_shapes=[
            pltpu.VMEM((2 * rows, whole), jnp.bfloat16),
            pltpu.VMEM((4 * rows, share), jnp.bfloat16),
            pltpu.VMEM((4, share, 2 * rows), jnp.bfloat16),
        ],
        compiler_params=pltpu.CompilerParams(vmem_limit_bytes=VMEM),
        cost_estimate=pl.CostEstimate(
            flops=2 * 4 * share * whole * 2 * rows,
            bytes_accessed=4 * share * whole * 2,
            transcendentals=0,
        ),
        name="solve",
    )(partner, coulomb, w, *panels, other)


def spread_kernel(q_index, terms, out):
    r, j, c, _, _ = where_am_i()
    ks = q_index.shape[0]
    row = lax.broadcasted_iota(jnp.int32, (ks, 128), 0)
    col = lax.broadcasted_iota(jnp.int32, (ks, 128), 1)
    slot = (col & 63) >> 4
    hit = row == 8 * j + 4 * (slot >> 1) + 2 * c + (slot & 1)
    seen = jnp.zeros((ks // 2, 128), jnp.float32)
    for k in range(2):
        rows = q_index[pl.ds(k, ks // 2, stride=2), :].astype(jnp.float32).astype(jnp.bfloat16)
        pick = jnp.where(hit & (col >> 6 == k), 1.0, 0.0).astype(jnp.bfloat16)
        seen = seen + jnp.dot(rows, pick, preferred_element_type=jnp.float32)
    seen = seen.astype(jnp.int32)
    lane = lax.broadcasted_iota(jnp.int32, (16, 128), 1)
    blocks = []
    for two in range(2):
        full = terms[0, two]
        for i in range(1, 8):
            full = full + terms[i, two]
        turned = pltpu.roll(full, 64, 1)
        blocks.append(jnp.where(lane < 64, full, turned))
        blocks.append(jnp.where(lane < 64, turned, full))
    mine = (2 * r, 2 * r + 1, 2 * (r ^ 1), 2 * (r ^ 1) + 1)
    for target in range(out.shape[0]):
        wanted = jnp.broadcast_to(seen[target : target + 1, :], (16, 128))
        block = jnp.zeros((16, 128), jnp.float32)
        for q in range(4):
            block = jnp.where(wanted == mine[q], blocks[q], block)
        out[target] = block.astype(out.dtype)


def spread(q_index, terms):
    vmem = pl.BlockSpec(memory_space=pltpu.VMEM)
    return pl.pallas_call(
        spread_kernel,
        in_specs=[vmem, vmem],
        out_specs=vmem,
        out_shape=jax.ShapeDtypeStruct((32, 16, 128), jnp.float32),
        name="spread",
    )(q_index, terms)


def settle_kernel(arrived, out):
    lane = lax.broadcasted_iota(jnp.int32, (16, 128), 1) // 32
    sums = []
    for c in range(2):
        full = arrived[c].astype(jnp.float32)
        for r in range(2 + c, arrived.shape[0], 2):
            full = full + arrived[r].astype(jnp.float32)
        sums.append(full)
    for k in range(2):
        block = jnp.zeros((16, 128), jnp.float32)
        for z in range(2):
            for c in range(2):
                move = (z * 64 + c * 32 - k * 64 - z * 32) % 128
                turned = pltpu.roll(sums[c], move, 1) if move else sums[c]
                block = jnp.where(lane == 2 * z + c, turned, block)
        out[16 * k : 16 * k + 16, :] = block


def settle(arrived):
    vmem = pl.BlockSpec(memory_space=pltpu.VMEM)
    return pl.pallas_call(
        settle_kernel,
        in_specs=[vmem],
        out_specs=vmem,
        out_shape=jax.ShapeDtypeStruct((32, 128), jnp.float32),
        name="settle",
    )(arrived)


def local(pair_matrix, screened, coulomb, q_index):
    bands, share = pair_matrix.shape[1:]
    r, _, c, _, y_lo = where_am_i()
    w_other = send(screened, SWAP)
    own = pair_matrix.reshape(1, 2 * bands, share)
    even = jnp.concatenate([own] + [send(own, along_z(s)) for s in ZSHIFTS[1:]], axis=0)
    stack = jnp.concatenate([even, send(even, ZPAIR)], axis=0).reshape(1, NZ * 32, share)
    parts = [send(stack, first_plane(s)) for s in SHIFTS[1:]]
    p01 = jnp.concatenate([stack, parts[0]], axis=0)
    p23 = jnp.concatenate([parts[1], parts[2]], axis=0)

    f0 = send(p01, second_plane(1))
    g1 = send(p23, second_plane(-1))
    f1 = send(p23, second_plane(1))
    g0 = send(p01, second_plane(-1))
    ff0 = send(f0, second_plane(1))
    gg1 = send(g1, second_plane(-1))

    q_mine = jnp.stack([2 * r, 2 * r + 1, 2 * (r ^ 1), 2 * (r ^ 1) + 1])
    ks = lax.iota(jnp.int32, q_index.shape[0])
    partner = jnp.sum(
        jnp.where(q_index[None] == q_mine[:, None, None], ks[None, :, None], 0), axis=1
    )

    w = load(screened, w_other)
    w, f1, g0 = lax.optimization_barrier((w, f1, g0))
    up = jnp.where(c == 0, g0[0], parts[2][0])
    down = jnp.where(c == 0, f0[0], parts[1][0])
    across = jnp.where(y_lo == 0, up, down)
    mine = jnp.stack(
        [jnp.where(y_lo == 0, stack[0], across), jnp.where(y_lo == 0, across, stack[0])]
    )
    other = send(mine, SWAP)

    panels = (p01, p23, f0, f1, g0, g1, ff0, gg1)
    terms = solve(partner.astype(jnp.int32), coulomb.reshape(1, share), w, panels, other)
    terms = lax.all_to_all(terms, "col", split_axis=0, concat_axis=0, tiled=True)
    placed = spread(q_index, terms)
    arrived = lax.all_to_all(placed, "row", split_axis=0, concat_axis=0, tiled=True)
    return settle(arrived)


def solution(mesh):
    placed = (P("row", None, "col"), P("row", "col", None), P("col"), P())
    return jax.shard_map(
        local, mesh=mesh, in_specs=placed, out_specs=P("row", "col"), check_vma=False
    )
```

time: 102 us -> 99.7 us (0.977)
  Pallas kernels: 25.3 us -> 13.3 us
  local copies, waits for them, and re-layouts: 2.54 us -> 10.6 us
  starting transfers between devices: 29.1 us -> 34.6 us
  blocking collectives: 33.7 us -> 29.2 us
  other arithmetic: 1.12 us -> 2.64 us
  waiting for transfers between devices: 10.1 us -> 8.79 us
    pallas_call x3 -> x2, Pallas kernels: 21.8 us -> 9.82 us  [the longest x1 7.15 us: solve(): pl.pallas_call(solve_kernel, in_specs=[pl.BlockSpec(memory_space=pltpu.SM...]
    unnamed x11 -> x17, local copies, waits for them, and re-layouts: 2.49 us -> 10.5 us
    ppermute x15, starting transfers between devices: 29.1 us -> 34.6 us  [send(): return lax.ppermute(value, AXES, perm)]
    all_to_all x1, blocking collectives: 13.2 us -> 9.99 us  [local(): lax.all_to_all(terms, 'col', split_axis=0, concat_axis=0, tiled=True)]
    all_to_all x1, blocking collectives: 20.5 us -> 19.2 us  [local(): lax.all_to_all(placed, 'row', split_axis=0, concat_axis=0, tiled=True)]
    ppermute x15, waiting for transfers between devices: 10.1 us -> 8.79 us  [send(): return lax.ppermute(value, AXES, perm)]
  transfers between devices with their start and end apart: 15 -> 15, of which waited for: 6 -> 6; matrix products, arithmetic and copies ran while one was open for 2% -> 4% of each run, Pallas kernels for 16% -> 3%
where the time goes in v5:
time: 99.7 us; the launch traced here: 99.2 us
  starting transfers between devices  34.6 us (35%)
  blocking collectives  29.2 us (29%)
  Pallas kernels  13.3 us (13%)
  local copies, waits for them, and re-layouts  10.6 us (11%)
  waiting for transfers between devices  8.79 us (9%)
  other arithmetic  2.64 us (3%)
    ppermute x15, starting transfers between devices, send(): return lax.ppermute(value, AXES, perm)  34.6 us
    all_to_all x1, blocking collectives, local(): lax.all_to_all(placed, 'row', split_axis=0, concat_axis=0, tiled=True)  19.2 us
    unnamed x17, local copies, waits for them, and re-layouts  10.5 us
    all_to_all x1, blocking collectives, local(): lax.all_to_all(terms, 'col', split_axis=0, concat_axis=0, tiled=True)  9.99 us
    ppermute x15, waiting for transfers between devices, send(): return lax.ppermute(value, AXES, perm)  8.79 us
    pallas_call x1, Pallas kernels, solve(): pl.pallas_call(solve_kernel, in_specs=[pl.BlockSpec(memory_space=pltpu.SM...  7.15 us
    pallas_call x1, Pallas kernels, load(): pl.pallas_call(load_kernel, in_specs=[pl.BlockSpec(memory_space=pl.ANY)]...  2.67 us
  transfers between devices with their start and end apart: 15, of which 6 were waited for; matrix products, arithmetic and copies ran while one was open for 4% of the time, Pallas kernels for 3%

profile of v5, /device:TPU:1, one launch (start us, length us, event | category | flops | bytes accessed | tf_op | source)
XLA Modules:
  0.0 99.2 jit_solution(1582956153409543293)
XLA Ops:
  0.0 3.2 %collective-permute-start = (bf16[2,384,3072]{2,1,0:T(8,128)(2,1)}, bf16[2,384,3072]{2,1,0:T(8,128)(2,1)}, u32[]{:S(2)}, u32[]{:S(2)}) collective-permute-start(bf16[2,384,3072]{2,1,0:T(8,128)(2,1)} %own.1), channel_id=1, source_target_pairs={{0,8},{8,0},{16,24},{24,16},{32,40},{40,32},{48,56},{56,48},{64,72... | collective-permute-start | bytes 14155784 | tf_op jit(solution)/shard_map/ppermute | solution.py:48
  3.2 1.3 %collective-permute-start.1 = (bf16[1,32,384]{2,1,0:T(8,128)(2,1)}, bf16[1,32,384]{2,1,0:T(8,128)(2,1)S(1)}, u32[]{:S(2)}, u32[]{:S(2)}) collective-permute-start(bf16[1,32,384]{2,1,0:T(8,128)(2,1)} %bitcast.18), channel_id=1, source_target_pairs={{0,32},{8,40},{16,48},{24,56},{32,64},{40,72},{48,80},{56,88},{64,... | collective-permute-start | bytes 73736 | tf_op jit(solution)/shard_map/ppermute | solution.py:48
  4.5 5.1 %collective-permute-start.2 = (bf16[1,32,384]{2,1,0:T(8,128)(2,1)}, bf16[1,32,384]{2,1,0:T(8,128)(2,1)S(1)}, u32[]{:S(2)}, u32[]{:S(2)}) collective-permute-start(bf16[1,32,384]{2,1,0:T(8,128)(2,1)} %bitcast.19), channel_id=1, source_target_pairs={{0,64},{8,72},{16,80},{24,88},{32,96},{40,104},{48,112},{56,120},{... | collective-permute-start | bytes 73736 | tf_op jit(solution)/shard_map/ppermute | solution.py:48
  9.6 2.4 %collective-permute-start.3 = (bf16[1,32,384]{2,1,0:T(8,128)(2,1)}, bf16[1,32,384]{2,1,0:T(8,128)(2,1)S(1)}, u32[]{:S(2)}, u32[]{:S(2)}) collective-permute-start(bf16[1,32,384]{2,1,0:T(8,128)(2,1)} %bitcast.20), channel_id=1, source_target_pairs={{0,96},{8,104},{16,112},{24,120},{32,0},{40,8},{48,16},{56,24},{64... | collective-permute-start | bytes 73736 | tf_op jit(solution)/shard_map/ppermute | solution.py:48
  12.8 1.1 %collective-permute-done.3 = bf16[1,32,384]{2,1,0:T(8,128)(2,1)S(1)} collective-permute-done((bf16[1,32,384]{2,1,0:T(8,128)(2,1)}, bf16[1,32,384]{2,1,0:T(8,128)(2,1)S(1)}, u32[]{:S(2)}, u32[]{:S(2)}) %collective-permute-start.3) | collective-permute-done | bytes 24608 | tf_op jit(solution)/shard_map/ppermute | solution.py:48
  15.0 3.2 %collective-permute-done.4 = bf16[4,32,384]{2,1,0:T(8,128)(2,1)S(1)} collective-permute-done((bf16[4,32,384]{2,1,0:T(8,128)(2,1)S(1)}, bf16[4,32,384]{2,1,0:T(8,128)(2,1)S(1)}, u32[]{:S(2)}, u32[]{:S(2)}) %collective-permute-start.4) | collective-permute-done | bytes 98336 | tf_op jit(solution)/shard_map/ppermute | solution.py:48
  18.2 3.0 %collective-permute-start.8 = (bf16[1,256,384]{2,1,0:T(8,128)(2,1)S(1)}, bf16[1,256,384]{2,1,0:T(8,128)(2,1)S(1)}, u32[]{:S(2)}, u32[]{:S(2)}) collective-permute-start(bf16[1,256,384]{2,1,0:T(8,128)(2,1)S(1)} %bitcast.12), channel_id=1, source_target_pairs={{0,2},{8,12},{16,18},{24,28},{32,34},{40,44},{48,50},{56,60},{64,6... | collective-permute-start | bytes 589832 | tf_op jit(solution)/shard_map/ppermute | solution.py:48
  21.6 2.3 %collective-permute-start.6 = (bf16[1,256,384]{2,1,0:T(8,128)(2,1)S(1)}, bf16[1,256,384]{2,1,0:T(8,128)(2,1)S(1)}, u32[]{:S(2)}, u32[]{:S(2)}) collective-permute-start(bf16[1,256,384]{2,1,0:T(8,128)(2,1)S(1)} %bitcast.14), channel_id=1, source_target_pairs={{0,3},{8,140},{16,19},{24,156},{32,35},{40,172},{48,51},{56,188},{... | collective-permute-start | bytes 589832 | tf_op jit(solution)/shard_map/ppermute | solution.py:48
  24.4 1.3 %collective-permute-start.10 = (bf16[2,256,384]{2,1,0:T(8,128)(2,1)S(1)}, bf16[2,256,384]{2,1,0:T(8,128)(2,1)S(1)}, u32[]{:S(2)}, u32[]{:S(2)}) collective-permute-start(bf16[2,256,384]{2,1,0:T(8,128)(2,1)S(1)} %pad_maximum_fusion.p01), channel_id=1, source_target_pairs={{0,128},{8,9},{16,144},{24,25},{32,160},{40,41},{48,176},{56,57},{... | collective-permute-start | bytes 1179656 | tf_op jit(solution)/shard_map/ppermute | solution.py:48
  25.7 1.6 %collective-permute-done.5 = bf16[1,256,384]{2,1,0:T(8,128)(2,1)S(1)} collective-permute-done((bf16[1,256,384]{2,1,0:T(8,128)(2,1)S(1)}, bf16[1,256,384]{2,1,0:T(8,128)(2,1)S(1)}, u32[]{:S(2)}, u32[]{:S(2)}) %collective-permute-start.5) | collective-permute-done | bytes 196640 | tf_op jit(solution)/shard_map/ppermute | solution.py:48
  27.4 2.6 %collective-permute-start.11 = (bf16[2,256,384]{2,1,0:T(8,128)(2,1)S(1)}, bf16[2,256,384]{2,1,0:T(8,128)(2,1)S(1)}, u32[]{:S(2)}, u32[]{:S(2)}) collective-permute-start(bf16[2,256,384]{2,1,0:T(8,128)(2,1)S(1)} %constant_dynamic-update-slice_fusion.5.p23), channel_id=1, source_target_pairs={{0,132},{8,11},{16,148},{24,27},{32,164},{40,43},{48,180},{56,59},... | collective-permute-start | bytes 1179656 | tf_op jit(solution)/shard_map/ppermute | solution.py:48
  29.9 2.7 %collective-permute-start.9 = (bf16[2,256,384]{2,1,0:T(8,128)(2,1)S(1)}, bf16[2,256,384]{2,1,0:T(8,128)(2,1)S(1)}, u32[]{:S(2)}, u32[]{:S(2)}) collective-permute-start(bf16[2,256,384]{2,1,0:T(8,128)(2,1)S(1)} %pad_maximum_fusion.p01), channel_id=1, source_target_pairs={{0,132},{8,11},{16,148},{24,27},{32,164},{40,43},{48,180},{56,59},... | collective-permute-start | bytes 1179656 | tf_op jit(solution)/shard_map/ppermute | solution.py:48
  32.6 1.8 %collective-permute-done.10.f0 = bf16[2,256,384]{2,1,0:T(8,128)(2,1)S(1)} collective-permute-done((bf16[2,256,384]{2,1,0:T(8,128)(2,1)S(1)}, bf16[2,256,384]{2,1,0:T(8,128)(2,1)S(1)}, u32[]{:S(2)}, u32[]{:S(2)}) %collective-permute-start.10) | collective-permute-done | bytes 393248 | tf_op jit(solution)/shard_map/ppermute | solution.py:48
  35.1 3.0 %collective-permute-start.13 = (bf16[2,256,384]{2,1,0:T(8,128)(2,1)S(1)}, bf16[2,256,384]{2,1,0:T(8,128)(2,1)S(1)}, u32[]{:S(2)}, u32[]{:S(2)}) collective-permute-start(bf16[2,256,384]{2,1,0:T(8,128)(2,1)S(1)} %collective-permute-done.11.g1), channel_id=1, source_target_pairs={{0,132},{8,11},{16,148},{24,27},{32,164},{40,43},{48,180},{56,59},... | collective-permute-start | bytes 1179656 | tf_op jit(solution)/shard_map/ppermute | solution.py:48
  38.1 2.3 %copy-done.2 = bf16[2,384,3072]{2,1,0:T(8,128)(2,1)S(1)} copy-done((bf16[2,384,3072]{2,1,0:T(8,128)(2,1)S(1)}, bf16[2,384,3072]{2,1,0:T(8,128)(2,1)}, u32[]{:S(2)}) %copy-start.2) | copy-done | bytes 4718616
  40.4 2.7 %load.1.w = bf16[4,384,3072]{2,1,0:T(8,128)(2,1)S(1)} custom-call(bf16[2,384,3072]{2,1,0:T(8,128)(2,1)S(1)} %copy-done.2, bf16[2,384,3072]{2,1,0:T(8,128)(2,1)} %collective-permute-done.other), custom_call_target="tpu_custom_call" | custom-call | bytes 18874368 | tf_op jit(solution)/shard_map/load/pallas_call | solution.py:87
  43.1 3.6 %copy-done = bf16[4,384,3072]{2,1,0:T(8,128)(2,1)} copy-done((bf16[4,384,3072]{2,1,0:T(8,128)(2,1)}, bf16[4,384,3072]{2,1,0:T(8,128)(2,1)S(1)}, u32[]{:S(2)}) %copy-start) | copy-done | bytes 9437208
  47.6 6.5 %collective-permute-start.14 = (bf16[2,256,384]{2,1,0:T(8,128)(2,1)}, bf16[2,256,384]{2,1,0:T(8,128)(2,1)S(1)}, u32[]{:S(2)}, u32[]{:S(2)}) collective-permute-start(bf16[2,256,384]{2,1,0:T(8,128)(2,1)} %pad_maximum_fusion.1), channel_id=1, source_target_pairs={{0,8},{8,0},{16,24},{24,16},{32,40},{40,32},{48,56},{56,48},{64,72... | collective-permute-start | bytes 1179656 | tf_op jit(solution)/shard_map/ppermute | solution.py:48
  55.7 3.7 %copy-done.1 = bf16[4,384,3072]{2,1,0:T(8,128)(2,1)S(1)} copy-done((bf16[4,384,3072]{2,1,0:T(8,128)(2,1)S(1)}, bf16[4,384,3072]{2,1,0:T(8,128)(2,1)}, u32[]{:S(2)}) %copy-start.1) | copy-done | bytes 9437208
  59.4 7.2 %solve.1 = f32[8,2,16,128]{3,2,1,0:T(8,128)S(1)} custom-call(s32[4,64]{1,0:T(4,128)S(1)} %select_reduce_fusion.partner, f32[1,384]{1,0:T(1,128)S(1)} %reshape.13.coulomb, bf16[4,384,3072]{2,1,0:T(8,128)(2,1)S(1)} %copy-done.1, bf16[2,256,384]{2,1,0:T(8,128)(2,1)S(1)} %pad_maximum_fusion.p01, ...), custom_call_target="tpu_custom_call" | custom-call | flops 4831838208 | bytes 9437184 | tf_op jit(solution)/shard_map/solve/pallas_call | solution.py:156
  66.5 10.0 %all_to_all.10.terms = f32[8,2,16,128]{3,2,1,0:T(8,128)} all-to-all(f32[8,2,16,128]{3,2,1,0:T(8,128)S(1)} %solve.1), channel_id=1, replica_groups=mesh['row'=32,'col'=8] {'col'}, dimensions={0} | all-to-all | bytes 262144 | tf_op jit(solution)/shard_map/all_to_all | solution.py:283
  76.5 1.8 %spread.1 = f32[32,16,128]{2,1,0:T(8,128)} custom-call(s32[64,64]{1,0:T(8,128)} %q_index.1, f32[8,2,16,128]{3,2,1,0:T(8,128)} %all_to_all.10.terms), custom_call_target="tpu_custom_call" | custom-call | tf_op jit(solution)/shard_map/spread/pallas_call | solution.py:209
  78.3 19.2 %all_to_all.11.arrived = f32[32,16,128]{2,1,0:T(8,128)} all-to-all(f32[32,16,128]{2,1,0:T(8,128)} %spread.1), channel_id=1, replica_groups=mesh['row'=32,'col'=8] {'row'}, dimensions={0} | all-to-all | bytes 524288 | tf_op jit(solution)/shard_map/all_to_all | solution.py:285
  97.5 1.7 %settle.1 = f32[32,128]{1,0:T(8,128)} custom-call(f32[32,16,128]{2,1,0:T(8,128)} %all_to_all.11.arrived), custom_call_target="tpu_custom_call" | custom-call | tf_op jit(solution)/shard_map/settle/pallas_call | solution.py:238
  (39 shorter events, 6.0 us)
Async XLA Ops:
  0.0 38.1 %collective-permute-start = (bf16[2,384,3072]{2,1,0:T(8,128)(2,1)}, bf16[2,384,3072]{2,1,0:T(8,128)(2,1)}, u32[]{:S(2)}, u32[]{:S(2)}) collective-permute-start(bf16[2,384,3072]{2,1,0:T(8,128)(2,1)} %own.1), channel_id=1, source_target_pairs={{0,8},{8,0},{16,24},{24,16},{32,40},{40,32},{48,56},{56,48},{64,72... | collective-permute-start | bytes 14155784 | tf_op jit(solution)/shard_map/ppermute | solution.py:48
  3.2 9.5 %collective-permute-start.1 = (bf16[1,32,384]{2,1,0:T(8,128)(2,1)}, bf16[1,32,384]{2,1,0:T(8,128)(2,1)S(1)}, u32[]{:S(2)}, u32[]{:S(2)}) collective-permute-start(bf16[1,32,384]{2,1,0:T(8,128)(2,1)} %bitcast.18), channel_id=1, source_target_pairs={{0,32},{8,40},{16,48},{24,56},{32,64},{40,72},{48,80},{56,88},{64,... | collective-permute-start | bytes 73736 | tf_op jit(solution)/shard_map/ppermute | solution.py:48
  4.5 8.3 %collective-permute-start.2 = (bf16[1,32,384]{2,1,0:T(8,128)(2,1)}, bf16[1,32,384]{2,1,0:T(8,128)(2,1)S(1)}, u32[]{:S(2)}, u32[]{:S(2)}) collective-permute-start(bf16[1,32,384]{2,1,0:T(8,128)(2,1)} %bitcast.19), channel_id=1, source_target_pairs={{0,64},{8,72},{16,80},{24,88},{32,96},{40,104},{48,112},{56,120},{... | collective-permute-start | bytes 73736 | tf_op jit(solution)/shard_map/ppermute | solution.py:48
  9.6 4.3 %collective-permute-start.3 = (bf16[1,32,384]{2,1,0:T(8,128)(2,1)}, bf16[1,32,384]{2,1,0:T(8,128)(2,1)S(1)}, u32[]{:S(2)}, u32[]{:S(2)}) collective-permute-start(bf16[1,32,384]{2,1,0:T(8,128)(2,1)} %bitcast.20), channel_id=1, source_target_pairs={{0,96},{8,104},{16,112},{24,120},{32,0},{40,8},{48,16},{56,24},{64... | collective-permute-start | bytes 73736 | tf_op jit(solution)/shard_map/ppermute | solution.py:48
  14.7 3.6 %collective-permute-start.4 = (bf16[4,32,384]{2,1,0:T(8,128)(2,1)S(1)}, bf16[4,32,384]{2,1,0:T(8,128)(2,1)S(1)}, u32[]{:S(2)}, u32[]{:S(2)}) collective-permute-start(bf16[4,32,384]{2,1,0:T(8,128)(2,1)S(1)} %pad_maximum_fusion.2), channel_id=1, source_target_pairs={{0,16},{8,24},{16,0},{24,8},{32,48},{40,56},{48,32},{56,40},{64,80... | collective-permute-start | bytes 294920 | tf_op jit(solution)/shard_map/ppermute | solution.py:48
  18.2 6.1 %collective-permute-start.8 = (bf16[1,256,384]{2,1,0:T(8,128)(2,1)S(1)}, bf16[1,256,384]{2,1,0:T(8,128)(2,1)S(1)}, u32[]{:S(2)}, u32[]{:S(2)}) collective-permute-start(bf16[1,256,384]{2,1,0:T(8,128)(2,1)S(1)} %bitcast.12), channel_id=1, source_target_pairs={{0,2},{8,12},{16,18},{24,28},{32,34},{40,44},{48,50},{56,60},{64,6... | collective-permute-start | bytes 589832 | tf_op jit(solution)/shard_map/ppermute | solution.py:48
  21.3 6.0 %collective-permute-start.5 = (bf16[1,256,384]{2,1,0:T(8,128)(2,1)S(1)}, bf16[1,256,384]{2,1,0:T(8,128)(2,1)S(1)}, u32[]{:S(2)}, u32[]{:S(2)}) collective-permute-start(bf16[1,256,384]{2,1,0:T(8,128)(2,1)S(1)} %bitcast.13), channel_id=1, source_target_pairs={{0,1},{8,136},{16,17},{24,152},{32,33},{40,168},{48,49},{56,184},{... | collective-permute-start | bytes 589832 | tf_op jit(solution)/shard_map/ppermute | solution.py:48
  21.6 5.7 %collective-permute-start.6 = (bf16[1,256,384]{2,1,0:T(8,128)(2,1)S(1)}, bf16[1,256,384]{2,1,0:T(8,128)(2,1)S(1)}, u32[]{:S(2)}, u32[]{:S(2)}) collective-permute-start(bf16[1,256,384]{2,1,0:T(8,128)(2,1)S(1)} %bitcast.14), channel_id=1, source_target_pairs={{0,3},{8,140},{16,19},{24,156},{32,35},{40,172},{48,51},{56,188},{... | collective-permute-start | bytes 589832 | tf_op jit(solution)/shard_map/ppermute | solution.py:48
  24.4 10.0 %collective-permute-start.10 = (bf16[2,256,384]{2,1,0:T(8,128)(2,1)S(1)}, bf16[2,256,384]{2,1,0:T(8,128)(2,1)S(1)}, u32[]{:S(2)}, u32[]{:S(2)}) collective-permute-start(bf16[2,256,384]{2,1,0:T(8,128)(2,1)S(1)} %pad_maximum_fusion.p01), channel_id=1, source_target_pairs={{0,128},{8,9},{16,144},{24,25},{32,160},{40,41},{48,176},{56,57},{... | collective-permute-start | bytes 1179656 | tf_op jit(solution)/shard_map/ppermute | solution.py:48
  27.3 2.6 %copy-start.3 = (bf16[1,256,384]{2,1,0:T(8,128)(2,1)}, bf16[1,256,384]{2,1,0:T(8,128)(2,1)S(1)}, u32[]{:S(2)}) copy-start(bf16[1,256,384]{2,1,0:T(8,128)(2,1)S(1)} %collective-permute-done.6) | copy-start | bytes 589828
  27.4 7.7 %collective-permute-start.11 = (bf16[2,256,384]{2,1,0:T(8,128)(2,1)S(1)}, bf16[2,256,384]{2,1,0:T(8,128)(2,1)S(1)}, u32[]{:S(2)}, u32[]{:S(2)}) collective-permute-start(bf16[2,256,384]{2,1,0:T(8,128)(2,1)S(1)} %constant_dynamic-update-slice_fusion.5.p23), channel_id=1, source_target_pairs={{0,132},{8,11},{16,148},{24,27},{32,164},{40,43},{48,180},{56,59},... | collective-permute-start | bytes 1179656 | tf_op jit(solution)/shard_map/ppermute | solution.py:48
  29.9 16.8 %collective-permute-start.7 = (bf16[2,256,384]{2,1,0:T(8,128)(2,1)S(1)}, bf16[2,256,384]{2,1,0:T(8,128)(2,1)S(1)}, u32[]{:S(2)}, u32[]{:S(2)}) collective-permute-start(bf16[2,256,384]{2,1,0:T(8,128)(2,1)S(1)} %constant_dynamic-update-slice_fusion.5.p23), channel_id=1, source_target_pairs={{0,128},{8,9},{16,144},{24,25},{32,160},{40,41},{48,176},{56,57},{... | collective-permute-start | bytes 1179656 | tf_op jit(solution)/shard_map/ppermute | solution.py:48
  29.9 16.8 %collective-permute-start.9 = (bf16[2,256,384]{2,1,0:T(8,128)(2,1)S(1)}, bf16[2,256,384]{2,1,0:T(8,128)(2,1)S(1)}, u32[]{:S(2)}, u32[]{:S(2)}) collective-permute-start(bf16[2,256,384]{2,1,0:T(8,128)(2,1)S(1)} %pad_maximum_fusion.p01), channel_id=1, source_target_pairs={{0,132},{8,11},{16,148},{24,27},{32,164},{40,43},{48,180},{56,59},... | collective-permute-start | bytes 1179656 | tf_op jit(solution)/shard_map/ppermute | solution.py:48
  32.6 21.5 %copy-start.5 = (f32[384]{0:T(512)S(1)}, f32[384]{0:T(512)}, u32[]{:S(2)}) copy-start(f32[384]{0:T(512)} %param.6) | copy-start | bytes 4612
  34.4 20.7 %collective-permute-start.12 = (bf16[2,256,384]{2,1,0:T(8,128)(2,1)S(1)}, bf16[2,256,384]{2,1,0:T(8,128)(2,1)S(1)}, u32[]{:S(2)}, u32[]{:S(2)}) collective-permute-start(bf16[2,256,384]{2,1,0:T(8,128)(2,1)S(1)} %collective-permute-done.10.f0), channel_id=1, source_target_pairs={{0,128},{8,9},{16,144},{24,25},{32,160},{40,41},{48,176},{56,57},{... | collective-permute-start | bytes 1179656 | tf_op jit(solution)/shard_map/ppermute | solution.py:48
  35.1 20.0 %collective-permute-start.13 = (bf16[2,256,384]{2,1,0:T(8,128)(2,1)S(1)}, bf16[2,256,384]{2,1,0:T(8,128)(2,1)S(1)}, u32[]{:S(2)}, u32[]{:S(2)}) collective-permute-start(bf16[2,256,384]{2,1,0:T(8,128)(2,1)S(1)} %collective-permute-done.11.g1), channel_id=1, source_target_pairs={{0,132},{8,11},{16,148},{24,27},{32,164},{40,43},{48,180},{56,59},... | collective-permute-start | bytes 1179656 | tf_op jit(solution)/shard_map/ppermute | solution.py:48
  38.1 2.3 %copy-start.2 = (bf16[2,384,3072]{2,1,0:T(8,128)(2,1)S(1)}, bf16[2,384,3072]{2,1,0:T(8,128)(2,1)}, u32[]{:S(2)}) copy-start(bf16[2,384,3072]{2,1,0:T(8,128)(2,1)} %own.1) | copy-start | bytes 14155780
  40.4 6.3 %copy-start.4 = (bf16[1,256,384]{2,1,0:T(8,128)(2,1)S(1)}, bf16[1,256,384]{2,1,0:T(8,128)(2,1)}, u32[]{:S(2)}) copy-start(bf16[1,256,384]{2,1,0:T(8,128)(2,1)} %copy-done.3) | copy-start | bytes 589828
  43.1 3.7 %copy-start = (bf16[4,384,3072]{2,1,0:T(8,128)(2,1)}, bf16[4,384,3072]{2,1,0:T(8,128)(2,1)S(1)}, u32[]{:S(2)}) copy-start(bf16[4,384,3072]{2,1,0:T(8,128)(2,1)S(1)} %load.1.w) | copy-start | bytes 28311556
  47.6 8.0 %collective-permute-start.14 = (bf16[2,256,384]{2,1,0:T(8,128)(2,1)}, bf16[2,256,384]{2,1,0:T(8,128)(2,1)S(1)}, u32[]{:S(2)}, u32[]{:S(2)}) collective-permute-start(bf16[2,256,384]{2,1,0:T(8,128)(2,1)} %pad_maximum_fusion.1), channel_id=1, source_target_pairs={{0,8},{8,0},{16,24},{24,16},{32,40},{40,32},{48,56},{56,48},{64,72... | collective-permute-start | bytes 1179656 | tf_op jit(solution)/shard_map/ppermute | solution.py:48
  55.7 3.7 %copy-start.1 = (bf16[4,384,3072]{2,1,0:T(8,128)(2,1)S(1)}, bf16[4,384,3072]{2,1,0:T(8,128)(2,1)}, u32[]{:S(2)}) copy-start(bf16[4,384,3072]{2,1,0:T(8,128)(2,1)} %copy-done) | copy-start | bytes 28311556

commit v6 on v5

--- a/solution.py
+++ b/solution.py
@@ -9,7 +9,7 @@
 NX, NY, NZ, NCORE = 4, 4, 8, 2
 SHIFTS = (0, 2, 1, -1)
 ZSHIFTS = (0, 2, 4, -2)
-VMEM = 24 * 1024 * 1024
+VMEM = 58 * 1024 * 1024
 
 
 def device_index(x, y, z, c):
@@ -71,36 +71,16 @@
     return side * 4 + ((((z ^ side) - z_wanted) & 7) >> 1)
 
 
-def load_kernel(own, other, out, sems):
+def solve_kernel(
+    partner, coulomb, w_own, w_other, p01, p23, f0, f1, g0, g1, ff0, gg1, other, out,
+    panel, left_rows, image, w, sems,
+):
     copies = [
-        pltpu.make_async_copy(own, out.at[pl.ds(0, 2)], sems.at[0]),
-        pltpu.make_async_copy(other, out.at[pl.ds(2, 2)], sems.at[1]),
+        pltpu.make_async_copy((w_own, w_other)[q // 2].at[q % 2], w.at[q], sems.at[q])
+        for q in range(4)
     ]
-    for copy in copies:
-        copy.start()
-    for copy in copies:
-        copy.wait()
-
-
-def load(own, other):
-    _, share, whole = own.shape
-    return pl.pallas_call(
-        load_kernel,
-        in_specs=[pl.BlockSpec(memory_space=pl.ANY)] * 2,
-        out_specs=pl.BlockSpec(memory_space=pltpu.VMEM),
-        out_shape=jax.ShapeDtypeStruct((4, share, whole), own.dtype),
-        scratch_shapes=[pltpu.SemaphoreType.DMA((2,))],
-        compiler_params=pltpu.CompilerParams(vmem_limit_bytes=VMEM),
-        cost_estimate=pl.CostEstimate(
-            flops=0, bytes_accessed=8 * share * whole * 2, transcendentals=0
-        ),
-        name="load",
-    )(own, other)
-
-
-def solve_kernel(
-    partner, coulomb, w, p01, p23, f0, f1, g0, g1, ff0, gg1, other, out, panel, left_rows, image
-):
+    copies[0].start()
+    copies[1].start()
     rows, share = p01.shape[1:]
     r, j, c, _, _ = where_am_i()
     starts = [pl.multiple_of(place_of(z) * 32, 32) for z in range(NZ)]
@@ -118,6 +98,9 @@
             to = (2 + low) * rows + z * 32
             left_rows[to : to + 32, :] = other[low, pl.ds(starts[z], 32), :]
     for q in range(4):
+        copies[q].wait()
+        if q < 2:
+            copies[q + 2].start()
         image[q] = contract(w[q], panel[...]).astype(image.dtype)
 
     lane = lax.broadcasted_iota(jnp.int32, (16, 128), 1)
@@ -149,19 +132,23 @@
             out[2 * pair + 1, two] = jnp.where(lane < 64, pltpu.roll(even, 64, 1), odd)
 
 
-def solve(partner, coulomb, w, panels, other):
+def solve(partner, coulomb, w_own, w_other, panels, other):
     rows, share = panels[0].shape[1:]
-    whole = w.shape[2]
+    whole = w_own.shape[2]
     vmem = pl.BlockSpec(memory_space=pltpu.VMEM)
     return pl.pallas_call(
         solve_kernel,
-        in_specs=[pl.BlockSpec(memory_space=pltpu.SMEM)] + [vmem] * 11,
+        in_specs=[pl.BlockSpec(memory_space=pltpu.SMEM), vmem]
+        + [pl.BlockSpec(memory_space=pl.ANY)] * 2
+        + [vmem] * 9,
         out_specs=vmem,
         out_shape=jax.ShapeDtypeStruct((8, 2, 16, 128), jnp.float32),
         scratch_shapes=[
             pltpu.VMEM((2 * rows, whole), jnp.bfloat16),
             pltpu.VMEM((4 * rows, share), jnp.bfloat16),
             pltpu.VMEM((4, share, 2 * rows), jnp.bfloat16),
+            pltpu.VMEM((4, share, whole), jnp.bfloat16),
+            pltpu.SemaphoreType.DMA((4,)),
         ],
         compiler_params=pltpu.CompilerParams(vmem_limit_bytes=VMEM),
         cost_estimate=pl.CostEstimate(
@@ -170,7 +157,7 @@
             transcendentals=0,
         ),
         name="solve",
-    )(partner, coulomb, w, *panels, other)
+    )(partner, coulomb, w_own, w_other, *panels, other)
 
 
 def spread_kernel(q_index, terms, out):
@@ -257,8 +244,8 @@
 
     f0 = send(p01, second_plane(1))
     g1 = send(p23, second_plane(-1))
+    g0 = send(p01, second_plane(-1))
     f1 = send(p23, second_plane(1))
-    g0 = send(p01, second_plane(-1))
     ff0 = send(f0, second_plane(1))
     gg1 = send(g1, second_plane(-1))
 
@@ -268,8 +255,6 @@
         jnp.where(q_index[None] == q_mine[:, None, None], ks[None, :, None], 0), axis=1
     )
 
-    w = load(screened, w_other)
-    w, f1, g0 = lax.optimization_barrier((w, f1, g0))
     up = jnp.where(c == 0, g0[0], parts[2][0])
     down = jnp.where(c == 0, f0[0], parts[1][0])
     across = jnp.where(y_lo == 0, up, down)
@@ -279,7 +264,9 @@
     other = send(mine, SWAP)
 
     panels = (p01, p23, f0, f1, g0, g1, ff0, gg1)
-    terms = solve(partner.astype(jnp.int32), coulomb.reshape(1, share), w, panels, other)
+    terms = solve(
+        partner.astype(jnp.int32), coulomb.reshape(1, share), screened, w_other, panels, other
+    )
     terms = lax.all_to_all(terms, "col", split_axis=0, concat_axis=0, tiled=True)
     placed = spread(q_index, terms)
     arrived = lax.all_to_all(placed, "row", split_axis=0, concat_axis=0, tiled=True)

time: 99.7 us -> 108 us (1.083)
  blocking collectives: 29.2 us -> 39.5 us
  local copies, waits for them, and re-layouts: 10.6 us -> 1.45 us
  waiting for transfers between devices: 8.79 us -> 17.7 us
  starting transfers between devices: 34.6 us -> 32.6 us
  Pallas kernels: 13.3 us -> 14.6 us
    unnamed x17 -> x23, local copies, waits for them, and re-layouts: 10.5 us -> 0.86 us
    ppermute x15, waiting for transfers between devices: 8.79 us -> 17.7 us  [send(): return lax.ppermute(value, AXES, perm)]
    all_to_all x1, blocking collectives: 19.2 us -> 27.6 us  [local(): lax.all_to_all(placed, 'row', split_axis=0, concat_axis=0, tiled=True)]
    pallas_call x1, Pallas kernels: 7.15 us -> 11.1 us  [solve(): pl.pallas_call(solve_kernel, in_specs=[pl.BlockSpec(memory_space=pltpu.SM...]
    pallas_call x1 -> x0, Pallas kernels: 2.67 us -> none  [load(): pl.pallas_call(load_kernel, in_specs=[pl.BlockSpec(memory_space=pl.ANY)]...]
    ppermute x15, starting transfers between devices: 34.6 us -> 32.6 us  [send(): return lax.ppermute(value, AXES, perm)]
    all_to_all x1, blocking collectives: 9.99 us -> 11.9 us  [local(): lax.all_to_all(terms, 'col', split_axis=0, concat_axis=0, tiled=True)]
  transfers between devices with their start and end apart: 15 -> 15, of which waited for: 6 -> 8; matrix products, arithmetic and copies ran while one was open for 4% -> 3% of each run, Pallas kernels for 3% -> 0%
where the time goes in v6:
time: 108 us
  blocking collectives  39.5 us (37%)
  starting transfers between devices  32.6 us (30%)
  waiting for transfers between devices  17.7 us (16%)
  Pallas kernels  14.6 us (14%)
  other arithmetic  1.79 us (2%)
  local copies, waits for them, and re-layouts  1.45 us (1%)
    ppermute x15, starting transfers between devices, send(): return lax.ppermute(value, AXES, perm)  32.6 us
    all_to_all x1, blocking collectives, local(): lax.all_to_all(placed, 'row', split_axis=0, concat_axis=0, tiled=True)  27.6 us
    ppermute x15, waiting for transfers between devices, send(): return lax.ppermute(value, AXES, perm)  17.7 us
    all_to_all x1, blocking collectives, local(): lax.all_to_all(terms, 'col', split_axis=0, concat_axis=0, tiled=True)  11.9 us
    pallas_call x1, Pallas kernels, solve(): pl.pallas_call(solve_kernel, in_specs=[pl.BlockSpec(memory_space=pltpu.SM...  11.1 us
  transfers between devices with their start and end apart: 15, of which 8 were waited for; matrix products, arithmetic and copies ran while one was open for 3% of the time, Pallas kernels for 0%

profile of v6, /device:TPU:1, one launch (start us, length us, event | category | flops | bytes accessed | tf_op | source)
XLA Modules:
  0.0 107.8 jit_solution(7893751912729066698)
XLA Ops:
  0.0 3.2 %collective-permute-start = (bf16[2,384,3072]{2,1,0:T(8,128)(2,1)}, bf16[2,384,3072]{2,1,0:T(8,128)(2,1)}, u32[]{:S(2)}, u32[]{:S(2)}) collective-permute-start(bf16[2,384,3072]{2,1,0:T(8,128)(2,1)} %w_own.1), channel_id=1, source_target_pairs={{0,8},{8,0},{16,24},{24,16},{32,40},{40,32},{48,56},{56,48},{64,72... | collective-permute-start | bytes 14155784 | tf_op jit(solution)/shard_map/ppermute | solution.py:48
  3.2 4.3 %collective-permute-start.3 = (bf16[1,32,384]{2,1,0:T(8,128)(2,1)}, bf16[1,32,384]{2,1,0:T(8,128)(2,1)S(1)}, u32[]{:S(2)}, u32[]{:S(2)}) collective-permute-start(bf16[1,32,384]{2,1,0:T(8,128)(2,1)} %bitcast.18), channel_id=1, source_target_pairs={{0,96},{8,104},{16,112},{24,120},{32,0},{40,8},{48,16},{56,24},{64... | collective-permute-start | bytes 73736 | tf_op jit(solution)/shard_map/ppermute | solution.py:48
  7.5 0.9 collective-permute-start.2
  8.4 2.4 %collective-permute-start.1 = (bf16[1,32,384]{2,1,0:T(8,128)(2,1)}, bf16[1,32,384]{2,1,0:T(8,128)(2,1)S(1)}, u32[]{:S(2)}, u32[]{:S(2)}) collective-permute-start(bf16[1,32,384]{2,1,0:T(8,128)(2,1)} %bitcast.20), channel_id=1, source_target_pairs={{0,32},{8,40},{16,48},{24,56},{32,64},{40,72},{48,80},{56,88},{64,... | collective-permute-start | bytes 73736 | tf_op jit(solution)/shard_map/ppermute | solution.py:48
  11.6 2.8 %collective-permute-done.2 = bf16[1,32,384]{2,1,0:T(8,128)(2,1)S(1)} collective-permute-done((bf16[1,32,384]{2,1,0:T(8,128)(2,1)}, bf16[1,32,384]{2,1,0:T(8,128)(2,1)S(1)}, u32[]{:S(2)}, u32[]{:S(2)}) %collective-permute-start.2) | collective-permute-done | bytes 24608 | tf_op jit(solution)/shard_map/ppermute | solution.py:48
  15.1 0.8 collective-permute-start.4
  16.0 2.7 %collective-permute-done.4 = bf16[4,32,384]{2,1,0:T(8,128)(2,1)S(1)} collective-permute-done((bf16[4,32,384]{2,1,0:T(8,128)(2,1)S(1)}, bf16[4,32,384]{2,1,0:T(8,128)(2,1)S(1)}, u32[]{:S(2)}, u32[]{:S(2)}) %collective-permute-start.4) | collective-permute-done | bytes 98336 | tf_op jit(solution)/shard_map/ppermute | solution.py:48
  18.7 3.0 %collective-permute-start.5 = (bf16[1,256,384]{2,1,0:T(8,128)(2,1)S(1)}, bf16[1,256,384]{2,1,0:T(8,128)(2,1)S(1)}, u32[]{:S(2)}, u32[]{:S(2)}) collective-permute-start(bf16[1,256,384]{2,1,0:T(8,128)(2,1)S(1)} %bitcast.12), channel_id=1, source_target_pairs={{0,2},{8,12},{16,18},{24,28},{32,34},{40,44},{48,50},{56,60},{64,6... | collective-permute-start | bytes 589832 | tf_op jit(solution)/shard_map/ppermute | solution.py:48
  21.7 3.1 %collective-permute-done.5 = bf16[1,256,384]{2,1,0:T(8,128)(2,1)S(1)} collective-permute-done((bf16[1,256,384]{2,1,0:T(8,128)(2,1)S(1)}, bf16[1,256,384]{2,1,0:T(8,128)(2,1)S(1)}, u32[]{:S(2)}, u32[]{:S(2)}) %collective-permute-start.5) | collective-permute-done | bytes 196640 | tf_op jit(solution)/shard_map/ppermute | solution.py:48
  24.9 2.6 %collective-permute-start.10 = (bf16[2,256,384]{2,1,0:T(8,128)(2,1)S(1)}, bf16[2,256,384]{2,1,0:T(8,128)(2,1)S(1)}, u32[]{:S(2)}, u32[]{:S(2)}) collective-permute-start(bf16[2,256,384]{2,1,0:T(8,128)(2,1)S(1)} %pad_maximum_fusion.p01), channel_id=1, source_target_pairs={{0,132},{8,11},{16,148},{24,27},{32,164},{40,43},{48,180},{56,59},... | collective-permute-start | bytes 1179656 | tf_op jit(solution)/shard_map/ppermute | solution.py:48
  27.4 1.3 %collective-permute-start.6 = (bf16[1,256,384]{2,1,0:T(8,128)(2,1)S(1)}, bf16[1,256,384]{2,1,0:T(8,128)(2,1)S(1)}, u32[]{:S(2)}, u32[]{:S(2)}) collective-permute-start(bf16[1,256,384]{2,1,0:T(8,128)(2,1)S(1)} %bitcast.14), channel_id=1, source_target_pairs={{0,1},{8,136},{16,17},{24,152},{32,33},{40,168},{48,49},{56,184},{... | collective-permute-start | bytes 589832 | tf_op jit(solution)/shard_map/ppermute | solution.py:48
  28.7 1.4 %collective-permute-start.7 = (bf16[1,256,384]{2,1,0:T(8,128)(2,1)S(1)}, bf16[1,256,384]{2,1,0:T(8,128)(2,1)S(1)}, u32[]{:S(2)}, u32[]{:S(2)}) collective-permute-start(bf16[1,256,384]{2,1,0:T(8,128)(2,1)S(1)} %bitcast.15), channel_id=1, source_target_pairs={{0,3},{8,140},{16,19},{24,156},{32,35},{40,172},{48,51},{56,188},{... | collective-permute-start | bytes 589832 | tf_op jit(solution)/shard_map/ppermute | solution.py:48
  30.2 3.1 %collective-permute-done.6 = bf16[1,256,384]{2,1,0:T(8,128)(2,1)S(1)} collective-permute-done((bf16[1,256,384]{2,1,0:T(8,128)(2,1)S(1)}, bf16[1,256,384]{2,1,0:T(8,128)(2,1)S(1)}, u32[]{:S(2)}, u32[]{:S(2)}) %collective-permute-start.6) | collective-permute-done | bytes 196640 | tf_op jit(solution)/shard_map/ppermute | solution.py:48
  33.2 1.7 %collective-permute-done.7 = bf16[1,256,384]{2,1,0:T(8,128)(2,1)S(1)} collective-permute-done((bf16[1,256,384]{2,1,0:T(8,128)(2,1)S(1)}, bf16[1,256,384]{2,1,0:T(8,128)(2,1)S(1)}, u32[]{:S(2)}, u32[]{:S(2)}) %collective-permute-start.7) | collective-permute-done | bytes 196640 | tf_op jit(solution)/shard_map/ppermute | solution.py:48
  35.4 1.7 %collective-permute-start.11 = (bf16[2,256,384]{2,1,0:T(8,128)(2,1)S(1)}, bf16[2,256,384]{2,1,0:T(8,128)(2,1)S(1)}, u32[]{:S(2)}, u32[]{:S(2)}) collective-permute-start(bf16[2,256,384]{2,1,0:T(8,128)(2,1)S(1)} %get-tuple-element.7.p23), channel_id=1, source_target_pairs={{0,132},{8,11},{16,148},{24,27},{32,164},{40,43},{48,180},{56,59},... | collective-permute-start | bytes 1179656 | tf_op jit(solution)/shard_map/ppermute | solution.py:48
  37.2 7.3 %collective-permute-start.14 = (bf16[2,256,384]{2,1,0:T(8,128)(2,1)S(1)}, bf16[2,256,384]{2,1,0:T(8,128)(2,1)S(1)}, u32[]{:S(2)}, u32[]{:S(2)}) collective-permute-start(bf16[2,256,384]{2,1,0:T(8,128)(2,1)S(1)} %pad_maximum_fusion.1), channel_id=1, source_target_pairs={{0,8},{8,0},{16,24},{24,16},{32,40},{40,32},{48,56},{56,48},{64,72... | collective-permute-start | bytes 1179656 | tf_op jit(solution)/shard_map/ppermute | solution.py:48
  44.5 1.7 %collective-permute-start.12 = (bf16[2,256,384]{2,1,0:T(8,128)(2,1)S(1)}, bf16[2,256,384]{2,1,0:T(8,128)(2,1)}, u32[]{:S(2)}, u32[]{:S(2)}) collective-permute-start(bf16[2,256,384]{2,1,0:T(8,128)(2,1)S(1)} %collective-permute-done.8.f0), channel_id=1, source_target_pairs={{0,128},{8,9},{16,144},{24,25},{32,160},{40,41},{48,176},{56,57},{... | collective-permute-start | bytes 1179656 | tf_op jit(solution)/shard_map/ppermute | solution.py:48
  46.2 2.0 %collective-permute-start.13 = (bf16[2,256,384]{2,1,0:T(8,128)(2,1)S(1)}, bf16[2,256,384]{2,1,0:T(8,128)(2,1)}, u32[]{:S(2)}, u32[]{:S(2)}) collective-permute-start(bf16[2,256,384]{2,1,0:T(8,128)(2,1)S(1)} %collective-permute-done.11.g1), channel_id=1, source_target_pairs={{0,132},{8,11},{16,148},{24,27},{32,164},{40,43},{48,180},{56,59},... | collective-permute-start | bytes 1179656 | tf_op jit(solution)/shard_map/ppermute | solution.py:48
  49.6 3.9 %collective-permute-done.12.ff0 = bf16[2,256,384]{2,1,0:T(8,128)(2,1)} collective-permute-done((bf16[2,256,384]{2,1,0:T(8,128)(2,1)S(1)}, bf16[2,256,384]{2,1,0:T(8,128)(2,1)}, u32[]{:S(2)}, u32[]{:S(2)}) %collective-permute-start.12) | collective-permute-done | bytes 393248 | tf_op jit(solution)/shard_map/ppermute | solution.py:48
  53.7 11.1 %solve.1 = f32[8,2,16,128]{3,2,1,0:T(8,128)} custom-call(s32[4,64]{1,0:T(4,128)} %select_reduce_fusion.partner, f32[1,384]{1,0:T(1,128)} %reshape.13.coulomb, bf16[2,384,3072]{2,1,0:T(8,128)(2,1)} %w_own.1, bf16[2,384,3072]{2,1,0:T(8,128)(2,1)} %collective-permute-done.w_other, bf16[2,256,384]{2,1,0:T(8,128)(2,1)} %copy-done, ...), custom_call_target="tpu_custom_call" | custom-call | flops 4831838208 | bytes 9437184 | tf_op jit(solution)/shard_map/solve/pallas_call | solution.py:139
  64.8 11.9 %all_to_all.10.terms = f32[8,2,16,128]{3,2,1,0:T(8,128)} all-to-all(f32[8,2,16,128]{3,2,1,0:T(8,128)} %solve.1), channel_id=1, replica_groups=mesh['row'=32,'col'=8] {'col'}, dimensions={0} | all-to-all | bytes 262144 | tf_op jit(solution)/shard_map/all_to_all | solution.py:270
  76.7 1.8 %spread.1 = f32[32,16,128]{2,1,0:T(8,128)} custom-call(s32[64,64]{1,0:T(8,128)} %q_index.1, f32[8,2,16,128]{3,2,1,0:T(8,128)} %all_to_all.10.terms), custom_call_target="tpu_custom_call" | custom-call | tf_op jit(solution)/shard_map/spread/pallas_call | solution.py:196
  78.5 27.6 %all_to_all.11.arrived = f32[32,16,128]{2,1,0:T(8,128)} all-to-all(f32[32,16,128]{2,1,0:T(8,128)} %spread.1), channel_id=1, replica_groups=mesh['row'=32,'col'=8] {'row'}, dimensions={0} | all-to-all | bytes 524288 | tf_op jit(solution)/shard_map/all_to_all | solution.py:272
  106.1 1.7 %settle.1 = f32[32,128]{1,0:T(8,128)} custom-call(f32[32,16,128]{2,1,0:T(8,128)} %all_to_all.11.arrived), custom_call_target="tpu_custom_call" | custom-call | tf_op jit(solution)/shard_map/settle/pallas_call | solution.py:225
  (43 shorter events, 3.7 us)
Async XLA Ops:
  0.0 48.2 %copy-start.5 = (f32[384]{0:T(512)S(1)}, f32[384]{0:T(512)}, u32[]{:S(2)}) copy-start(f32[384]{0:T(512)} %param.6) | copy-start | bytes 4612
  0.0 48.9 %copy-start.1 = (s32[64,64]{1,0:T(8,128)S(1)}, s32[64,64]{1,0:T(8,128)}, u32[]{:S(2)}) copy-start(s32[64,64]{1,0:T(8,128)} %q_index.1) | copy-start | bytes 49156
  0.0 53.6 %collective-permute-start = (bf16[2,384,3072]{2,1,0:T(8,128)(2,1)}, bf16[2,384,3072]{2,1,0:T(8,128)(2,1)}, u32[]{:S(2)}, u32[]{:S(2)}) collective-permute-start(bf16[2,384,3072]{2,1,0:T(8,128)(2,1)} %w_own.1), channel_id=1, source_target_pairs={{0,8},{8,0},{16,24},{24,16},{32,40},{40,32},{48,56},{56,48},{64,72... | collective-permute-start | bytes 14155784 | tf_op jit(solution)/shard_map/ppermute | solution.py:48
  3.2 8.3 %collective-permute-start.3 = (bf16[1,32,384]{2,1,0:T(8,128)(2,1)}, bf16[1,32,384]{2,1,0:T(8,128)(2,1)S(1)}, u32[]{:S(2)}, u32[]{:S(2)}) collective-permute-start(bf16[1,32,384]{2,1,0:T(8,128)(2,1)} %bitcast.18), channel_id=1, source_target_pairs={{0,96},{8,104},{16,112},{24,120},{32,0},{40,8},{48,16},{56,24},{64... | collective-permute-start | bytes 73736 | tf_op jit(solution)/shard_map/ppermute | solution.py:48
  7.5 6.8 %collective-permute-start.2 = (bf16[1,32,384]{2,1,0:T(8,128)(2,1)}, bf16[1,32,384]{2,1,0:T(8,128)(2,1)S(1)}, u32[]{:S(2)}, u32[]{:S(2)}) collective-permute-start(bf16[1,32,384]{2,1,0:T(8,128)(2,1)} %bitcast.19), channel_id=1, source_target_pairs={{0,64},{8,72},{16,80},{24,88},{32,96},{40,104},{48,112},{56,120},{... | collective-permute-start | bytes 73736 | tf_op jit(solution)/shard_map/ppermute | solution.py:48
  8.4 5.9 %collective-permute-start.1 = (bf16[1,32,384]{2,1,0:T(8,128)(2,1)}, bf16[1,32,384]{2,1,0:T(8,128)(2,1)S(1)}, u32[]{:S(2)}, u32[]{:S(2)}) collective-permute-start(bf16[1,32,384]{2,1,0:T(8,128)(2,1)} %bitcast.20), channel_id=1, source_target_pairs={{0,32},{8,40},{16,48},{24,56},{32,64},{40,72},{48,80},{56,88},{64,... | collective-permute-start | bytes 73736 | tf_op jit(solution)/shard_map/ppermute | solution.py:48
  15.1 3.6 %collective-permute-start.4 = (bf16[4,32,384]{2,1,0:T(8,128)(2,1)S(1)}, bf16[4,32,384]{2,1,0:T(8,128)(2,1)S(1)}, u32[]{:S(2)}, u32[]{:S(2)}) collective-permute-start(bf16[4,32,384]{2,1,0:T(8,128)(2,1)S(1)} %pad_maximum_fusion.2), channel_id=1, source_target_pairs={{0,16},{8,24},{16,0},{24,8},{32,48},{40,56},{48,32},{56,40},{64,80... | collective-permute-start | bytes 294920 | tf_op jit(solution)/shard_map/ppermute | solution.py:48
  18.7 6.1 %collective-permute-start.5 = (bf16[1,256,384]{2,1,0:T(8,128)(2,1)S(1)}, bf16[1,256,384]{2,1,0:T(8,128)(2,1)S(1)}, u32[]{:S(2)}, u32[]{:S(2)}) collective-permute-start(bf16[1,256,384]{2,1,0:T(8,128)(2,1)S(1)} %bitcast.12), channel_id=1, source_target_pairs={{0,2},{8,12},{16,18},{24,28},{32,34},{40,44},{48,50},{56,60},{64,6... | collective-permute-start | bytes 589832 | tf_op jit(solution)/shard_map/ppermute | solution.py:48
  24.9 28.7 %copy-start = (bf16[2,256,384]{2,1,0:T(8,128)(2,1)}, bf16[2,256,384]{2,1,0:T(8,128)(2,1)S(1)}, u32[]{:S(2)}) copy-start(bf16[2,256,384]{2,1,0:T(8,128)(2,1)S(1)} %pad_maximum_fusion.p01) | copy-start | bytes 1179652
  24.9 10.1 %collective-permute-start.10 = (bf16[2,256,384]{2,1,0:T(8,128)(2,1)S(1)}, bf16[2,256,384]{2,1,0:T(8,128)(2,1)S(1)}, u32[]{:S(2)}, u32[]{:S(2)}) collective-permute-start(bf16[2,256,384]{2,1,0:T(8,128)(2,1)S(1)} %pad_maximum_fusion.p01), channel_id=1, source_target_pairs={{0,132},{8,11},{16,148},{24,27},{32,164},{40,43},{48,180},{56,59},... | collective-permute-start | bytes 1179656 | tf_op jit(solution)/shard_map/ppermute | solution.py:48
  27.4 7.8 %collective-permute-start.8 = (bf16[2,256,384]{2,1,0:T(8,128)(2,1)S(1)}, bf16[2,256,384]{2,1,0:T(8,128)(2,1)S(1)}, u32[]{:S(2)}, u32[]{:S(2)}) collective-permute-start(bf16[2,256,384]{2,1,0:T(8,128)(2,1)S(1)} %pad_maximum_fusion.p01), channel_id=1, source_target_pairs={{0,128},{8,9},{16,144},{24,25},{32,160},{40,41},{48,176},{56,57},{... | collective-permute-start | bytes 1179656 | tf_op jit(solution)/shard_map/ppermute | solution.py:48
  27.4 5.8 %collective-permute-start.6 = (bf16[1,256,384]{2,1,0:T(8,128)(2,1)S(1)}, bf16[1,256,384]{2,1,0:T(8,128)(2,1)S(1)}, u32[]{:S(2)}, u32[]{:S(2)}) collective-permute-start(bf16[1,256,384]{2,1,0:T(8,128)(2,1)S(1)} %bitcast.14), channel_id=1, source_target_pairs={{0,1},{8,136},{16,17},{24,152},{32,33},{40,168},{48,49},{56,184},{... | collective-permute-start | bytes 589832 | tf_op jit(solution)/shard_map/ppermute | solution.py:48
  28.7 6.2 %collective-permute-start.7 = (bf16[1,256,384]{2,1,0:T(8,128)(2,1)S(1)}, bf16[1,256,384]{2,1,0:T(8,128)(2,1)S(1)}, u32[]{:S(2)}, u32[]{:S(2)}) collective-permute-start(bf16[1,256,384]{2,1,0:T(8,128)(2,1)S(1)} %bitcast.15), channel_id=1, source_target_pairs={{0,3},{8,140},{16,19},{24,156},{32,35},{40,172},{48,51},{56,188},{... | collective-permute-start | bytes 589832 | tf_op jit(solution)/shard_map/ppermute | solution.py:48
  35.0 18.6 %copy-start.3 = (bf16[2,256,384]{2,1,0:T(8,128)(2,1)}, bf16[2,256,384]{2,1,0:T(8,128)(2,1)S(1)}, u32[]{:S(2)}) copy-start(bf16[2,256,384]{2,1,0:T(8,128)(2,1)S(1)} %collective-permute-done.10.g0) | copy-start | bytes 1179652
  35.3 18.3 %copy-start.4 = (bf16[2,256,384]{2,1,0:T(8,128)(2,1)}, bf16[2,256,384]{2,1,0:T(8,128)(2,1)S(1)}, u32[]{:S(2)}) copy-start(bf16[2,256,384]{2,1,0:T(8,128)(2,1)S(1)} %collective-permute-done.8.f0) | copy-start | bytes 1179652
  35.4 18.2 %copy-start.2 = (bf16[2,256,384]{2,1,0:T(8,128)(2,1)}, bf16[2,256,384]{2,1,0:T(8,128)(2,1)S(1)}, u32[]{:S(2)}) copy-start(bf16[2,256,384]{2,1,0:T(8,128)(2,1)S(1)} %get-tuple-element.7.p23) | copy-start | bytes 1179652
  35.4 10.8 %collective-permute-start.11 = (bf16[2,256,384]{2,1,0:T(8,128)(2,1)S(1)}, bf16[2,256,384]{2,1,0:T(8,128)(2,1)S(1)}, u32[]{:S(2)}, u32[]{:S(2)}) collective-permute-start(bf16[2,256,384]{2,1,0:T(8,128)(2,1)S(1)} %get-tuple-element.7.p23), channel_id=1, source_target_pairs={{0,132},{8,11},{16,148},{24,27},{32,164},{40,43},{48,180},{56,59},... | collective-permute-start | bytes 1179656 | tf_op jit(solution)/shard_map/ppermute | solution.py:48
  37.2 12.4 %collective-permute-start.9 = (bf16[2,256,384]{2,1,0:T(8,128)(2,1)S(1)}, bf16[2,256,384]{2,1,0:T(8,128)(2,1)S(1)}, u32[]{:S(2)}, u32[]{:S(2)}) collective-permute-start(bf16[2,256,384]{2,1,0:T(8,128)(2,1)S(1)} %get-tuple-element.7.p23), channel_id=1, source_target_pairs={{0,128},{8,9},{16,144},{24,25},{32,160},{40,41},{48,176},{56,57},{... | collective-permute-start | bytes 1179656 | tf_op jit(solution)/shard_map/ppermute | solution.py:48
  37.2 12.3 %collective-permute-start.14 = (bf16[2,256,384]{2,1,0:T(8,128)(2,1)S(1)}, bf16[2,256,384]{2,1,0:T(8,128)(2,1)S(1)}, u32[]{:S(2)}, u32[]{:S(2)}) collective-permute-start(bf16[2,256,384]{2,1,0:T(8,128)(2,1)S(1)} %pad_maximum_fusion.1), channel_id=1, source_target_pairs={{0,8},{8,0},{16,24},{24,16},{32,40},{40,32},{48,56},{56,48},{64,72... | collective-permute-start | bytes 1179656 | tf_op jit(solution)/shard_map/ppermute | solution.py:48
  44.5 9.0 %collective-permute-start.12 = (bf16[2,256,384]{2,1,0:T(8,128)(2,1)S(1)}, bf16[2,256,384]{2,1,0:T(8,128)(2,1)}, u32[]{:S(2)}, u32[]{:S(2)}) collective-permute-start(bf16[2,256,384]{2,1,0:T(8,128)(2,1)S(1)} %collective-permute-done.8.f0), channel_id=1, source_target_pairs={{0,128},{8,9},{16,144},{24,25},{32,160},{40,41},{48,176},{56,57},{... | collective-permute-start | bytes 1179656 | tf_op jit(solution)/shard_map/ppermute | solution.py:48
  46.2 7.4 %copy-start.6 = (bf16[2,256,384]{2,1,0:T(8,128)(2,1)}, bf16[2,256,384]{2,1,0:T(8,128)(2,1)S(1)}, u32[]{:S(2)}) copy-start(bf16[2,256,384]{2,1,0:T(8,128)(2,1)S(1)} %collective-permute-done.11.g1) | copy-start | bytes 1179652
  46.2 7.4 %collective-permute-start.13 = (bf16[2,256,384]{2,1,0:T(8,128)(2,1)S(1)}, bf16[2,256,384]{2,1,0:T(8,128)(2,1)}, u32[]{:S(2)}, u32[]{:S(2)}) collective-permute-start(bf16[2,256,384]{2,1,0:T(8,128)(2,1)S(1)} %collective-permute-done.11.g1), channel_id=1, source_target_pairs={{0,132},{8,11},{16,148},{24,27},{32,164},{40,43},{48,180},{56,59},... | collective-permute-start | bytes 1179656 | tf_op jit(solution)/shard_map/ppermute | solution.py:48
  49.6 4.1 %copy-start.8 = (bf16[2,256,384]{2,1,0:T(8,128)(2,1)}, bf16[2,256,384]{2,1,0:T(8,128)(2,1)S(1)}, u32[]{:S(2)}) copy-start(bf16[2,256,384]{2,1,0:T(8,128)(2,1)S(1)} %collective-permute-done.14.other) | copy-start | bytes 1179652
  49.6 4.1 %copy-start.7 = (bf16[2,256,384]{2,1,0:T(8,128)(2,1)}, bf16[2,256,384]{2,1,0:T(8,128)(2,1)S(1)}, u32[]{:S(2)}) copy-start(bf16[2,256,384]{2,1,0:T(8,128)(2,1)S(1)} %collective-permute-done.9.f1) | copy-start | bytes 1179652

commit v7 on v6

--- a/solution.py
+++ b/solution.py
@@ -9,7 +9,7 @@
 NX, NY, NZ, NCORE = 4, 4, 8, 2
 SHIFTS = (0, 2, 1, -1)
 ZSHIFTS = (0, 2, 4, -2)
-VMEM = 58 * 1024 * 1024
+VMEM = 48 * 1024 * 1024
 
 
 def device_index(x, y, z, c):
@@ -29,6 +29,7 @@
 
 
 SWAP = pairs(lambda x, y, z, c: (x, y, z, 1 - c))
+ACROSS = pairs(lambda x, y, z, c: (x, y ^ 1, z, 1 - c))
 ZPAIR = pairs(lambda x, y, z, c: (x, y, z ^ 1, c))
 
 
@@ -72,7 +73,7 @@
 
 
 def solve_kernel(
-    partner, coulomb, w_own, w_other, p01, p23, f0, f1, g0, g1, ff0, gg1, other, out,
+    partner, coulomb, w_own, w_other, p01, p23, f0, f1, g0, g1, ff0, gg1, near, far, out,
     panel, left_rows, image, w, sems,
 ):
     copies = [
@@ -82,7 +83,7 @@
     copies[0].start()
     copies[1].start()
     rows, share = p01.shape[1:]
-    r, j, c, _, _ = where_am_i()
+    _, j, c, _, y_lo = where_am_i()
     starts = [pl.multiple_of(place_of(z) * 32, 32) for z in range(NZ)]
     arrays = ((p01, p23), (ff0, gg1), (f0, f1), (g0, g1))
     for k in range(4):
@@ -93,10 +94,10 @@
                 piece = arrays[k][i // 2][i % 2, pl.ds(starts[z], 32), :]
                 panel[pl.ds(to, 32), pl.ds(pl.multiple_of(col * share, share), share)] = piece
     left_rows[: 2 * rows, :] = panel[:, pl.ds(pl.multiple_of(j * share, share), share)]
-    for low in range(2):
+    for low, stack in ((y_lo, near), (1 - y_lo, far)):
         for z in range(NZ):
-            to = (2 + low) * rows + z * 32
-            left_rows[to : to + 32, :] = other[low, pl.ds(starts[z], 32), :]
+            to = pl.multiple_of((2 + low) * rows + z * 32, 32)
+            left_rows[pl.ds(to, 32), :] = stack[0, pl.ds(starts[z], 32), :]
     for q in range(4):
         copies[q].wait()
         if q < 2:
@@ -132,7 +133,7 @@
             out[2 * pair + 1, two] = jnp.where(lane < 64, pltpu.roll(even, 64, 1), odd)
 
 
-def solve(partner, coulomb, w_own, w_other, panels, other):
+def solve(partner, coulomb, w_own, w_other, panels, near, far):
     rows, share = panels[0].shape[1:]
     whole = w_own.shape[2]
     vmem = pl.BlockSpec(memory_space=pltpu.VMEM)
@@ -140,7 +141,7 @@
         solve_kernel,
         in_specs=[pl.BlockSpec(memory_space=pltpu.SMEM), vmem]
         + [pl.BlockSpec(memory_space=pl.ANY)] * 2
-        + [vmem] * 9,
+        + [vmem] * 10,
         out_specs=vmem,
         out_shape=jax.ShapeDtypeStruct((8, 2, 16, 128), jnp.float32),
         scratch_shapes=[
@@ -157,7 +158,7 @@
             transcendentals=0,
         ),
         name="solve",
-    )(partner, coulomb, w_own, w_other, *panels, other)
+    )(partner, coulomb, w_own, w_other, *panels, near, far)
 
 
 def spread_kernel(q_index, terms, out):
@@ -233,12 +234,23 @@
 
 def local(pair_matrix, screened, coulomb, q_index):
     bands, share = pair_matrix.shape[1:]
-    r, _, c, _, y_lo = where_am_i()
+    r = lax.axis_index("row")
     w_other = send(screened, SWAP)
     own = pair_matrix.reshape(1, 2 * bands, share)
     even = jnp.concatenate([own] + [send(own, along_z(s)) for s in ZSHIFTS[1:]], axis=0)
-    stack = jnp.concatenate([even, send(even, ZPAIR)], axis=0).reshape(1, NZ * 32, share)
-    parts = [send(stack, first_plane(s)) for s in SHIFTS[1:]]
+    paired = send(even, ZPAIR)
+    q_mine = jnp.stack([2 * r, 2 * r + 1, 2 * (r ^ 1), 2 * (r ^ 1) + 1])
+    ks = lax.iota(jnp.int32, q_index.shape[0])
+    partner = jnp.sum(
+        jnp.where(q_index[None] == q_mine[:, None, None], ks[None, :, None], 0), axis=1
+    ).astype(jnp.int32)
+    paired, partner, coulomb = lax.optimization_barrier(
+        (paired, partner, coulomb.reshape(1, share))
+    )
+    stack = jnp.concatenate([even, paired], axis=0).reshape(1, NZ * 32, share)
+    near = send(stack, SWAP)
+    far = send(stack, ACROSS)
+    parts = lax.optimization_barrier([send(stack, first_plane(s)) for s in SHIFTS[1:]])
     p01 = jnp.concatenate([stack, parts[0]], axis=0)
     p23 = jnp.concatenate([parts[1], parts[2]], axis=0)
 
@@ -249,24 +261,8 @@
     ff0 = send(f0, second_plane(1))
     gg1 = send(g1, second_plane(-1))
 
-    q_mine = jnp.stack([2 * r, 2 * r + 1, 2 * (r ^ 1), 2 * (r ^ 1) + 1])
-    ks = lax.iota(jnp.int32, q_index.shape[0])
-    partner = jnp.sum(
-        jnp.where(q_index[None] == q_mine[:, None, None], ks[None, :, None], 0), axis=1
-    )
-
-    up = jnp.where(c == 0, g0[0], parts[2][0])
-    down = jnp.where(c == 0, f0[0], parts[1][0])
-    across = jnp.where(y_lo == 0, up, down)
-    mine = jnp.stack(
-        [jnp.where(y_lo == 0, stack[0], across), jnp.where(y_lo == 0, across, stack[0])]
-    )
-    other = send(mine, SWAP)
-
     panels = (p01, p23, f0, f1, g0, g1, ff0, gg1)
-    terms = solve(
-        partner.astype(jnp.int32), coulomb.reshape(1, share), screened, w_other, panels, other
-    )
+    terms = solve(partner, coulomb, screened, w_other, panels, near, far)
     terms = lax.all_to_all(terms, "col", split_axis=0, concat_axis=0, tiled=True)
     placed = spread(q_index, terms)
     arrived = lax.all_to_all(placed, "row", split_axis=0, concat_axis=0, tiled=True)

time: 108 us -> 105 us (0.972)
  waiting for transfers between devices: 17.7 us -> 27.1 us
  starting transfers between devices: 32.6 us -> 27 us
  blocking collectives: 39.5 us -> 34.3 us
  Pallas kernels: 14.6 us -> 12.5 us
    ppermute x15 -> x16, waiting for transfers between devices: 17.7 us -> 27.1 us  [send(): return lax.ppermute(value, AXES, perm)]
    all_to_all x1, blocking collectives: 27.6 us -> 21 us  [local(): lax.all_to_all(placed, 'row', split_axis=0, concat_axis=0, tiled=True)]
    ppermute x15 -> x16, starting transfers between devices: 32.6 us -> 27 us  [send(): return lax.ppermute(value, AXES, perm)]
    pallas_call x1, Pallas kernels: 11.1 us -> 9.06 us  [solve(): pl.pallas_call(solve_kernel, in_specs=[pl.BlockSpec(memory_space=pltpu.SM...]
    all_to_all x1, blocking collectives: 11.9 us -> 13.3 us  [local(): lax.all_to_all(terms, 'col', split_axis=0, concat_axis=0, tiled=True)]
  transfers between devices with their start and end apart: 15 -> 16, of which waited for: 8 -> 8; matrix products, arithmetic and copies ran while one was open for 3% -> 3% of each run, Pallas kernels for 0% -> 0%
where the time goes in v7:
time: 105 us; the launch traced here: 104 us
  blocking collectives  34.3 us (33%)
  waiting for transfers between devices  27.1 us (26%)
  starting transfers between devices  27 us (26%)
  Pallas kernels  12.5 us (12%)
  other arithmetic  1.74 us (2%)
  local copies, waits for them, and re-layouts  1.52 us (1%)
    ppermute x16, waiting for transfers between devices, send(): return lax.ppermute(value, AXES, perm)  27.1 us
    ppermute x16, starting transfers between devices, send(): return lax.ppermute(value, AXES, perm)  27 us
    all_to_all x1, blocking collectives, local(): lax.all_to_all(placed, 'row', split_axis=0, concat_axis=0, tiled=True)  21 us
    all_to_all x1, blocking collectives, local(): lax.all_to_all(terms, 'col', split_axis=0, concat_axis=0, tiled=True)  13.3 us
    pallas_call x1, Pallas kernels, solve(): pl.pallas_call(solve_kernel, in_specs=[pl.BlockSpec(memory_space=pltpu.SM...  9.06 us
  transfers between devices with their start and end apart: 16, of which 8 were waited for; matrix products, arithmetic and copies ran while one was open for 3% of the time, Pallas kernels for 0%

profile of v7, /device:TPU:1, one launch (start us, length us, event | category | flops | bytes accessed | tf_op | source)
XLA Modules:
  0.0 104.3 jit_solution(1502328303118027622)
XLA Ops:
  0.0 3.2 %collective-permute-start.4 = (bf16[2,384,3072]{2,1,0:T(8,128)(2,1)}, bf16[2,384,3072]{2,1,0:T(8,128)(2,1)}, u32[]{:S(2)}, u32[]{:S(2)}) collective-permute-start(bf16[2,384,3072]{2,1,0:T(8,128)(2,1)} %w_own.1), channel_id=1, source_target_pairs={{0,8},{8,0},{16,24},{24,16},{32,40},{40,32},{48,56},{56,48},{64,72... | collective-permute-start | bytes 14155784 | tf_op jit(solution)/shard_map/ppermute | solution.py:49
  3.2 4.3 %collective-permute-start.2 = (bf16[1,32,384]{2,1,0:T(8,128)(2,1)}, bf16[1,32,384]{2,1,0:T(8,128)(2,1)S(1)}, u32[]{:S(2)}, u32[]{:S(2)}) collective-permute-start(bf16[1,32,384]{2,1,0:T(8,128)(2,1)} %bitcast.14), channel_id=1, source_target_pairs={{0,96},{8,104},{16,112},{24,120},{32,0},{40,8},{48,16},{56,24},{64... | collective-permute-start | bytes 73736 | tf_op jit(solution)/shard_map/ppermute | solution.py:49
  7.5 0.9 collective-permute-start.1
  8.4 2.3 %collective-permute-start = (bf16[1,32,384]{2,1,0:T(8,128)(2,1)}, bf16[1,32,384]{2,1,0:T(8,128)(2,1)S(1)}, u32[]{:S(2)}, u32[]{:S(2)}) collective-permute-start(bf16[1,32,384]{2,1,0:T(8,128)(2,1)} %bitcast.16), channel_id=1, source_target_pairs={{0,32},{8,40},{16,48},{24,56},{32,64},{40,72},{48,80},{56,88},{64,... | collective-permute-start | bytes 73736 | tf_op jit(solution)/shard_map/ppermute | solution.py:49
  10.9 0.9 select_reduce_fusion.partner
  13.1 1.3 %collective-permute-done.1 = bf16[1,32,384]{2,1,0:T(8,128)(2,1)S(1)} collective-permute-done((bf16[1,32,384]{2,1,0:T(8,128)(2,1)}, bf16[1,32,384]{2,1,0:T(8,128)(2,1)S(1)}, u32[]{:S(2)}, u32[]{:S(2)}) %collective-permute-start.1) | collective-permute-done | bytes 24608 | tf_op jit(solution)/shard_map/ppermute | solution.py:49
  14.5 0.8 pad_maximum_fusion.1
  15.9 2.8 %collective-permute-done.3 = bf16[4,32,384]{2,1,0:T(8,128)(2,1)S(1)} collective-permute-done((bf16[4,32,384]{2,1,0:T(8,128)(2,1)S(1)}, bf16[4,32,384]{2,1,0:T(8,128)(2,1)S(1)}, u32[]{:S(2)}, u32[]{:S(2)}) %collective-permute-start.3) | collective-permute-done | bytes 98336 | tf_op jit(solution)/shard_map/ppermute | solution.py:49
  18.8 2.8 %collective-permute-start.7 = (bf16[1,256,384]{2,1,0:T(8,128)(2,1)S(1)}, bf16[1,256,384]{2,1,0:T(8,128)(2,1)S(1)}, u32[]{:S(2)}, u32[]{:S(2)}) collective-permute-start(bf16[1,256,384]{2,1,0:T(8,128)(2,1)S(1)} %bitcast.8), channel_id=1, source_target_pairs={{0,3},{8,140},{16,19},{24,156},{32,35},{40,172},{48,51},{56,188},{... | collective-permute-start | bytes 589832 | tf_op jit(solution)/shard_map/ppermute | solution.py:49
  21.6 1.6 %collective-permute-start.5 = (bf16[1,256,384]{2,1,0:T(8,128)(2,1)S(1)}, bf16[1,256,384]{2,1,0:T(8,128)(2,1)S(1)}, u32[]{:S(2)}, u32[]{:S(2)}) collective-permute-start(bf16[1,256,384]{2,1,0:T(8,128)(2,1)S(1)} %bitcast.10), channel_id=1, source_target_pairs={{0,2},{8,12},{16,18},{24,28},{32,34},{40,44},{48,50},{56,60},{64,6... | collective-permute-start | bytes 589832 | tf_op jit(solution)/shard_map/ppermute | solution.py:49
  23.2 1.0 collective-permute-done.7
  24.2 5.5 %collective-permute-done.6 = bf16[1,256,384]{2,1,0:T(8,128)(2,1)S(1)} collective-permute-done((bf16[1,256,384]{2,1,0:T(8,128)(2,1)S(1)}, bf16[1,256,384]{2,1,0:T(8,128)(2,1)S(1)}, u32[]{:S(2)}, u32[]{:S(2)}) %collective-permute-start.6) | collective-permute-done | bytes 196640 | tf_op jit(solution)/shard_map/ppermute | solution.py:49
  29.8 2.6 %collective-permute-start.11 = (bf16[2,256,384]{2,1,0:T(8,128)(2,1)S(1)}, bf16[2,256,384]{2,1,0:T(8,128)(2,1)S(1)}, u32[]{:S(2)}, u32[]{:S(2)}) collective-permute-start(bf16[2,256,384]{2,1,0:T(8,128)(2,1)S(1)} %constant_dynamic-update-slice_fusion.5.p23), channel_id=1, source_target_pairs={{0,132},{8,11},{16,148},{24,27},{32,164},{40,43},{48,180},{56,59},... | collective-permute-start | bytes 1179656 | tf_op jit(solution)/shard_map/ppermute | solution.py:49
  32.5 4.3 %collective-permute-start.15 = (bf16[1,256,384]{2,1,0:T(8,128)(2,1)S(1)}, bf16[1,256,384]{2,1,0:T(8,128)(2,1)S(1)}, u32[]{:S(2)}, u32[]{:S(2)}) collective-permute-start(bf16[1,256,384]{2,1,0:T(8,128)(2,1)S(1)} %bitcast.12), channel_id=1, source_target_pairs={{0,136},{8,128},{16,152},{24,144},{32,168},{40,160},{48,184},{56,1... | collective-permute-start | bytes 589832 | tf_op jit(solution)/shard_map/ppermute | solution.py:49
  36.8 8.3 %collective-permute-done.15.far = bf16[1,256,384]{2,1,0:T(8,128)(2,1)S(1)} collective-permute-done((bf16[1,256,384]{2,1,0:T(8,128)(2,1)S(1)}, bf16[1,256,384]{2,1,0:T(8,128)(2,1)S(1)}, u32[]{:S(2)}, u32[]{:S(2)}) %collective-permute-start.15) | collective-permute-done | bytes 196640 | tf_op jit(solution)/shard_map/ppermute | solution.py:49
  45.1 2.7 %collective-permute-start.10 = (bf16[2,256,384]{2,1,0:T(8,128)(2,1)S(1)}, bf16[2,256,384]{2,1,0:T(8,128)(2,1)S(1)}, u32[]{:S(2)}, u32[]{:S(2)}) collective-permute-start(bf16[2,256,384]{2,1,0:T(8,128)(2,1)S(1)} %pad_maximum_fusion.p01), channel_id=1, source_target_pairs={{0,132},{8,11},{16,148},{24,27},{32,164},{40,43},{48,180},{56,59},... | collective-permute-start | bytes 1179656 | tf_op jit(solution)/shard_map/ppermute | solution.py:49
  47.8 1.4 %collective-permute-start.13 = (bf16[2,256,384]{2,1,0:T(8,128)(2,1)S(1)}, bf16[2,256,384]{2,1,0:T(8,128)(2,1)S(1)}, u32[]{:S(2)}, u32[]{:S(2)}) collective-permute-start(bf16[2,256,384]{2,1,0:T(8,128)(2,1)S(1)} %collective-permute-done.11.g1), channel_id=1, source_target_pairs={{0,132},{8,11},{16,148},{24,27},{32,164},{40,43},{48,180},{56,59},... | collective-permute-start | bytes 1179656 | tf_op jit(solution)/shard_map/ppermute | solution.py:49
  49.2 4.0 %collective-permute-done.9.f1 = bf16[2,256,384]{2,1,0:T(8,128)(2,1)S(1)} collective-permute-done((bf16[2,256,384]{2,1,0:T(8,128)(2,1)S(1)}, bf16[2,256,384]{2,1,0:T(8,128)(2,1)S(1)}, u32[]{:S(2)}, u32[]{:S(2)}) %collective-permute-start.9) | collective-permute-done | bytes 393248 | tf_op jit(solution)/shard_map/ppermute | solution.py:49
  53.2 3.5 %collective-permute-done.13.gg1 = bf16[2,256,384]{2,1,0:T(8,128)(2,1)S(1)} collective-permute-done((bf16[2,256,384]{2,1,0:T(8,128)(2,1)S(1)}, bf16[2,256,384]{2,1,0:T(8,128)(2,1)S(1)}, u32[]{:S(2)}, u32[]{:S(2)}) %collective-permute-start.13) | collective-permute-done | bytes 393248 | tf_op jit(solution)/shard_map/ppermute | solution.py:49
  57.4 9.1 %solve.1 = f32[8,2,16,128]{3,2,1,0:T(8,128)S(1)} custom-call(s32[4,64]{1,0:T(4,128)S(1)} %select_reduce_fusion.partner, f32[1,384]{1,0:T(1,128)S(1)} %reshape.12.coulomb, bf16[2,384,3072]{2,1,0:T(8,128)(2,1)} %w_own.1, bf16[2,384,3072]{2,1,0:T(8,128)(2,1)} %collective-permute-done.4.w_other, bf16[2,256,384]{2,1,0:T(8,128)(2,1)S(1)} %pad_maximum_fusion.p01, ...), custom_call_target="tpu_custom_call" | custom-call | flops 4831838208 | bytes 9437184 | tf_op jit(solution)/shard_map/solve/pallas_call | solution.py:140
  66.5 13.3 %all_to_all.10.terms = f32[8,2,16,128]{3,2,1,0:T(8,128)} all-to-all(f32[8,2,16,128]{3,2,1,0:T(8,128)S(1)} %solve.1), channel_id=1, replica_groups=mesh['row'=32,'col'=8] {'col'}, dimensions={0} | all-to-all | bytes 262144 | tf_op jit(solution)/shard_map/all_to_all | solution.py:266
  79.8 1.8 %spread.1 = f32[32,16,128]{2,1,0:T(8,128)} custom-call(s32[64,64]{1,0:T(8,128)} %q_index.1, f32[8,2,16,128]{3,2,1,0:T(8,128)} %all_to_all.10.terms), custom_call_target="tpu_custom_call" | custom-call | tf_op jit(solution)/shard_map/spread/pallas_call | solution.py:197
  81.7 21.0 %all_to_all.11.arrived = f32[32,16,128]{2,1,0:T(8,128)} all-to-all(f32[32,16,128]{2,1,0:T(8,128)} %spread.1), channel_id=1, replica_groups=mesh['row'=32,'col'=8] {'row'}, dimensions={0} | all-to-all | bytes 524288 | tf_op jit(solution)/shard_map/all_to_all | solution.py:268
  102.7 1.7 %settle.1 = f32[32,128]{1,0:T(8,128)} custom-call(f32[32,16,128]{2,1,0:T(8,128)} %all_to_all.11.arrived), custom_call_target="tpu_custom_call" | custom-call | tf_op jit(solution)/shard_map/settle/pallas_call | solution.py:226
  (25 shorter events, 3.3 us)
Async XLA Ops:
  0.0 57.4 %collective-permute-start.4 = (bf16[2,384,3072]{2,1,0:T(8,128)(2,1)}, bf16[2,384,3072]{2,1,0:T(8,128)(2,1)}, u32[]{:S(2)}, u32[]{:S(2)}) collective-permute-start(bf16[2,384,3072]{2,1,0:T(8,128)(2,1)} %w_own.1), channel_id=1, source_target_pairs={{0,8},{8,0},{16,24},{24,16},{32,40},{40,32},{48,56},{56,48},{64,72... | collective-permute-start | bytes 14155784 | tf_op jit(solution)/shard_map/ppermute | solution.py:49
  3.2 9.9 %collective-permute-start.2 = (bf16[1,32,384]{2,1,0:T(8,128)(2,1)}, bf16[1,32,384]{2,1,0:T(8,128)(2,1)S(1)}, u32[]{:S(2)}, u32[]{:S(2)}) collective-permute-start(bf16[1,32,384]{2,1,0:T(8,128)(2,1)} %bitcast.14), channel_id=1, source_target_pairs={{0,96},{8,104},{16,112},{24,120},{32,0},{40,8},{48,16},{56,24},{64... | collective-permute-start | bytes 73736 | tf_op jit(solution)/shard_map/ppermute | solution.py:49
  7.5 6.9 %collective-permute-start.1 = (bf16[1,32,384]{2,1,0:T(8,128)(2,1)}, bf16[1,32,384]{2,1,0:T(8,128)(2,1)S(1)}, u32[]{:S(2)}, u32[]{:S(2)}) collective-permute-start(bf16[1,32,384]{2,1,0:T(8,128)(2,1)} %bitcast.15), channel_id=1, source_target_pairs={{0,64},{8,72},{16,80},{24,88},{32,96},{40,104},{48,112},{56,120},{... | collective-permute-start | bytes 73736 | tf_op jit(solution)/shard_map/ppermute | solution.py:49
  8.4 6.0 %collective-permute-start = (bf16[1,32,384]{2,1,0:T(8,128)(2,1)}, bf16[1,32,384]{2,1,0:T(8,128)(2,1)S(1)}, u32[]{:S(2)}, u32[]{:S(2)}) collective-permute-start(bf16[1,32,384]{2,1,0:T(8,128)(2,1)} %bitcast.16), channel_id=1, source_target_pairs={{0,32},{8,40},{16,48},{24,56},{32,64},{40,72},{48,80},{56,88},{64,... | collective-permute-start | bytes 73736 | tf_op jit(solution)/shard_map/ppermute | solution.py:49
  15.2 3.6 %collective-permute-start.3 = (bf16[4,32,384]{2,1,0:T(8,128)(2,1)S(1)}, bf16[4,32,384]{2,1,0:T(8,128)(2,1)S(1)}, u32[]{:S(2)}, u32[]{:S(2)}) collective-permute-start(bf16[4,32,384]{2,1,0:T(8,128)(2,1)S(1)} %pad_maximum_fusion.1), channel_id=1, source_target_pairs={{0,16},{8,24},{16,0},{24,8},{32,48},{40,56},{48,32},{56,40},{64,80... | collective-permute-start | bytes 294920 | tf_op jit(solution)/shard_map/ppermute | solution.py:49
  18.8 5.4 %collective-permute-start.7 = (bf16[1,256,384]{2,1,0:T(8,128)(2,1)S(1)}, bf16[1,256,384]{2,1,0:T(8,128)(2,1)S(1)}, u32[]{:S(2)}, u32[]{:S(2)}) collective-permute-start(bf16[1,256,384]{2,1,0:T(8,128)(2,1)S(1)} %bitcast.8), channel_id=1, source_target_pairs={{0,3},{8,140},{16,19},{24,156},{32,35},{40,172},{48,51},{56,188},{... | collective-permute-start | bytes 589832 | tf_op jit(solution)/shard_map/ppermute | solution.py:49
  21.6 8.1 %collective-permute-start.6 = (bf16[1,256,384]{2,1,0:T(8,128)(2,1)S(1)}, bf16[1,256,384]{2,1,0:T(8,128)(2,1)S(1)}, u32[]{:S(2)}, u32[]{:S(2)}) collective-permute-start(bf16[1,256,384]{2,1,0:T(8,128)(2,1)S(1)} %bitcast.9), channel_id=1, source_target_pairs={{0,1},{8,136},{16,17},{24,152},{32,33},{40,168},{48,49},{56,184},{... | collective-permute-start | bytes 589832 | tf_op jit(solution)/shard_map/ppermute | solution.py:49
  21.6 8.1 %collective-permute-start.5 = (bf16[1,256,384]{2,1,0:T(8,128)(2,1)S(1)}, bf16[1,256,384]{2,1,0:T(8,128)(2,1)S(1)}, u32[]{:S(2)}, u32[]{:S(2)}) collective-permute-start(bf16[1,256,384]{2,1,0:T(8,128)(2,1)S(1)} %bitcast.10), channel_id=1, source_target_pairs={{0,2},{8,12},{16,18},{24,28},{32,34},{40,44},{48,50},{56,60},{64,6... | collective-permute-start | bytes 589832 | tf_op jit(solution)/shard_map/ppermute | solution.py:49
  29.8 18.0 %collective-permute-start.11 = (bf16[2,256,384]{2,1,0:T(8,128)(2,1)S(1)}, bf16[2,256,384]{2,1,0:T(8,128)(2,1)S(1)}, u32[]{:S(2)}, u32[]{:S(2)}) collective-permute-start(bf16[2,256,384]{2,1,0:T(8,128)(2,1)S(1)} %constant_dynamic-update-slice_fusion.5.p23), channel_id=1, source_target_pairs={{0,132},{8,11},{16,148},{24,27},{32,164},{40,43},{48,180},{56,59},... | collective-permute-start | bytes 1179656 | tf_op jit(solution)/shard_map/ppermute | solution.py:49
  32.4 16.7 %collective-permute-start.8 = (bf16[2,256,384]{2,1,0:T(8,128)(2,1)S(1)}, bf16[2,256,384]{2,1,0:T(8,128)(2,1)S(1)}, u32[]{:S(2)}, u32[]{:S(2)}) collective-permute-start(bf16[2,256,384]{2,1,0:T(8,128)(2,1)S(1)} %pad_maximum_fusion.p01), channel_id=1, source_target_pairs={{0,128},{8,9},{16,144},{24,25},{32,160},{40,41},{48,176},{56,57},{... | collective-permute-start | bytes 1179656 | tf_op jit(solution)/shard_map/ppermute | solution.py:49
  32.5 12.6 %collective-permute-start.15 = (bf16[1,256,384]{2,1,0:T(8,128)(2,1)S(1)}, bf16[1,256,384]{2,1,0:T(8,128)(2,1)S(1)}, u32[]{:S(2)}, u32[]{:S(2)}) collective-permute-start(bf16[1,256,384]{2,1,0:T(8,128)(2,1)S(1)} %bitcast.12), channel_id=1, source_target_pairs={{0,136},{8,128},{16,152},{24,144},{32,168},{40,160},{48,184},{56,1... | collective-permute-start | bytes 589832 | tf_op jit(solution)/shard_map/ppermute | solution.py:49
  36.8 8.3 %collective-permute-start.14 = (bf16[1,256,384]{2,1,0:T(8,128)(2,1)S(1)}, bf16[1,256,384]{2,1,0:T(8,128)(2,1)S(1)}, u32[]{:S(2)}, u32[]{:S(2)}) collective-permute-start(bf16[1,256,384]{2,1,0:T(8,128)(2,1)S(1)} %bitcast.13), channel_id=1, source_target_pairs={{0,8},{8,0},{16,24},{24,16},{32,40},{40,32},{48,56},{56,48},{64,72... | collective-permute-start | bytes 589832 | tf_op jit(solution)/shard_map/ppermute | solution.py:49
  45.1 8.1 %collective-permute-start.9 = (bf16[2,256,384]{2,1,0:T(8,128)(2,1)S(1)}, bf16[2,256,384]{2,1,0:T(8,128)(2,1)S(1)}, u32[]{:S(2)}, u32[]{:S(2)}) collective-permute-start(bf16[2,256,384]{2,1,0:T(8,128)(2,1)S(1)} %constant_dynamic-update-slice_fusion.5.p23), channel_id=1, source_target_pairs={{0,128},{8,9},{16,144},{24,25},{32,160},{40,41},{48,176},{56,57},{... | collective-permute-start | bytes 1179656 | tf_op jit(solution)/shard_map/ppermute | solution.py:49
  45.1 8.1 %collective-permute-start.10 = (bf16[2,256,384]{2,1,0:T(8,128)(2,1)S(1)}, bf16[2,256,384]{2,1,0:T(8,128)(2,1)S(1)}, u32[]{:S(2)}, u32[]{:S(2)}) collective-permute-start(bf16[2,256,384]{2,1,0:T(8,128)(2,1)S(1)} %pad_maximum_fusion.p01), channel_id=1, source_target_pairs={{0,132},{8,11},{16,148},{24,27},{32,164},{40,43},{48,180},{56,59},... | collective-permute-start | bytes 1179656 | tf_op jit(solution)/shard_map/ppermute | solution.py:49
  47.8 8.9 %collective-permute-start.13 = (bf16[2,256,384]{2,1,0:T(8,128)(2,1)S(1)}, bf16[2,256,384]{2,1,0:T(8,128)(2,1)S(1)}, u32[]{:S(2)}, u32[]{:S(2)}) collective-permute-start(bf16[2,256,384]{2,1,0:T(8,128)(2,1)S(1)} %collective-permute-done.11.g1), channel_id=1, source_target_pairs={{0,132},{8,11},{16,148},{24,27},{32,164},{40,43},{48,180},{56,59},... | collective-permute-start | bytes 1179656 | tf_op jit(solution)/shard_map/ppermute | solution.py:49
  49.1 8.3 %collective-permute-start.12 = (bf16[2,256,384]{2,1,0:T(8,128)(2,1)S(1)}, bf16[2,256,384]{2,1,0:T(8,128)(2,1)S(1)}, u32[]{:S(2)}, u32[]{:S(2)}) collective-permute-start(bf16[2,256,384]{2,1,0:T(8,128)(2,1)S(1)} %collective-permute-done.8.f0), channel_id=1, source_target_pairs={{0,128},{8,9},{16,144},{24,25},{32,160},{40,41},{48,176},{56,57},{... | collective-permute-start | bytes 1179656 | tf_op jit(solution)/shard_map/ppermute | solution.py:49

commit v8 on v7

--- a/solution.py
+++ b/solution.py
@@ -244,8 +244,8 @@
     partner = jnp.sum(
         jnp.where(q_index[None] == q_mine[:, None, None], ks[None, :, None], 0), axis=1
     ).astype(jnp.int32)
-    paired, partner, coulomb = lax.optimization_barrier(
-        (paired, partner, coulomb.reshape(1, share))
+    paired, partner, coulomb, w_other = lax.optimization_barrier(
+        (paired, partner, coulomb.reshape(1, share), w_other)
     )
     stack = jnp.concatenate([even, paired], axis=0).reshape(1, NZ * 32, share)
     near = send(stack, SWAP)

time: 105 us -> 101 us (0.962)
  waiting for transfers between devices: 27.1 us -> 17.1 us
  blocking collectives: 34.3 us -> 38.2 us
  starting transfers between devices: 27 us -> 29 us
    ppermute x16, waiting for transfers between devices: 27.1 us -> 17.1 us  [send(): return lax.ppermute(value, AXES, perm)]
    all_to_all x1, blocking collectives: 21 us -> 24.4 us  [local(): lax.all_to_all(placed, 'row', split_axis=0, concat_axis=0, tiled=True)]
    ppermute x16, starting transfers between devices: 27 us -> 29 us  [send(): return lax.ppermute(value, AXES, perm)]
where the time goes in v8:
time: 101 us; the launch traced here: 100 us
  blocking collectives  38.2 us (38%)
  starting transfers between devices  29 us (29%)
  waiting for transfers between devices  17.1 us (17%)
  Pallas kernels  12.6 us (12%)
  other arithmetic  1.74 us (2%)
  local copies, waits for them, and re-layouts  1.52 us (2%)
    ppermute x16, starting transfers between devices, send(): return lax.ppermute(value, AXES, perm)  29 us
    all_to_all x1, blocking collectives, local(): lax.all_to_all(placed, 'row', split_axis=0, concat_axis=0, tiled=True)  24.4 us
    ppermute x16, waiting for transfers between devices, send(): return lax.ppermute(value, AXES, perm)  17.1 us
    all_to_all x1, blocking collectives, local(): lax.all_to_all(terms, 'col', split_axis=0, concat_axis=0, tiled=True)  13.8 us
    pallas_call x1, Pallas kernels, solve(): pl.pallas_call(solve_kernel, in_specs=[pl.BlockSpec(memory_space=pltpu.SM...  9.07 us
  transfers between devices with their start and end apart: 16, of which 8 were waited for; matrix products, arithmetic and copies ran while one was open for 3% of the time, Pallas kernels for 0%

profile of v8, /device:TPU:1, one launch (start us, length us, event | category | flops | bytes accessed | tf_op | source)
XLA Modules:
  0.0 100.2 jit_solution(5049329565364606942)
XLA Ops:
  0.0 3.2 %collective-permute-start.4 = (bf16[2,384,3072]{2,1,0:T(8,128)(2,1)}, bf16[2,384,3072]{2,1,0:T(8,128)(2,1)}, u32[]{:S(2)}, u32[]{:S(2)}) collective-permute-start(bf16[2,384,3072]{2,1,0:T(8,128)(2,1)} %w_own.1), channel_id=1, source_target_pairs={{0,8},{8,0},{16,24},{24,16},{32,40},{40,32},{48,56},{56,48},{64,72... | collective-permute-start | bytes 14155784 | tf_op jit(solution)/shard_map/ppermute | solution.py:49
  3.2 4.3 %collective-permute-start.2 = (bf16[1,32,384]{2,1,0:T(8,128)(2,1)}, bf16[1,32,384]{2,1,0:T(8,128)(2,1)S(1)}, u32[]{:S(2)}, u32[]{:S(2)}) collective-permute-start(bf16[1,32,384]{2,1,0:T(8,128)(2,1)} %bitcast.14), channel_id=1, source_target_pairs={{0,96},{8,104},{16,112},{24,120},{32,0},{40,8},{48,16},{56,24},{64... | collective-permute-start | bytes 73736 | tf_op jit(solution)/shard_map/ppermute | solution.py:49
  7.5 0.9 collective-permute-start.1
  8.4 2.3 %collective-permute-start = (bf16[1,32,384]{2,1,0:T(8,128)(2,1)}, bf16[1,32,384]{2,1,0:T(8,128)(2,1)S(1)}, u32[]{:S(2)}, u32[]{:S(2)}) collective-permute-start(bf16[1,32,384]{2,1,0:T(8,128)(2,1)} %bitcast.16), channel_id=1, source_target_pairs={{0,32},{8,40},{16,48},{24,56},{32,64},{40,72},{48,80},{56,88},{64,... | collective-permute-start | bytes 73736 | tf_op jit(solution)/shard_map/ppermute | solution.py:49
  10.9 0.9 select_reduce_fusion.partner
  13.1 1.3 %collective-permute-done.1 = bf16[1,32,384]{2,1,0:T(8,128)(2,1)S(1)} collective-permute-done((bf16[1,32,384]{2,1,0:T(8,128)(2,1)}, bf16[1,32,384]{2,1,0:T(8,128)(2,1)S(1)}, u32[]{:S(2)}, u32[]{:S(2)}) %collective-permute-start.1) | collective-permute-done | bytes 24608 | tf_op jit(solution)/shard_map/ppermute | solution.py:49
  15.9 2.8 %collective-permute-done.3 = bf16[4,32,384]{2,1,0:T(8,128)(2,1)S(1)} collective-permute-done((bf16[4,32,384]{2,1,0:T(8,128)(2,1)S(1)}, bf16[4,32,384]{2,1,0:T(8,128)(2,1)S(1)}, u32[]{:S(2)}, u32[]{:S(2)}) %collective-permute-start.3) | collective-permute-done | bytes 98336 | tf_op jit(solution)/shard_map/ppermute | solution.py:49
  18.8 2.8 %collective-permute-start.7 = (bf16[1,256,384]{2,1,0:T(8,128)(2,1)S(1)}, bf16[1,256,384]{2,1,0:T(8,128)(2,1)S(1)}, u32[]{:S(2)}, u32[]{:S(2)}) collective-permute-start(bf16[1,256,384]{2,1,0:T(8,128)(2,1)S(1)} %bitcast.8), channel_id=1, source_target_pairs={{0,3},{8,140},{16,19},{24,156},{32,35},{40,172},{48,51},{56,188},{... | collective-permute-start | bytes 589832 | tf_op jit(solution)/shard_map/ppermute | solution.py:49
  21.6 1.6 %collective-permute-start.5 = (bf16[1,256,384]{2,1,0:T(8,128)(2,1)S(1)}, bf16[1,256,384]{2,1,0:T(8,128)(2,1)S(1)}, u32[]{:S(2)}, u32[]{:S(2)}) collective-permute-start(bf16[1,256,384]{2,1,0:T(8,128)(2,1)S(1)} %bitcast.10), channel_id=1, source_target_pairs={{0,2},{8,12},{16,18},{24,28},{32,34},{40,44},{48,50},{56,60},{64,6... | collective-permute-start | bytes 589832 | tf_op jit(solution)/shard_map/ppermute | solution.py:49
  23.3 1.0 collective-permute-done.7
  24.2 5.5 %collective-permute-done.6 = bf16[1,256,384]{2,1,0:T(8,128)(2,1)S(1)} collective-permute-done((bf16[1,256,384]{2,1,0:T(8,128)(2,1)S(1)}, bf16[1,256,384]{2,1,0:T(8,128)(2,1)S(1)}, u32[]{:S(2)}, u32[]{:S(2)}) %collective-permute-start.6) | collective-permute-done | bytes 196640 | tf_op jit(solution)/shard_map/ppermute | solution.py:49
  29.8 2.6 %collective-permute-start.11 = (bf16[2,256,384]{2,1,0:T(8,128)(2,1)S(1)}, bf16[2,256,384]{2,1,0:T(8,128)(2,1)S(1)}, u32[]{:S(2)}, u32[]{:S(2)}) collective-permute-start(bf16[2,256,384]{2,1,0:T(8,128)(2,1)S(1)} %constant_dynamic-update-slice_fusion.5.p23), channel_id=1, source_target_pairs={{0,132},{8,11},{16,148},{24,27},{32,164},{40,43},{48,180},{56,59},... | collective-permute-start | bytes 1179656 | tf_op jit(solution)/shard_map/ppermute | solution.py:49
  32.5 4.3 %collective-permute-start.15 = (bf16[1,256,384]{2,1,0:T(8,128)(2,1)S(1)}, bf16[1,256,384]{2,1,0:T(8,128)(2,1)S(1)}, u32[]{:S(2)}, u32[]{:S(2)}) collective-permute-start(bf16[1,256,384]{2,1,0:T(8,128)(2,1)S(1)} %bitcast.12), channel_id=1, source_target_pairs={{0,136},{8,128},{16,152},{24,144},{32,168},{40,160},{48,184},{56,1... | collective-permute-start | bytes 589832 | tf_op jit(solution)/shard_map/ppermute | solution.py:49
  36.9 3.1 %collective-permute-start.10 = (bf16[2,256,384]{2,1,0:T(8,128)(2,1)S(1)}, bf16[2,256,384]{2,1,0:T(8,128)(2,1)S(1)}, u32[]{:S(2)}, u32[]{:S(2)}) collective-permute-start(bf16[2,256,384]{2,1,0:T(8,128)(2,1)S(1)} %pad_maximum_fusion.p01), channel_id=1, source_target_pairs={{0,132},{8,11},{16,148},{24,27},{32,164},{40,43},{48,180},{56,59},... | collective-permute-start | bytes 1179656 | tf_op jit(solution)/shard_map/ppermute | solution.py:49
  40.1 1.5 %collective-permute-start.13 = (bf16[2,256,384]{2,1,0:T(8,128)(2,1)S(1)}, bf16[2,256,384]{2,1,0:T(8,128)(2,1)S(1)}, u32[]{:S(2)}, u32[]{:S(2)}) collective-permute-start(bf16[2,256,384]{2,1,0:T(8,128)(2,1)S(1)} %collective-permute-done.11.g1), channel_id=1, source_target_pairs={{0,132},{8,11},{16,148},{24,27},{32,164},{40,43},{48,180},{56,59},... | collective-permute-start | bytes 1179656 | tf_op jit(solution)/shard_map/ppermute | solution.py:49
  41.5 3.5 %collective-permute-done.15.far = bf16[1,256,384]{2,1,0:T(8,128)(2,1)S(1)} collective-permute-done((bf16[1,256,384]{2,1,0:T(8,128)(2,1)S(1)}, bf16[1,256,384]{2,1,0:T(8,128)(2,1)S(1)}, u32[]{:S(2)}, u32[]{:S(2)}) %collective-permute-start.15) | collective-permute-done | bytes 196640 | tf_op jit(solution)/shard_map/ppermute | solution.py:49
  45.1 1.4 %collective-permute-start.14 = (bf16[1,256,384]{2,1,0:T(8,128)(2,1)S(1)}, bf16[1,256,384]{2,1,0:T(8,128)(2,1)S(1)}, u32[]{:S(2)}, u32[]{:S(2)}) collective-permute-start(bf16[1,256,384]{2,1,0:T(8,128)(2,1)S(1)} %bitcast.13), channel_id=1, source_target_pairs={{0,8},{8,0},{16,24},{24,16},{32,40},{40,32},{48,56},{56,48},{64,72... | collective-permute-start | bytes 589832 | tf_op jit(solution)/shard_map/ppermute | solution.py:49
  46.5 1.1 %collective-permute-done.14.near = bf16[1,256,384]{2,1,0:T(8,128)(2,1)S(1)} collective-permute-done((bf16[1,256,384]{2,1,0:T(8,128)(2,1)S(1)}, bf16[1,256,384]{2,1,0:T(8,128)(2,1)S(1)}, u32[]{:S(2)}, u32[]{:S(2)}) %collective-permute-start.14) | collective-permute-done | bytes 196640 | tf_op jit(solution)/shard_map/ppermute | solution.py:49
  47.6 1.4 %collective-permute-done.13.gg1 = bf16[2,256,384]{2,1,0:T(8,128)(2,1)S(1)} collective-permute-done((bf16[2,256,384]{2,1,0:T(8,128)(2,1)S(1)}, bf16[2,256,384]{2,1,0:T(8,128)(2,1)S(1)}, u32[]{:S(2)}, u32[]{:S(2)}) %collective-permute-start.13) | collective-permute-done | bytes 393248 | tf_op jit(solution)/shard_map/ppermute | solution.py:49
  49.4 9.1 %solve.1 = f32[8,2,16,128]{3,2,1,0:T(8,128)S(1)} custom-call(s32[4,64]{1,0:T(4,128)S(1)} %select_reduce_fusion.partner, f32[1,384]{1,0:T(1,128)S(1)} %reshape.12.coulomb, bf16[2,384,3072]{2,1,0:T(8,128)(2,1)} %w_own.1, bf16[2,384,3072]{2,1,0:T(8,128)(2,1)} %collective-permute-done.4.w_other, bf16[2,256,384]{2,1,0:T(8,128)(2,1)S(1)} %pad_maximum_fusion.p01, ...), custom_call_target="tpu_custom_call" | custom-call | flops 4831838208 | bytes 9437184 | tf_op jit(solution)/shard_map/solve/pallas_call | solution.py:140
  58.5 13.8 %all_to_all.10.terms = f32[8,2,16,128]{3,2,1,0:T(8,128)} all-to-all(f32[8,2,16,128]{3,2,1,0:T(8,128)S(1)} %solve.1), channel_id=1, replica_groups=mesh['row'=32,'col'=8] {'col'}, dimensions={0} | all-to-all | bytes 262144 | tf_op jit(solution)/shard_map/all_to_all | solution.py:266
  72.3 1.8 %spread.1 = f32[32,16,128]{2,1,0:T(8,128)} custom-call(s32[64,64]{1,0:T(8,128)} %q_index.1, f32[8,2,16,128]{3,2,1,0:T(8,128)} %all_to_all.10.terms), custom_call_target="tpu_custom_call" | custom-call | tf_op jit(solution)/shard_map/spread/pallas_call | solution.py:197
  74.2 24.4 %all_to_all.11.arrived = f32[32,16,128]{2,1,0:T(8,128)} all-to-all(f32[32,16,128]{2,1,0:T(8,128)} %spread.1), channel_id=1, replica_groups=mesh['row'=32,'col'=8] {'row'}, dimensions={0} | all-to-all | bytes 524288 | tf_op jit(solution)/shard_map/all_to_all | solution.py:268
  98.5 1.7 %settle.1 = f32[32,128]{1,0:T(8,128)} custom-call(f32[32,16,128]{2,1,0:T(8,128)} %all_to_all.11.arrived), custom_call_target="tpu_custom_call" | custom-call | tf_op jit(solution)/shard_map/settle/pallas_call | solution.py:226
  (25 shorter events, 3.8 us)
Async XLA Ops:
  0.0 18.8 %collective-permute-start.4 = (bf16[2,384,3072]{2,1,0:T(8,128)(2,1)}, bf16[2,384,3072]{2,1,0:T(8,128)(2,1)}, u32[]{:S(2)}, u32[]{:S(2)}) collective-permute-start(bf16[2,384,3072]{2,1,0:T(8,128)(2,1)} %w_own.1), channel_id=1, source_target_pairs={{0,8},{8,0},{16,24},{24,16},{32,40},{40,32},{48,56},{56,48},{64,72... | collective-permute-start | bytes 14155784 | tf_op jit(solution)/shard_map/ppermute | solution.py:49
  3.2 9.9 %collective-permute-start.2 = (bf16[1,32,384]{2,1,0:T(8,128)(2,1)}, bf16[1,32,384]{2,1,0:T(8,128)(2,1)S(1)}, u32[]{:S(2)}, u32[]{:S(2)}) collective-permute-start(bf16[1,32,384]{2,1,0:T(8,128)(2,1)} %bitcast.14), channel_id=1, source_target_pairs={{0,96},{8,104},{16,112},{24,120},{32,0},{40,8},{48,16},{56,24},{64... | collective-permute-start | bytes 73736 | tf_op jit(solution)/shard_map/ppermute | solution.py:49
  7.5 6.9 %collective-permute-start.1 = (bf16[1,32,384]{2,1,0:T(8,128)(2,1)}, bf16[1,32,384]{2,1,0:T(8,128)(2,1)S(1)}, u32[]{:S(2)}, u32[]{:S(2)}) collective-permute-start(bf16[1,32,384]{2,1,0:T(8,128)(2,1)} %bitcast.15), channel_id=1, source_target_pairs={{0,64},{8,72},{16,80},{24,88},{32,96},{40,104},{48,112},{56,120},{... | collective-permute-start | bytes 73736 | tf_op jit(solution)/shard_map/ppermute | solution.py:49
  8.4 6.0 %collective-permute-start = (bf16[1,32,384]{2,1,0:T(8,128)(2,1)}, bf16[1,32,384]{2,1,0:T(8,128)(2,1)S(1)}, u32[]{:S(2)}, u32[]{:S(2)}) collective-permute-start(bf16[1,32,384]{2,1,0:T(8,128)(2,1)} %bitcast.16), channel_id=1, source_target_pairs={{0,32},{8,40},{16,48},{24,56},{32,64},{40,72},{48,80},{56,88},{64,... | collective-permute-start | bytes 73736 | tf_op jit(solution)/shard_map/ppermute | solution.py:49
  15.2 3.6 %collective-permute-start.3 = (bf16[4,32,384]{2,1,0:T(8,128)(2,1)S(1)}, bf16[4,32,384]{2,1,0:T(8,128)(2,1)S(1)}, u32[]{:S(2)}, u32[]{:S(2)}) collective-permute-start(bf16[4,32,384]{2,1,0:T(8,128)(2,1)S(1)} %pad_maximum_fusion.1), channel_id=1, source_target_pairs={{0,16},{8,24},{16,0},{24,8},{32,48},{40,56},{48,32},{56,40},{64,80... | collective-permute-start | bytes 294920 | tf_op jit(solution)/shard_map/ppermute | solution.py:49
  18.8 5.4 %collective-permute-start.7 = (bf16[1,256,384]{2,1,0:T(8,128)(2,1)S(1)}, bf16[1,256,384]{2,1,0:T(8,128)(2,1)S(1)}, u32[]{:S(2)}, u32[]{:S(2)}) collective-permute-start(bf16[1,256,384]{2,1,0:T(8,128)(2,1)S(1)} %bitcast.8), channel_id=1, source_target_pairs={{0,3},{8,140},{16,19},{24,156},{32,35},{40,172},{48,51},{56,188},{... | collective-permute-start | bytes 589832 | tf_op jit(solution)/shard_map/ppermute | solution.py:49
  21.6 8.1 %collective-permute-start.6 = (bf16[1,256,384]{2,1,0:T(8,128)(2,1)S(1)}, bf16[1,256,384]{2,1,0:T(8,128)(2,1)S(1)}, u32[]{:S(2)}, u32[]{:S(2)}) collective-permute-start(bf16[1,256,384]{2,1,0:T(8,128)(2,1)S(1)} %bitcast.9), channel_id=1, source_target_pairs={{0,1},{8,136},{16,17},{24,152},{32,33},{40,168},{48,49},{56,184},{... | collective-permute-start | bytes 589832 | tf_op jit(solution)/shard_map/ppermute | solution.py:49
  21.6 8.1 %collective-permute-start.5 = (bf16[1,256,384]{2,1,0:T(8,128)(2,1)S(1)}, bf16[1,256,384]{2,1,0:T(8,128)(2,1)S(1)}, u32[]{:S(2)}, u32[]{:S(2)}) collective-permute-start(bf16[1,256,384]{2,1,0:T(8,128)(2,1)S(1)} %bitcast.10), channel_id=1, source_target_pairs={{0,2},{8,12},{16,18},{24,28},{32,34},{40,44},{48,50},{56,60},{64,6... | collective-permute-start | bytes 589832 | tf_op jit(solution)/shard_map/ppermute | solution.py:49
  29.8 10.3 %collective-permute-start.11 = (bf16[2,256,384]{2,1,0:T(8,128)(2,1)S(1)}, bf16[2,256,384]{2,1,0:T(8,128)(2,1)S(1)}, u32[]{:S(2)}, u32[]{:S(2)}) collective-permute-start(bf16[2,256,384]{2,1,0:T(8,128)(2,1)S(1)} %constant_dynamic-update-slice_fusion.5.p23), channel_id=1, source_target_pairs={{0,132},{8,11},{16,148},{24,27},{32,164},{40,43},{48,180},{56,59},... | collective-permute-start | bytes 1179656 | tf_op jit(solution)/shard_map/ppermute | solution.py:49
  32.4 9.1 %collective-permute-start.8 = (bf16[2,256,384]{2,1,0:T(8,128)(2,1)S(1)}, bf16[2,256,384]{2,1,0:T(8,128)(2,1)S(1)}, u32[]{:S(2)}, u32[]{:S(2)}) collective-permute-start(bf16[2,256,384]{2,1,0:T(8,128)(2,1)S(1)} %pad_maximum_fusion.p01), channel_id=1, source_target_pairs={{0,128},{8,9},{16,144},{24,25},{32,160},{40,41},{48,176},{56,57},{... | collective-permute-start | bytes 1179656 | tf_op jit(solution)/shard_map/ppermute | solution.py:49
  32.5 12.6 %collective-permute-start.15 = (bf16[1,256,384]{2,1,0:T(8,128)(2,1)S(1)}, bf16[1,256,384]{2,1,0:T(8,128)(2,1)S(1)}, u32[]{:S(2)}, u32[]{:S(2)}) collective-permute-start(bf16[1,256,384]{2,1,0:T(8,128)(2,1)S(1)} %bitcast.12), channel_id=1, source_target_pairs={{0,136},{8,128},{16,152},{24,144},{32,168},{40,160},{48,184},{56,1... | collective-permute-start | bytes 589832 | tf_op jit(solution)/shard_map/ppermute | solution.py:49
  36.8 10.8 %collective-permute-start.9 = (bf16[2,256,384]{2,1,0:T(8,128)(2,1)S(1)}, bf16[2,256,384]{2,1,0:T(8,128)(2,1)S(1)}, u32[]{:S(2)}, u32[]{:S(2)}) collective-permute-start(bf16[2,256,384]{2,1,0:T(8,128)(2,1)S(1)} %constant_dynamic-update-slice_fusion.5.p23), channel_id=1, source_target_pairs={{0,128},{8,9},{16,144},{24,25},{32,160},{40,41},{48,176},{56,57},{... | collective-permute-start | bytes 1179656 | tf_op jit(solution)/shard_map/ppermute | solution.py:49
  36.9 10.7 %collective-permute-start.10 = (bf16[2,256,384]{2,1,0:T(8,128)(2,1)S(1)}, bf16[2,256,384]{2,1,0:T(8,128)(2,1)S(1)}, u32[]{:S(2)}, u32[]{:S(2)}) collective-permute-start(bf16[2,256,384]{2,1,0:T(8,128)(2,1)S(1)} %pad_maximum_fusion.p01), channel_id=1, source_target_pairs={{0,132},{8,11},{16,148},{24,27},{32,164},{40,43},{48,180},{56,59},... | collective-permute-start | bytes 1179656 | tf_op jit(solution)/shard_map/ppermute | solution.py:49
  40.1 8.9 %collective-permute-start.13 = (bf16[2,256,384]{2,1,0:T(8,128)(2,1)S(1)}, bf16[2,256,384]{2,1,0:T(8,128)(2,1)S(1)}, u32[]{:S(2)}, u32[]{:S(2)}) collective-permute-start(bf16[2,256,384]{2,1,0:T(8,128)(2,1)S(1)} %collective-permute-done.11.g1), channel_id=1, source_target_pairs={{0,132},{8,11},{16,148},{24,27},{32,164},{40,43},{48,180},{56,59},... | collective-permute-start | bytes 1179656 | tf_op jit(solution)/shard_map/ppermute | solution.py:49
  41.5 7.9 %collective-permute-start.12 = (bf16[2,256,384]{2,1,0:T(8,128)(2,1)S(1)}, bf16[2,256,384]{2,1,0:T(8,128)(2,1)S(1)}, u32[]{:S(2)}, u32[]{:S(2)}) collective-permute-start(bf16[2,256,384]{2,1,0:T(8,128)(2,1)S(1)} %collective-permute-done.8.f0), channel_id=1, source_target_pairs={{0,128},{8,9},{16,144},{24,25},{32,160},{40,41},{48,176},{56,57},{... | collective-permute-start | bytes 1179656 | tf_op jit(solution)/shard_map/ppermute | solution.py:49
  45.1 2.5 %collective-permute-start.14 = (bf16[1,256,384]{2,1,0:T(8,128)(2,1)S(1)}, bf16[1,256,384]{2,1,0:T(8,128)(2,1)S(1)}, u32[]{:S(2)}, u32[]{:S(2)}) collective-permute-start(bf16[1,256,384]{2,1,0:T(8,128)(2,1)S(1)} %bitcast.13), channel_id=1, source_target_pairs={{0,8},{8,0},{16,24},{24,16},{32,40},{40,32},{48,56},{56,48},{64,72... | collective-permute-start | bytes 589832 | tf_op jit(solution)/shard_map/ppermute | solution.py:49

commit v9 on v8

--- a/solution.py
+++ b/solution.py
@@ -7,7 +7,8 @@
 
 AXES = ("row", "col")
 NX, NY, NZ, NCORE = 4, 4, 8, 2
-SHIFTS = (0, 2, 1, -1)
+FIRST = (0, 1, 2, -1)
+SECOND = (0, 2, 1, -1)
 ZSHIFTS = (0, 2, 4, -2)
 VMEM = 48 * 1024 * 1024
 
@@ -60,7 +61,7 @@
 
 def spot(k, i):
     r, j, c, _, y_lo = where_am_i()
-    first, second = SHIFTS[i], SHIFTS[k]
+    first, second = FIRST[i], SECOND[k]
     x = ((j & 3) - first - c * (second - first)) & 3
     y = (2 * (j >> 2) + y_lo - second - c * (first - second)) & 3
     return (y >> 1) * NX + x, y & 1
@@ -81,7 +82,6 @@
         for q in range(4)
     ]
     copies[0].start()
-    copies[1].start()
     rows, share = p01.shape[1:]
     _, j, c, _, y_lo = where_am_i()
     starts = [pl.multiple_of(place_of(z) * 32, 32) for z in range(NZ)]
@@ -100,8 +100,8 @@
             left_rows[pl.ds(to, 32), :] = stack[0, pl.ds(starts[z], 32), :]
     for q in range(4):
         copies[q].wait()
-        if q < 2:
-            copies[q + 2].start()
+        if q < 3:
+            copies[q + 1].start()
         image[q] = contract(w[q], panel[...]).astype(image.dtype)
 
     lane = lax.broadcasted_iota(jnp.int32, (16, 128), 1)
@@ -250,14 +250,15 @@
     stack = jnp.concatenate([even, paired], axis=0).reshape(1, NZ * 32, share)
     near = send(stack, SWAP)
     far = send(stack, ACROSS)
-    parts = lax.optimization_barrier([send(stack, first_plane(s)) for s in SHIFTS[1:]])
+    parts = [send(stack, first_plane(s)) for s in FIRST[1:]]
     p01 = jnp.concatenate([stack, parts[0]], axis=0)
     p23 = jnp.concatenate([parts[1], parts[2]], axis=0)
 
     f0 = send(p01, second_plane(1))
     g1 = send(p23, second_plane(-1))
-    g0 = send(p01, second_plane(-1))
-    f1 = send(p23, second_plane(1))
+    late01, late23, near, far = lax.optimization_barrier((p01, p23, near, far))
+    g0 = send(late01, second_plane(-1))
+    f1 = send(late23, second_plane(1))
     ff0 = send(f0, second_plane(1))
     gg1 = send(g1, second_plane(-1))
 

time: 101 us -> 103 us (1.020)
  blocking collectives: 38.2 us -> 31.4 us
  waiting for transfers between devices: 17.1 us -> 21.6 us
  starting transfers between devices: 29 us -> 32.6 us
    all_to_all x1, blocking collectives: 24.4 us -> 17.6 us  [local(): lax.all_to_all(placed, 'row', split_axis=0, concat_axis=0, tiled=True)]
    ppermute x16, waiting for transfers between devices: 17.1 us -> 21.6 us  [send(): return lax.ppermute(value, AXES, perm)]
    ppermute x16, starting transfers between devices: 29 us -> 32.6 us  [send(): return lax.ppermute(value, AXES, perm)]
  transfers between devices with their start and end apart: 16 -> 16, of which waited for: 8 -> 7; matrix products, arithmetic and copies ran while one was open for 3% -> 3% of each run, Pallas kernels for 0% -> 0%
where the time goes in v9:
time: 103 us; the launch traced here: 102 us
  starting transfers between devices  32.6 us (32%)
  blocking collectives  31.4 us (30%)
  waiting for transfers between devices  21.6 us (21%)
  Pallas kernels  13.3 us (13%)
  other arithmetic  1.74 us (2%)
  local copies, waits for them, and re-layouts  1.52 us (1%)
    ppermute x16, starting transfers between devices, send(): return lax.ppermute(value, AXES, perm)  32.6 us
    ppermute x16, waiting for transfers between devices, send(): return lax.ppermute(value, AXES, perm)  21.6 us
    all_to_all x1, blocking collectives, local(): lax.all_to_all(placed, 'row', split_axis=0, concat_axis=0, tiled=True)  17.6 us
    all_to_all x1, blocking collectives, local(): lax.all_to_all(terms, 'col', split_axis=0, concat_axis=0, tiled=True)  13.9 us
    pallas_call x1, Pallas kernels, solve(): pl.pallas_call(solve_kernel, in_specs=[pl.BlockSpec(memory_space=pltpu.SM...  9.82 us
  transfers between devices with their start and end apart: 16, of which 7 were waited for; matrix products, arithmetic and copies ran while one was open for 3% of the time, Pallas kernels for 0%

profile of v9, /device:TPU:1, one launch (start us, length us, event | category | flops | bytes accessed | tf_op | source)
XLA Modules:
  0.0 102.2 jit_solution(4954009233213849133)
XLA Ops:
  0.0 3.2 %collective-permute-start.4 = (bf16[2,384,3072]{2,1,0:T(8,128)(2,1)}, bf16[2,384,3072]{2,1,0:T(8,128)(2,1)}, u32[]{:S(2)}, u32[]{:S(2)}) collective-permute-start(bf16[2,384,3072]{2,1,0:T(8,128)(2,1)} %w_own.1), channel_id=1, source_target_pairs={{0,8},{8,0},{16,24},{24,16},{32,40},{40,32},{48,56},{56,48},{64,72... | collective-permute-start | bytes 14155784 | tf_op jit(solution)/shard_map/ppermute | solution.py:50
  3.2 4.3 %collective-permute-start.2 = (bf16[1,32,384]{2,1,0:T(8,128)(2,1)}, bf16[1,32,384]{2,1,0:T(8,128)(2,1)S(1)}, u32[]{:S(2)}, u32[]{:S(2)}) collective-permute-start(bf16[1,32,384]{2,1,0:T(8,128)(2,1)} %bitcast.14), channel_id=1, source_target_pairs={{0,96},{8,104},{16,112},{24,120},{32,0},{40,8},{48,16},{56,24},{64... | collective-permute-start | bytes 73736 | tf_op jit(solution)/shard_map/ppermute | solution.py:50
  7.5 0.9 collective-permute-start.1
  8.4 2.3 %collective-permute-start = (bf16[1,32,384]{2,1,0:T(8,128)(2,1)}, bf16[1,32,384]{2,1,0:T(8,128)(2,1)S(1)}, u32[]{:S(2)}, u32[]{:S(2)}) collective-permute-start(bf16[1,32,384]{2,1,0:T(8,128)(2,1)} %bitcast.16), channel_id=1, source_target_pairs={{0,32},{8,40},{16,48},{24,56},{32,64},{40,72},{48,80},{56,88},{64,... | collective-permute-start | bytes 73736 | tf_op jit(solution)/shard_map/ppermute | solution.py:50
  13.1 1.3 %collective-permute-done.1 = bf16[1,32,384]{2,1,0:T(8,128)(2,1)S(1)} collective-permute-done((bf16[1,32,384]{2,1,0:T(8,128)(2,1)}, bf16[1,32,384]{2,1,0:T(8,128)(2,1)S(1)}, u32[]{:S(2)}, u32[]{:S(2)}) %collective-permute-start.1) | collective-permute-done | bytes 24608 | tf_op jit(solution)/shard_map/ppermute | solution.py:50
  15.9 2.8 %collective-permute-done.3 = bf16[4,32,384]{2,1,0:T(8,128)(2,1)S(1)} collective-permute-done((bf16[4,32,384]{2,1,0:T(8,128)(2,1)S(1)}, bf16[4,32,384]{2,1,0:T(8,128)(2,1)S(1)}, u32[]{:S(2)}, u32[]{:S(2)}) %collective-permute-start.3) | collective-permute-done | bytes 98336 | tf_op jit(solution)/shard_map/ppermute | solution.py:50
  18.8 1.4 %collective-permute-start.5 = (bf16[1,256,384]{2,1,0:T(8,128)(2,1)S(1)}, bf16[1,256,384]{2,1,0:T(8,128)(2,1)S(1)}, u32[]{:S(2)}, u32[]{:S(2)}) collective-permute-start(bf16[1,256,384]{2,1,0:T(8,128)(2,1)S(1)} %bitcast.8), channel_id=1, source_target_pairs={{0,1},{8,136},{16,17},{24,152},{32,33},{40,168},{48,49},{56,184},{... | collective-permute-start | bytes 589832 | tf_op jit(solution)/shard_map/ppermute | solution.py:50
  20.2 2.6 %collective-permute-start.6 = (bf16[1,256,384]{2,1,0:T(8,128)(2,1)S(1)}, bf16[1,256,384]{2,1,0:T(8,128)(2,1)S(1)}, u32[]{:S(2)}, u32[]{:S(2)}) collective-permute-start(bf16[1,256,384]{2,1,0:T(8,128)(2,1)S(1)} %bitcast.9), channel_id=1, source_target_pairs={{0,2},{8,12},{16,18},{24,28},{32,34},{40,44},{48,50},{56,60},{64,6... | collective-permute-start | bytes 589832 | tf_op jit(solution)/shard_map/ppermute | solution.py:50
  22.8 1.1 %collective-permute-start.7 = (bf16[1,256,384]{2,1,0:T(8,128)(2,1)S(1)}, bf16[1,256,384]{2,1,0:T(8,128)(2,1)S(1)}, u32[]{:S(2)}, u32[]{:S(2)}) collective-permute-start(bf16[1,256,384]{2,1,0:T(8,128)(2,1)S(1)} %bitcast.10), channel_id=1, source_target_pairs={{0,3},{8,140},{16,19},{24,156},{32,35},{40,172},{48,51},{56,188},{... | collective-permute-start | bytes 589832 | tf_op jit(solution)/shard_map/ppermute | solution.py:50
  24.7 1.3 %collective-permute-start.8 = (bf16[2,256,384]{2,1,0:T(8,128)(2,1)S(1)}, bf16[2,256,384]{2,1,0:T(8,128)(2,1)S(1)}, u32[]{:S(2)}, u32[]{:S(2)}) collective-permute-start(bf16[2,256,384]{2,1,0:T(8,128)(2,1)S(1)} %pad_maximum_fusion.p01), channel_id=1, source_target_pairs={{0,128},{8,9},{16,144},{24,25},{32,160},{40,41},{48,176},{56,57},{... | collective-permute-start | bytes 1179656 | tf_op jit(solution)/shard_map/ppermute | solution.py:50
  26.0 1.9 %collective-permute-done.6 = bf16[1,256,384]{2,1,0:T(8,128)(2,1)S(1)} collective-permute-done((bf16[1,256,384]{2,1,0:T(8,128)(2,1)S(1)}, bf16[1,256,384]{2,1,0:T(8,128)(2,1)S(1)}, u32[]{:S(2)}, u32[]{:S(2)}) %collective-permute-start.6) | collective-permute-done | bytes 196640 | tf_op jit(solution)/shard_map/ppermute | solution.py:50
  28.0 2.9 %collective-permute-start.13 = (bf16[2,256,384]{2,1,0:T(8,128)(2,1)S(1)}, bf16[2,256,384]{2,1,0:T(8,128)(2,1)S(1)}, u32[]{:S(2)}, u32[]{:S(2)}) collective-permute-start(bf16[2,256,384]{2,1,0:T(8,128)(2,1)S(1)} %constant_dynamic-update-slice_fusion.5.p23), channel_id=1, source_target_pairs={{0,132},{8,11},{16,148},{24,27},{32,164},{40,43},{48,180},{56,59},... | collective-permute-start | bytes 1179656 | tf_op jit(solution)/shard_map/ppermute | solution.py:50
  30.9 4.8 %collective-permute-start.10 = (bf16[1,256,384]{2,1,0:T(8,128)(2,1)S(1)}, bf16[1,256,384]{2,1,0:T(8,128)(2,1)S(1)}, u32[]{:S(2)}, u32[]{:S(2)}) collective-permute-start(bf16[1,256,384]{2,1,0:T(8,128)(2,1)S(1)} %bitcast.12), channel_id=1, source_target_pairs={{0,136},{8,128},{16,152},{24,144},{32,168},{40,160},{48,184},{56,1... | collective-permute-start | bytes 589832 | tf_op jit(solution)/shard_map/ppermute | solution.py:50
  35.7 1.7 %collective-permute-start.9 = (bf16[1,256,384]{2,1,0:T(8,128)(2,1)S(1)}, bf16[1,256,384]{2,1,0:T(8,128)(2,1)S(1)}, u32[]{:S(2)}, u32[]{:S(2)}) collective-permute-start(bf16[1,256,384]{2,1,0:T(8,128)(2,1)S(1)} %bitcast.13), channel_id=1, source_target_pairs={{0,8},{8,0},{16,24},{24,16},{32,40},{40,32},{48,56},{56,48},{64,72... | collective-permute-start | bytes 589832 | tf_op jit(solution)/shard_map/ppermute | solution.py:50
  37.4 7.8 %collective-permute-done.10.far = bf16[1,256,384]{2,1,0:T(8,128)(2,1)S(1)} collective-permute-done((bf16[1,256,384]{2,1,0:T(8,128)(2,1)S(1)}, bf16[1,256,384]{2,1,0:T(8,128)(2,1)S(1)}, u32[]{:S(2)}, u32[]{:S(2)}) %collective-permute-start.10) | collective-permute-done | bytes 196640 | tf_op jit(solution)/shard_map/ppermute | solution.py:50
  45.3 2.6 %collective-permute-start.12 = (bf16[2,256,384]{2,1,0:T(8,128)(2,1)S(1)}, bf16[2,256,384]{2,1,0:T(8,128)(2,1)S(1)}, u32[]{:S(2)}, u32[]{:S(2)}) collective-permute-start(bf16[2,256,384]{2,1,0:T(8,128)(2,1)S(1)} %pad_maximum_fusion.p01), channel_id=1, source_target_pairs={{0,132},{8,11},{16,148},{24,27},{32,164},{40,43},{48,180},{56,59},... | collective-permute-start | bytes 1179656 | tf_op jit(solution)/shard_map/ppermute | solution.py:50
  47.9 2.7 %collective-permute-start.15 = (bf16[2,256,384]{2,1,0:T(8,128)(2,1)S(1)}, bf16[2,256,384]{2,1,0:T(8,128)(2,1)S(1)}, u32[]{:S(2)}, u32[]{:S(2)}) collective-permute-start(bf16[2,256,384]{2,1,0:T(8,128)(2,1)S(1)} %collective-permute-done.13.g1), channel_id=1, source_target_pairs={{0,132},{8,11},{16,148},{24,27},{32,164},{40,43},{48,180},{56,59},... | collective-permute-start | bytes 1179656 | tf_op jit(solution)/shard_map/ppermute | solution.py:50
  50.6 2.8 %collective-permute-done.11.f1 = bf16[2,256,384]{2,1,0:T(8,128)(2,1)S(1)} collective-permute-done((bf16[2,256,384]{2,1,0:T(8,128)(2,1)S(1)}, bf16[2,256,384]{2,1,0:T(8,128)(2,1)S(1)}, u32[]{:S(2)}, u32[]{:S(2)}) %collective-permute-start.11) | collective-permute-done | bytes 393248 | tf_op jit(solution)/shard_map/ppermute | solution.py:50
  53.4 4.1 %collective-permute-done.14.ff0 = bf16[2,256,384]{2,1,0:T(8,128)(2,1)S(1)} collective-permute-done((bf16[2,256,384]{2,1,0:T(8,128)(2,1)S(1)}, bf16[2,256,384]{2,1,0:T(8,128)(2,1)S(1)}, u32[]{:S(2)}, u32[]{:S(2)}) %collective-permute-start.14) | collective-permute-done | bytes 393248 | tf_op jit(solution)/shard_map/ppermute | solution.py:50
  57.5 9.8 %solve.1 = f32[8,2,16,128]{3,2,1,0:T(8,128)S(1)} custom-call(s32[4,64]{1,0:T(4,128)S(1)} %select_reduce_fusion.partner, f32[1,384]{1,0:T(1,128)S(1)} %reshape.12.coulomb, bf16[2,384,3072]{2,1,0:T(8,128)(2,1)} %w_own.1, bf16[2,384,3072]{2,1,0:T(8,128)(2,1)} %collective-permute-done.4.w_other, bf16[2,256,384]{2,1,0:T(8,128)(2,1)S(1)} %pad_maximum_fusion.p01, ...), custom_call_target="tpu_custom_call" | custom-call | flops 4831838208 | bytes 9437184 | tf_op jit(solution)/shard_map/solve/pallas_call | solution.py:140
  67.3 13.9 %all_to_all.10.terms = f32[8,2,16,128]{3,2,1,0:T(8,128)} all-to-all(f32[8,2,16,128]{3,2,1,0:T(8,128)S(1)} %solve.1), channel_id=1, replica_groups=mesh['row'=32,'col'=8] {'col'}, dimensions={0} | all-to-all | bytes 262144 | tf_op jit(solution)/shard_map/all_to_all | solution.py:267
  81.2 1.8 %spread.1 = f32[32,16,128]{2,1,0:T(8,128)} custom-call(s32[64,64]{1,0:T(8,128)} %q_index.1, f32[8,2,16,128]{3,2,1,0:T(8,128)} %all_to_all.10.terms), custom_call_target="tpu_custom_call" | custom-call | tf_op jit(solution)/shard_map/spread/pallas_call | solution.py:197
  83.0 17.6 %all_to_all.11.arrived = f32[32,16,128]{2,1,0:T(8,128)} all-to-all(f32[32,16,128]{2,1,0:T(8,128)} %spread.1), channel_id=1, replica_groups=mesh['row'=32,'col'=8] {'row'}, dimensions={0} | all-to-all | bytes 524288 | tf_op jit(solution)/shard_map/all_to_all | solution.py:269
  100.6 1.7 %settle.1 = f32[32,128]{1,0:T(8,128)} custom-call(f32[32,16,128]{2,1,0:T(8,128)} %all_to_all.11.arrived), custom_call_target="tpu_custom_call" | custom-call | tf_op jit(solution)/shard_map/settle/pallas_call | solution.py:226
  (25 shorter events, 4.8 us)
Async XLA Ops:
  0.0 18.8 %collective-permute-start.4 = (bf16[2,384,3072]{2,1,0:T(8,128)(2,1)}, bf16[2,384,3072]{2,1,0:T(8,128)(2,1)}, u32[]{:S(2)}, u32[]{:S(2)}) collective-permute-start(bf16[2,384,3072]{2,1,0:T(8,128)(2,1)} %w_own.1), channel_id=1, source_target_pairs={{0,8},{8,0},{16,24},{24,16},{32,40},{40,32},{48,56},{56,48},{64,72... | collective-permute-start | bytes 14155784 | tf_op jit(solution)/shard_map/ppermute | solution.py:50
  3.2 9.9 %collective-permute-start.2 = (bf16[1,32,384]{2,1,0:T(8,128)(2,1)}, bf16[1,32,384]{2,1,0:T(8,128)(2,1)S(1)}, u32[]{:S(2)}, u32[]{:S(2)}) collective-permute-start(bf16[1,32,384]{2,1,0:T(8,128)(2,1)} %bitcast.14), channel_id=1, source_target_pairs={{0,96},{8,104},{16,112},{24,120},{32,0},{40,8},{48,16},{56,24},{64... | collective-permute-start | bytes 73736 | tf_op jit(solution)/shard_map/ppermute | solution.py:50
  7.5 6.9 %collective-permute-start.1 = (bf16[1,32,384]{2,1,0:T(8,128)(2,1)}, bf16[1,32,384]{2,1,0:T(8,128)(2,1)S(1)}, u32[]{:S(2)}, u32[]{:S(2)}) collective-permute-start(bf16[1,32,384]{2,1,0:T(8,128)(2,1)} %bitcast.15), channel_id=1, source_target_pairs={{0,64},{8,72},{16,80},{24,88},{32,96},{40,104},{48,112},{56,120},{... | collective-permute-start | bytes 73736 | tf_op jit(solution)/shard_map/ppermute | solution.py:50
  8.4 6.0 %collective-permute-start = (bf16[1,32,384]{2,1,0:T(8,128)(2,1)}, bf16[1,32,384]{2,1,0:T(8,128)(2,1)S(1)}, u32[]{:S(2)}, u32[]{:S(2)}) collective-permute-start(bf16[1,32,384]{2,1,0:T(8,128)(2,1)} %bitcast.16), channel_id=1, source_target_pairs={{0,32},{8,40},{16,48},{24,56},{32,64},{40,72},{48,80},{56,88},{64,... | collective-permute-start | bytes 73736 | tf_op jit(solution)/shard_map/ppermute | solution.py:50
  15.2 3.6 %collective-permute-start.3 = (bf16[4,32,384]{2,1,0:T(8,128)(2,1)S(1)}, bf16[4,32,384]{2,1,0:T(8,128)(2,1)S(1)}, u32[]{:S(2)}, u32[]{:S(2)}) collective-permute-start(bf16[4,32,384]{2,1,0:T(8,128)(2,1)S(1)} %pad_maximum_fusion.1), channel_id=1, source_target_pairs={{0,16},{8,24},{16,0},{24,8},{32,48},{40,56},{48,32},{56,40},{64,80... | collective-permute-start | bytes 294920 | tf_op jit(solution)/shard_map/ppermute | solution.py:50
  18.8 5.9 %collective-permute-start.5 = (bf16[1,256,384]{2,1,0:T(8,128)(2,1)S(1)}, bf16[1,256,384]{2,1,0:T(8,128)(2,1)S(1)}, u32[]{:S(2)}, u32[]{:S(2)}) collective-permute-start(bf16[1,256,384]{2,1,0:T(8,128)(2,1)S(1)} %bitcast.8), channel_id=1, source_target_pairs={{0,1},{8,136},{16,17},{24,152},{32,33},{40,168},{48,49},{56,184},{... | collective-permute-start | bytes 589832 | tf_op jit(solution)/shard_map/ppermute | solution.py:50
  20.2 7.8 %collective-permute-start.6 = (bf16[1,256,384]{2,1,0:T(8,128)(2,1)S(1)}, bf16[1,256,384]{2,1,0:T(8,128)(2,1)S(1)}, u32[]{:S(2)}, u32[]{:S(2)}) collective-permute-start(bf16[1,256,384]{2,1,0:T(8,128)(2,1)S(1)} %bitcast.9), channel_id=1, source_target_pairs={{0,2},{8,12},{16,18},{24,28},{32,34},{40,44},{48,50},{56,60},{64,6... | collective-permute-start | bytes 589832 | tf_op jit(solution)/shard_map/ppermute | solution.py:50
  22.8 5.2 %collective-permute-start.7 = (bf16[1,256,384]{2,1,0:T(8,128)(2,1)S(1)}, bf16[1,256,384]{2,1,0:T(8,128)(2,1)S(1)}, u32[]{:S(2)}, u32[]{:S(2)}) collective-permute-start(bf16[1,256,384]{2,1,0:T(8,128)(2,1)S(1)} %bitcast.10), channel_id=1, source_target_pairs={{0,3},{8,140},{16,19},{24,156},{32,35},{40,172},{48,51},{56,188},{... | collective-permute-start | bytes 589832 | tf_op jit(solution)/shard_map/ppermute | solution.py:50
  24.7 23.2 %collective-permute-start.8 = (bf16[2,256,384]{2,1,0:T(8,128)(2,1)S(1)}, bf16[2,256,384]{2,1,0:T(8,128)(2,1)S(1)}, u32[]{:S(2)}, u32[]{:S(2)}) collective-permute-start(bf16[2,256,384]{2,1,0:T(8,128)(2,1)S(1)} %pad_maximum_fusion.p01), channel_id=1, source_target_pairs={{0,128},{8,9},{16,144},{24,25},{32,160},{40,41},{48,176},{56,57},{... | collective-permute-start | bytes 1179656 | tf_op jit(solution)/shard_map/ppermute | solution.py:50
  28.0 19.9 %collective-permute-start.13 = (bf16[2,256,384]{2,1,0:T(8,128)(2,1)S(1)}, bf16[2,256,384]{2,1,0:T(8,128)(2,1)S(1)}, u32[]{:S(2)}, u32[]{:S(2)}) collective-permute-start(bf16[2,256,384]{2,1,0:T(8,128)(2,1)S(1)} %constant_dynamic-update-slice_fusion.5.p23), channel_id=1, source_target_pairs={{0,132},{8,11},{16,148},{24,27},{32,164},{40,43},{48,180},{56,59},... | collective-permute-start | bytes 1179656 | tf_op jit(solution)/shard_map/ppermute | solution.py:50
  30.9 14.4 %collective-permute-start.10 = (bf16[1,256,384]{2,1,0:T(8,128)(2,1)S(1)}, bf16[1,256,384]{2,1,0:T(8,128)(2,1)S(1)}, u32[]{:S(2)}, u32[]{:S(2)}) collective-permute-start(bf16[1,256,384]{2,1,0:T(8,128)(2,1)S(1)} %bitcast.12), channel_id=1, source_target_pairs={{0,136},{8,128},{16,152},{24,144},{32,168},{40,160},{48,184},{56,1... | collective-permute-start | bytes 589832 | tf_op jit(solution)/shard_map/ppermute | solution.py:50
  35.7 9.6 %collective-permute-start.9 = (bf16[1,256,384]{2,1,0:T(8,128)(2,1)S(1)}, bf16[1,256,384]{2,1,0:T(8,128)(2,1)S(1)}, u32[]{:S(2)}, u32[]{:S(2)}) collective-permute-start(bf16[1,256,384]{2,1,0:T(8,128)(2,1)S(1)} %bitcast.13), channel_id=1, source_target_pairs={{0,8},{8,0},{16,24},{24,16},{32,40},{40,32},{48,56},{56,48},{64,72... | collective-permute-start | bytes 589832 | tf_op jit(solution)/shard_map/ppermute | solution.py:50
  45.3 8.1 %collective-permute-start.11 = (bf16[2,256,384]{2,1,0:T(8,128)(2,1)S(1)}, bf16[2,256,384]{2,1,0:T(8,128)(2,1)S(1)}, u32[]{:S(2)}, u32[]{:S(2)}) collective-permute-start(bf16[2,256,384]{2,1,0:T(8,128)(2,1)S(1)} %constant_dynamic-update-slice_fusion.5.p23), channel_id=1, source_target_pairs={{0,128},{8,9},{16,144},{24,25},{32,160},{40,41},{48,176},{56,57},{... | collective-permute-start | bytes 1179656 | tf_op jit(solution)/shard_map/ppermute | solution.py:50
  45.3 8.1 %collective-permute-start.12 = (bf16[2,256,384]{2,1,0:T(8,128)(2,1)S(1)}, bf16[2,256,384]{2,1,0:T(8,128)(2,1)S(1)}, u32[]{:S(2)}, u32[]{:S(2)}) collective-permute-start(bf16[2,256,384]{2,1,0:T(8,128)(2,1)S(1)} %pad_maximum_fusion.p01), channel_id=1, source_target_pairs={{0,132},{8,11},{16,148},{24,27},{32,164},{40,43},{48,180},{56,59},... | collective-permute-start | bytes 1179656 | tf_op jit(solution)/shard_map/ppermute | solution.py:50
  47.9 9.5 %collective-permute-start.14 = (bf16[2,256,384]{2,1,0:T(8,128)(2,1)S(1)}, bf16[2,256,384]{2,1,0:T(8,128)(2,1)S(1)}, u32[]{:S(2)}, u32[]{:S(2)}) collective-permute-start(bf16[2,256,384]{2,1,0:T(8,128)(2,1)S(1)} %collective-permute-done.8.f0), channel_id=1, source_target_pairs={{0,128},{8,9},{16,144},{24,25},{32,160},{40,41},{48,176},{56,57},{... | collective-permute-start | bytes 1179656 | tf_op jit(solution)/shard_map/ppermute | solution.py:50
  47.9 9.5 %collective-permute-start.15 = (bf16[2,256,384]{2,1,0:T(8,128)(2,1)S(1)}, bf16[2,256,384]{2,1,0:T(8,128)(2,1)S(1)}, u32[]{:S(2)}, u32[]{:S(2)}) collective-permute-start(bf16[2,256,384]{2,1,0:T(8,128)(2,1)S(1)} %collective-permute-done.13.g1), channel_id=1, source_target_pairs={{0,132},{8,11},{16,148},{24,27},{32,164},{40,43},{48,180},{56,59},... | collective-permute-start | bytes 1179656 | tf_op jit(solution)/shard_map/ppermute | solution.py:50

commit v10 on v9

--- a/solution.py
+++ b/solution.py
@@ -10,7 +10,7 @@
 FIRST = (0, 1, 2, -1)
 SECOND = (0, 2, 1, -1)
 ZSHIFTS = (0, 2, 4, -2)
-VMEM = 48 * 1024 * 1024
+MIB = 1024 * 1024
 
 
 def device_index(x, y, z, c):
@@ -73,15 +73,38 @@
     return side * 4 + ((((z ^ side) - z_wanted) & 7) >> 1)
 
 
+def load_kernel(own, other, out, sems):
+    copies = [
+        pltpu.make_async_copy(w.at[q], out.at[2 * i + q], sems.at[2 * i + q])
+        for i, w in enumerate((own, other))
+        for q in range(2)
+    ]
+    for copy in copies:
+        copy.start()
+    for copy in copies:
+        copy.wait()
+
+
+def load(own, other):
+    _, share, whole = own.shape
+    return pl.pallas_call(
+        load_kernel,
+        in_specs=[pl.BlockSpec(memory_space=pl.ANY)] * 2,
+        out_specs=pl.BlockSpec(memory_space=pltpu.VMEM),
+        out_shape=jax.ShapeDtypeStruct((4, share, whole), own.dtype),
+        scratch_shapes=[pltpu.SemaphoreType.DMA((4,))],
+        compiler_params=pltpu.CompilerParams(vmem_limit_bytes=16 * MIB),
+        cost_estimate=pl.CostEstimate(
+            flops=0, bytes_accessed=8 * share * whole * 2, transcendentals=0
+        ),
+        name="load",
+    )(own, other)
+
+
 def solve_kernel(
-    partner, coulomb, w_own, w_other, p01, p23, f0, f1, g0, g1, ff0, gg1, near, far, out,
-    panel, left_rows, image, w, sems,
+    partner, coulomb, w, p01, p23, f0, f1, g0, g1, ff0, gg1, near, far, out,
+    panel, left_rows, image,
 ):
-    copies = [
-        pltpu.make_async_copy((w_own, w_other)[q // 2].at[q % 2], w.at[q], sems.at[q])
-        for q in range(4)
-    ]
-    copies[0].start()
     rows, share = p01.shape[1:]
     _, j, c, _, y_lo = where_am_i()
     starts = [pl.multiple_of(place_of(z) * 32, 32) for z in range(NZ)]
@@ -99,9 +122,6 @@
             to = pl.multiple_of((2 + low) * rows + z * 32, 32)
             left_rows[pl.ds(to, 32), :] = stack[0, pl.ds(starts[z], 32), :]
     for q in range(4):
-        copies[q].wait()
-        if q < 3:
-            copies[q + 1].start()
         image[q] = contract(w[q], panel[...]).astype(image.dtype)
 
     lane = lax.broadcasted_iota(jnp.int32, (16, 128), 1)
@@ -133,32 +153,28 @@
             out[2 * pair + 1, two] = jnp.where(lane < 64, pltpu.roll(even, 64, 1), odd)
 
 
-def solve(partner, coulomb, w_own, w_other, panels, near, far):
+def solve(partner, coulomb, w, panels, near, far):
     rows, share = panels[0].shape[1:]
-    whole = w_own.shape[2]
+    whole = w.shape[2]
     vmem = pl.BlockSpec(memory_space=pltpu.VMEM)
     return pl.pallas_call(
         solve_kernel,
-        in_specs=[pl.BlockSpec(memory_space=pltpu.SMEM), vmem]
-        + [pl.BlockSpec(memory_space=pl.ANY)] * 2
-        + [vmem] * 10,
+        in_specs=[pl.BlockSpec(memory_space=pltpu.SMEM)] + [vmem] * 12,
         out_specs=vmem,
         out_shape=jax.ShapeDtypeStruct((8, 2, 16, 128), jnp.float32),
         scratch_shapes=[
             pltpu.VMEM((2 * rows, whole), jnp.bfloat16),
             pltpu.VMEM((4 * rows, share), jnp.bfloat16),
             pltpu.VMEM((4, share, 2 * rows), jnp.bfloat16),
-            pltpu.VMEM((4, share, whole), jnp.bfloat16),
-            pltpu.SemaphoreType.DMA((4,)),
         ],
-        compiler_params=pltpu.CompilerParams(vmem_limit_bytes=VMEM),
+        compiler_params=pltpu.CompilerParams(vmem_limit_bytes=24 * MIB),
         cost_estimate=pl.CostEstimate(
             flops=2 * 4 * share * whole * 2 * rows,
             bytes_accessed=4 * share * whole * 2,
             transcendentals=0,
         ),
         name="solve",
-    )(partner, coulomb, w_own, w_other, *panels, near, far)
+    )(partner, coulomb, w, *panels, near, far)
 
 
 def spread_kernel(q_index, terms, out):
@@ -251,19 +267,21 @@
     near = send(stack, SWAP)
     far = send(stack, ACROSS)
     parts = [send(stack, first_plane(s)) for s in FIRST[1:]]
+    parts, near, far = lax.optimization_barrier((parts, near, far))
     p01 = jnp.concatenate([stack, parts[0]], axis=0)
     p23 = jnp.concatenate([parts[1], parts[2]], axis=0)
 
     f0 = send(p01, second_plane(1))
     g1 = send(p23, second_plane(-1))
-    late01, late23, near, far = lax.optimization_barrier((p01, p23, near, far))
-    g0 = send(late01, second_plane(-1))
-    f1 = send(late23, second_plane(1))
+    g0 = send(p01, second_plane(-1))
+    f1 = send(p23, second_plane(1))
     ff0 = send(f0, second_plane(1))
     gg1 = send(g1, second_plane(-1))
 
+    w_own, w_other, f0, g1 = lax.optimization_barrier((screened, w_other, f0, g1))
+    w = load(w_own, w_other)
     panels = (p01, p23, f0, f1, g0, g1, ff0, gg1)
-    terms = solve(partner, coulomb, screened, w_other, panels, near, far)
+    terms = solve(partner, coulomb, w, panels, near, far)
     terms = lax.all_to_all(terms, "col", split_axis=0, concat_axis=0, tiled=True)
     placed = spread(q_index, terms)
     arrived = lax.all_to_all(placed, "row", split_axis=0, concat_axis=0, tiled=True)

time: 103 us -> 93.7 us (0.910)
  waiting for transfers between devices: 21.6 us -> 12.6 us
  starting transfers between devices: 32.6 us -> 29.4 us
  local copies, waits for them, and re-layouts: 1.52 us -> 3.86 us
    ppermute x16, waiting for transfers between devices: 21.6 us -> 12.6 us  [send(): return lax.ppermute(value, AXES, perm)]
    ppermute x16, starting transfers between devices: 32.6 us -> 29.4 us  [send(): return lax.ppermute(value, AXES, perm)]
    pallas_call x0 -> x1, Pallas kernels: none -> 2.72 us  [load(): pl.pallas_call(load_kernel, in_specs=[pl.BlockSpec(memory_space=pl.ANY)]...]
    pallas_call x1, Pallas kernels: 9.82 us -> 7.21 us  [solve(): pl.pallas_call(solve_kernel, in_specs=[pl.BlockSpec(memory_space=pltpu.SM...]
    unnamed x5 -> x7, local copies, waits for them, and re-layouts: 0.79 us -> 3.13 us
  transfers between devices with their start and end apart: 16 -> 16, of which waited for: 7 -> 5; matrix products, arithmetic and copies ran while one was open for 3% -> 3% of each run, Pallas kernels for 0% -> 3%
where the time goes in v10:
time: 93.7 us; the launch traced here: 93.3 us
  blocking collectives  32.1 us (34%)
  starting transfers between devices  29.4 us (31%)
  Pallas kernels  13.4 us (14%)
  waiting for transfers between devices  12.6 us (13%)
  local copies, waits for them, and re-layouts  3.86 us (4%)
  other arithmetic  1.74 us (2%)
    ppermute x16, starting transfers between devices, send(): return lax.ppermute(value, AXES, perm)  29.4 us
    all_to_all x1, blocking collectives, local(): lax.all_to_all(placed, 'row', split_axis=0, concat_axis=0, tiled=True)  18.4 us
    all_to_all x1, blocking collectives, local(): lax.all_to_all(terms, 'col', split_axis=0, concat_axis=0, tiled=True)  13.7 us
    ppermute x16, waiting for transfers between devices, send(): return lax.ppermute(value, AXES, perm)  12.6 us
    pallas_call x1, Pallas kernels, solve(): pl.pallas_call(solve_kernel, in_specs=[pl.BlockSpec(memory_space=pltpu.SM...  7.21 us
    unnamed x7, local copies, waits for them, and re-layouts  3.13 us
    pallas_call x1, Pallas kernels, load(): pl.pallas_call(load_kernel, in_specs=[pl.BlockSpec(memory_space=pl.ANY)]...  2.72 us
  transfers between devices with their start and end apart: 16, of which 5 were waited for; matrix products, arithmetic and copies ran while one was open for 3% of the time, Pallas kernels for 3%

profile of v10, /device:TPU:1, one launch (start us, length us, event | category | flops | bytes accessed | tf_op | source)
XLA Modules:
  0.0 93.3 jit_solution(15607699689289795353)
XLA Ops:
  0.0 3.2 %collective-permute-start.4 = (bf16[2,384,3072]{2,1,0:T(8,128)(2,1)}, bf16[2,384,3072]{2,1,0:T(8,128)(2,1)}, u32[]{:S(2)}, u32[]{:S(2)}) collective-permute-start(bf16[2,384,3072]{2,1,0:T(8,128)(2,1)} %own), channel_id=1, source_target_pairs={{0,8},{8,0},{16,24},{24,16},{32,40},{40,32},{48,56},{56,48},{64,72... | collective-permute-start | bytes 14155784 | tf_op jit(solution)/shard_map/ppermute | solution.py:50
  3.2 4.3 %collective-permute-start.2 = (bf16[1,32,384]{2,1,0:T(8,128)(2,1)}, bf16[1,32,384]{2,1,0:T(8,128)(2,1)S(1)}, u32[]{:S(2)}, u32[]{:S(2)}) collective-permute-start(bf16[1,32,384]{2,1,0:T(8,128)(2,1)} %bitcast.14), channel_id=1, source_target_pairs={{0,96},{8,104},{16,112},{24,120},{32,0},{40,8},{48,16},{56,24},{64... | collective-permute-start | bytes 73736 | tf_op jit(solution)/shard_map/ppermute | solution.py:50
  7.5 0.9 collective-permute-start.1
  8.4 2.3 %collective-permute-start = (bf16[1,32,384]{2,1,0:T(8,128)(2,1)}, bf16[1,32,384]{2,1,0:T(8,128)(2,1)S(1)}, u32[]{:S(2)}, u32[]{:S(2)}) collective-permute-start(bf16[1,32,384]{2,1,0:T(8,128)(2,1)} %bitcast.16), channel_id=1, source_target_pairs={{0,32},{8,40},{16,48},{24,56},{32,64},{40,72},{48,80},{56,88},{64,... | collective-permute-start | bytes 73736 | tf_op jit(solution)/shard_map/ppermute | solution.py:50
  10.9 0.9 select_reduce_fusion.partner
  13.1 1.3 %collective-permute-done.1 = bf16[1,32,384]{2,1,0:T(8,128)(2,1)S(1)} collective-permute-done((bf16[1,32,384]{2,1,0:T(8,128)(2,1)}, bf16[1,32,384]{2,1,0:T(8,128)(2,1)S(1)}, u32[]{:S(2)}, u32[]{:S(2)}) %collective-permute-start.1) | collective-permute-done | bytes 24608 | tf_op jit(solution)/shard_map/ppermute | solution.py:50
  15.9 2.8 %collective-permute-done.3 = bf16[4,32,384]{2,1,0:T(8,128)(2,1)S(1)} collective-permute-done((bf16[4,32,384]{2,1,0:T(8,128)(2,1)S(1)}, bf16[4,32,384]{2,1,0:T(8,128)(2,1)S(1)}, u32[]{:S(2)}, u32[]{:S(2)}) %collective-permute-start.3) | collective-permute-done | bytes 98336 | tf_op jit(solution)/shard_map/ppermute | solution.py:50
  18.8 1.4 %collective-permute-start.5 = (bf16[1,256,384]{2,1,0:T(8,128)(2,1)S(1)}, bf16[1,256,384]{2,1,0:T(8,128)(2,1)S(1)}, u32[]{:S(2)}, u32[]{:S(2)}) collective-permute-start(bf16[1,256,384]{2,1,0:T(8,128)(2,1)S(1)} %bitcast.8), channel_id=1, source_target_pairs={{0,1},{8,136},{16,17},{24,152},{32,33},{40,168},{48,49},{56,184},{... | collective-permute-start | bytes 589832 | tf_op jit(solution)/shard_map/ppermute | solution.py:50
  20.2 2.6 %collective-permute-start.6 = (bf16[1,256,384]{2,1,0:T(8,128)(2,1)S(1)}, bf16[1,256,384]{2,1,0:T(8,128)(2,1)S(1)}, u32[]{:S(2)}, u32[]{:S(2)}) collective-permute-start(bf16[1,256,384]{2,1,0:T(8,128)(2,1)S(1)} %bitcast.9), channel_id=1, source_target_pairs={{0,2},{8,12},{16,18},{24,28},{32,34},{40,44},{48,50},{56,60},{64,6... | collective-permute-start | bytes 589832 | tf_op jit(solution)/shard_map/ppermute | solution.py:50
  22.8 1.1 %collective-permute-start.7 = (bf16[1,256,384]{2,1,0:T(8,128)(2,1)S(1)}, bf16[1,256,384]{2,1,0:T(8,128)(2,1)S(1)}, u32[]{:S(2)}, u32[]{:S(2)}) collective-permute-start(bf16[1,256,384]{2,1,0:T(8,128)(2,1)S(1)} %bitcast.10), channel_id=1, source_target_pairs={{0,3},{8,140},{16,19},{24,156},{32,35},{40,172},{48,51},{56,188},{... | collective-permute-start | bytes 589832 | tf_op jit(solution)/shard_map/ppermute | solution.py:50
  23.9 3.4 %collective-permute-start.8 = (bf16[1,256,384]{2,1,0:T(8,128)(2,1)S(1)}, bf16[1,256,384]{2,1,0:T(8,128)(2,1)S(1)}, u32[]{:S(2)}, u32[]{:S(2)}) collective-permute-start(bf16[1,256,384]{2,1,0:T(8,128)(2,1)S(1)} %bitcast.11), channel_id=1, source_target_pairs={{0,8},{8,0},{16,24},{24,16},{32,40},{40,32},{48,56},{56,48},{64,72... | collective-permute-start | bytes 589832 | tf_op jit(solution)/shard_map/ppermute | solution.py:50
  27.2 1.2 %collective-permute-start.9 = (bf16[1,256,384]{2,1,0:T(8,128)(2,1)S(1)}, bf16[1,256,384]{2,1,0:T(8,128)(2,1)S(1)}, u32[]{:S(2)}, u32[]{:S(2)}) collective-permute-start(bf16[1,256,384]{2,1,0:T(8,128)(2,1)S(1)} %bitcast.12), channel_id=1, source_target_pairs={{0,136},{8,128},{16,152},{24,144},{32,168},{40,160},{48,184},{56,1... | collective-permute-start | bytes 589832 | tf_op jit(solution)/shard_map/ppermute | solution.py:50
  28.5 5.3 %collective-permute-done.9.far = bf16[1,256,384]{2,1,0:T(8,128)(2,1)S(1)} collective-permute-done((bf16[1,256,384]{2,1,0:T(8,128)(2,1)S(1)}, bf16[1,256,384]{2,1,0:T(8,128)(2,1)S(1)}, u32[]{:S(2)}, u32[]{:S(2)}) %collective-permute-start.9) | collective-permute-done | bytes 196640 | tf_op jit(solution)/shard_map/ppermute | solution.py:50
  34.3 2.4 %collective-permute-start.11 = (bf16[2,256,384]{2,1,0:T(8,128)(2,1)S(1)}, bf16[2,256,384]{2,1,0:T(8,128)(2,1)S(1)}, u32[]{:S(2)}, u32[]{:S(2)}) collective-permute-start(bf16[2,256,384]{2,1,0:T(8,128)(2,1)S(1)} %constant_dynamic-update-slice_fusion.5.p23), channel_id=1, source_target_pairs={{0,132},{8,11},{16,148},{24,27},{32,164},{40,43},{48,180},{56,59},... | collective-permute-start | bytes 1179656 | tf_op jit(solution)/shard_map/ppermute | solution.py:50
  36.7 2.7 %collective-permute-start.13 = (bf16[2,256,384]{2,1,0:T(8,128)(2,1)S(1)}, bf16[2,256,384]{2,1,0:T(8,128)(2,1)S(1)}, u32[]{:S(2)}, u32[]{:S(2)}) collective-permute-start(bf16[2,256,384]{2,1,0:T(8,128)(2,1)S(1)} %pad_maximum_fusion.p01), channel_id=1, source_target_pairs={{0,132},{8,11},{16,148},{24,27},{32,164},{40,43},{48,180},{56,59},... | collective-permute-start | bytes 1179656 | tf_op jit(solution)/shard_map/ppermute | solution.py:50
  39.4 2.6 %collective-permute-done.10.f0 = bf16[2,256,384]{2,1,0:T(8,128)(2,1)S(1)} collective-permute-done((bf16[2,256,384]{2,1,0:T(8,128)(2,1)S(1)}, bf16[2,256,384]{2,1,0:T(8,128)(2,1)S(1)}, u32[]{:S(2)}, u32[]{:S(2)}) %collective-permute-start.10) | collective-permute-done | bytes 393248 | tf_op jit(solution)/shard_map/ppermute | solution.py:50
  42.0 2.8 %collective-permute-start.15 = (bf16[2,256,384]{2,1,0:T(8,128)(2,1)S(1)}, bf16[2,256,384]{2,1,0:T(8,128)(2,1)S(1)}, u32[]{:S(2)}, u32[]{:S(2)}) collective-permute-start(bf16[2,256,384]{2,1,0:T(8,128)(2,1)S(1)} %collective-permute-done.11.g1), channel_id=1, source_target_pairs={{0,132},{8,11},{16,148},{24,27},{32,164},{40,43},{48,180},{56,59},... | collective-permute-start | bytes 1179656 | tf_op jit(solution)/shard_map/ppermute | solution.py:50
  44.8 2.3 %copy-done = bf16[2,384,3072]{2,1,0:T(8,128)(2,1)S(1)} copy-done((bf16[2,384,3072]{2,1,0:T(8,128)(2,1)S(1)}, bf16[2,384,3072]{2,1,0:T(8,128)(2,1)}, u32[]{:S(2)}) %copy-start) | copy-done | bytes 4718616
  47.2 2.7 %load.1.w = bf16[4,384,3072]{2,1,0:T(8,128)(2,1)S(1)} custom-call(bf16[2,384,3072]{2,1,0:T(8,128)(2,1)S(1)} %copy-done, bf16[2,384,3072]{2,1,0:T(8,128)(2,1)} %collective-permute-done.4.other), custom_call_target="tpu_custom_call" | custom-call | bytes 18874368 | tf_op jit(solution)/shard_map/load/pallas_call | solution.py:90
  50.5 7.2 %solve.1 = f32[8,2,16,128]{3,2,1,0:T(8,128)S(1)} custom-call(s32[4,64]{1,0:T(4,128)S(1)} %select_reduce_fusion.partner, f32[1,384]{1,0:T(1,128)S(1)} %reshape.12.coulomb, bf16[4,384,3072]{2,1,0:T(8,128)(2,1)S(1)} %load.1.w, bf16[2,256,384]{2,1,0:T(8,128)(2,1)S(1)} %pad_maximum_fusion.p01, bf16[2,256,384]{2,1,0:T(8,128)(2,1)S(1)} %constant_dynamic-update-slice_fusion.5.p23, ...), custom_call_target="tpu_custom_call" | custom-call | flops 4831838208 | bytes 9437184 | tf_op jit(solution)/shard_map/solve/pallas_call | solution.py:160
  57.7 13.7 %all_to_all.10.terms = f32[8,2,16,128]{3,2,1,0:T(8,128)} all-to-all(f32[8,2,16,128]{3,2,1,0:T(8,128)S(1)} %solve.1), channel_id=1, replica_groups=mesh['row'=32,'col'=8] {'col'}, dimensions={0} | all-to-all | bytes 262144 | tf_op jit(solution)/shard_map/all_to_all | solution.py:285
  71.4 1.8 %spread.1 = f32[32,16,128]{2,1,0:T(8,128)} custom-call(s32[64,64]{1,0:T(8,128)} %q_index.1, f32[8,2,16,128]{3,2,1,0:T(8,128)} %all_to_all.10.terms), custom_call_target="tpu_custom_call" | custom-call | tf_op jit(solution)/shard_map/spread/pallas_call | solution.py:213
  73.2 18.4 %all_to_all.11.arrived = f32[32,16,128]{2,1,0:T(8,128)} all-to-all(f32[32,16,128]{2,1,0:T(8,128)} %spread.1), channel_id=1, replica_groups=mesh['row'=32,'col'=8] {'row'}, dimensions={0} | all-to-all | bytes 524288 | tf_op jit(solution)/shard_map/all_to_all | solution.py:287
  91.6 1.7 %settle.1 = f32[32,128]{1,0:T(8,128)} custom-call(f32[32,16,128]{2,1,0:T(8,128)} %all_to_all.11.arrived), custom_call_target="tpu_custom_call" | custom-call | tf_op jit(solution)/shard_map/settle/pallas_call | solution.py:242
  (28 shorter events, 4.0 us)
Async XLA Ops:
  0.0 18.8 %collective-permute-start.4 = (bf16[2,384,3072]{2,1,0:T(8,128)(2,1)}, bf16[2,384,3072]{2,1,0:T(8,128)(2,1)}, u32[]{:S(2)}, u32[]{:S(2)}) collective-permute-start(bf16[2,384,3072]{2,1,0:T(8,128)(2,1)} %own), channel_id=1, source_target_pairs={{0,8},{8,0},{16,24},{24,16},{32,40},{40,32},{48,56},{56,48},{64,72... | collective-permute-start | bytes 14155784 | tf_op jit(solution)/shard_map/ppermute | solution.py:50
  3.2 9.9 %collective-permute-start.2 = (bf16[1,32,384]{2,1,0:T(8,128)(2,1)}, bf16[1,32,384]{2,1,0:T(8,128)(2,1)S(1)}, u32[]{:S(2)}, u32[]{:S(2)}) collective-permute-start(bf16[1,32,384]{2,1,0:T(8,128)(2,1)} %bitcast.14), channel_id=1, source_target_pairs={{0,96},{8,104},{16,112},{24,120},{32,0},{40,8},{48,16},{56,24},{64... | collective-permute-start | bytes 73736 | tf_op jit(solution)/shard_map/ppermute | solution.py:50
  7.5 6.9 %collective-permute-start.1 = (bf16[1,32,384]{2,1,0:T(8,128)(2,1)}, bf16[1,32,384]{2,1,0:T(8,128)(2,1)S(1)}, u32[]{:S(2)}, u32[]{:S(2)}) collective-permute-start(bf16[1,32,384]{2,1,0:T(8,128)(2,1)} %bitcast.15), channel_id=1, source_target_pairs={{0,64},{8,72},{16,80},{24,88},{32,96},{40,104},{48,112},{56,120},{... | collective-permute-start | bytes 73736 | tf_op jit(solution)/shard_map/ppermute | solution.py:50
  8.4 6.0 %collective-permute-start = (bf16[1,32,384]{2,1,0:T(8,128)(2,1)}, bf16[1,32,384]{2,1,0:T(8,128)(2,1)S(1)}, u32[]{:S(2)}, u32[]{:S(2)}) collective-permute-start(bf16[1,32,384]{2,1,0:T(8,128)(2,1)} %bitcast.16), channel_id=1, source_target_pairs={{0,32},{8,40},{16,48},{24,56},{32,64},{40,72},{48,80},{56,88},{64,... | collective-permute-start | bytes 73736 | tf_op jit(solution)/shard_map/ppermute | solution.py:50
  15.2 3.6 %collective-permute-start.3 = (bf16[4,32,384]{2,1,0:T(8,128)(2,1)S(1)}, bf16[4,32,384]{2,1,0:T(8,128)(2,1)S(1)}, u32[]{:S(2)}, u32[]{:S(2)}) collective-permute-start(bf16[4,32,384]{2,1,0:T(8,128)(2,1)S(1)} %pad_maximum_fusion.1), channel_id=1, source_target_pairs={{0,16},{8,24},{16,0},{24,8},{32,48},{40,56},{48,32},{56,40},{64,80... | collective-permute-start | bytes 294920 | tf_op jit(solution)/shard_map/ppermute | solution.py:50
  18.8 9.6 %collective-permute-start.5 = (bf16[1,256,384]{2,1,0:T(8,128)(2,1)S(1)}, bf16[1,256,384]{2,1,0:T(8,128)(2,1)S(1)}, u32[]{:S(2)}, u32[]{:S(2)}) collective-permute-start(bf16[1,256,384]{2,1,0:T(8,128)(2,1)S(1)} %bitcast.8), channel_id=1, source_target_pairs={{0,1},{8,136},{16,17},{24,152},{32,33},{40,168},{48,49},{56,184},{... | collective-permute-start | bytes 589832 | tf_op jit(solution)/shard_map/ppermute | solution.py:50
  20.2 8.3 %collective-permute-start.6 = (bf16[1,256,384]{2,1,0:T(8,128)(2,1)S(1)}, bf16[1,256,384]{2,1,0:T(8,128)(2,1)S(1)}, u32[]{:S(2)}, u32[]{:S(2)}) collective-permute-start(bf16[1,256,384]{2,1,0:T(8,128)(2,1)S(1)} %bitcast.9), channel_id=1, source_target_pairs={{0,2},{8,12},{16,18},{24,28},{32,34},{40,44},{48,50},{56,60},{64,6... | collective-permute-start | bytes 589832 | tf_op jit(solution)/shard_map/ppermute | solution.py:50
  22.8 5.7 %collective-permute-start.7 = (bf16[1,256,384]{2,1,0:T(8,128)(2,1)S(1)}, bf16[1,256,384]{2,1,0:T(8,128)(2,1)S(1)}, u32[]{:S(2)}, u32[]{:S(2)}) collective-permute-start(bf16[1,256,384]{2,1,0:T(8,128)(2,1)S(1)} %bitcast.10), channel_id=1, source_target_pairs={{0,3},{8,140},{16,19},{24,156},{32,35},{40,172},{48,51},{56,188},{... | collective-permute-start | bytes 589832 | tf_op jit(solution)/shard_map/ppermute | solution.py:50
  23.9 4.6 %collective-permute-start.8 = (bf16[1,256,384]{2,1,0:T(8,128)(2,1)S(1)}, bf16[1,256,384]{2,1,0:T(8,128)(2,1)S(1)}, u32[]{:S(2)}, u32[]{:S(2)}) collective-permute-start(bf16[1,256,384]{2,1,0:T(8,128)(2,1)S(1)} %bitcast.11), channel_id=1, source_target_pairs={{0,8},{8,0},{16,24},{24,16},{32,40},{40,32},{48,56},{56,48},{64,72... | collective-permute-start | bytes 589832 | tf_op jit(solution)/shard_map/ppermute | solution.py:50
  27.2 6.5 %collective-permute-start.9 = (bf16[1,256,384]{2,1,0:T(8,128)(2,1)S(1)}, bf16[1,256,384]{2,1,0:T(8,128)(2,1)S(1)}, u32[]{:S(2)}, u32[]{:S(2)}) collective-permute-start(bf16[1,256,384]{2,1,0:T(8,128)(2,1)S(1)} %bitcast.12), channel_id=1, source_target_pairs={{0,136},{8,128},{16,152},{24,144},{32,168},{40,160},{48,184},{56,1... | collective-permute-start | bytes 589832 | tf_op jit(solution)/shard_map/ppermute | solution.py:50
  33.8 8.2 %collective-permute-start.10 = (bf16[2,256,384]{2,1,0:T(8,128)(2,1)S(1)}, bf16[2,256,384]{2,1,0:T(8,128)(2,1)S(1)}, u32[]{:S(2)}, u32[]{:S(2)}) collective-permute-start(bf16[2,256,384]{2,1,0:T(8,128)(2,1)S(1)} %pad_maximum_fusion.p01), channel_id=1, source_target_pairs={{0,128},{8,9},{16,144},{24,25},{32,160},{40,41},{48,176},{56,57},{... | collective-permute-start | bytes 1179656 | tf_op jit(solution)/shard_map/ppermute | solution.py:50
  34.3 7.8 %collective-permute-start.11 = (bf16[2,256,384]{2,1,0:T(8,128)(2,1)S(1)}, bf16[2,256,384]{2,1,0:T(8,128)(2,1)S(1)}, u32[]{:S(2)}, u32[]{:S(2)}) collective-permute-start(bf16[2,256,384]{2,1,0:T(8,128)(2,1)S(1)} %constant_dynamic-update-slice_fusion.5.p23), channel_id=1, source_target_pairs={{0,132},{8,11},{16,148},{24,27},{32,164},{40,43},{48,180},{56,59},... | collective-permute-start | bytes 1179656 | tf_op jit(solution)/shard_map/ppermute | solution.py:50
  36.7 13.2 %collective-permute-start.12 = (bf16[2,256,384]{2,1,0:T(8,128)(2,1)S(1)}, bf16[2,256,384]{2,1,0:T(8,128)(2,1)S(1)}, u32[]{:S(2)}, u32[]{:S(2)}) collective-permute-start(bf16[2,256,384]{2,1,0:T(8,128)(2,1)S(1)} %constant_dynamic-update-slice_fusion.5.p23), channel_id=1, source_target_pairs={{0,128},{8,9},{16,144},{24,25},{32,160},{40,41},{48,176},{56,57},{... | collective-permute-start | bytes 1179656 | tf_op jit(solution)/shard_map/ppermute | solution.py:50
  36.7 13.2 %collective-permute-start.13 = (bf16[2,256,384]{2,1,0:T(8,128)(2,1)S(1)}, bf16[2,256,384]{2,1,0:T(8,128)(2,1)S(1)}, u32[]{:S(2)}, u32[]{:S(2)}) collective-permute-start(bf16[2,256,384]{2,1,0:T(8,128)(2,1)S(1)} %pad_maximum_fusion.p01), channel_id=1, source_target_pairs={{0,132},{8,11},{16,148},{24,27},{32,164},{40,43},{48,180},{56,59},... | collective-permute-start | bytes 1179656 | tf_op jit(solution)/shard_map/ppermute | solution.py:50
  42.0 8.4 %collective-permute-start.14 = (bf16[2,256,384]{2,1,0:T(8,128)(2,1)S(1)}, bf16[2,256,384]{2,1,0:T(8,128)(2,1)S(1)}, u32[]{:S(2)}, u32[]{:S(2)}) collective-permute-start(bf16[2,256,384]{2,1,0:T(8,128)(2,1)S(1)} %collective-permute-done.10.f0), channel_id=1, source_target_pairs={{0,128},{8,9},{16,144},{24,25},{32,160},{40,41},{48,176},{56,57},{... | collective-permute-start | bytes 1179656 | tf_op jit(solution)/shard_map/ppermute | solution.py:50
  42.0 8.4 %collective-permute-start.15 = (bf16[2,256,384]{2,1,0:T(8,128)(2,1)S(1)}, bf16[2,256,384]{2,1,0:T(8,128)(2,1)S(1)}, u32[]{:S(2)}, u32[]{:S(2)}) collective-permute-start(bf16[2,256,384]{2,1,0:T(8,128)(2,1)S(1)} %collective-permute-done.11.g1), channel_id=1, source_target_pairs={{0,132},{8,11},{16,148},{24,27},{32,164},{40,43},{48,180},{56,59},... | collective-permute-start | bytes 1179656 | tf_op jit(solution)/shard_map/ppermute | solution.py:50
  44.8 2.3 %copy-start = (bf16[2,384,3072]{2,1,0:T(8,128)(2,1)S(1)}, bf16[2,384,3072]{2,1,0:T(8,128)(2,1)}, u32[]{:S(2)}) copy-start(bf16[2,384,3072]{2,1,0:T(8,128)(2,1)} %own) | copy-start | bytes 14155780

commit v11 on v10

--- a/solution.py
+++ b/solution.py
@@ -214,7 +214,8 @@
         spread_kernel,
         in_specs=[vmem, vmem],
         out_specs=vmem,
-        out_shape=jax.ShapeDtypeStruct((32, 16, 128), jnp.float32),
+        out_shape=jax.ShapeDtypeStruct((32, 16, 128), jnp.bfloat16),
+        compiler_params=pltpu.CompilerParams(vmem_limit_bytes=4 * MIB),
         name="spread",
     )(q_index, terms)
 
@@ -244,6 +245,7 @@
         in_specs=[vmem],
         out_specs=vmem,
         out_shape=jax.ShapeDtypeStruct((32, 128), jnp.float32),
+        compiler_params=pltpu.CompilerParams(vmem_limit_bytes=4 * MIB),
         name="settle",
     )(arrived)
 

time: 93.7 us -> 87.9 us (0.938)
  blocking collectives: 32.1 us -> 28.8 us
  Pallas kernels: 13.4 us -> 10.9 us
    all_to_all x1, blocking collectives: 18.4 us -> 15.2 us  [local(): lax.all_to_all(placed, 'row', split_axis=0, concat_axis=0, tiled=True)]
    pallas_call x1, Pallas kernels: 1.84 us -> 0.21 us  [spread(): pl.pallas_call(spread_kernel, in_specs=[vmem, vmem], out_specs=vmem, out_...]
    pallas_call x1, Pallas kernels: 1.65 us -> 0.71 us  [settle(): pl.pallas_call(settle_kernel, in_specs=[vmem], out_specs=vmem, out_shape=...]
    unnamed x7 -> x9, local copies, waits for them, and re-layouts: 3.13 us -> 3.13 us
  transfers between devices with their start and end apart: 16 -> 16, of which waited for: 5 -> 5; matrix products, arithmetic and copies ran while one was open for 3% -> 4% of each run, Pallas kernels for 3% -> 3%
where the time goes in v11:
time: 87.9 us; the launch traced here: 87.4 us
  starting transfers between devices  29.4 us (33%)
  blocking collectives  28.8 us (33%)
  waiting for transfers between devices  12.6 us (14%)
  Pallas kernels  10.9 us (12%)
  local copies, waits for them, and re-layouts  3.86 us (4%)
  other arithmetic  1.74 us (2%)
    ppermute x16, starting transfers between devices, send(): return lax.ppermute(value, AXES, perm)  29.4 us
    all_to_all x1, blocking collectives, local(): lax.all_to_all(placed, 'row', split_axis=0, concat_axis=0, tiled=True)  15.2 us
    all_to_all x1, blocking collectives, local(): lax.all_to_all(terms, 'col', split_axis=0, concat_axis=0, tiled=True)  13.6 us
    ppermute x16, waiting for transfers between devices, send(): return lax.ppermute(value, AXES, perm)  12.6 us
    pallas_call x1, Pallas kernels, solve(): pl.pallas_call(solve_kernel, in_specs=[pl.BlockSpec(memory_space=pltpu.SM...  7.25 us
    unnamed x9, local copies, waits for them, and re-layouts  3.13 us
    pallas_call x1, Pallas kernels, load(): pl.pallas_call(load_kernel, in_specs=[pl.BlockSpec(memory_space=pl.ANY)]...  2.72 us
  transfers between devices with their start and end apart: 16, of which 5 were waited for; matrix products, arithmetic and copies ran while one was open for 4% of the time, Pallas kernels for 3%

profile of v11, /device:TPU:1, one launch (start us, length us, event | category | flops | bytes accessed | tf_op | source)
XLA Modules:
  0.0 87.4 jit_solution(9300609654214683498)
XLA Ops:
  0.0 3.2 %collective-permute-start.4 = (bf16[2,384,3072]{2,1,0:T(8,128)(2,1)}, bf16[2,384,3072]{2,1,0:T(8,128)(2,1)}, u32[]{:S(2)}, u32[]{:S(2)}) collective-permute-start(bf16[2,384,3072]{2,1,0:T(8,128)(2,1)} %own), channel_id=1, source_target_pairs={{0,8},{8,0},{16,24},{24,16},{32,40},{40,32},{48,56},{56,48},{64,72... | collective-permute-start | bytes 14155784 | tf_op jit(solution)/shard_map/ppermute | solution.py:50
  3.2 4.3 %collective-permute-start.2 = (bf16[1,32,384]{2,1,0:T(8,128)(2,1)}, bf16[1,32,384]{2,1,0:T(8,128)(2,1)S(1)}, u32[]{:S(2)}, u32[]{:S(2)}) collective-permute-start(bf16[1,32,384]{2,1,0:T(8,128)(2,1)} %bitcast.14), channel_id=1, source_target_pairs={{0,96},{8,104},{16,112},{24,120},{32,0},{40,8},{48,16},{56,24},{64... | collective-permute-start | bytes 73736 | tf_op jit(solution)/shard_map/ppermute | solution.py:50
  7.5 0.9 %collective-permute-start.1 = (bf16[1,32,384]{2,1,0:T(8,128)(2,1)}, bf16[1,32,384]{2,1,0:T(8,128)(2,1)S(1)}, u32[]{:S(2)}, u32[]{:S(2)}) collective-permute-start(bf16[1,32,384]{2,1,0:T(8,128)(2,1)} %bitcast.15), channel_id=1, source_target_pairs={{0,64},{8,72},{16,80},{24,88},{32,96},{40,104},{48,112},{56,120},{... | collective-permute-start | bytes 73736 | tf_op jit(solution)/shard_map/ppermute | solution.py:50
  8.4 2.3 %collective-permute-start = (bf16[1,32,384]{2,1,0:T(8,128)(2,1)}, bf16[1,32,384]{2,1,0:T(8,128)(2,1)S(1)}, u32[]{:S(2)}, u32[]{:S(2)}) collective-permute-start(bf16[1,32,384]{2,1,0:T(8,128)(2,1)} %bitcast.16), channel_id=1, source_target_pairs={{0,32},{8,40},{16,48},{24,56},{32,64},{40,72},{48,80},{56,88},{64,... | collective-permute-start | bytes 73736 | tf_op jit(solution)/shard_map/ppermute | solution.py:50
  10.9 0.9 select_reduce_fusion.partner
  11.7 0.7 constant_dynamic-update-slice_fusion.4
  13.1 1.3 %collective-permute-done.1 = bf16[1,32,384]{2,1,0:T(8,128)(2,1)S(1)} collective-permute-done((bf16[1,32,384]{2,1,0:T(8,128)(2,1)}, bf16[1,32,384]{2,1,0:T(8,128)(2,1)S(1)}, u32[]{:S(2)}, u32[]{:S(2)}) %collective-permute-start.1) | collective-permute-done | bytes 24608 | tf_op jit(solution)/shard_map/ppermute | solution.py:50
  14.5 0.8 pad_maximum_fusion.1
  15.9 2.8 %collective-permute-done.3 = bf16[4,32,384]{2,1,0:T(8,128)(2,1)S(1)} collective-permute-done((bf16[4,32,384]{2,1,0:T(8,128)(2,1)S(1)}, bf16[4,32,384]{2,1,0:T(8,128)(2,1)S(1)}, u32[]{:S(2)}, u32[]{:S(2)}) %collective-permute-start.3) | collective-permute-done | bytes 98336 | tf_op jit(solution)/shard_map/ppermute | solution.py:50
  18.8 1.4 %collective-permute-start.5 = (bf16[1,256,384]{2,1,0:T(8,128)(2,1)S(1)}, bf16[1,256,384]{2,1,0:T(8,128)(2,1)S(1)}, u32[]{:S(2)}, u32[]{:S(2)}) collective-permute-start(bf16[1,256,384]{2,1,0:T(8,128)(2,1)S(1)} %bitcast.8), channel_id=1, source_target_pairs={{0,1},{8,136},{16,17},{24,152},{32,33},{40,168},{48,49},{56,184},{... | collective-permute-start | bytes 589832 | tf_op jit(solution)/shard_map/ppermute | solution.py:50
  20.2 2.6 %collective-permute-start.6 = (bf16[1,256,384]{2,1,0:T(8,128)(2,1)S(1)}, bf16[1,256,384]{2,1,0:T(8,128)(2,1)S(1)}, u32[]{:S(2)}, u32[]{:S(2)}) collective-permute-start(bf16[1,256,384]{2,1,0:T(8,128)(2,1)S(1)} %bitcast.9), channel_id=1, source_target_pairs={{0,2},{8,12},{16,18},{24,28},{32,34},{40,44},{48,50},{56,60},{64,6... | collective-permute-start | bytes 589832 | tf_op jit(solution)/shard_map/ppermute | solution.py:50
  22.8 1.1 %collective-permute-start.7 = (bf16[1,256,384]{2,1,0:T(8,128)(2,1)S(1)}, bf16[1,256,384]{2,1,0:T(8,128)(2,1)S(1)}, u32[]{:S(2)}, u32[]{:S(2)}) collective-permute-start(bf16[1,256,384]{2,1,0:T(8,128)(2,1)S(1)} %bitcast.10), channel_id=1, source_target_pairs={{0,3},{8,140},{16,19},{24,156},{32,35},{40,172},{48,51},{56,188},{... | collective-permute-start | bytes 589832 | tf_op jit(solution)/shard_map/ppermute | solution.py:50
  23.9 3.4 %collective-permute-start.8 = (bf16[1,256,384]{2,1,0:T(8,128)(2,1)S(1)}, bf16[1,256,384]{2,1,0:T(8,128)(2,1)S(1)}, u32[]{:S(2)}, u32[]{:S(2)}) collective-permute-start(bf16[1,256,384]{2,1,0:T(8,128)(2,1)S(1)} %bitcast.11), channel_id=1, source_target_pairs={{0,8},{8,0},{16,24},{24,16},{32,40},{40,32},{48,56},{56,48},{64,72... | collective-permute-start | bytes 589832 | tf_op jit(solution)/shard_map/ppermute | solution.py:50
  27.2 1.2 %collective-permute-start.9 = (bf16[1,256,384]{2,1,0:T(8,128)(2,1)S(1)}, bf16[1,256,384]{2,1,0:T(8,128)(2,1)S(1)}, u32[]{:S(2)}, u32[]{:S(2)}) collective-permute-start(bf16[1,256,384]{2,1,0:T(8,128)(2,1)S(1)} %bitcast.12), channel_id=1, source_target_pairs={{0,136},{8,128},{16,152},{24,144},{32,168},{40,160},{48,184},{56,1... | collective-permute-start | bytes 589832 | tf_op jit(solution)/shard_map/ppermute | solution.py:50
  28.5 5.3 %collective-permute-done.9.far = bf16[1,256,384]{2,1,0:T(8,128)(2,1)S(1)} collective-permute-done((bf16[1,256,384]{2,1,0:T(8,128)(2,1)S(1)}, bf16[1,256,384]{2,1,0:T(8,128)(2,1)S(1)}, u32[]{:S(2)}, u32[]{:S(2)}) %collective-permute-start.9) | collective-permute-done | bytes 196640 | tf_op jit(solution)/shard_map/ppermute | solution.py:50
  34.3 2.4 %collective-permute-start.11 = (bf16[2,256,384]{2,1,0:T(8,128)(2,1)S(1)}, bf16[2,256,384]{2,1,0:T(8,128)(2,1)S(1)}, u32[]{:S(2)}, u32[]{:S(2)}) collective-permute-start(bf16[2,256,384]{2,1,0:T(8,128)(2,1)S(1)} %constant_dynamic-update-slice_fusion.5.p23), channel_id=1, source_target_pairs={{0,132},{8,11},{16,148},{24,27},{32,164},{40,43},{48,180},{56,59},... | collective-permute-start | bytes 1179656 | tf_op jit(solution)/shard_map/ppermute | solution.py:50
  36.7 2.7 %collective-permute-start.13 = (bf16[2,256,384]{2,1,0:T(8,128)(2,1)S(1)}, bf16[2,256,384]{2,1,0:T(8,128)(2,1)S(1)}, u32[]{:S(2)}, u32[]{:S(2)}) collective-permute-start(bf16[2,256,384]{2,1,0:T(8,128)(2,1)S(1)} %pad_maximum_fusion.p01), channel_id=1, source_target_pairs={{0,132},{8,11},{16,148},{24,27},{32,164},{40,43},{48,180},{56,59},... | collective-permute-start | bytes 1179656 | tf_op jit(solution)/shard_map/ppermute | solution.py:50
  39.4 2.6 %collective-permute-done.10.f0 = bf16[2,256,384]{2,1,0:T(8,128)(2,1)S(1)} collective-permute-done((bf16[2,256,384]{2,1,0:T(8,128)(2,1)S(1)}, bf16[2,256,384]{2,1,0:T(8,128)(2,1)S(1)}, u32[]{:S(2)}, u32[]{:S(2)}) %collective-permute-start.10) | collective-permute-done | bytes 393248 | tf_op jit(solution)/shard_map/ppermute | solution.py:50
  42.0 2.8 %collective-permute-start.15 = (bf16[2,256,384]{2,1,0:T(8,128)(2,1)S(1)}, bf16[2,256,384]{2,1,0:T(8,128)(2,1)S(1)}, u32[]{:S(2)}, u32[]{:S(2)}) collective-permute-start(bf16[2,256,384]{2,1,0:T(8,128)(2,1)S(1)} %collective-permute-done.11.g1), channel_id=1, source_target_pairs={{0,132},{8,11},{16,148},{24,27},{32,164},{40,43},{48,180},{56,59},... | collective-permute-start | bytes 1179656 | tf_op jit(solution)/shard_map/ppermute | solution.py:50
  44.8 2.3 %copy-done = bf16[2,384,3072]{2,1,0:T(8,128)(2,1)S(1)} copy-done((bf16[2,384,3072]{2,1,0:T(8,128)(2,1)S(1)}, bf16[2,384,3072]{2,1,0:T(8,128)(2,1)}, u32[]{:S(2)}) %copy-start) | copy-done | bytes 4718616
  47.2 2.7 %load.1.w = bf16[4,384,3072]{2,1,0:T(8,128)(2,1)S(1)} custom-call(bf16[2,384,3072]{2,1,0:T(8,128)(2,1)S(1)} %copy-done, bf16[2,384,3072]{2,1,0:T(8,128)(2,1)} %collective-permute-done.4.other), custom_call_target="tpu_custom_call" | custom-call | bytes 18874368 | tf_op jit(solution)/shard_map/load/pallas_call | solution.py:90
  50.5 7.3 %solve.1 = f32[8,2,16,128]{3,2,1,0:T(8,128)S(1)} custom-call(s32[4,64]{1,0:T(4,128)S(1)} %select_reduce_fusion.partner, f32[1,384]{1,0:T(1,128)S(1)} %reshape.12.coulomb, bf16[4,384,3072]{2,1,0:T(8,128)(2,1)S(1)} %load.1.w, bf16[2,256,384]{2,1,0:T(8,128)(2,1)S(1)} %pad_maximum_fusion.p01, bf16[2,256,384]{2,1,0:T(8,128)(2,1)S(1)} %constant_dynamic-update-slice_fusion.5.p23, ...), custom_call_target="tpu_custom_call" | custom-call | flops 4831838208 | bytes 9437184 | tf_op jit(solution)/shard_map/solve/pallas_call | solution.py:160
  57.7 13.6 %all_to_all.10.terms = f32[8,2,16,128]{3,2,1,0:T(8,128)S(1)} all-to-all(f32[8,2,16,128]{3,2,1,0:T(8,128)S(1)} %solve.1), channel_id=1, replica_groups=mesh['row'=32,'col'=8] {'col'}, dimensions={0} | all-to-all | bytes 262144 | tf_op jit(solution)/shard_map/all_to_all | solution.py:287
  71.5 15.2 %all_to_all.11.arrived = bf16[32,16,128]{2,1,0:T(8,128)(2,1)S(1)} all-to-all(bf16[32,16,128]{2,1,0:T(8,128)(2,1)S(1)} %spread.1), channel_id=1, replica_groups=mesh['row'=32,'col'=8] {'row'}, dimensions={0} | all-to-all | bytes 262144 | tf_op jit(solution)/shard_map/all_to_all | solution.py:289
  (30 shorter events, 3.5 us)
Async XLA Ops:
  0.0 18.8 %collective-permute-start.4 = (bf16[2,384,3072]{2,1,0:T(8,128)(2,1)}, bf16[2,384,3072]{2,1,0:T(8,128)(2,1)}, u32[]{:S(2)}, u32[]{:S(2)}) collective-permute-start(bf16[2,384,3072]{2,1,0:T(8,128)(2,1)} %own), channel_id=1, source_target_pairs={{0,8},{8,0},{16,24},{24,16},{32,40},{40,32},{48,56},{56,48},{64,72... | collective-permute-start | bytes 14155784 | tf_op jit(solution)/shard_map/ppermute | solution.py:50
  3.2 9.9 %collective-permute-start.2 = (bf16[1,32,384]{2,1,0:T(8,128)(2,1)}, bf16[1,32,384]{2,1,0:T(8,128)(2,1)S(1)}, u32[]{:S(2)}, u32[]{:S(2)}) collective-permute-start(bf16[1,32,384]{2,1,0:T(8,128)(2,1)} %bitcast.14), channel_id=1, source_target_pairs={{0,96},{8,104},{16,112},{24,120},{32,0},{40,8},{48,16},{56,24},{64... | collective-permute-start | bytes 73736 | tf_op jit(solution)/shard_map/ppermute | solution.py:50
  7.5 6.9 %collective-permute-start.1 = (bf16[1,32,384]{2,1,0:T(8,128)(2,1)}, bf16[1,32,384]{2,1,0:T(8,128)(2,1)S(1)}, u32[]{:S(2)}, u32[]{:S(2)}) collective-permute-start(bf16[1,32,384]{2,1,0:T(8,128)(2,1)} %bitcast.15), channel_id=1, source_target_pairs={{0,64},{8,72},{16,80},{24,88},{32,96},{40,104},{48,112},{56,120},{... | collective-permute-start | bytes 73736 | tf_op jit(solution)/shard_map/ppermute | solution.py:50
  8.4 6.0 %collective-permute-start = (bf16[1,32,384]{2,1,0:T(8,128)(2,1)}, bf16[1,32,384]{2,1,0:T(8,128)(2,1)S(1)}, u32[]{:S(2)}, u32[]{:S(2)}) collective-permute-start(bf16[1,32,384]{2,1,0:T(8,128)(2,1)} %bitcast.16), channel_id=1, source_target_pairs={{0,32},{8,40},{16,48},{24,56},{32,64},{40,72},{48,80},{56,88},{64,... | collective-permute-start | bytes 73736 | tf_op jit(solution)/shard_map/ppermute | solution.py:50
  15.2 3.6 %collective-permute-start.3 = (bf16[4,32,384]{2,1,0:T(8,128)(2,1)S(1)}, bf16[4,32,384]{2,1,0:T(8,128)(2,1)S(1)}, u32[]{:S(2)}, u32[]{:S(2)}) collective-permute-start(bf16[4,32,384]{2,1,0:T(8,128)(2,1)S(1)} %pad_maximum_fusion.1), channel_id=1, source_target_pairs={{0,16},{8,24},{16,0},{24,8},{32,48},{40,56},{48,32},{56,40},{64,80... | collective-permute-start | bytes 294920 | tf_op jit(solution)/shard_map/ppermute | solution.py:50
  18.8 9.6 %collective-permute-start.5 = (bf16[1,256,384]{2,1,0:T(8,128)(2,1)S(1)}, bf16[1,256,384]{2,1,0:T(8,128)(2,1)S(1)}, u32[]{:S(2)}, u32[]{:S(2)}) collective-permute-start(bf16[1,256,384]{2,1,0:T(8,128)(2,1)S(1)} %bitcast.8), channel_id=1, source_target_pairs={{0,1},{8,136},{16,17},{24,152},{32,33},{40,168},{48,49},{56,184},{... | collective-permute-start | bytes 589832 | tf_op jit(solution)/shard_map/ppermute | solution.py:50
  20.2 8.3 %collective-permute-start.6 = (bf16[1,256,384]{2,1,0:T(8,128)(2,1)S(1)}, bf16[1,256,384]{2,1,0:T(8,128)(2,1)S(1)}, u32[]{:S(2)}, u32[]{:S(2)}) collective-permute-start(bf16[1,256,384]{2,1,0:T(8,128)(2,1)S(1)} %bitcast.9), channel_id=1, source_target_pairs={{0,2},{8,12},{16,18},{24,28},{32,34},{40,44},{48,50},{56,60},{64,6... | collective-permute-start | bytes 589832 | tf_op jit(solution)/shard_map/ppermute | solution.py:50
  22.8 5.7 %collective-permute-start.7 = (bf16[1,256,384]{2,1,0:T(8,128)(2,1)S(1)}, bf16[1,256,384]{2,1,0:T(8,128)(2,1)S(1)}, u32[]{:S(2)}, u32[]{:S(2)}) collective-permute-start(bf16[1,256,384]{2,1,0:T(8,128)(2,1)S(1)} %bitcast.10), channel_id=1, source_target_pairs={{0,3},{8,140},{16,19},{24,156},{32,35},{40,172},{48,51},{56,188},{... | collective-permute-start | bytes 589832 | tf_op jit(solution)/shard_map/ppermute | solution.py:50
  23.9 4.6 %collective-permute-start.8 = (bf16[1,256,384]{2,1,0:T(8,128)(2,1)S(1)}, bf16[1,256,384]{2,1,0:T(8,128)(2,1)S(1)}, u32[]{:S(2)}, u32[]{:S(2)}) collective-permute-start(bf16[1,256,384]{2,1,0:T(8,128)(2,1)S(1)} %bitcast.11), channel_id=1, source_target_pairs={{0,8},{8,0},{16,24},{24,16},{32,40},{40,32},{48,56},{56,48},{64,72... | collective-permute-start | bytes 589832 | tf_op jit(solution)/shard_map/ppermute | solution.py:50
  27.2 6.5 %collective-permute-start.9 = (bf16[1,256,384]{2,1,0:T(8,128)(2,1)S(1)}, bf16[1,256,384]{2,1,0:T(8,128)(2,1)S(1)}, u32[]{:S(2)}, u32[]{:S(2)}) collective-permute-start(bf16[1,256,384]{2,1,0:T(8,128)(2,1)S(1)} %bitcast.12), channel_id=1, source_target_pairs={{0,136},{8,128},{16,152},{24,144},{32,168},{40,160},{48,184},{56,1... | collective-permute-start | bytes 589832 | tf_op jit(solution)/shard_map/ppermute | solution.py:50
  33.8 8.2 %collective-permute-start.10 = (bf16[2,256,384]{2,1,0:T(8,128)(2,1)S(1)}, bf16[2,256,384]{2,1,0:T(8,128)(2,1)S(1)}, u32[]{:S(2)}, u32[]{:S(2)}) collective-permute-start(bf16[2,256,384]{2,1,0:T(8,128)(2,1)S(1)} %pad_maximum_fusion.p01), channel_id=1, source_target_pairs={{0,128},{8,9},{16,144},{24,25},{32,160},{40,41},{48,176},{56,57},{... | collective-permute-start | bytes 1179656 | tf_op jit(solution)/shard_map/ppermute | solution.py:50
  34.3 7.8 %collective-permute-start.11 = (bf16[2,256,384]{2,1,0:T(8,128)(2,1)S(1)}, bf16[2,256,384]{2,1,0:T(8,128)(2,1)S(1)}, u32[]{:S(2)}, u32[]{:S(2)}) collective-permute-start(bf16[2,256,384]{2,1,0:T(8,128)(2,1)S(1)} %constant_dynamic-update-slice_fusion.5.p23), channel_id=1, source_target_pairs={{0,132},{8,11},{16,148},{24,27},{32,164},{40,43},{48,180},{56,59},... | collective-permute-start | bytes 1179656 | tf_op jit(solution)/shard_map/ppermute | solution.py:50
  36.7 13.2 %collective-permute-start.12 = (bf16[2,256,384]{2,1,0:T(8,128)(2,1)S(1)}, bf16[2,256,384]{2,1,0:T(8,128)(2,1)S(1)}, u32[]{:S(2)}, u32[]{:S(2)}) collective-permute-start(bf16[2,256,384]{2,1,0:T(8,128)(2,1)S(1)} %constant_dynamic-update-slice_fusion.5.p23), channel_id=1, source_target_pairs={{0,128},{8,9},{16,144},{24,25},{32,160},{40,41},{48,176},{56,57},{... | collective-permute-start | bytes 1179656 | tf_op jit(solution)/shard_map/ppermute | solution.py:50
  36.7 13.2 %collective-permute-start.13 = (bf16[2,256,384]{2,1,0:T(8,128)(2,1)S(1)}, bf16[2,256,384]{2,1,0:T(8,128)(2,1)S(1)}, u32[]{:S(2)}, u32[]{:S(2)}) collective-permute-start(bf16[2,256,384]{2,1,0:T(8,128)(2,1)S(1)} %pad_maximum_fusion.p01), channel_id=1, source_target_pairs={{0,132},{8,11},{16,148},{24,27},{32,164},{40,43},{48,180},{56,59},... | collective-permute-start | bytes 1179656 | tf_op jit(solution)/shard_map/ppermute | solution.py:50
  42.0 8.4 %collective-permute-start.14 = (bf16[2,256,384]{2,1,0:T(8,128)(2,1)S(1)}, bf16[2,256,384]{2,1,0:T(8,128)(2,1)S(1)}, u32[]{:S(2)}, u32[]{:S(2)}) collective-permute-start(bf16[2,256,384]{2,1,0:T(8,128)(2,1)S(1)} %collective-permute-done.10.f0), channel_id=1, source_target_pairs={{0,128},{8,9},{16,144},{24,25},{32,160},{40,41},{48,176},{56,57},{... | collective-permute-start | bytes 1179656 | tf_op jit(solution)/shard_map/ppermute | solution.py:50
  42.0 8.4 %collective-permute-start.15 = (bf16[2,256,384]{2,1,0:T(8,128)(2,1)S(1)}, bf16[2,256,384]{2,1,0:T(8,128)(2,1)S(1)}, u32[]{:S(2)}, u32[]{:S(2)}) collective-permute-start(bf16[2,256,384]{2,1,0:T(8,128)(2,1)S(1)} %collective-permute-done.11.g1), channel_id=1, source_target_pairs={{0,132},{8,11},{16,148},{24,27},{32,164},{40,43},{48,180},{56,59},... | collective-permute-start | bytes 1179656 | tf_op jit(solution)/shard_map/ppermute | solution.py:50
  44.8 2.3 %copy-start = (bf16[2,384,3072]{2,1,0:T(8,128)(2,1)S(1)}, bf16[2,384,3072]{2,1,0:T(8,128)(2,1)}, u32[]{:S(2)}) copy-start(bf16[2,384,3072]{2,1,0:T(8,128)(2,1)} %own) | copy-start | bytes 14155780
  49.9 21.4 %copy-start.1 = (s32[64,64]{1,0:T(8,128)S(1)}, s32[64,64]{1,0:T(8,128)}, u32[]{:S(2)}) copy-start(s32[64,64]{1,0:T(8,128)} %q_index.1) | copy-start | bytes 49156

commit v12 on v11

--- a/solution.py
+++ b/solution.py
@@ -30,7 +30,7 @@
 
 
 SWAP = pairs(lambda x, y, z, c: (x, y, z, 1 - c))
-ACROSS = pairs(lambda x, y, z, c: (x, y ^ 1, z, 1 - c))
+ACROSS = pairs(lambda x, y, z, c: (x, y ^ 1, z, 1) if c == 0 else (x, y, z, 0))
 ZPAIR = pairs(lambda x, y, z, c: (x, y, z ^ 1, c))
 
 
@@ -266,10 +266,8 @@
         (paired, partner, coulomb.reshape(1, share), w_other)
     )
     stack = jnp.concatenate([even, paired], axis=0).reshape(1, NZ * 32, share)
-    near = send(stack, SWAP)
-    far = send(stack, ACROSS)
     parts = [send(stack, first_plane(s)) for s in FIRST[1:]]
-    parts, near, far = lax.optimization_barrier((parts, near, far))
+    parts[0], near = lax.optimization_barrier((parts[0], send(stack, SWAP)))
     p01 = jnp.concatenate([stack, parts[0]], axis=0)
     p23 = jnp.concatenate([parts[1], parts[2]], axis=0)
 
@@ -280,7 +278,12 @@
     ff0 = send(f0, second_plane(1))
     gg1 = send(g1, second_plane(-1))
 
-    w_own, w_other, f0, g1 = lax.optimization_barrier((screened, w_other, f0, g1))
+    core, low = r & 1, r >> 4
+    passed = jnp.where(core == 0, stack, jnp.where(low == 0, parts[2], parts[0]))
+    w_own, w_other, f0, g1, passed = lax.optimization_barrier(
+        (screened, w_other, f0, g1, passed)
+    )
+    far = send(passed, ACROSS)
     w = load(w_own, w_other)
     panels = (p01, p23, f0, f1, g0, g1, ff0, gg1)
     terms = solve(partner, coulomb, w, panels, near, far)

time: 87.9 us -> 87.8 us (level)
  starting transfers between devices: 29.4 us -> 33 us
  waiting for transfers between devices: 12.6 us -> 10.5 us
  blocking collectives: 28.8 us -> 27.3 us
    ppermute x16, starting transfers between devices: 29.4 us -> 33 us  [send(): return lax.ppermute(value, AXES, perm)]
    all_to_all x1, blocking collectives: 13.6 us -> 11.1 us  [local(): lax.all_to_all(terms, 'col', split_axis=0, concat_axis=0, tiled=True)]
    ppermute x16, waiting for transfers between devices: 12.6 us -> 10.5 us  [send(): return lax.ppermute(value, AXES, perm)]
    all_to_all x1, blocking collectives: 15.2 us -> 16.2 us  [local(): lax.all_to_all(placed, 'row', split_axis=0, concat_axis=0, tiled=True)]
  transfers between devices with their start and end apart: 16 -> 16, of which waited for: 5 -> 6; matrix products, arithmetic and copies ran while one was open for 4% -> 4% of each run, Pallas kernels for 3% -> 3%
where the time goes in v12:
time: 87.8 us; the launch traced here: 87.4 us
  starting transfers between devices  33 us (38%)
  blocking collectives  27.3 us (31%)
  Pallas kernels  10.9 us (12%)
  waiting for transfers between devices  10.5 us (12%)
  local copies, waits for them, and re-layouts  3.83 us (4%)
  other arithmetic  1.84 us (2%)
    ppermute x16, starting transfers between devices, send(): return lax.ppermute(value, AXES, perm)  33 us
    all_to_all x1, blocking collectives, local(): lax.all_to_all(placed, 'row', split_axis=0, concat_axis=0, tiled=True)  16.2 us
    all_to_all x1, blocking collectives, local(): lax.all_to_all(terms, 'col', split_axis=0, concat_axis=0, tiled=True)  11.1 us
    ppermute x16, waiting for transfers between devices, send(): return lax.ppermute(value, AXES, perm)  10.5 us
    pallas_call x1, Pallas kernels, solve(): pl.pallas_call(solve_kernel, in_specs=[pl.BlockSpec(memory_space=pltpu.SM...  7.24 us
    unnamed x9, local copies, waits for them, and re-layouts  3.13 us
    pallas_call x1, Pallas kernels, load(): pl.pallas_call(load_kernel, in_specs=[pl.BlockSpec(memory_space=pl.ANY)]...  2.72 us
  transfers between devices with their start and end apart: 16, of which 6 were waited for; matrix products, arithmetic and copies ran while one was open for 4% of the time, Pallas kernels for 3%

profile of v12, /device:TPU:1, one launch (start us, length us, event | category | flops | bytes accessed | tf_op | source)
XLA Modules:
  0.0 87.4 jit_solution(17561773445324110276)
XLA Ops:
  0.0 3.2 %collective-permute-start.4 = (bf16[2,384,3072]{2,1,0:T(8,128)(2,1)}, bf16[2,384,3072]{2,1,0:T(8,128)(2,1)}, u32[]{:S(2)}, u32[]{:S(2)}) collective-permute-start(bf16[2,384,3072]{2,1,0:T(8,128)(2,1)} %own), channel_id=1, source_target_pairs={{0,8},{8,0},{16,24},{24,16},{32,40},{40,32},{48,56},{56,48},{64,72... | collective-permute-start | bytes 14155784 | tf_op jit(solution)/shard_map/ppermute | solution.py:50
  3.2 4.3 %collective-permute-start.2 = (bf16[1,32,384]{2,1,0:T(8,128)(2,1)}, bf16[1,32,384]{2,1,0:T(8,128)(2,1)S(1)}, u32[]{:S(2)}, u32[]{:S(2)}) collective-permute-start(bf16[1,32,384]{2,1,0:T(8,128)(2,1)} %bitcast.16), channel_id=1, source_target_pairs={{0,96},{8,104},{16,112},{24,120},{32,0},{40,8},{48,16},{56,24},{64... | collective-permute-start | bytes 73736 | tf_op jit(solution)/shard_map/ppermute | solution.py:50
  7.5 0.9 %collective-permute-start.1 = (bf16[1,32,384]{2,1,0:T(8,128)(2,1)}, bf16[1,32,384]{2,1,0:T(8,128)(2,1)S(1)}, u32[]{:S(2)}, u32[]{:S(2)}) collective-permute-start(bf16[1,32,384]{2,1,0:T(8,128)(2,1)} %bitcast.17), channel_id=1, source_target_pairs={{0,64},{8,72},{16,80},{24,88},{32,96},{40,104},{48,112},{56,120},{... | collective-permute-start | bytes 73736 | tf_op jit(solution)/shard_map/ppermute | solution.py:50
  8.4 2.3 %collective-permute-start = (bf16[1,32,384]{2,1,0:T(8,128)(2,1)}, bf16[1,32,384]{2,1,0:T(8,128)(2,1)S(1)}, u32[]{:S(2)}, u32[]{:S(2)}) collective-permute-start(bf16[1,32,384]{2,1,0:T(8,128)(2,1)} %bitcast.18), channel_id=1, source_target_pairs={{0,32},{8,40},{16,48},{24,56},{32,64},{40,72},{48,80},{56,88},{64,... | collective-permute-start | bytes 73736 | tf_op jit(solution)/shard_map/ppermute | solution.py:50
  10.9 0.9 select_reduce_fusion.partner
  13.1 1.3 %collective-permute-done.1 = bf16[1,32,384]{2,1,0:T(8,128)(2,1)S(1)} collective-permute-done((bf16[1,32,384]{2,1,0:T(8,128)(2,1)}, bf16[1,32,384]{2,1,0:T(8,128)(2,1)S(1)}, u32[]{:S(2)}, u32[]{:S(2)}) %collective-permute-start.1) | collective-permute-done | bytes 24608 | tf_op jit(solution)/shard_map/ppermute | solution.py:50
  15.9 2.8 %collective-permute-done.3 = bf16[4,32,384]{2,1,0:T(8,128)(2,1)S(1)} collective-permute-done((bf16[4,32,384]{2,1,0:T(8,128)(2,1)S(1)}, bf16[4,32,384]{2,1,0:T(8,128)(2,1)S(1)}, u32[]{:S(2)}, u32[]{:S(2)}) %collective-permute-start.3) | collective-permute-done | bytes 98336 | tf_op jit(solution)/shard_map/ppermute | solution.py:50
  18.8 1.4 %collective-permute-start.5 = (bf16[1,256,384]{2,1,0:T(8,128)(2,1)S(1)}, bf16[1,256,384]{2,1,0:T(8,128)(2,1)S(1)}, u32[]{:S(2)}, u32[]{:S(2)}) collective-permute-start(bf16[1,256,384]{2,1,0:T(8,128)(2,1)S(1)} %bitcast.10), channel_id=1, source_target_pairs={{0,1},{8,136},{16,17},{24,152},{32,33},{40,168},{48,49},{56,184},{... | collective-permute-start | bytes 589832 | tf_op jit(solution)/shard_map/ppermute | solution.py:50
  20.2 2.9 %collective-permute-start.6 = (bf16[1,256,384]{2,1,0:T(8,128)(2,1)S(1)}, bf16[1,256,384]{2,1,0:T(8,128)(2,1)S(1)}, u32[]{:S(2)}, u32[]{:S(2)}) collective-permute-start(bf16[1,256,384]{2,1,0:T(8,128)(2,1)S(1)} %bitcast.11), channel_id=1, source_target_pairs={{0,8},{8,0},{16,24},{24,16},{32,40},{40,32},{48,56},{56,48},{64,72... | collective-permute-start | bytes 589832 | tf_op jit(solution)/shard_map/ppermute | solution.py:50
  23.1 2.9 %collective-permute-start.8 = (bf16[1,256,384]{2,1,0:T(8,128)(2,1)S(1)}, bf16[1,256,384]{2,1,0:T(8,128)(2,1)S(1)}, u32[]{:S(2)}, u32[]{:S(2)}) collective-permute-start(bf16[1,256,384]{2,1,0:T(8,128)(2,1)S(1)} %bitcast.12), channel_id=1, source_target_pairs={{0,2},{8,12},{16,18},{24,28},{32,34},{40,44},{48,50},{56,60},{64,6... | collective-permute-start | bytes 589832 | tf_op jit(solution)/shard_map/ppermute | solution.py:50
  26.0 0.8 collective-permute-start.9
  26.8 1.3 %collective-permute-start.7 = (bf16[2,256,384]{2,1,0:T(8,128)(2,1)S(1)}, bf16[2,256,384]{2,1,0:T(8,128)(2,1)S(1)}, u32[]{:S(2)}, u32[]{:S(2)}) collective-permute-start(bf16[2,256,384]{2,1,0:T(8,128)(2,1)S(1)} %pad_maximum_fusion.p01), channel_id=1, source_target_pairs={{0,128},{8,9},{16,144},{24,25},{32,160},{40,41},{48,176},{56,57},{... | collective-permute-start | bytes 1179656 | tf_op jit(solution)/shard_map/ppermute | solution.py:50
  28.1 1.3 %collective-permute-done.8 = bf16[1,256,384]{2,1,0:T(8,128)(2,1)S(1)} collective-permute-done((bf16[1,256,384]{2,1,0:T(8,128)(2,1)S(1)}, bf16[1,256,384]{2,1,0:T(8,128)(2,1)S(1)}, u32[]{:S(2)}, u32[]{:S(2)}) %collective-permute-start.8) | collective-permute-done | bytes 196640 | tf_op jit(solution)/shard_map/ppermute | solution.py:50
  29.4 2.1 %collective-permute-done.9 = bf16[1,256,384]{2,1,0:T(8,128)(2,1)S(1)} collective-permute-done((bf16[1,256,384]{2,1,0:T(8,128)(2,1)S(1)}, bf16[1,256,384]{2,1,0:T(8,128)(2,1)S(1)}, u32[]{:S(2)}, u32[]{:S(2)}) %collective-permute-start.9) | collective-permute-done | bytes 196640 | tf_op jit(solution)/shard_map/ppermute | solution.py:50
  31.7 1.8 %collective-permute-start.10 = (bf16[2,256,384]{2,1,0:T(8,128)(2,1)S(1)}, bf16[2,256,384]{2,1,0:T(8,128)(2,1)S(1)}, u32[]{:S(2)}, u32[]{:S(2)}) collective-permute-start(bf16[2,256,384]{2,1,0:T(8,128)(2,1)S(1)} %get-tuple-element.28.p23), channel_id=1, source_target_pairs={{0,132},{8,11},{16,148},{24,27},{32,164},{40,43},{48,180},{56,59},... | collective-permute-start | bytes 1179656 | tf_op jit(solution)/shard_map/ppermute | solution.py:50
  33.5 2.7 %collective-permute-start.12 = (bf16[2,256,384]{2,1,0:T(8,128)(2,1)S(1)}, bf16[2,256,384]{2,1,0:T(8,128)(2,1)S(1)}, u32[]{:S(2)}, u32[]{:S(2)}) collective-permute-start(bf16[2,256,384]{2,1,0:T(8,128)(2,1)S(1)} %pad_maximum_fusion.p01), channel_id=1, source_target_pairs={{0,132},{8,11},{16,148},{24,27},{32,164},{40,43},{48,180},{56,59},... | collective-permute-start | bytes 1179656 | tf_op jit(solution)/shard_map/ppermute | solution.py:50
  36.2 2.5 %collective-permute-done.10.g1 = bf16[2,256,384]{2,1,0:T(8,128)(2,1)S(1)} collective-permute-done((bf16[2,256,384]{2,1,0:T(8,128)(2,1)S(1)}, bf16[2,256,384]{2,1,0:T(8,128)(2,1)S(1)}, u32[]{:S(2)}, u32[]{:S(2)}) %collective-permute-start.10) | collective-permute-done | bytes 393248 | tf_op jit(solution)/shard_map/ppermute | solution.py:50
  38.7 2.9 %collective-permute-start.14 = (bf16[2,256,384]{2,1,0:T(8,128)(2,1)S(1)}, bf16[2,256,384]{2,1,0:T(8,128)(2,1)S(1)}, u32[]{:S(2)}, u32[]{:S(2)}) collective-permute-start(bf16[2,256,384]{2,1,0:T(8,128)(2,1)S(1)} %collective-permute-done.10.g1), channel_id=1, source_target_pairs={{0,132},{8,11},{16,148},{24,27},{32,164},{40,43},{48,180},{56,59},... | collective-permute-start | bytes 1179656 | tf_op jit(solution)/shard_map/ppermute | solution.py:50
  41.6 4.8 %collective-permute-start.15 = (bf16[1,256,384]{2,1,0:T(8,128)(2,1)S(1)}, bf16[1,256,384]{2,1,0:T(8,128)(2,1)S(1)}, u32[]{:S(2)}, u32[]{:S(2)}) collective-permute-start(bf16[1,256,384]{2,1,0:T(8,128)(2,1)S(1)} %get-tuple-element.26), channel_id=1, source_target_pairs={{0,136},{8,0},{16,152},{24,16},{32,168},{40,32},{48,184},{56,48},{... | collective-permute-start | bytes 589832 | tf_op jit(solution)/shard_map/ppermute | solution.py:50
  46.5 2.3 %copy-done = bf16[2,384,3072]{2,1,0:T(8,128)(2,1)S(1)} copy-done((bf16[2,384,3072]{2,1,0:T(8,128)(2,1)S(1)}, bf16[2,384,3072]{2,1,0:T(8,128)(2,1)}, u32[]{:S(2)}) %copy-start) | copy-done | bytes 4718616
  48.8 2.7 %load.1.w = bf16[4,384,3072]{2,1,0:T(8,128)(2,1)S(1)} custom-call(bf16[2,384,3072]{2,1,0:T(8,128)(2,1)S(1)} %copy-done, bf16[2,384,3072]{2,1,0:T(8,128)(2,1)} %collective-permute-done.4.other), custom_call_target="tpu_custom_call" | custom-call | bytes 18874368 | tf_op jit(solution)/shard_map/load/pallas_call | solution.py:90
  52.0 7.2 %solve.1 = f32[8,2,16,128]{3,2,1,0:T(8,128)S(1)} custom-call(s32[4,64]{1,0:T(4,128)S(1)} %select_reduce_fusion.partner, f32[1,384]{1,0:T(1,128)S(1)} %reshape.12.coulomb, bf16[4,384,3072]{2,1,0:T(8,128)(2,1)S(1)} %load.1.w, bf16[2,256,384]{2,1,0:T(8,128)(2,1)S(1)} %pad_maximum_fusion.p01, bf16[2,256,384]{2,1,0:T(8,128)(2,1)S(1)} %get-tuple-element.28.p23, ...), custom_call_target="tpu_custom_call" | custom-call | flops 4831838208 | bytes 9437184 | tf_op jit(solution)/shard_map/solve/pallas_call | solution.py:160
  59.2 11.1 %all_to_all.10.terms = f32[8,2,16,128]{3,2,1,0:T(8,128)S(1)} all-to-all(f32[8,2,16,128]{3,2,1,0:T(8,128)S(1)} %solve.1), channel_id=1, replica_groups=mesh['row'=32,'col'=8] {'col'}, dimensions={0} | all-to-all | bytes 262144 | tf_op jit(solution)/shard_map/all_to_all | solution.py:290
  70.5 16.2 %all_to_all.11.arrived = bf16[32,16,128]{2,1,0:T(8,128)(2,1)S(1)} all-to-all(bf16[32,16,128]{2,1,0:T(8,128)(2,1)S(1)} %spread.1), channel_id=1, replica_groups=mesh['row'=32,'col'=8] {'row'}, dimensions={0} | all-to-all | bytes 262144 | tf_op jit(solution)/shard_map/all_to_all | solution.py:292
  (30 shorter events, 4.5 us)
Async XLA Ops:
  0.0 18.8 %collective-permute-start.4 = (bf16[2,384,3072]{2,1,0:T(8,128)(2,1)}, bf16[2,384,3072]{2,1,0:T(8,128)(2,1)}, u32[]{:S(2)}, u32[]{:S(2)}) collective-permute-start(bf16[2,384,3072]{2,1,0:T(8,128)(2,1)} %own), channel_id=1, source_target_pairs={{0,8},{8,0},{16,24},{24,16},{32,40},{40,32},{48,56},{56,48},{64,72... | collective-permute-start | bytes 14155784 | tf_op jit(solution)/shard_map/ppermute | solution.py:50
  3.2 9.9 %collective-permute-start.2 = (bf16[1,32,384]{2,1,0:T(8,128)(2,1)}, bf16[1,32,384]{2,1,0:T(8,128)(2,1)S(1)}, u32[]{:S(2)}, u32[]{:S(2)}) collective-permute-start(bf16[1,32,384]{2,1,0:T(8,128)(2,1)} %bitcast.16), channel_id=1, source_target_pairs={{0,96},{8,104},{16,112},{24,120},{32,0},{40,8},{48,16},{56,24},{64... | collective-permute-start | bytes 73736 | tf_op jit(solution)/shard_map/ppermute | solution.py:50
  7.5 6.9 %collective-permute-start.1 = (bf16[1,32,384]{2,1,0:T(8,128)(2,1)}, bf16[1,32,384]{2,1,0:T(8,128)(2,1)S(1)}, u32[]{:S(2)}, u32[]{:S(2)}) collective-permute-start(bf16[1,32,384]{2,1,0:T(8,128)(2,1)} %bitcast.17), channel_id=1, source_target_pairs={{0,64},{8,72},{16,80},{24,88},{32,96},{40,104},{48,112},{56,120},{... | collective-permute-start | bytes 73736 | tf_op jit(solution)/shard_map/ppermute | solution.py:50
  8.4 6.0 %collective-permute-start = (bf16[1,32,384]{2,1,0:T(8,128)(2,1)}, bf16[1,32,384]{2,1,0:T(8,128)(2,1)S(1)}, u32[]{:S(2)}, u32[]{:S(2)}) collective-permute-start(bf16[1,32,384]{2,1,0:T(8,128)(2,1)} %bitcast.18), channel_id=1, source_target_pairs={{0,32},{8,40},{16,48},{24,56},{32,64},{40,72},{48,80},{56,88},{64,... | collective-permute-start | bytes 73736 | tf_op jit(solution)/shard_map/ppermute | solution.py:50
  15.2 3.6 %collective-permute-start.3 = (bf16[4,32,384]{2,1,0:T(8,128)(2,1)S(1)}, bf16[4,32,384]{2,1,0:T(8,128)(2,1)S(1)}, u32[]{:S(2)}, u32[]{:S(2)}) collective-permute-start(bf16[4,32,384]{2,1,0:T(8,128)(2,1)S(1)} %pad_maximum_fusion.1), channel_id=1, source_target_pairs={{0,16},{8,24},{16,0},{24,8},{32,48},{40,56},{48,32},{56,40},{64,80... | collective-permute-start | bytes 294920 | tf_op jit(solution)/shard_map/ppermute | solution.py:50
  18.8 8.0 %collective-permute-start.5 = (bf16[1,256,384]{2,1,0:T(8,128)(2,1)S(1)}, bf16[1,256,384]{2,1,0:T(8,128)(2,1)S(1)}, u32[]{:S(2)}, u32[]{:S(2)}) collective-permute-start(bf16[1,256,384]{2,1,0:T(8,128)(2,1)S(1)} %bitcast.10), channel_id=1, source_target_pairs={{0,1},{8,136},{16,17},{24,152},{32,33},{40,168},{48,49},{56,184},{... | collective-permute-start | bytes 589832 | tf_op jit(solution)/shard_map/ppermute | solution.py:50
  20.2 6.6 %collective-permute-start.6 = (bf16[1,256,384]{2,1,0:T(8,128)(2,1)S(1)}, bf16[1,256,384]{2,1,0:T(8,128)(2,1)S(1)}, u32[]{:S(2)}, u32[]{:S(2)}) collective-permute-start(bf16[1,256,384]{2,1,0:T(8,128)(2,1)S(1)} %bitcast.11), channel_id=1, source_target_pairs={{0,8},{8,0},{16,24},{24,16},{32,40},{40,32},{48,56},{56,48},{64,72... | collective-permute-start | bytes 589832 | tf_op jit(solution)/shard_map/ppermute | solution.py:50
  23.1 6.3 %collective-permute-start.8 = (bf16[1,256,384]{2,1,0:T(8,128)(2,1)S(1)}, bf16[1,256,384]{2,1,0:T(8,128)(2,1)S(1)}, u32[]{:S(2)}, u32[]{:S(2)}) collective-permute-start(bf16[1,256,384]{2,1,0:T(8,128)(2,1)S(1)} %bitcast.12), channel_id=1, source_target_pairs={{0,2},{8,12},{16,18},{24,28},{32,34},{40,44},{48,50},{56,60},{64,6... | collective-permute-start | bytes 589832 | tf_op jit(solution)/shard_map/ppermute | solution.py:50
  26.0 5.6 %collective-permute-start.9 = (bf16[1,256,384]{2,1,0:T(8,128)(2,1)S(1)}, bf16[1,256,384]{2,1,0:T(8,128)(2,1)S(1)}, u32[]{:S(2)}, u32[]{:S(2)}) collective-permute-start(bf16[1,256,384]{2,1,0:T(8,128)(2,1)S(1)} %bitcast.13), channel_id=1, source_target_pairs={{0,3},{8,140},{16,19},{24,156},{32,35},{40,172},{48,51},{56,188},{... | collective-permute-start | bytes 589832 | tf_op jit(solution)/shard_map/ppermute | solution.py:50
  26.8 9.3 %collective-permute-start.7 = (bf16[2,256,384]{2,1,0:T(8,128)(2,1)S(1)}, bf16[2,256,384]{2,1,0:T(8,128)(2,1)S(1)}, u32[]{:S(2)}, u32[]{:S(2)}) collective-permute-start(bf16[2,256,384]{2,1,0:T(8,128)(2,1)S(1)} %pad_maximum_fusion.p01), channel_id=1, source_target_pairs={{0,128},{8,9},{16,144},{24,25},{32,160},{40,41},{48,176},{56,57},{... | collective-permute-start | bytes 1179656 | tf_op jit(solution)/shard_map/ppermute | solution.py:50
  31.7 7.0 %collective-permute-start.10 = (bf16[2,256,384]{2,1,0:T(8,128)(2,1)S(1)}, bf16[2,256,384]{2,1,0:T(8,128)(2,1)S(1)}, u32[]{:S(2)}, u32[]{:S(2)}) collective-permute-start(bf16[2,256,384]{2,1,0:T(8,128)(2,1)S(1)} %get-tuple-element.28.p23), channel_id=1, source_target_pairs={{0,132},{8,11},{16,148},{24,27},{32,164},{40,43},{48,180},{56,59},... | collective-permute-start | bytes 1179656 | tf_op jit(solution)/shard_map/ppermute | solution.py:50
  33.5 18.1 %collective-permute-start.11 = (bf16[2,256,384]{2,1,0:T(8,128)(2,1)S(1)}, bf16[2,256,384]{2,1,0:T(8,128)(2,1)S(1)}, u32[]{:S(2)}, u32[]{:S(2)}) collective-permute-start(bf16[2,256,384]{2,1,0:T(8,128)(2,1)S(1)} %get-tuple-element.28.p23), channel_id=1, source_target_pairs={{0,128},{8,9},{16,144},{24,25},{32,160},{40,41},{48,176},{56,57},{... | collective-permute-start | bytes 1179656 | tf_op jit(solution)/shard_map/ppermute | solution.py:50
  33.5 18.1 %collective-permute-start.12 = (bf16[2,256,384]{2,1,0:T(8,128)(2,1)S(1)}, bf16[2,256,384]{2,1,0:T(8,128)(2,1)S(1)}, u32[]{:S(2)}, u32[]{:S(2)}) collective-permute-start(bf16[2,256,384]{2,1,0:T(8,128)(2,1)S(1)} %pad_maximum_fusion.p01), channel_id=1, source_target_pairs={{0,132},{8,11},{16,148},{24,27},{32,164},{40,43},{48,180},{56,59},... | collective-permute-start | bytes 1179656 | tf_op jit(solution)/shard_map/ppermute | solution.py:50
  36.2 15.8 %collective-permute-start.13 = (bf16[2,256,384]{2,1,0:T(8,128)(2,1)S(1)}, bf16[2,256,384]{2,1,0:T(8,128)(2,1)S(1)}, u32[]{:S(2)}, u32[]{:S(2)}) collective-permute-start(bf16[2,256,384]{2,1,0:T(8,128)(2,1)S(1)} %collective-permute-done.7.f0), channel_id=1, source_target_pairs={{0,128},{8,9},{16,144},{24,25},{32,160},{40,41},{48,176},{56,57},{... | collective-permute-start | bytes 1179656 | tf_op jit(solution)/shard_map/ppermute | solution.py:50
  38.7 13.3 %collective-permute-start.14 = (bf16[2,256,384]{2,1,0:T(8,128)(2,1)S(1)}, bf16[2,256,384]{2,1,0:T(8,128)(2,1)S(1)}, u32[]{:S(2)}, u32[]{:S(2)}) collective-permute-start(bf16[2,256,384]{2,1,0:T(8,128)(2,1)S(1)} %collective-permute-done.10.g1), channel_id=1, source_target_pairs={{0,132},{8,11},{16,148},{24,27},{32,164},{40,43},{48,180},{56,59},... | collective-permute-start | bytes 1179656 | tf_op jit(solution)/shard_map/ppermute | solution.py:50
  41.6 10.3 %collective-permute-start.15 = (bf16[1,256,384]{2,1,0:T(8,128)(2,1)S(1)}, bf16[1,256,384]{2,1,0:T(8,128)(2,1)S(1)}, u32[]{:S(2)}, u32[]{:S(2)}) collective-permute-start(bf16[1,256,384]{2,1,0:T(8,128)(2,1)S(1)} %get-tuple-element.26), channel_id=1, source_target_pairs={{0,136},{8,0},{16,152},{24,16},{32,168},{40,32},{48,184},{56,48},{... | collective-permute-start | bytes 589832 | tf_op jit(solution)/shard_map/ppermute | solution.py:50
  46.5 2.3 %copy-start = (bf16[2,384,3072]{2,1,0:T(8,128)(2,1)S(1)}, bf16[2,384,3072]{2,1,0:T(8,128)(2,1)}, u32[]{:S(2)}) copy-start(bf16[2,384,3072]{2,1,0:T(8,128)(2,1)} %own) | copy-start | bytes 14155780
  51.5 18.8 %copy-start.1 = (s32[64,64]{1,0:T(8,128)S(1)}, s32[64,64]{1,0:T(8,128)}, u32[]{:S(2)}) copy-start(s32[64,64]{1,0:T(8,128)} %q_index.1) | copy-start | bytes 49156

commit v13 on v12

--- a/solution.py
+++ b/solution.py
@@ -253,7 +253,6 @@
 def local(pair_matrix, screened, coulomb, q_index):
     bands, share = pair_matrix.shape[1:]
     r = lax.axis_index("row")
-    w_other = send(screened, SWAP)
     own = pair_matrix.reshape(1, 2 * bands, share)
     even = jnp.concatenate([own] + [send(own, along_z(s)) for s in ZSHIFTS[1:]], axis=0)
     paired = send(even, ZPAIR)
@@ -262,12 +261,12 @@
     partner = jnp.sum(
         jnp.where(q_index[None] == q_mine[:, None, None], ks[None, :, None], 0), axis=1
     ).astype(jnp.int32)
-    paired, partner, coulomb, w_other = lax.optimization_barrier(
-        (paired, partner, coulomb.reshape(1, share), w_other)
+    paired, partner, coulomb, screened = lax.optimization_barrier(
+        (paired, partner, coulomb.reshape(1, share), screened)
     )
+    w_other = send(screened, SWAP)
     stack = jnp.concatenate([even, paired], axis=0).reshape(1, NZ * 32, share)
     parts = [send(stack, first_plane(s)) for s in FIRST[1:]]
-    parts[0], near = lax.optimization_barrier((parts[0], send(stack, SWAP)))
     p01 = jnp.concatenate([stack, parts[0]], axis=0)
     p23 = jnp.concatenate([parts[1], parts[2]], axis=0)
 
@@ -280,9 +279,10 @@
 
     core, low = r & 1, r >> 4
     passed = jnp.where(core == 0, stack, jnp.where(low == 0, parts[2], parts[0]))
-    w_own, w_other, f0, g1, passed = lax.optimization_barrier(
-        (screened, w_other, f0, g1, passed)
+    w_own, w_other, f0, g1, passed, kept = lax.optimization_barrier(
+        (screened, w_other, f0, g1, passed, stack)
     )
+    near = send(kept, SWAP)
     far = send(passed, ACROSS)
     w = load(w_own, w_other)
     panels = (p01, p23, f0, f1, g0, g1, ff0, gg1)

time: 87.8 us -> 88 us (level)
  blocking collectives: 27.3 us -> 29.6 us
  starting transfers between devices: 33 us -> 31.2 us
    all_to_all x1, blocking collectives: 11.1 us -> 13.3 us  [local(): lax.all_to_all(terms, 'col', split_axis=0, concat_axis=0, tiled=True)]
    ppermute x16, starting transfers between devices: 33 us -> 31.2 us  [send(): return lax.ppermute(value, AXES, perm)]
  transfers between devices with their start and end apart: 16 -> 16, of which waited for: 6 -> 6; matrix products, arithmetic and copies ran while one was open for 4% -> 3% of each run, Pallas kernels for 3% -> 3%
where the time goes in v13:
time: 88 us; the launch traced here: 87.6 us
  starting transfers between devices  31.2 us (35%)
  blocking collectives  29.6 us (34%)
  Pallas kernels  10.8 us (12%)
  waiting for transfers between devices  10.2 us (12%)
  local copies, waits for them, and re-layouts  3.84 us (4%)
  other arithmetic  1.86 us (2%)
    ppermute x16, starting transfers between devices, send(): return lax.ppermute(value, AXES, perm)  31.2 us
    all_to_all x1, blocking collectives, local(): lax.all_to_all(placed, 'row', split_axis=0, concat_axis=0, tiled=True)  16.3 us
    all_to_all x1, blocking collectives, local(): lax.all_to_all(terms, 'col', split_axis=0, concat_axis=0, tiled=True)  13.3 us
    ppermute x16, waiting for transfers between devices, send(): return lax.ppermute(value, AXES, perm)  10.2 us
    pallas_call x1, Pallas kernels, solve(): pl.pallas_call(solve_kernel, in_specs=[pl.BlockSpec(memory_space=pltpu.SM...  7.16 us
    unnamed x9, local copies, waits for them, and re-layouts  3.13 us
    pallas_call x1, Pallas kernels, load(): pl.pallas_call(load_kernel, in_specs=[pl.BlockSpec(memory_space=pl.ANY)]...  2.72 us
  transfers between devices with their start and end apart: 16, of which 6 were waited for; matrix products, arithmetic and copies ran while one was open for 3% of the time, Pallas kernels for 3%

profile of v13, /device:TPU:1, one launch (start us, length us, event | category | flops | bytes accessed | tf_op | source)
XLA Modules:
  0.0 87.6 jit_solution(10911840351534953404)
XLA Ops:
  0.0 6.8 %collective-permute-start.2 = (bf16[1,32,384]{2,1,0:T(8,128)(2,1)}, bf16[1,32,384]{2,1,0:T(8,128)(2,1)S(1)}, u32[]{:S(2)}, u32[]{:S(2)}) collective-permute-start(bf16[1,32,384]{2,1,0:T(8,128)(2,1)} %bitcast.16), channel_id=1, source_target_pairs={{0,96},{8,104},{16,112},{24,120},{32,0},{40,8},{48,16},{56,24},{64... | collective-permute-start | bytes 73736 | tf_op jit(solution)/shard_map/ppermute | solution.py:50
  6.9 0.9 %collective-permute-start.1 = (bf16[1,32,384]{2,1,0:T(8,128)(2,1)}, bf16[1,32,384]{2,1,0:T(8,128)(2,1)S(1)}, u32[]{:S(2)}, u32[]{:S(2)}) collective-permute-start(bf16[1,32,384]{2,1,0:T(8,128)(2,1)} %bitcast.17), channel_id=1, source_target_pairs={{0,64},{8,72},{16,80},{24,88},{32,96},{40,104},{48,112},{56,120},{... | collective-permute-start | bytes 73736 | tf_op jit(solution)/shard_map/ppermute | solution.py:50
  7.7 2.4 %collective-permute-start = (bf16[1,32,384]{2,1,0:T(8,128)(2,1)}, bf16[1,32,384]{2,1,0:T(8,128)(2,1)S(1)}, u32[]{:S(2)}, u32[]{:S(2)}) collective-permute-start(bf16[1,32,384]{2,1,0:T(8,128)(2,1)} %bitcast.18), channel_id=1, source_target_pairs={{0,32},{8,40},{16,48},{24,56},{32,64},{40,72},{48,80},{56,88},{64,... | collective-permute-start | bytes 73736 | tf_op jit(solution)/shard_map/ppermute | solution.py:50
  10.9 2.8 %collective-permute-done.1 = bf16[1,32,384]{2,1,0:T(8,128)(2,1)S(1)} collective-permute-done((bf16[1,32,384]{2,1,0:T(8,128)(2,1)}, bf16[1,32,384]{2,1,0:T(8,128)(2,1)S(1)}, u32[]{:S(2)}, u32[]{:S(2)}) %collective-permute-start.1) | collective-permute-done | bytes 24608 | tf_op jit(solution)/shard_map/ppermute | solution.py:50
  14.4 0.8 collective-permute-start.3
  15.2 0.9 select_reduce_fusion.partner
  16.1 1.9 %collective-permute-done.3 = bf16[4,32,384]{2,1,0:T(8,128)(2,1)S(1)} collective-permute-done((bf16[4,32,384]{2,1,0:T(8,128)(2,1)S(1)}, bf16[4,32,384]{2,1,0:T(8,128)(2,1)S(1)}, u32[]{:S(2)}, u32[]{:S(2)}) %collective-permute-start.3) | collective-permute-done | bytes 98336 | tf_op jit(solution)/shard_map/ppermute | solution.py:50
  18.0 3.3 %collective-permute-start.4 = (bf16[2,384,3072]{2,1,0:T(8,128)(2,1)}, bf16[2,384,3072]{2,1,0:T(8,128)(2,1)}, u32[]{:S(2)}, u32[]{:S(2)}) collective-permute-start(bf16[2,384,3072]{2,1,0:T(8,128)(2,1)} %own), channel_id=1, source_target_pairs={{0,8},{8,0},{16,24},{24,16},{32,40},{40,32},{48,56},{56,48},{64,72... | collective-permute-start | bytes 14155784 | tf_op jit(solution)/shard_map/ppermute | solution.py:50
  22.0 1.4 %collective-permute-start.5 = (bf16[1,256,384]{2,1,0:T(8,128)(2,1)S(1)}, bf16[1,256,384]{2,1,0:T(8,128)(2,1)S(1)}, u32[]{:S(2)}, u32[]{:S(2)}) collective-permute-start(bf16[1,256,384]{2,1,0:T(8,128)(2,1)S(1)} %bitcast.10), channel_id=1, source_target_pairs={{0,1},{8,136},{16,17},{24,152},{32,33},{40,168},{48,49},{56,184},{... | collective-permute-start | bytes 589832 | tf_op jit(solution)/shard_map/ppermute | solution.py:50
  23.4 2.6 %collective-permute-start.7 = (bf16[1,256,384]{2,1,0:T(8,128)(2,1)S(1)}, bf16[1,256,384]{2,1,0:T(8,128)(2,1)S(1)}, u32[]{:S(2)}, u32[]{:S(2)}) collective-permute-start(bf16[1,256,384]{2,1,0:T(8,128)(2,1)S(1)} %bitcast.11), channel_id=1, source_target_pairs={{0,2},{8,12},{16,18},{24,28},{32,34},{40,44},{48,50},{56,60},{64,6... | collective-permute-start | bytes 589832 | tf_op jit(solution)/shard_map/ppermute | solution.py:50
  26.0 1.1 %collective-permute-start.8 = (bf16[1,256,384]{2,1,0:T(8,128)(2,1)S(1)}, bf16[1,256,384]{2,1,0:T(8,128)(2,1)S(1)}, u32[]{:S(2)}, u32[]{:S(2)}) collective-permute-start(bf16[1,256,384]{2,1,0:T(8,128)(2,1)S(1)} %bitcast.12), channel_id=1, source_target_pairs={{0,3},{8,140},{16,19},{24,156},{32,35},{40,172},{48,51},{56,188},{... | collective-permute-start | bytes 589832 | tf_op jit(solution)/shard_map/ppermute | solution.py:50
  27.1 1.1 %collective-permute-done.5 = bf16[1,256,384]{2,1,0:T(8,128)(2,1)S(1)} collective-permute-done((bf16[1,256,384]{2,1,0:T(8,128)(2,1)S(1)}, bf16[1,256,384]{2,1,0:T(8,128)(2,1)S(1)}, u32[]{:S(2)}, u32[]{:S(2)}) %collective-permute-start.5) | collective-permute-done | bytes 196640 | tf_op jit(solution)/shard_map/ppermute | solution.py:50
  28.2 1.0 %collective-permute-start.6 = (bf16[2,256,384]{2,1,0:T(8,128)(2,1)S(1)}, bf16[2,256,384]{2,1,0:T(8,128)(2,1)S(1)}, u32[]{:S(2)}, u32[]{:S(2)}) collective-permute-start(bf16[2,256,384]{2,1,0:T(8,128)(2,1)S(1)} %pad_maximum_fusion.p01), channel_id=1, source_target_pairs={{0,128},{8,9},{16,144},{24,25},{32,160},{40,41},{48,176},{56,57},{... | collective-permute-start | bytes 1179656 | tf_op jit(solution)/shard_map/ppermute | solution.py:50
  29.2 2.2 %collective-permute-done.7 = bf16[1,256,384]{2,1,0:T(8,128)(2,1)S(1)} collective-permute-done((bf16[1,256,384]{2,1,0:T(8,128)(2,1)S(1)}, bf16[1,256,384]{2,1,0:T(8,128)(2,1)S(1)}, u32[]{:S(2)}, u32[]{:S(2)}) %collective-permute-start.7) | collective-permute-done | bytes 196640 | tf_op jit(solution)/shard_map/ppermute | solution.py:50
  31.6 2.3 %collective-permute-start.9 = (bf16[2,256,384]{2,1,0:T(8,128)(2,1)S(1)}, bf16[2,256,384]{2,1,0:T(8,128)(2,1)S(1)}, u32[]{:S(2)}, u32[]{:S(2)}) collective-permute-start(bf16[2,256,384]{2,1,0:T(8,128)(2,1)S(1)} %get-tuple-element.26.p23), channel_id=1, source_target_pairs={{0,132},{8,11},{16,148},{24,27},{32,164},{40,43},{48,180},{56,59},... | collective-permute-start | bytes 1179656 | tf_op jit(solution)/shard_map/ppermute | solution.py:50
  33.9 2.7 %collective-permute-start.11 = (bf16[2,256,384]{2,1,0:T(8,128)(2,1)S(1)}, bf16[2,256,384]{2,1,0:T(8,128)(2,1)S(1)}, u32[]{:S(2)}, u32[]{:S(2)}) collective-permute-start(bf16[2,256,384]{2,1,0:T(8,128)(2,1)S(1)} %pad_maximum_fusion.p01), channel_id=1, source_target_pairs={{0,132},{8,11},{16,148},{24,27},{32,164},{40,43},{48,180},{56,59},... | collective-permute-start | bytes 1179656 | tf_op jit(solution)/shard_map/ppermute | solution.py:50
  36.6 2.1 %collective-permute-done.9.g1 = bf16[2,256,384]{2,1,0:T(8,128)(2,1)S(1)} collective-permute-done((bf16[2,256,384]{2,1,0:T(8,128)(2,1)S(1)}, bf16[2,256,384]{2,1,0:T(8,128)(2,1)S(1)}, u32[]{:S(2)}, u32[]{:S(2)}) %collective-permute-start.9) | collective-permute-done | bytes 393248 | tf_op jit(solution)/shard_map/ppermute | solution.py:50
  38.6 3.4 %collective-permute-start.13 = (bf16[2,256,384]{2,1,0:T(8,128)(2,1)S(1)}, bf16[2,256,384]{2,1,0:T(8,128)(2,1)S(1)}, u32[]{:S(2)}, u32[]{:S(2)}) collective-permute-start(bf16[2,256,384]{2,1,0:T(8,128)(2,1)S(1)} %collective-permute-done.9.g1), channel_id=1, source_target_pairs={{0,132},{8,11},{16,148},{24,27},{32,164},{40,43},{48,180},{56,59},... | collective-permute-start | bytes 1179656 | tf_op jit(solution)/shard_map/ppermute | solution.py:50
  42.0 2.4 %collective-permute-start.14 = (bf16[1,256,384]{2,1,0:T(8,128)(2,1)S(1)}, bf16[1,256,384]{2,1,0:T(8,128)(2,1)S(1)}, u32[]{:S(2)}, u32[]{:S(2)}) collective-permute-start(bf16[1,256,384]{2,1,0:T(8,128)(2,1)S(1)} %bitcast.15), channel_id=1, source_target_pairs={{0,8},{8,0},{16,24},{24,16},{32,40},{40,32},{48,56},{56,48},{64,72... | collective-permute-start | bytes 589832 | tf_op jit(solution)/shard_map/ppermute | solution.py:50
  44.7 2.3 %copy-done = bf16[2,384,3072]{2,1,0:T(8,128)(2,1)S(1)} copy-done((bf16[2,384,3072]{2,1,0:T(8,128)(2,1)S(1)}, bf16[2,384,3072]{2,1,0:T(8,128)(2,1)}, u32[]{:S(2)}) %copy-start) | copy-done | bytes 4718616
  47.0 2.7 %load.1.w = bf16[4,384,3072]{2,1,0:T(8,128)(2,1)S(1)} custom-call(bf16[2,384,3072]{2,1,0:T(8,128)(2,1)S(1)} %copy-done, bf16[2,384,3072]{2,1,0:T(8,128)(2,1)} %collective-permute-done.4.other), custom_call_target="tpu_custom_call" | custom-call | bytes 18874368 | tf_op jit(solution)/shard_map/load/pallas_call | solution.py:90
  49.9 7.2 %solve.1 = f32[8,2,16,128]{3,2,1,0:T(8,128)S(1)} custom-call(s32[4,64]{1,0:T(4,128)S(1)} %select_reduce_fusion.partner, f32[1,384]{1,0:T(1,128)S(1)} %reshape.12.coulomb, bf16[4,384,3072]{2,1,0:T(8,128)(2,1)S(1)} %load.1.w, bf16[2,256,384]{2,1,0:T(8,128)(2,1)S(1)} %pad_maximum_fusion.p01, bf16[2,256,384]{2,1,0:T(8,128)(2,1)S(1)} %get-tuple-element.26.p23, ...), custom_call_target="tpu_custom_call" | custom-call | flops 4831838208 | bytes 9437184 | tf_op jit(solution)/shard_map/solve/pallas_call | solution.py:160
  57.1 13.3 %all_to_all.10.terms = f32[8,2,16,128]{3,2,1,0:T(8,128)S(1)} all-to-all(f32[8,2,16,128]{3,2,1,0:T(8,128)S(1)} %solve.1), channel_id=1, replica_groups=mesh['row'=32,'col'=8] {'col'}, dimensions={0} | all-to-all | bytes 262144 | tf_op jit(solution)/shard_map/all_to_all | solution.py:290
  70.6 16.3 %all_to_all.11.arrived = bf16[32,16,128]{2,1,0:T(8,128)(2,1)S(1)} all-to-all(bf16[32,16,128]{2,1,0:T(8,128)(2,1)S(1)} %spread.1), channel_id=1, replica_groups=mesh['row'=32,'col'=8] {'row'}, dimensions={0} | all-to-all | bytes 262144 | tf_op jit(solution)/shard_map/all_to_all | solution.py:292
  (30 shorter events, 3.9 us)
Async XLA Ops:
  0.0 10.9 %collective-permute-start.2 = (bf16[1,32,384]{2,1,0:T(8,128)(2,1)}, bf16[1,32,384]{2,1,0:T(8,128)(2,1)S(1)}, u32[]{:S(2)}, u32[]{:S(2)}) collective-permute-start(bf16[1,32,384]{2,1,0:T(8,128)(2,1)} %bitcast.16), channel_id=1, source_target_pairs={{0,96},{8,104},{16,112},{24,120},{32,0},{40,8},{48,16},{56,24},{64... | collective-permute-start | bytes 73736 | tf_op jit(solution)/shard_map/ppermute | solution.py:50
  6.9 6.8 %collective-permute-start.1 = (bf16[1,32,384]{2,1,0:T(8,128)(2,1)}, bf16[1,32,384]{2,1,0:T(8,128)(2,1)S(1)}, u32[]{:S(2)}, u32[]{:S(2)}) collective-permute-start(bf16[1,32,384]{2,1,0:T(8,128)(2,1)} %bitcast.17), channel_id=1, source_target_pairs={{0,64},{8,72},{16,80},{24,88},{32,96},{40,104},{48,112},{56,120},{... | collective-permute-start | bytes 73736 | tf_op jit(solution)/shard_map/ppermute | solution.py:50
  7.7 5.9 %collective-permute-start = (bf16[1,32,384]{2,1,0:T(8,128)(2,1)}, bf16[1,32,384]{2,1,0:T(8,128)(2,1)S(1)}, u32[]{:S(2)}, u32[]{:S(2)}) collective-permute-start(bf16[1,32,384]{2,1,0:T(8,128)(2,1)} %bitcast.18), channel_id=1, source_target_pairs={{0,32},{8,40},{16,48},{24,56},{32,64},{40,72},{48,80},{56,88},{64,... | collective-permute-start | bytes 73736 | tf_op jit(solution)/shard_map/ppermute | solution.py:50
  14.4 3.6 %collective-permute-start.3 = (bf16[4,32,384]{2,1,0:T(8,128)(2,1)S(1)}, bf16[4,32,384]{2,1,0:T(8,128)(2,1)S(1)}, u32[]{:S(2)}, u32[]{:S(2)}) collective-permute-start(bf16[4,32,384]{2,1,0:T(8,128)(2,1)S(1)} %pad_maximum_fusion.1), channel_id=1, source_target_pairs={{0,16},{8,24},{16,0},{24,8},{32,48},{40,56},{48,32},{56,40},{64,80... | collective-permute-start | bytes 294920 | tf_op jit(solution)/shard_map/ppermute | solution.py:50
  18.0 24.1 %collective-permute-start.4 = (bf16[2,384,3072]{2,1,0:T(8,128)(2,1)}, bf16[2,384,3072]{2,1,0:T(8,128)(2,1)}, u32[]{:S(2)}, u32[]{:S(2)}) collective-permute-start(bf16[2,384,3072]{2,1,0:T(8,128)(2,1)} %own), channel_id=1, source_target_pairs={{0,8},{8,0},{16,24},{24,16},{32,40},{40,32},{48,56},{56,48},{64,72... | collective-permute-start | bytes 14155784 | tf_op jit(solution)/shard_map/ppermute | solution.py:50
  22.0 6.2 %collective-permute-start.5 = (bf16[1,256,384]{2,1,0:T(8,128)(2,1)S(1)}, bf16[1,256,384]{2,1,0:T(8,128)(2,1)S(1)}, u32[]{:S(2)}, u32[]{:S(2)}) collective-permute-start(bf16[1,256,384]{2,1,0:T(8,128)(2,1)S(1)} %bitcast.10), channel_id=1, source_target_pairs={{0,1},{8,136},{16,17},{24,152},{32,33},{40,168},{48,49},{56,184},{... | collective-permute-start | bytes 589832 | tf_op jit(solution)/shard_map/ppermute | solution.py:50
  23.4 8.1 %collective-permute-start.7 = (bf16[1,256,384]{2,1,0:T(8,128)(2,1)S(1)}, bf16[1,256,384]{2,1,0:T(8,128)(2,1)S(1)}, u32[]{:S(2)}, u32[]{:S(2)}) collective-permute-start(bf16[1,256,384]{2,1,0:T(8,128)(2,1)S(1)} %bitcast.11), channel_id=1, source_target_pairs={{0,2},{8,12},{16,18},{24,28},{32,34},{40,44},{48,50},{56,60},{64,6... | collective-permute-start | bytes 589832 | tf_op jit(solution)/shard_map/ppermute | solution.py:50
  26.0 5.5 %collective-permute-start.8 = (bf16[1,256,384]{2,1,0:T(8,128)(2,1)S(1)}, bf16[1,256,384]{2,1,0:T(8,128)(2,1)S(1)}, u32[]{:S(2)}, u32[]{:S(2)}) collective-permute-start(bf16[1,256,384]{2,1,0:T(8,128)(2,1)S(1)} %bitcast.12), channel_id=1, source_target_pairs={{0,3},{8,140},{16,19},{24,156},{32,35},{40,172},{48,51},{56,188},{... | collective-permute-start | bytes 589832 | tf_op jit(solution)/shard_map/ppermute | solution.py:50
  28.2 8.3 %collective-permute-start.6 = (bf16[2,256,384]{2,1,0:T(8,128)(2,1)S(1)}, bf16[2,256,384]{2,1,0:T(8,128)(2,1)S(1)}, u32[]{:S(2)}, u32[]{:S(2)}) collective-permute-start(bf16[2,256,384]{2,1,0:T(8,128)(2,1)S(1)} %pad_maximum_fusion.p01), channel_id=1, source_target_pairs={{0,128},{8,9},{16,144},{24,25},{32,160},{40,41},{48,176},{56,57},{... | collective-permute-start | bytes 1179656 | tf_op jit(solution)/shard_map/ppermute | solution.py:50
  31.6 7.0 %collective-permute-start.9 = (bf16[2,256,384]{2,1,0:T(8,128)(2,1)S(1)}, bf16[2,256,384]{2,1,0:T(8,128)(2,1)S(1)}, u32[]{:S(2)}, u32[]{:S(2)}) collective-permute-start(bf16[2,256,384]{2,1,0:T(8,128)(2,1)S(1)} %get-tuple-element.26.p23), channel_id=1, source_target_pairs={{0,132},{8,11},{16,148},{24,27},{32,164},{40,43},{48,180},{56,59},... | collective-permute-start | bytes 1179656 | tf_op jit(solution)/shard_map/ppermute | solution.py:50
  33.9 10.5 %collective-permute-start.10 = (bf16[2,256,384]{2,1,0:T(8,128)(2,1)S(1)}, bf16[2,256,384]{2,1,0:T(8,128)(2,1)S(1)}, u32[]{:S(2)}, u32[]{:S(2)}) collective-permute-start(bf16[2,256,384]{2,1,0:T(8,128)(2,1)S(1)} %get-tuple-element.26.p23), channel_id=1, source_target_pairs={{0,128},{8,9},{16,144},{24,25},{32,160},{40,41},{48,176},{56,57},{... | collective-permute-start | bytes 1179656 | tf_op jit(solution)/shard_map/ppermute | solution.py:50
  33.9 15.8 %collective-permute-start.11 = (bf16[2,256,384]{2,1,0:T(8,128)(2,1)S(1)}, bf16[2,256,384]{2,1,0:T(8,128)(2,1)S(1)}, u32[]{:S(2)}, u32[]{:S(2)}) collective-permute-start(bf16[2,256,384]{2,1,0:T(8,128)(2,1)S(1)} %pad_maximum_fusion.p01), channel_id=1, source_target_pairs={{0,132},{8,11},{16,148},{24,27},{32,164},{40,43},{48,180},{56,59},... | collective-permute-start | bytes 1179656 | tf_op jit(solution)/shard_map/ppermute | solution.py:50
  36.6 13.2 %collective-permute-start.12 = (bf16[2,256,384]{2,1,0:T(8,128)(2,1)S(1)}, bf16[2,256,384]{2,1,0:T(8,128)(2,1)S(1)}, u32[]{:S(2)}, u32[]{:S(2)}) collective-permute-start(bf16[2,256,384]{2,1,0:T(8,128)(2,1)S(1)} %collective-permute-done.6.f0), channel_id=1, source_target_pairs={{0,128},{8,9},{16,144},{24,25},{32,160},{40,41},{48,176},{56,57},{... | collective-permute-start | bytes 1179656 | tf_op jit(solution)/shard_map/ppermute | solution.py:50
  38.6 11.1 %collective-permute-start.13 = (bf16[2,256,384]{2,1,0:T(8,128)(2,1)S(1)}, bf16[2,256,384]{2,1,0:T(8,128)(2,1)S(1)}, u32[]{:S(2)}, u32[]{:S(2)}) collective-permute-start(bf16[2,256,384]{2,1,0:T(8,128)(2,1)S(1)} %collective-permute-done.9.g1), channel_id=1, source_target_pairs={{0,132},{8,11},{16,148},{24,27},{32,164},{40,43},{48,180},{56,59},... | collective-permute-start | bytes 1179656 | tf_op jit(solution)/shard_map/ppermute | solution.py:50
  42.0 7.7 %collective-permute-start.14 = (bf16[1,256,384]{2,1,0:T(8,128)(2,1)S(1)}, bf16[1,256,384]{2,1,0:T(8,128)(2,1)S(1)}, u32[]{:S(2)}, u32[]{:S(2)}) collective-permute-start(bf16[1,256,384]{2,1,0:T(8,128)(2,1)S(1)} %bitcast.15), channel_id=1, source_target_pairs={{0,8},{8,0},{16,24},{24,16},{32,40},{40,32},{48,56},{56,48},{64,72... | collective-permute-start | bytes 589832 | tf_op jit(solution)/shard_map/ppermute | solution.py:50
  44.4 5.5 %collective-permute-start.15 = (bf16[1,256,384]{2,1,0:T(8,128)(2,1)S(1)}, bf16[1,256,384]{2,1,0:T(8,128)(2,1)S(1)}, u32[]{:S(2)}, u32[]{:S(2)}) collective-permute-start(bf16[1,256,384]{2,1,0:T(8,128)(2,1)S(1)} %get-tuple-element.24), channel_id=1, source_target_pairs={{0,136},{8,0},{16,152},{24,16},{32,168},{40,32},{48,184},{56,48},{... | collective-permute-start | bytes 589832 | tf_op jit(solution)/shard_map/ppermute | solution.py:50
  44.7 2.3 %copy-start = (bf16[2,384,3072]{2,1,0:T(8,128)(2,1)S(1)}, bf16[2,384,3072]{2,1,0:T(8,128)(2,1)}, u32[]{:S(2)}) copy-start(bf16[2,384,3072]{2,1,0:T(8,128)(2,1)} %own) | copy-start | bytes 14155780
  49.7 20.7 %copy-start.1 = (s32[64,64]{1,0:T(8,128)S(1)}, s32[64,64]{1,0:T(8,128)}, u32[]{:S(2)}) copy-start(s32[64,64]{1,0:T(8,128)} %q_index.1) | copy-start | bytes 49156

commit v14 on v12

--- a/solution.py
+++ b/solution.py
@@ -102,19 +102,25 @@
 
 
 def solve_kernel(
-    partner, coulomb, w, p01, p23, f0, f1, g0, g1, ff0, gg1, near, far, out,
+    partner, coulomb, w, p01, p23, two01, two2, two3, up01, up23, down012, down3, near, far, out,
     panel, left_rows, image,
 ):
     rows, share = p01.shape[1:]
     _, j, c, _, y_lo = where_am_i()
     starts = [pl.multiple_of(place_of(z) * 32, 32) for z in range(NZ)]
-    arrays = ((p01, p23), (ff0, gg1), (f0, f1), (g0, g1))
+    pieces = (
+        ((p01, 0), (p01, 1), (p23, 0), (p23, 1)),
+        ((two01, 0), (two01, 1), (two2, 0), (two3, 0)),
+        ((up01, 0), (up01, 1), (up23, 0), (up23, 1)),
+        ((down012, 0), (down012, 1), (down012, 2), (down3, 0)),
+    )
     for k in range(4):
         for i in range(4):
             col, low = spot(k, i)
+            array, at = pieces[k][i]
             for z in range(NZ):
                 to = pl.multiple_of(low * rows + z * 32, 32)
-                piece = arrays[k][i // 2][i % 2, pl.ds(starts[z], 32), :]
+                piece = array[at, pl.ds(starts[z], 32), :]
                 panel[pl.ds(to, 32), pl.ds(pl.multiple_of(col * share, share), share)] = piece
     left_rows[: 2 * rows, :] = panel[:, pl.ds(pl.multiple_of(j * share, share), share)]
     for low, stack in ((y_lo, near), (1 - y_lo, far)):
@@ -159,7 +165,7 @@
     vmem = pl.BlockSpec(memory_space=pltpu.VMEM)
     return pl.pallas_call(
         solve_kernel,
-        in_specs=[pl.BlockSpec(memory_space=pltpu.SMEM)] + [vmem] * 12,
+        in_specs=[pl.BlockSpec(memory_space=pltpu.SMEM)] + [vmem] * 13,
         out_specs=vmem,
         out_shape=jax.ShapeDtypeStruct((8, 2, 16, 128), jnp.float32),
         scratch_shapes=[
@@ -267,25 +273,27 @@
     )
     stack = jnp.concatenate([even, paired], axis=0).reshape(1, NZ * 32, share)
     parts = [send(stack, first_plane(s)) for s in FIRST[1:]]
-    parts[0], near = lax.optimization_barrier((parts[0], send(stack, SWAP)))
     p01 = jnp.concatenate([stack, parts[0]], axis=0)
     p23 = jnp.concatenate([parts[1], parts[2]], axis=0)
 
-    f0 = send(p01, second_plane(1))
-    g1 = send(p23, second_plane(-1))
-    g0 = send(p01, second_plane(-1))
-    f1 = send(p23, second_plane(1))
-    ff0 = send(f0, second_plane(1))
-    gg1 = send(g1, second_plane(-1))
+    up01 = send(p01, second_plane(1))
+    down3 = send(parts[2], second_plane(-1))
+    opposite, _ = lax.optimization_barrier((parts[1], parts[2]))
+    up23 = send(p23, second_plane(1))
+    down012 = send(jnp.concatenate([stack, parts[0], opposite], axis=0), second_plane(-1))
+    two2 = send(opposite, second_plane(2))
+    two01 = send(up01, second_plane(1))
+    two3 = send(down3, second_plane(-1))
 
     core, low = r & 1, r >> 4
     passed = jnp.where(core == 0, stack, jnp.where(low == 0, parts[2], parts[0]))
-    w_own, w_other, f0, g1, passed = lax.optimization_barrier(
-        (screened, w_other, f0, g1, passed)
+    w_own, w_other, up01, down3, passed, kept = lax.optimization_barrier(
+        (screened, w_other, up01, down3, passed, stack)
     )
+    near = send(kept, SWAP)
     far = send(passed, ACROSS)
     w = load(w_own, w_other)
-    panels = (p01, p23, f0, f1, g0, g1, ff0, gg1)
+    panels = (p01, p23, two01, two2, two3, up01, up23, down012, down3)
     terms = solve(partner, coulomb, w, panels, near, far)
     terms = lax.all_to_all(terms, "col", split_axis=0, concat_axis=0, tiled=True)
     placed = spread(q_index, terms)

time: 87.8 us -> 98.2 us (1.12)
  waiting for transfers between devices: 10.5 us -> 16.9 us
  starting transfers between devices: 33 us -> 35.7 us
  blocking collectives: 27.3 us -> 28.5 us
    ppermute x16 -> x17, waiting for transfers between devices: 10.5 us -> 16.9 us  [send(): return lax.ppermute(value, AXES, perm)]
    ppermute x16 -> x17, starting transfers between devices: 33 us -> 35.7 us  [send(): return lax.ppermute(value, AXES, perm)]
    all_to_all x1, blocking collectives: 11.1 us -> 12.3 us  [local(): lax.all_to_all(terms, 'col', split_axis=0, concat_axis=0, tiled=True)]
  transfers between devices with their start and end apart: 16 -> 17, of which waited for: 6 -> 6; matrix products, arithmetic and copies ran while one was open for 4% -> 3% of each run, Pallas kernels for 3% -> 3%
where the time goes in v14:
time: 98.2 us; the launch traced here: 97.8 us
  starting transfers between devices  35.7 us (36%)
  blocking collectives  28.5 us (29%)
  waiting for transfers between devices  16.9 us (17%)
  Pallas kernels  10.9 us (11%)
  local copies, waits for them, and re-layouts  3.83 us (4%)
  other arithmetic  1.93 us (2%)
    ppermute x17, starting transfers between devices, send(): return lax.ppermute(value, AXES, perm)  35.7 us
    ppermute x17, waiting for transfers between devices, send(): return lax.ppermute(value, AXES, perm)  16.9 us
    all_to_all x1, blocking collectives, local(): lax.all_to_all(placed, 'row', split_axis=0, concat_axis=0, tiled=True)  16.2 us
    all_to_all x1, blocking collectives, local(): lax.all_to_all(terms, 'col', split_axis=0, concat_axis=0, tiled=True)  12.3 us
    pallas_call x1, Pallas kernels, solve(): pl.pallas_call(solve_kernel, in_specs=[pl.BlockSpec(memory_space=pltpu.SM...  7.24 us
    unnamed x9, local copies, waits for them, and re-layouts  3.13 us
    pallas_call x1, Pallas kernels, load(): pl.pallas_call(load_kernel, in_specs=[pl.BlockSpec(memory_space=pl.ANY)]...  2.72 us
  transfers between devices with their start and end apart: 17, of which 6 were waited for; matrix products, arithmetic and copies ran while one was open for 3% of the time, Pallas kernels for 3%

profile of v14, /device:TPU:1, one launch (start us, length us, event | category | flops | bytes accessed | tf_op | source)
XLA Modules:
  0.0 97.8 jit_solution(14046480810455429843)
XLA Ops:
  0.0 3.2 %collective-permute-start.4 = (bf16[2,384,3072]{2,1,0:T(8,128)(2,1)}, bf16[2,384,3072]{2,1,0:T(8,128)(2,1)}, u32[]{:S(2)}, u32[]{:S(2)}) collective-permute-start(bf16[2,384,3072]{2,1,0:T(8,128)(2,1)} %own), channel_id=1, source_target_pairs={{0,8},{8,0},{16,24},{24,16},{32,40},{40,32},{48,56},{56,48},{64,72... | collective-permute-start | bytes 14155784 | tf_op jit(solution)/shard_map/ppermute | solution.py:50
  3.2 4.3 %collective-permute-start.2 = (bf16[1,32,384]{2,1,0:T(8,128)(2,1)}, bf16[1,32,384]{2,1,0:T(8,128)(2,1)S(1)}, u32[]{:S(2)}, u32[]{:S(2)}) collective-permute-start(bf16[1,32,384]{2,1,0:T(8,128)(2,1)} %bitcast.16), channel_id=1, source_target_pairs={{0,96},{8,104},{16,112},{24,120},{32,0},{40,8},{48,16},{56,24},{64... | collective-permute-start | bytes 73736 | tf_op jit(solution)/shard_map/ppermute | solution.py:50
  7.5 0.9 collective-permute-start.1
  8.4 2.3 %collective-permute-start = (bf16[1,32,384]{2,1,0:T(8,128)(2,1)}, bf16[1,32,384]{2,1,0:T(8,128)(2,1)S(1)}, u32[]{:S(2)}, u32[]{:S(2)}) collective-permute-start(bf16[1,32,384]{2,1,0:T(8,128)(2,1)} %bitcast.18), channel_id=1, source_target_pairs={{0,32},{8,40},{16,48},{24,56},{32,64},{40,72},{48,80},{56,88},{64,... | collective-permute-start | bytes 73736 | tf_op jit(solution)/shard_map/ppermute | solution.py:50
  13.1 1.3 %collective-permute-done.1 = bf16[1,32,384]{2,1,0:T(8,128)(2,1)S(1)} collective-permute-done((bf16[1,32,384]{2,1,0:T(8,128)(2,1)}, bf16[1,32,384]{2,1,0:T(8,128)(2,1)S(1)}, u32[]{:S(2)}, u32[]{:S(2)}) %collective-permute-start.1) | collective-permute-done | bytes 24608 | tf_op jit(solution)/shard_map/ppermute | solution.py:50
  15.9 2.8 %collective-permute-done.3 = bf16[4,32,384]{2,1,0:T(8,128)(2,1)S(1)} collective-permute-done((bf16[4,32,384]{2,1,0:T(8,128)(2,1)S(1)}, bf16[4,32,384]{2,1,0:T(8,128)(2,1)S(1)}, u32[]{:S(2)}, u32[]{:S(2)}) %collective-permute-start.3) | collective-permute-done | bytes 98336 | tf_op jit(solution)/shard_map/ppermute | solution.py:50
  18.8 1.4 %collective-permute-start.5 = (bf16[1,256,384]{2,1,0:T(8,128)(2,1)S(1)}, bf16[1,256,384]{2,1,0:T(8,128)(2,1)S(1)}, u32[]{:S(2)}, u32[]{:S(2)}) collective-permute-start(bf16[1,256,384]{2,1,0:T(8,128)(2,1)S(1)} %bitcast.9), channel_id=1, source_target_pairs={{0,1},{8,136},{16,17},{24,152},{32,33},{40,168},{48,49},{56,184},{... | collective-permute-start | bytes 589832 | tf_op jit(solution)/shard_map/ppermute | solution.py:50
  20.2 1.5 %collective-permute-start.7 = (bf16[1,256,384]{2,1,0:T(8,128)(2,1)S(1)}, bf16[1,256,384]{2,1,0:T(8,128)(2,1)S(1)}, u32[]{:S(2)}, u32[]{:S(2)}) collective-permute-start(bf16[1,256,384]{2,1,0:T(8,128)(2,1)S(1)} %bitcast.10), channel_id=1, source_target_pairs={{0,3},{8,140},{16,19},{24,156},{32,35},{40,172},{48,51},{56,188},{... | collective-permute-start | bytes 589832 | tf_op jit(solution)/shard_map/ppermute | solution.py:50
  21.7 1.6 %collective-permute-start.9 = (bf16[1,256,384]{2,1,0:T(8,128)(2,1)S(1)}, bf16[1,256,384]{2,1,0:T(8,128)(2,1)S(1)}, u32[]{:S(2)}, u32[]{:S(2)}) collective-permute-start(bf16[1,256,384]{2,1,0:T(8,128)(2,1)S(1)} %bitcast.11), channel_id=1, source_target_pairs={{0,2},{8,12},{16,18},{24,28},{32,34},{40,44},{48,50},{56,60},{64,6... | collective-permute-start | bytes 589832 | tf_op jit(solution)/shard_map/ppermute | solution.py:50
  23.3 1.4 %collective-permute-done.5 = bf16[1,256,384]{2,1,0:T(8,128)(2,1)S(1)} collective-permute-done((bf16[1,256,384]{2,1,0:T(8,128)(2,1)S(1)}, bf16[1,256,384]{2,1,0:T(8,128)(2,1)S(1)}, u32[]{:S(2)}, u32[]{:S(2)}) %collective-permute-start.5) | collective-permute-done | bytes 196640 | tf_op jit(solution)/shard_map/ppermute | solution.py:50
  24.7 1.3 %collective-permute-start.6 = (bf16[2,256,384]{2,1,0:T(8,128)(2,1)S(1)}, bf16[2,256,384]{2,1,0:T(8,128)(2,1)S(1)}, u32[]{:S(2)}, u32[]{:S(2)}) collective-permute-start(bf16[2,256,384]{2,1,0:T(8,128)(2,1)S(1)} %pad_maximum_fusion.1.p01), channel_id=1, source_target_pairs={{0,128},{8,9},{16,144},{24,25},{32,160},{40,41},{48,176},{56,57},{... | collective-permute-start | bytes 1179656 | tf_op jit(solution)/shard_map/ppermute | solution.py:50
  26.4 1.5 %collective-permute-done.9 = bf16[1,256,384]{2,1,0:T(8,128)(2,1)S(1)} collective-permute-done((bf16[1,256,384]{2,1,0:T(8,128)(2,1)S(1)}, bf16[1,256,384]{2,1,0:T(8,128)(2,1)S(1)}, u32[]{:S(2)}, u32[]{:S(2)}) %collective-permute-start.9) | collective-permute-done | bytes 196640 | tf_op jit(solution)/shard_map/ppermute | solution.py:50
  27.9 2.7 %collective-permute-start.11 = (bf16[1,256,384]{2,1,0:T(8,128)(2,1)S(1)}, bf16[1,256,384]{2,1,0:T(8,128)(2,1)S(1)}, u32[]{:S(2)}, u32[]{:S(2)}) collective-permute-start(bf16[1,256,384]{2,1,0:T(8,128)(2,1)S(1)} %collective-permute-done.9), channel_id=1, source_target_pairs={{0,4},{8,10},{16,20},{24,26},{32,36},{40,42},{48,52},{56,58},{64,6... | collective-permute-start | bytes 589832 | tf_op jit(solution)/shard_map/ppermute | solution.py:50
  30.8 0.9 collective-permute-start.14
  31.9 1.5 %collective-permute-start.13 = (bf16[2,256,384]{2,1,0:T(8,128)(2,1)S(1)}, bf16[2,256,384]{2,1,0:T(8,128)(2,1)S(1)}, u32[]{:S(2)}, u32[]{:S(2)}) collective-permute-start(bf16[2,256,384]{2,1,0:T(8,128)(2,1)S(1)} %get-tuple-element.27.p23), channel_id=1, source_target_pairs={{0,128},{8,9},{16,144},{24,25},{32,160},{40,41},{48,176},{56,57},{... | collective-permute-start | bytes 1179656 | tf_op jit(solution)/shard_map/ppermute | solution.py:50
  33.4 9.4 %collective-permute-done.8.down3 = bf16[1,256,384]{2,1,0:T(8,128)(2,1)S(1)} collective-permute-done((bf16[1,256,384]{2,1,0:T(8,128)(2,1)S(1)}, bf16[1,256,384]{2,1,0:T(8,128)(2,1)S(1)}, u32[]{:S(2)}, u32[]{:S(2)}) %collective-permute-start.8) | collective-permute-done | bytes 196640 | tf_op jit(solution)/shard_map/ppermute | solution.py:50
  42.8 2.4 %collective-permute-start.12 = (bf16[1,256,384]{2,1,0:T(8,128)(2,1)S(1)}, bf16[1,256,384]{2,1,0:T(8,128)(2,1)S(1)}, u32[]{:S(2)}, u32[]{:S(2)}) collective-permute-start(bf16[1,256,384]{2,1,0:T(8,128)(2,1)S(1)} %collective-permute-done.8.down3), channel_id=1, source_target_pairs={{0,132},{8,11},{16,148},{24,27},{32,164},{40,43},{48,180},{56,59},... | collective-permute-start | bytes 589832 | tf_op jit(solution)/shard_map/ppermute | solution.py:50
  45.2 7.8 %collective-permute-start.15 = (bf16[1,256,384]{2,1,0:T(8,128)(2,1)S(1)}, bf16[1,256,384]{2,1,0:T(8,128)(2,1)S(1)}, u32[]{:S(2)}, u32[]{:S(2)}) collective-permute-start(bf16[1,256,384]{2,1,0:T(8,128)(2,1)S(1)} %bitcast.15), channel_id=1, source_target_pairs={{0,8},{8,0},{16,24},{24,16},{32,40},{40,32},{48,56},{56,48},{64,72... | collective-permute-start | bytes 589832 | tf_op jit(solution)/shard_map/ppermute | solution.py:50
  53.0 3.1 %collective-permute-start.16 = (bf16[1,256,384]{2,1,0:T(8,128)(2,1)S(1)}, bf16[1,256,384]{2,1,0:T(8,128)(2,1)S(1)}, u32[]{:S(2)}, u32[]{:S(2)}) collective-permute-start(bf16[1,256,384]{2,1,0:T(8,128)(2,1)S(1)} %get-tuple-element.26), channel_id=1, source_target_pairs={{0,136},{8,0},{16,152},{24,16},{32,168},{40,32},{48,184},{56,48},{... | collective-permute-start | bytes 589832 | tf_op jit(solution)/shard_map/ppermute | solution.py:50
  56.1 2.3 %copy-done = bf16[2,384,3072]{2,1,0:T(8,128)(2,1)S(1)} copy-done((bf16[2,384,3072]{2,1,0:T(8,128)(2,1)S(1)}, bf16[2,384,3072]{2,1,0:T(8,128)(2,1)}, u32[]{:S(2)}) %copy-start) | copy-done | bytes 4718616
  58.4 2.7 %load.1.w = bf16[4,384,3072]{2,1,0:T(8,128)(2,1)S(1)} custom-call(bf16[2,384,3072]{2,1,0:T(8,128)(2,1)S(1)} %copy-done, bf16[2,384,3072]{2,1,0:T(8,128)(2,1)} %collective-permute-done.4.other), custom_call_target="tpu_custom_call" | custom-call | bytes 18874368 | tf_op jit(solution)/shard_map/load/pallas_call | solution.py:90
  61.2 7.2 %solve.1 = f32[8,2,16,128]{3,2,1,0:T(8,128)S(1)} custom-call(s32[4,64]{1,0:T(4,128)S(1)} %select_reduce_fusion.partner, f32[1,384]{1,0:T(1,128)S(1)} %reshape.12.coulomb, bf16[4,384,3072]{2,1,0:T(8,128)(2,1)S(1)} %load.1.w, bf16[2,256,384]{2,1,0:T(8,128)(2,1)S(1)} %pad_maximum_fusion.1.p01, bf16[2,256,384]{2,1,0:T(8,128)(2,1)S(1)} %get-tuple-element.27.p23, ...), custom_call_target="tpu_custom_call" | custom-call | flops 4831838208 | bytes 9437184 | tf_op jit(solution)/shard_map/solve/pallas_call | solution.py:166
  68.4 12.3 %all_to_all.10.terms = f32[8,2,16,128]{3,2,1,0:T(8,128)S(1)} all-to-all(f32[8,2,16,128]{3,2,1,0:T(8,128)S(1)} %solve.1), channel_id=1, replica_groups=mesh['row'=32,'col'=8] {'col'}, dimensions={0} | all-to-all | bytes 262144 | tf_op jit(solution)/shard_map/all_to_all | solution.py:298
  80.9 16.2 %all_to_all.11.arrived = bf16[32,16,128]{2,1,0:T(8,128)(2,1)S(1)} all-to-all(bf16[32,16,128]{2,1,0:T(8,128)(2,1)S(1)} %spread.1), channel_id=1, replica_groups=mesh['row'=32,'col'=8] {'row'}, dimensions={0} | all-to-all | bytes 262144 | tf_op jit(solution)/shard_map/all_to_all | solution.py:300
  (33 shorter events, 5.6 us)
Async XLA Ops:
  0.0 18.8 %collective-permute-start.4 = (bf16[2,384,3072]{2,1,0:T(8,128)(2,1)}, bf16[2,384,3072]{2,1,0:T(8,128)(2,1)}, u32[]{:S(2)}, u32[]{:S(2)}) collective-permute-start(bf16[2,384,3072]{2,1,0:T(8,128)(2,1)} %own), channel_id=1, source_target_pairs={{0,8},{8,0},{16,24},{24,16},{32,40},{40,32},{48,56},{56,48},{64,72... | collective-permute-start | bytes 14155784 | tf_op jit(solution)/shard_map/ppermute | solution.py:50
  3.2 9.9 %collective-permute-start.2 = (bf16[1,32,384]{2,1,0:T(8,128)(2,1)}, bf16[1,32,384]{2,1,0:T(8,128)(2,1)S(1)}, u32[]{:S(2)}, u32[]{:S(2)}) collective-permute-start(bf16[1,32,384]{2,1,0:T(8,128)(2,1)} %bitcast.16), channel_id=1, source_target_pairs={{0,96},{8,104},{16,112},{24,120},{32,0},{40,8},{48,16},{56,24},{64... | collective-permute-start | bytes 73736 | tf_op jit(solution)/shard_map/ppermute | solution.py:50
  7.5 6.9 %collective-permute-start.1 = (bf16[1,32,384]{2,1,0:T(8,128)(2,1)}, bf16[1,32,384]{2,1,0:T(8,128)(2,1)S(1)}, u32[]{:S(2)}, u32[]{:S(2)}) collective-permute-start(bf16[1,32,384]{2,1,0:T(8,128)(2,1)} %bitcast.17), channel_id=1, source_target_pairs={{0,64},{8,72},{16,80},{24,88},{32,96},{40,104},{48,112},{56,120},{... | collective-permute-start | bytes 73736 | tf_op jit(solution)/shard_map/ppermute | solution.py:50
  8.4 6.0 %collective-permute-start = (bf16[1,32,384]{2,1,0:T(8,128)(2,1)}, bf16[1,32,384]{2,1,0:T(8,128)(2,1)S(1)}, u32[]{:S(2)}, u32[]{:S(2)}) collective-permute-start(bf16[1,32,384]{2,1,0:T(8,128)(2,1)} %bitcast.18), channel_id=1, source_target_pairs={{0,32},{8,40},{16,48},{24,56},{32,64},{40,72},{48,80},{56,88},{64,... | collective-permute-start | bytes 73736 | tf_op jit(solution)/shard_map/ppermute | solution.py:50
  15.2 3.6 %collective-permute-start.3 = (bf16[4,32,384]{2,1,0:T(8,128)(2,1)S(1)}, bf16[4,32,384]{2,1,0:T(8,128)(2,1)S(1)}, u32[]{:S(2)}, u32[]{:S(2)}) collective-permute-start(bf16[4,32,384]{2,1,0:T(8,128)(2,1)S(1)} %pad_maximum_fusion.2), channel_id=1, source_target_pairs={{0,16},{8,24},{16,0},{24,8},{32,48},{40,56},{48,32},{56,40},{64,80... | collective-permute-start | bytes 294920 | tf_op jit(solution)/shard_map/ppermute | solution.py:50
  18.8 5.9 %collective-permute-start.5 = (bf16[1,256,384]{2,1,0:T(8,128)(2,1)S(1)}, bf16[1,256,384]{2,1,0:T(8,128)(2,1)S(1)}, u32[]{:S(2)}, u32[]{:S(2)}) collective-permute-start(bf16[1,256,384]{2,1,0:T(8,128)(2,1)S(1)} %bitcast.9), channel_id=1, source_target_pairs={{0,1},{8,136},{16,17},{24,152},{32,33},{40,168},{48,49},{56,184},{... | collective-permute-start | bytes 589832 | tf_op jit(solution)/shard_map/ppermute | solution.py:50
  20.2 6.3 %collective-permute-start.7 = (bf16[1,256,384]{2,1,0:T(8,128)(2,1)S(1)}, bf16[1,256,384]{2,1,0:T(8,128)(2,1)S(1)}, u32[]{:S(2)}, u32[]{:S(2)}) collective-permute-start(bf16[1,256,384]{2,1,0:T(8,128)(2,1)S(1)} %bitcast.10), channel_id=1, source_target_pairs={{0,3},{8,140},{16,19},{24,156},{32,35},{40,172},{48,51},{56,188},{... | collective-permute-start | bytes 589832 | tf_op jit(solution)/shard_map/ppermute | solution.py:50
  21.7 6.3 %collective-permute-start.9 = (bf16[1,256,384]{2,1,0:T(8,128)(2,1)S(1)}, bf16[1,256,384]{2,1,0:T(8,128)(2,1)S(1)}, u32[]{:S(2)}, u32[]{:S(2)}) collective-permute-start(bf16[1,256,384]{2,1,0:T(8,128)(2,1)S(1)} %bitcast.11), channel_id=1, source_target_pairs={{0,2},{8,12},{16,18},{24,28},{32,34},{40,44},{48,50},{56,60},{64,6... | collective-permute-start | bytes 589832 | tf_op jit(solution)/shard_map/ppermute | solution.py:50
  24.7 20.5 %collective-permute-start.6 = (bf16[2,256,384]{2,1,0:T(8,128)(2,1)S(1)}, bf16[2,256,384]{2,1,0:T(8,128)(2,1)S(1)}, u32[]{:S(2)}, u32[]{:S(2)}) collective-permute-start(bf16[2,256,384]{2,1,0:T(8,128)(2,1)S(1)} %pad_maximum_fusion.1.p01), channel_id=1, source_target_pairs={{0,128},{8,9},{16,144},{24,25},{32,160},{40,41},{48,176},{56,57},{... | collective-permute-start | bytes 1179656 | tf_op jit(solution)/shard_map/ppermute | solution.py:50
  27.9 17.2 %collective-permute-start.11 = (bf16[1,256,384]{2,1,0:T(8,128)(2,1)S(1)}, bf16[1,256,384]{2,1,0:T(8,128)(2,1)S(1)}, u32[]{:S(2)}, u32[]{:S(2)}) collective-permute-start(bf16[1,256,384]{2,1,0:T(8,128)(2,1)S(1)} %collective-permute-done.9), channel_id=1, source_target_pairs={{0,4},{8,10},{16,20},{24,26},{32,36},{40,42},{48,52},{56,58},{64,6... | collective-permute-start | bytes 589832 | tf_op jit(solution)/shard_map/ppermute | solution.py:50
  30.8 30.4 %collective-permute-start.14 = (bf16[3,256,384]{2,1,0:T(8,128)(2,1)S(1)}, bf16[3,256,384]{2,1,0:T(8,128)(2,1)S(1)}, u32[]{:S(2)}, u32[]{:S(2)}) collective-permute-start(bf16[3,256,384]{2,1,0:T(8,128)(2,1)S(1)} %pad_maximum_fusion), channel_id=1, source_target_pairs={{0,132},{8,11},{16,148},{24,27},{32,164},{40,43},{48,180},{56,59},... | collective-permute-start | bytes 1769480 | tf_op jit(solution)/shard_map/ppermute | solution.py:50
  31.7 11.1 %collective-permute-start.8 = (bf16[1,256,384]{2,1,0:T(8,128)(2,1)S(1)}, bf16[1,256,384]{2,1,0:T(8,128)(2,1)S(1)}, u32[]{:S(2)}, u32[]{:S(2)}) collective-permute-start(bf16[1,256,384]{2,1,0:T(8,128)(2,1)S(1)} %collective-permute-done.7), channel_id=1, source_target_pairs={{0,132},{8,11},{16,148},{24,27},{32,164},{40,43},{48,180},{56,59},... | collective-permute-start | bytes 589832 | tf_op jit(solution)/shard_map/ppermute | solution.py:50
  31.9 29.2 %collective-permute-start.13 = (bf16[2,256,384]{2,1,0:T(8,128)(2,1)S(1)}, bf16[2,256,384]{2,1,0:T(8,128)(2,1)S(1)}, u32[]{:S(2)}, u32[]{:S(2)}) collective-permute-start(bf16[2,256,384]{2,1,0:T(8,128)(2,1)S(1)} %get-tuple-element.27.p23), channel_id=1, source_target_pairs={{0,128},{8,9},{16,144},{24,25},{32,160},{40,41},{48,176},{56,57},{... | collective-permute-start | bytes 1179656 | tf_op jit(solution)/shard_map/ppermute | solution.py:50
  42.8 10.2 %collective-permute-start.12 = (bf16[1,256,384]{2,1,0:T(8,128)(2,1)S(1)}, bf16[1,256,384]{2,1,0:T(8,128)(2,1)S(1)}, u32[]{:S(2)}, u32[]{:S(2)}) collective-permute-start(bf16[1,256,384]{2,1,0:T(8,128)(2,1)S(1)} %collective-permute-done.8.down3), channel_id=1, source_target_pairs={{0,132},{8,11},{16,148},{24,27},{32,164},{40,43},{48,180},{56,59},... | collective-permute-start | bytes 589832 | tf_op jit(solution)/shard_map/ppermute | solution.py:50
  45.2 16.0 %collective-permute-start.10 = (bf16[2,256,384]{2,1,0:T(8,128)(2,1)S(1)}, bf16[2,256,384]{2,1,0:T(8,128)(2,1)S(1)}, u32[]{:S(2)}, u32[]{:S(2)}) collective-permute-start(bf16[2,256,384]{2,1,0:T(8,128)(2,1)S(1)} %collective-permute-done.6.up01), channel_id=1, source_target_pairs={{0,128},{8,9},{16,144},{24,25},{32,160},{40,41},{48,176},{56,57},{... | collective-permute-start | bytes 1179656 | tf_op jit(solution)/shard_map/ppermute | solution.py:50
  45.2 16.0 %collective-permute-start.15 = (bf16[1,256,384]{2,1,0:T(8,128)(2,1)S(1)}, bf16[1,256,384]{2,1,0:T(8,128)(2,1)S(1)}, u32[]{:S(2)}, u32[]{:S(2)}) collective-permute-start(bf16[1,256,384]{2,1,0:T(8,128)(2,1)S(1)} %bitcast.15), channel_id=1, source_target_pairs={{0,8},{8,0},{16,24},{24,16},{32,40},{40,32},{48,56},{56,48},{64,72... | collective-permute-start | bytes 589832 | tf_op jit(solution)/shard_map/ppermute | solution.py:50
  53.0 8.2 %collective-permute-start.16 = (bf16[1,256,384]{2,1,0:T(8,128)(2,1)S(1)}, bf16[1,256,384]{2,1,0:T(8,128)(2,1)S(1)}, u32[]{:S(2)}, u32[]{:S(2)}) collective-permute-start(bf16[1,256,384]{2,1,0:T(8,128)(2,1)S(1)} %get-tuple-element.26), channel_id=1, source_target_pairs={{0,136},{8,0},{16,152},{24,16},{32,168},{40,32},{48,184},{56,48},{... | collective-permute-start | bytes 589832 | tf_op jit(solution)/shard_map/ppermute | solution.py:50
  56.0 2.3 %copy-start = (bf16[2,384,3072]{2,1,0:T(8,128)(2,1)S(1)}, bf16[2,384,3072]{2,1,0:T(8,128)(2,1)}, u32[]{:S(2)}) copy-start(bf16[2,384,3072]{2,1,0:T(8,128)(2,1)} %own) | copy-start | bytes 14155780
  61.1 19.6 %copy-start.1 = (s32[64,64]{1,0:T(8,128)S(1)}, s32[64,64]{1,0:T(8,128)}, u32[]{:S(2)}) copy-start(s32[64,64]{1,0:T(8,128)} %q_index.1) | copy-start | bytes 49156

commit v15 on v13

--- a/solution.py
+++ b/solution.py
@@ -70,7 +70,7 @@
 def place_of(z_wanted):
     z = where_am_i()[3]
     side = (z ^ z_wanted) & 1
-    return side * 4 + ((((z ^ side) - z_wanted) & 7) >> 1)
+    return (((z ^ side) - z_wanted) & 7) + side
 
 
 def load_kernel(own, other, out, sems):
@@ -253,19 +253,19 @@
 def local(pair_matrix, screened, coulomb, q_index):
     bands, share = pair_matrix.shape[1:]
     r = lax.axis_index("row")
+    w_other = send(screened, SWAP)
     own = pair_matrix.reshape(1, 2 * bands, share)
-    even = jnp.concatenate([own] + [send(own, along_z(s)) for s in ZSHIFTS[1:]], axis=0)
-    paired = send(even, ZPAIR)
+    pair = jnp.concatenate([own, send(own, ZPAIR)], axis=0)
+    quads = [send(pair, along_z(s)) for s in ZSHIFTS[1:]]
     q_mine = jnp.stack([2 * r, 2 * r + 1, 2 * (r ^ 1), 2 * (r ^ 1) + 1])
     ks = lax.iota(jnp.int32, q_index.shape[0])
     partner = jnp.sum(
         jnp.where(q_index[None] == q_mine[:, None, None], ks[None, :, None], 0), axis=1
     ).astype(jnp.int32)
-    paired, partner, coulomb, screened = lax.optimization_barrier(
-        (paired, partner, coulomb.reshape(1, share), screened)
+    quads, partner, coulomb, w_other = lax.optimization_barrier(
+        (quads, partner, coulomb.reshape(1, share), w_other)
     )
-    w_other = send(screened, SWAP)
-    stack = jnp.concatenate([even, paired], axis=0).reshape(1, NZ * 32, share)
+    stack = jnp.concatenate([pair] + quads, axis=0).reshape(1, NZ * 32, share)
     parts = [send(stack, first_plane(s)) for s in FIRST[1:]]
     p01 = jnp.concatenate([stack, parts[0]], axis=0)
     p23 = jnp.concatenate([parts[1], parts[2]], axis=0)

time: 88 us -> 87.9 us (level)
  waiting for transfers between devices: 10.2 us -> 9.01 us
    all_to_all x1, blocking collectives: 16.3 us -> 17.8 us  [local(): lax.all_to_all(placed, 'row', split_axis=0, concat_axis=0, tiled=True)]
    ppermute x16, waiting for transfers between devices: 10.2 us -> 9.01 us  [send(): return lax.ppermute(value, AXES, perm)]
  transfers between devices with their start and end apart: 16 -> 16, of which waited for: 6 -> 8; matrix products, arithmetic and copies ran while one was open for 3% -> 4% of each run, Pallas kernels for 3% -> 3%
where the time goes in v15:
time: 87.9 us; the launch traced here: 87.5 us
  starting transfers between devices  31.4 us (36%)
  blocking collectives  30.4 us (35%)
  Pallas kernels  10.9 us (12%)
  waiting for transfers between devices  9.01 us (10%)
  local copies, waits for them, and re-layouts  3.83 us (4%)
  other arithmetic  1.84 us (2%)
    ppermute x16, starting transfers between devices, send(): return lax.ppermute(value, AXES, perm)  31.4 us
    all_to_all x1, blocking collectives, local(): lax.all_to_all(placed, 'row', split_axis=0, concat_axis=0, tiled=True)  17.8 us
    all_to_all x1, blocking collectives, local(): lax.all_to_all(terms, 'col', split_axis=0, concat_axis=0, tiled=True)  12.6 us
    ppermute x16, waiting for transfers between devices, send(): return lax.ppermute(value, AXES, perm)  9.01 us
    pallas_call x1, Pallas kernels, solve(): pl.pallas_call(solve_kernel, in_specs=[pl.BlockSpec(memory_space=pltpu.SM...  7.26 us
    unnamed x9, local copies, waits for them, and re-layouts  3.14 us
    pallas_call x1, Pallas kernels, load(): pl.pallas_call(load_kernel, in_specs=[pl.BlockSpec(memory_space=pl.ANY)]...  2.72 us
  transfers between devices with their start and end apart: 16, of which 8 were waited for; matrix products, arithmetic and copies ran while one was open for 4% of the time, Pallas kernels for 3%

profile of v15, /device:TPU:1, one launch (start us, length us, event | category | flops | bytes accessed | tf_op | source)
XLA Modules:
  0.0 87.5 jit_solution(12999519347504661957)
XLA Ops:
  0.0 3.2 %collective-permute-start.4 = (bf16[2,384,3072]{2,1,0:T(8,128)(2,1)}, bf16[2,384,3072]{2,1,0:T(8,128)(2,1)}, u32[]{:S(2)}, u32[]{:S(2)}) collective-permute-start(bf16[2,384,3072]{2,1,0:T(8,128)(2,1)} %own), channel_id=1, source_target_pairs={{0,8},{8,0},{16,24},{24,16},{32,40},{40,32},{48,56},{56,48},{64,72... | collective-permute-start | bytes 14155784 | tf_op jit(solution)/shard_map/ppermute | solution.py:50
  3.3 0.9 select_reduce_fusion.partner
  6.9 2.4 %collective-permute-start.1 = (bf16[2,32,384]{2,1,0:T(8,128)(2,1)S(1)}, bf16[2,32,384]{2,1,0:T(8,128)(2,1)S(1)}, u32[]{:S(2)}, u32[]{:S(2)}) collective-permute-start(bf16[2,32,384]{2,1,0:T(8,128)(2,1)S(1)} %pad_maximum_fusion.1), channel_id=1, source_target_pairs={{0,32},{8,40},{16,48},{24,56},{32,64},{40,72},{48,80},{56,88},{64,... | collective-permute-start | bytes 147464 | tf_op jit(solution)/shard_map/ppermute | solution.py:50
  9.2 4.2 %collective-permute-start.2 = (bf16[2,32,384]{2,1,0:T(8,128)(2,1)S(1)}, bf16[2,32,384]{2,1,0:T(8,128)(2,1)S(1)}, u32[]{:S(2)}, u32[]{:S(2)}) collective-permute-start(bf16[2,32,384]{2,1,0:T(8,128)(2,1)S(1)} %pad_maximum_fusion.1), channel_id=1, source_target_pairs={{0,64},{8,72},{16,80},{24,88},{32,96},{40,104},{48,112},{56,120},{... | collective-permute-start | bytes 147464 | tf_op jit(solution)/shard_map/ppermute | solution.py:50
  13.5 2.4 %collective-permute-start.3 = (bf16[2,32,384]{2,1,0:T(8,128)(2,1)S(1)}, bf16[2,32,384]{2,1,0:T(8,128)(2,1)S(1)}, u32[]{:S(2)}, u32[]{:S(2)}) collective-permute-start(bf16[2,32,384]{2,1,0:T(8,128)(2,1)S(1)} %pad_maximum_fusion.1), channel_id=1, source_target_pairs={{0,96},{8,104},{16,112},{24,120},{32,0},{40,8},{48,16},{56,24},{64... | collective-permute-start | bytes 147464 | tf_op jit(solution)/shard_map/ppermute | solution.py:50
  15.9 1.1 %collective-permute-done.2 = bf16[2,32,384]{2,1,0:T(8,128)(2,1)S(1)} collective-permute-done((bf16[2,32,384]{2,1,0:T(8,128)(2,1)S(1)}, bf16[2,32,384]{2,1,0:T(8,128)(2,1)S(1)}, u32[]{:S(2)}, u32[]{:S(2)}) %collective-permute-start.2) | collective-permute-done | bytes 49184 | tf_op jit(solution)/shard_map/ppermute | solution.py:50
  16.9 1.6 %collective-permute-done.3 = bf16[2,32,384]{2,1,0:T(8,128)(2,1)S(1)} collective-permute-done((bf16[2,32,384]{2,1,0:T(8,128)(2,1)S(1)}, bf16[2,32,384]{2,1,0:T(8,128)(2,1)S(1)}, u32[]{:S(2)}, u32[]{:S(2)}) %collective-permute-start.3) | collective-permute-done | bytes 49184 | tf_op jit(solution)/shard_map/ppermute | solution.py:50
  18.6 1.4 %collective-permute-start.5 = (bf16[1,256,384]{2,1,0:T(8,128)(2,1)S(1)}, bf16[1,256,384]{2,1,0:T(8,128)(2,1)S(1)}, u32[]{:S(2)}, u32[]{:S(2)}) collective-permute-start(bf16[1,256,384]{2,1,0:T(8,128)(2,1)S(1)} %bitcast.10), channel_id=1, source_target_pairs={{0,1},{8,136},{16,17},{24,152},{32,33},{40,168},{48,49},{56,184},{... | collective-permute-start | bytes 589832 | tf_op jit(solution)/shard_map/ppermute | solution.py:50
  20.0 2.6 %collective-permute-start.7 = (bf16[1,256,384]{2,1,0:T(8,128)(2,1)S(1)}, bf16[1,256,384]{2,1,0:T(8,128)(2,1)S(1)}, u32[]{:S(2)}, u32[]{:S(2)}) collective-permute-start(bf16[1,256,384]{2,1,0:T(8,128)(2,1)S(1)} %bitcast.11), channel_id=1, source_target_pairs={{0,2},{8,12},{16,18},{24,28},{32,34},{40,44},{48,50},{56,60},{64,6... | collective-permute-start | bytes 589832 | tf_op jit(solution)/shard_map/ppermute | solution.py:50
  22.6 1.1 %collective-permute-start.8 = (bf16[1,256,384]{2,1,0:T(8,128)(2,1)S(1)}, bf16[1,256,384]{2,1,0:T(8,128)(2,1)S(1)}, u32[]{:S(2)}, u32[]{:S(2)}) collective-permute-start(bf16[1,256,384]{2,1,0:T(8,128)(2,1)S(1)} %bitcast.12), channel_id=1, source_target_pairs={{0,3},{8,140},{16,19},{24,156},{32,35},{40,172},{48,51},{56,188},{... | collective-permute-start | bytes 589832 | tf_op jit(solution)/shard_map/ppermute | solution.py:50
  23.6 1.1 %collective-permute-done.5 = bf16[1,256,384]{2,1,0:T(8,128)(2,1)S(1)} collective-permute-done((bf16[1,256,384]{2,1,0:T(8,128)(2,1)S(1)}, bf16[1,256,384]{2,1,0:T(8,128)(2,1)S(1)}, u32[]{:S(2)}, u32[]{:S(2)}) %collective-permute-start.5) | collective-permute-done | bytes 196640 | tf_op jit(solution)/shard_map/ppermute | solution.py:50
  24.8 1.0 %collective-permute-start.6 = (bf16[2,256,384]{2,1,0:T(8,128)(2,1)S(1)}, bf16[2,256,384]{2,1,0:T(8,128)(2,1)S(1)}, u32[]{:S(2)}, u32[]{:S(2)}) collective-permute-start(bf16[2,256,384]{2,1,0:T(8,128)(2,1)S(1)} %pad_maximum_fusion.p01), channel_id=1, source_target_pairs={{0,128},{8,9},{16,144},{24,25},{32,160},{40,41},{48,176},{56,57},{... | collective-permute-start | bytes 1179656 | tf_op jit(solution)/shard_map/ppermute | solution.py:50
  25.8 2.2 %collective-permute-done.7 = bf16[1,256,384]{2,1,0:T(8,128)(2,1)S(1)} collective-permute-done((bf16[1,256,384]{2,1,0:T(8,128)(2,1)S(1)}, bf16[1,256,384]{2,1,0:T(8,128)(2,1)S(1)}, u32[]{:S(2)}, u32[]{:S(2)}) %collective-permute-start.7) | collective-permute-done | bytes 196640 | tf_op jit(solution)/shard_map/ppermute | solution.py:50
  28.2 2.3 %collective-permute-start.9 = (bf16[2,256,384]{2,1,0:T(8,128)(2,1)S(1)}, bf16[2,256,384]{2,1,0:T(8,128)(2,1)S(1)}, u32[]{:S(2)}, u32[]{:S(2)}) collective-permute-start(bf16[2,256,384]{2,1,0:T(8,128)(2,1)S(1)} %get-tuple-element.30.p23), channel_id=1, source_target_pairs={{0,132},{8,11},{16,148},{24,27},{32,164},{40,43},{48,180},{56,59},... | collective-permute-start | bytes 1179656 | tf_op jit(solution)/shard_map/ppermute | solution.py:50
  30.4 2.7 %collective-permute-start.11 = (bf16[2,256,384]{2,1,0:T(8,128)(2,1)S(1)}, bf16[2,256,384]{2,1,0:T(8,128)(2,1)S(1)}, u32[]{:S(2)}, u32[]{:S(2)}) collective-permute-start(bf16[2,256,384]{2,1,0:T(8,128)(2,1)S(1)} %pad_maximum_fusion.p01), channel_id=1, source_target_pairs={{0,132},{8,11},{16,148},{24,27},{32,164},{40,43},{48,180},{56,59},... | collective-permute-start | bytes 1179656 | tf_op jit(solution)/shard_map/ppermute | solution.py:50
  33.1 0.8 collective-permute-done.6.f0
  33.9 1.3 %collective-permute-done.9.g1 = bf16[2,256,384]{2,1,0:T(8,128)(2,1)S(1)} collective-permute-done((bf16[2,256,384]{2,1,0:T(8,128)(2,1)S(1)}, bf16[2,256,384]{2,1,0:T(8,128)(2,1)S(1)}, u32[]{:S(2)}, u32[]{:S(2)}) %collective-permute-start.9) | collective-permute-done | bytes 393248 | tf_op jit(solution)/shard_map/ppermute | solution.py:50
  35.2 3.1 %collective-permute-start.13 = (bf16[2,256,384]{2,1,0:T(8,128)(2,1)S(1)}, bf16[2,256,384]{2,1,0:T(8,128)(2,1)S(1)}, u32[]{:S(2)}, u32[]{:S(2)}) collective-permute-start(bf16[2,256,384]{2,1,0:T(8,128)(2,1)S(1)} %collective-permute-done.9.g1), channel_id=1, source_target_pairs={{0,132},{8,11},{16,148},{24,27},{32,164},{40,43},{48,180},{56,59},... | collective-permute-start | bytes 1179656 | tf_op jit(solution)/shard_map/ppermute | solution.py:50
  38.3 5.1 %collective-permute-start.14 = (bf16[1,256,384]{2,1,0:T(8,128)(2,1)S(1)}, bf16[1,256,384]{2,1,0:T(8,128)(2,1)S(1)}, u32[]{:S(2)}, u32[]{:S(2)}) collective-permute-start(bf16[1,256,384]{2,1,0:T(8,128)(2,1)S(1)} %bitcast.15), channel_id=1, source_target_pairs={{0,8},{8,0},{16,24},{24,16},{32,40},{40,32},{48,56},{56,48},{64,72... | collective-permute-start | bytes 589832 | tf_op jit(solution)/shard_map/ppermute | solution.py:50
  43.4 2.3 %copy-done = bf16[2,384,3072]{2,1,0:T(8,128)(2,1)S(1)} copy-done((bf16[2,384,3072]{2,1,0:T(8,128)(2,1)S(1)}, bf16[2,384,3072]{2,1,0:T(8,128)(2,1)}, u32[]{:S(2)}) %copy-start) | copy-done | bytes 4718616
  45.8 2.7 %load.1.w = bf16[4,384,3072]{2,1,0:T(8,128)(2,1)S(1)} custom-call(bf16[2,384,3072]{2,1,0:T(8,128)(2,1)S(1)} %copy-done, bf16[2,384,3072]{2,1,0:T(8,128)(2,1)} %collective-permute-done.4.other), custom_call_target="tpu_custom_call" | custom-call | bytes 18874368 | tf_op jit(solution)/shard_map/load/pallas_call | solution.py:90
  48.9 7.3 %solve.1 = f32[8,2,16,128]{3,2,1,0:T(8,128)S(1)} custom-call(s32[4,64]{1,0:T(4,128)S(1)} %select_reduce_fusion.partner, f32[1,384]{1,0:T(1,128)S(1)} %reshape.12.coulomb, bf16[4,384,3072]{2,1,0:T(8,128)(2,1)S(1)} %load.1.w, bf16[2,256,384]{2,1,0:T(8,128)(2,1)S(1)} %pad_maximum_fusion.p01, bf16[2,256,384]{2,1,0:T(8,128)(2,1)S(1)} %get-tuple-element.30.p23, ...), custom_call_target="tpu_custom_call" | custom-call | flops 4831838208 | bytes 9437184 | tf_op jit(solution)/shard_map/solve/pallas_call | solution.py:160
  56.2 12.6 %all_to_all.10.terms = f32[8,2,16,128]{3,2,1,0:T(8,128)S(1)} all-to-all(f32[8,2,16,128]{3,2,1,0:T(8,128)S(1)} %solve.1), channel_id=1, replica_groups=mesh['row'=32,'col'=8] {'col'}, dimensions={0} | all-to-all | bytes 262144 | tf_op jit(solution)/shard_map/all_to_all | solution.py:290
  69.0 17.8 %all_to_all.11.arrived = bf16[32,16,128]{2,1,0:T(8,128)(2,1)S(1)} all-to-all(bf16[32,16,128]{2,1,0:T(8,128)(2,1)S(1)} %spread.1), channel_id=1, replica_groups=mesh['row'=32,'col'=8] {'row'}, dimensions={0} | all-to-all | bytes 262144 | tf_op jit(solution)/shard_map/all_to_all | solution.py:292
  (30 shorter events, 4.3 us)
Async XLA Ops:
  0.0 18.5 %collective-permute-start.4 = (bf16[2,384,3072]{2,1,0:T(8,128)(2,1)}, bf16[2,384,3072]{2,1,0:T(8,128)(2,1)}, u32[]{:S(2)}, u32[]{:S(2)}) collective-permute-start(bf16[2,384,3072]{2,1,0:T(8,128)(2,1)} %own), channel_id=1, source_target_pairs={{0,8},{8,0},{16,24},{24,16},{32,40},{40,32},{48,56},{56,48},{64,72... | collective-permute-start | bytes 14155784 | tf_op jit(solution)/shard_map/ppermute | solution.py:50
  3.2 2.9 %collective-permute-start = (bf16[1,32,384]{2,1,0:T(8,128)(2,1)}, bf16[1,32,384]{2,1,0:T(8,128)(2,1)S(1)}, u32[]{:S(2)}, u32[]{:S(2)}) collective-permute-start(bf16[1,32,384]{2,1,0:T(8,128)(2,1)} %bitcast.16), channel_id=1, source_target_pairs={{0,16},{8,24},{16,0},{24,8},{32,48},{40,56},{48,32},{56,40},{64,80... | collective-permute-start | bytes 73736 | tf_op jit(solution)/shard_map/ppermute | solution.py:50
  6.9 9.0 %collective-permute-start.1 = (bf16[2,32,384]{2,1,0:T(8,128)(2,1)S(1)}, bf16[2,32,384]{2,1,0:T(8,128)(2,1)S(1)}, u32[]{:S(2)}, u32[]{:S(2)}) collective-permute-start(bf16[2,32,384]{2,1,0:T(8,128)(2,1)S(1)} %pad_maximum_fusion.1), channel_id=1, source_target_pairs={{0,32},{8,40},{16,48},{24,56},{32,64},{40,72},{48,80},{56,88},{64,... | collective-permute-start | bytes 147464 | tf_op jit(solution)/shard_map/ppermute | solution.py:50
  9.2 7.7 %collective-permute-start.2 = (bf16[2,32,384]{2,1,0:T(8,128)(2,1)S(1)}, bf16[2,32,384]{2,1,0:T(8,128)(2,1)S(1)}, u32[]{:S(2)}, u32[]{:S(2)}) collective-permute-start(bf16[2,32,384]{2,1,0:T(8,128)(2,1)S(1)} %pad_maximum_fusion.1), channel_id=1, source_target_pairs={{0,64},{8,72},{16,80},{24,88},{32,96},{40,104},{48,112},{56,120},{... | collective-permute-start | bytes 147464 | tf_op jit(solution)/shard_map/ppermute | solution.py:50
  13.5 5.1 %collective-permute-start.3 = (bf16[2,32,384]{2,1,0:T(8,128)(2,1)S(1)}, bf16[2,32,384]{2,1,0:T(8,128)(2,1)S(1)}, u32[]{:S(2)}, u32[]{:S(2)}) collective-permute-start(bf16[2,32,384]{2,1,0:T(8,128)(2,1)S(1)} %pad_maximum_fusion.1), channel_id=1, source_target_pairs={{0,96},{8,104},{16,112},{24,120},{32,0},{40,8},{48,16},{56,24},{64... | collective-permute-start | bytes 147464 | tf_op jit(solution)/shard_map/ppermute | solution.py:50
  18.6 6.2 %collective-permute-start.5 = (bf16[1,256,384]{2,1,0:T(8,128)(2,1)S(1)}, bf16[1,256,384]{2,1,0:T(8,128)(2,1)S(1)}, u32[]{:S(2)}, u32[]{:S(2)}) collective-permute-start(bf16[1,256,384]{2,1,0:T(8,128)(2,1)S(1)} %bitcast.10), channel_id=1, source_target_pairs={{0,1},{8,136},{16,17},{24,152},{32,33},{40,168},{48,49},{56,184},{... | collective-permute-start | bytes 589832 | tf_op jit(solution)/shard_map/ppermute | solution.py:50
  20.0 8.1 %collective-permute-start.7 = (bf16[1,256,384]{2,1,0:T(8,128)(2,1)S(1)}, bf16[1,256,384]{2,1,0:T(8,128)(2,1)S(1)}, u32[]{:S(2)}, u32[]{:S(2)}) collective-permute-start(bf16[1,256,384]{2,1,0:T(8,128)(2,1)S(1)} %bitcast.11), channel_id=1, source_target_pairs={{0,2},{8,12},{16,18},{24,28},{32,34},{40,44},{48,50},{56,60},{64,6... | collective-permute-start | bytes 589832 | tf_op jit(solution)/shard_map/ppermute | solution.py:50
  22.6 5.5 %collective-permute-start.8 = (bf16[1,256,384]{2,1,0:T(8,128)(2,1)S(1)}, bf16[1,256,384]{2,1,0:T(8,128)(2,1)S(1)}, u32[]{:S(2)}, u32[]{:S(2)}) collective-permute-start(bf16[1,256,384]{2,1,0:T(8,128)(2,1)S(1)} %bitcast.12), channel_id=1, source_target_pairs={{0,3},{8,140},{16,19},{24,156},{32,35},{40,172},{48,51},{56,188},{... | collective-permute-start | bytes 589832 | tf_op jit(solution)/shard_map/ppermute | solution.py:50
  24.8 9.1 %collective-permute-start.6 = (bf16[2,256,384]{2,1,0:T(8,128)(2,1)S(1)}, bf16[2,256,384]{2,1,0:T(8,128)(2,1)S(1)}, u32[]{:S(2)}, u32[]{:S(2)}) collective-permute-start(bf16[2,256,384]{2,1,0:T(8,128)(2,1)S(1)} %pad_maximum_fusion.p01), channel_id=1, source_target_pairs={{0,128},{8,9},{16,144},{24,25},{32,160},{40,41},{48,176},{56,57},{... | collective-permute-start | bytes 1179656 | tf_op jit(solution)/shard_map/ppermute | solution.py:50
  28.2 7.0 %collective-permute-start.9 = (bf16[2,256,384]{2,1,0:T(8,128)(2,1)S(1)}, bf16[2,256,384]{2,1,0:T(8,128)(2,1)S(1)}, u32[]{:S(2)}, u32[]{:S(2)}) collective-permute-start(bf16[2,256,384]{2,1,0:T(8,128)(2,1)S(1)} %get-tuple-element.30.p23), channel_id=1, source_target_pairs={{0,132},{8,11},{16,148},{24,27},{32,164},{40,43},{48,180},{56,59},... | collective-permute-start | bytes 1179656 | tf_op jit(solution)/shard_map/ppermute | solution.py:50
  30.4 13.0 %collective-permute-start.10 = (bf16[2,256,384]{2,1,0:T(8,128)(2,1)S(1)}, bf16[2,256,384]{2,1,0:T(8,128)(2,1)S(1)}, u32[]{:S(2)}, u32[]{:S(2)}) collective-permute-start(bf16[2,256,384]{2,1,0:T(8,128)(2,1)S(1)} %get-tuple-element.30.p23), channel_id=1, source_target_pairs={{0,128},{8,9},{16,144},{24,25},{32,160},{40,41},{48,176},{56,57},{... | collective-permute-start | bytes 1179656 | tf_op jit(solution)/shard_map/ppermute | solution.py:50
  30.4 18.1 %collective-permute-start.11 = (bf16[2,256,384]{2,1,0:T(8,128)(2,1)S(1)}, bf16[2,256,384]{2,1,0:T(8,128)(2,1)S(1)}, u32[]{:S(2)}, u32[]{:S(2)}) collective-permute-start(bf16[2,256,384]{2,1,0:T(8,128)(2,1)S(1)} %pad_maximum_fusion.p01), channel_id=1, source_target_pairs={{0,132},{8,11},{16,148},{24,27},{32,164},{40,43},{48,180},{56,59},... | collective-permute-start | bytes 1179656 | tf_op jit(solution)/shard_map/ppermute | solution.py:50
  33.9 15.0 %collective-permute-start.12 = (bf16[2,256,384]{2,1,0:T(8,128)(2,1)S(1)}, bf16[2,256,384]{2,1,0:T(8,128)(2,1)S(1)}, u32[]{:S(2)}, u32[]{:S(2)}) collective-permute-start(bf16[2,256,384]{2,1,0:T(8,128)(2,1)S(1)} %collective-permute-done.6.f0), channel_id=1, source_target_pairs={{0,128},{8,9},{16,144},{24,25},{32,160},{40,41},{48,176},{56,57},{... | collective-permute-start | bytes 1179656 | tf_op jit(solution)/shard_map/ppermute | solution.py:50
  35.2 13.7 %collective-permute-start.13 = (bf16[2,256,384]{2,1,0:T(8,128)(2,1)S(1)}, bf16[2,256,384]{2,1,0:T(8,128)(2,1)S(1)}, u32[]{:S(2)}, u32[]{:S(2)}) collective-permute-start(bf16[2,256,384]{2,1,0:T(8,128)(2,1)S(1)} %collective-permute-done.9.g1), channel_id=1, source_target_pairs={{0,132},{8,11},{16,148},{24,27},{32,164},{40,43},{48,180},{56,59},... | collective-permute-start | bytes 1179656 | tf_op jit(solution)/shard_map/ppermute | solution.py:50
  38.3 10.2 %collective-permute-start.14 = (bf16[1,256,384]{2,1,0:T(8,128)(2,1)S(1)}, bf16[1,256,384]{2,1,0:T(8,128)(2,1)S(1)}, u32[]{:S(2)}, u32[]{:S(2)}) collective-permute-start(bf16[1,256,384]{2,1,0:T(8,128)(2,1)S(1)} %bitcast.15), channel_id=1, source_target_pairs={{0,8},{8,0},{16,24},{24,16},{32,40},{40,32},{48,56},{56,48},{64,72... | collective-permute-start | bytes 589832 | tf_op jit(solution)/shard_map/ppermute | solution.py:50
  43.4 5.5 %collective-permute-start.15 = (bf16[1,256,384]{2,1,0:T(8,128)(2,1)S(1)}, bf16[1,256,384]{2,1,0:T(8,128)(2,1)S(1)}, u32[]{:S(2)}, u32[]{:S(2)}) collective-permute-start(bf16[1,256,384]{2,1,0:T(8,128)(2,1)S(1)} %get-tuple-element.28), channel_id=1, source_target_pairs={{0,136},{8,0},{16,152},{24,16},{32,168},{40,32},{48,184},{56,48},{... | collective-permute-start | bytes 589832 | tf_op jit(solution)/shard_map/ppermute | solution.py:50
  43.4 2.3 %copy-start = (bf16[2,384,3072]{2,1,0:T(8,128)(2,1)S(1)}, bf16[2,384,3072]{2,1,0:T(8,128)(2,1)}, u32[]{:S(2)}) copy-start(bf16[2,384,3072]{2,1,0:T(8,128)(2,1)} %own) | copy-start | bytes 14155780
  48.5 20.2 %copy-start.1 = (s32[64,64]{1,0:T(8,128)S(1)}, s32[64,64]{1,0:T(8,128)}, u32[]{:S(2)}) copy-start(s32[64,64]{1,0:T(8,128)} %q_index.1) | copy-start | bytes 49156

commit v16 on v15

--- a/solution.py
+++ b/solution.py
@@ -7,7 +7,7 @@
 
 AXES = ("row", "col")
 NX, NY, NZ, NCORE = 4, 4, 8, 2
-FIRST = (0, 1, 2, -1)
+FIRST = (0, 2, 1, -1)
 SECOND = (0, 2, 1, -1)
 ZSHIFTS = (0, 2, 4, -2)
 MIB = 1024 * 1024
@@ -278,7 +278,7 @@
     gg1 = send(g1, second_plane(-1))
 
     core, low = r & 1, r >> 4
-    passed = jnp.where(core == 0, stack, jnp.where(low == 0, parts[2], parts[0]))
+    passed = jnp.where(core == 0, stack, jnp.where(low == 0, parts[2], parts[1]))
     w_own, w_other, f0, g1, passed, kept = lax.optimization_barrier(
         (screened, w_other, f0, g1, passed, stack)
     )

time: 87.9 us -> 87.8 us (level)
  blocking collectives: 30.4 us -> 28.5 us
  starting transfers between devices: 31.4 us -> 32.6 us
    all_to_all x1, blocking collectives: 12.6 us -> 10.9 us  [local(): lax.all_to_all(terms, 'col', split_axis=0, concat_axis=0, tiled=True)]
    ppermute x16, starting transfers between devices: 31.4 us -> 32.6 us  [send(): return lax.ppermute(value, AXES, perm)]
    unnamed x9 -> x8, local copies, waits for them, and re-layouts: 3.14 us -> 3.12 us
  transfers between devices with their start and end apart: 16 -> 16, of which waited for: 8 -> 9; matrix products, arithmetic and copies ran while one was open for 4% -> 4% of each run, Pallas kernels for 3% -> 3%
where the time goes in v16:
time: 87.8 us; the launch traced here: 87.4 us
  starting transfers between devices  32.6 us (37%)
  blocking collectives  28.5 us (32%)
  Pallas kernels  10.9 us (12%)
  waiting for transfers between devices  9.76 us (11%)
  local copies, waits for them, and re-layouts  3.84 us (4%)
  other arithmetic  1.82 us (2%)
    ppermute x16, starting transfers between devices, send(): return lax.ppermute(value, AXES, perm)  32.6 us
    all_to_all x1, blocking collectives, local(): lax.all_to_all(placed, 'row', split_axis=0, concat_axis=0, tiled=True)  17.5 us
    all_to_all x1, blocking collectives, local(): lax.all_to_all(terms, 'col', split_axis=0, concat_axis=0, tiled=True)  10.9 us
    ppermute x16, waiting for transfers between devices, send(): return lax.ppermute(value, AXES, perm)  9.76 us
    pallas_call x1, Pallas kernels, solve(): pl.pallas_call(solve_kernel, in_specs=[pl.BlockSpec(memory_space=pltpu.SM...  7.25 us
    unnamed x8, local copies, waits for them, and re-layouts  3.12 us
    pallas_call x1, Pallas kernels, load(): pl.pallas_call(load_kernel, in_specs=[pl.BlockSpec(memory_space=pl.ANY)]...  2.72 us
  transfers between devices with their start and end apart: 16, of which 9 were waited for; matrix products, arithmetic and copies ran while one was open for 4% of the time, Pallas kernels for 3%

profile of v16, /device:TPU:1, one launch (start us, length us, event | category | flops | bytes accessed | tf_op | source)
XLA Modules:
  0.0 87.4 jit_solution(6880887148501571357)
XLA Ops:
  0.0 3.2 %collective-permute-start.4 = (bf16[2,384,3072]{2,1,0:T(8,128)(2,1)}, bf16[2,384,3072]{2,1,0:T(8,128)(2,1)}, u32[]{:S(2)}, u32[]{:S(2)}) collective-permute-start(bf16[2,384,3072]{2,1,0:T(8,128)(2,1)} %own), channel_id=1, source_target_pairs={{0,8},{8,0},{16,24},{24,16},{32,40},{40,32},{48,56},{56,48},{64,72... | collective-permute-start | bytes 14155784 | tf_op jit(solution)/shard_map/ppermute | solution.py:50
  3.3 0.9 select_reduce_fusion.partner
  6.1 0.7 pad_maximum_fusion.1
  6.9 2.4 %collective-permute-start.1 = (bf16[2,32,384]{2,1,0:T(8,128)(2,1)S(1)}, bf16[2,32,384]{2,1,0:T(8,128)(2,1)S(1)}, u32[]{:S(2)}, u32[]{:S(2)}) collective-permute-start(bf16[2,32,384]{2,1,0:T(8,128)(2,1)S(1)} %pad_maximum_fusion.1), channel_id=1, source_target_pairs={{0,32},{8,40},{16,48},{24,56},{32,64},{40,72},{48,80},{56,88},{64,... | collective-permute-start | bytes 147464 | tf_op jit(solution)/shard_map/ppermute | solution.py:50
  9.2 4.2 %collective-permute-start.2 = (bf16[2,32,384]{2,1,0:T(8,128)(2,1)S(1)}, bf16[2,32,384]{2,1,0:T(8,128)(2,1)S(1)}, u32[]{:S(2)}, u32[]{:S(2)}) collective-permute-start(bf16[2,32,384]{2,1,0:T(8,128)(2,1)S(1)} %pad_maximum_fusion.1), channel_id=1, source_target_pairs={{0,64},{8,72},{16,80},{24,88},{32,96},{40,104},{48,112},{56,120},{... | collective-permute-start | bytes 147464 | tf_op jit(solution)/shard_map/ppermute | solution.py:50
  13.5 2.4 %collective-permute-start.3 = (bf16[2,32,384]{2,1,0:T(8,128)(2,1)S(1)}, bf16[2,32,384]{2,1,0:T(8,128)(2,1)S(1)}, u32[]{:S(2)}, u32[]{:S(2)}) collective-permute-start(bf16[2,32,384]{2,1,0:T(8,128)(2,1)S(1)} %pad_maximum_fusion.1), channel_id=1, source_target_pairs={{0,96},{8,104},{16,112},{24,120},{32,0},{40,8},{48,16},{56,24},{64... | collective-permute-start | bytes 147464 | tf_op jit(solution)/shard_map/ppermute | solution.py:50
  15.9 1.1 %collective-permute-done.2 = bf16[2,32,384]{2,1,0:T(8,128)(2,1)S(1)} collective-permute-done((bf16[2,32,384]{2,1,0:T(8,128)(2,1)S(1)}, bf16[2,32,384]{2,1,0:T(8,128)(2,1)S(1)}, u32[]{:S(2)}, u32[]{:S(2)}) %collective-permute-start.2) | collective-permute-done | bytes 49184 | tf_op jit(solution)/shard_map/ppermute | solution.py:50
  16.9 1.6 %collective-permute-done.3 = bf16[2,32,384]{2,1,0:T(8,128)(2,1)S(1)} collective-permute-done((bf16[2,32,384]{2,1,0:T(8,128)(2,1)S(1)}, bf16[2,32,384]{2,1,0:T(8,128)(2,1)S(1)}, u32[]{:S(2)}, u32[]{:S(2)}) %collective-permute-start.3) | collective-permute-done | bytes 49184 | tf_op jit(solution)/shard_map/ppermute | solution.py:50
  18.6 3.0 %collective-permute-start.5 = (bf16[1,256,384]{2,1,0:T(8,128)(2,1)S(1)}, bf16[1,256,384]{2,1,0:T(8,128)(2,1)S(1)}, u32[]{:S(2)}, u32[]{:S(2)}) collective-permute-start(bf16[1,256,384]{2,1,0:T(8,128)(2,1)S(1)} %bitcast.10), channel_id=1, source_target_pairs={{0,2},{8,12},{16,18},{24,28},{32,34},{40,44},{48,50},{56,60},{64,6... | collective-permute-start | bytes 589832 | tf_op jit(solution)/shard_map/ppermute | solution.py:50
  21.6 0.8 collective-permute-start.8
  23.1 1.9 %collective-permute-done.5 = bf16[1,256,384]{2,1,0:T(8,128)(2,1)S(1)} collective-permute-done((bf16[1,256,384]{2,1,0:T(8,128)(2,1)S(1)}, bf16[1,256,384]{2,1,0:T(8,128)(2,1)S(1)}, u32[]{:S(2)}, u32[]{:S(2)}) %collective-permute-start.5) | collective-permute-done | bytes 196640 | tf_op jit(solution)/shard_map/ppermute | solution.py:50
  25.0 1.0 %collective-permute-start.6 = (bf16[2,256,384]{2,1,0:T(8,128)(2,1)S(1)}, bf16[2,256,384]{2,1,0:T(8,128)(2,1)S(1)}, u32[]{:S(2)}, u32[]{:S(2)}) collective-permute-start(bf16[2,256,384]{2,1,0:T(8,128)(2,1)S(1)} %pad_maximum_fusion.p01), channel_id=1, source_target_pairs={{0,128},{8,9},{16,144},{24,25},{32,160},{40,41},{48,176},{56,57},{... | collective-permute-start | bytes 1179656 | tf_op jit(solution)/shard_map/ppermute | solution.py:50
  26.0 1.4 %collective-permute-done.8 = bf16[1,256,384]{2,1,0:T(8,128)(2,1)S(1)} collective-permute-done((bf16[1,256,384]{2,1,0:T(8,128)(2,1)S(1)}, bf16[1,256,384]{2,1,0:T(8,128)(2,1)S(1)}, u32[]{:S(2)}, u32[]{:S(2)}) %collective-permute-start.8) | collective-permute-done | bytes 196640 | tf_op jit(solution)/shard_map/ppermute | solution.py:50
  28.2 2.9 %collective-permute-start.9 = (bf16[2,256,384]{2,1,0:T(8,128)(2,1)S(1)}, bf16[2,256,384]{2,1,0:T(8,128)(2,1)S(1)}, u32[]{:S(2)}, u32[]{:S(2)}) collective-permute-start(bf16[2,256,384]{2,1,0:T(8,128)(2,1)S(1)} %constant_dynamic-update-slice_fusion.5.p23), channel_id=1, source_target_pairs={{0,132},{8,11},{16,148},{24,27},{32,164},{40,43},{48,180},{56,59},... | collective-permute-start | bytes 1179656 | tf_op jit(solution)/shard_map/ppermute | solution.py:50
  31.1 2.7 %collective-permute-start.11 = (bf16[2,256,384]{2,1,0:T(8,128)(2,1)S(1)}, bf16[2,256,384]{2,1,0:T(8,128)(2,1)S(1)}, u32[]{:S(2)}, u32[]{:S(2)}) collective-permute-start(bf16[2,256,384]{2,1,0:T(8,128)(2,1)S(1)} %pad_maximum_fusion.p01), channel_id=1, source_target_pairs={{0,132},{8,11},{16,148},{24,27},{32,164},{40,43},{48,180},{56,59},... | collective-permute-start | bytes 1179656 | tf_op jit(solution)/shard_map/ppermute | solution.py:50
  33.8 1.2 %collective-permute-done.6.f0 = bf16[2,256,384]{2,1,0:T(8,128)(2,1)S(1)} collective-permute-done((bf16[2,256,384]{2,1,0:T(8,128)(2,1)S(1)}, bf16[2,256,384]{2,1,0:T(8,128)(2,1)S(1)}, u32[]{:S(2)}, u32[]{:S(2)}) %collective-permute-start.6) | collective-permute-done | bytes 393248 | tf_op jit(solution)/shard_map/ppermute | solution.py:50
  35.0 0.8 collective-permute-done.9.g1
  35.8 3.1 %collective-permute-start.13 = (bf16[2,256,384]{2,1,0:T(8,128)(2,1)S(1)}, bf16[2,256,384]{2,1,0:T(8,128)(2,1)S(1)}, u32[]{:S(2)}, u32[]{:S(2)}) collective-permute-start(bf16[2,256,384]{2,1,0:T(8,128)(2,1)S(1)} %collective-permute-done.9.g1), channel_id=1, source_target_pairs={{0,132},{8,11},{16,148},{24,27},{32,164},{40,43},{48,180},{56,59},... | collective-permute-start | bytes 1179656 | tf_op jit(solution)/shard_map/ppermute | solution.py:50
  38.9 6.2 %collective-permute-start.14 = (bf16[1,256,384]{2,1,0:T(8,128)(2,1)S(1)}, bf16[1,256,384]{2,1,0:T(8,128)(2,1)S(1)}, u32[]{:S(2)}, u32[]{:S(2)}) collective-permute-start(bf16[1,256,384]{2,1,0:T(8,128)(2,1)S(1)} %bitcast.15), channel_id=1, source_target_pairs={{0,8},{8,0},{16,24},{24,16},{32,40},{40,32},{48,56},{56,48},{64,72... | collective-permute-start | bytes 589832 | tf_op jit(solution)/shard_map/ppermute | solution.py:50
  45.2 2.3 %copy-done = bf16[2,384,3072]{2,1,0:T(8,128)(2,1)S(1)} copy-done((bf16[2,384,3072]{2,1,0:T(8,128)(2,1)S(1)}, bf16[2,384,3072]{2,1,0:T(8,128)(2,1)}, u32[]{:S(2)}) %copy-start) | copy-done | bytes 4718616
  47.5 2.7 %load.1.w = bf16[4,384,3072]{2,1,0:T(8,128)(2,1)S(1)} custom-call(bf16[2,384,3072]{2,1,0:T(8,128)(2,1)S(1)} %copy-done, bf16[2,384,3072]{2,1,0:T(8,128)(2,1)} %collective-permute-done.4.other), custom_call_target="tpu_custom_call" | custom-call | bytes 18874368 | tf_op jit(solution)/shard_map/load/pallas_call | solution.py:90
  50.8 7.3 %solve.1 = f32[8,2,16,128]{3,2,1,0:T(8,128)S(1)} custom-call(s32[4,64]{1,0:T(4,128)S(1)} %select_reduce_fusion.partner, f32[1,384]{1,0:T(1,128)S(1)} %reshape.12.coulomb, bf16[4,384,3072]{2,1,0:T(8,128)(2,1)S(1)} %load.1.w, bf16[2,256,384]{2,1,0:T(8,128)(2,1)S(1)} %pad_maximum_fusion.p01, bf16[2,256,384]{2,1,0:T(8,128)(2,1)S(1)} %constant_dynamic-update-slice_fusion.5.p23, ...), custom_call_target="tpu_custom_call" | custom-call | flops 4831838208 | bytes 9437184 | tf_op jit(solution)/shard_map/solve/pallas_call | solution.py:160
  58.0 10.9 %all_to_all.10.terms = f32[8,2,16,128]{3,2,1,0:T(8,128)S(1)} all-to-all(f32[8,2,16,128]{3,2,1,0:T(8,128)S(1)} %solve.1), channel_id=1, replica_groups=mesh['row'=32,'col'=8] {'col'}, dimensions={0} | all-to-all | bytes 262144 | tf_op jit(solution)/shard_map/all_to_all | solution.py:290
  69.2 17.5 %all_to_all.11.arrived = bf16[32,16,128]{2,1,0:T(8,128)(2,1)S(1)} all-to-all(bf16[32,16,128]{2,1,0:T(8,128)(2,1)S(1)} %spread.1), channel_id=1, replica_groups=mesh['row'=32,'col'=8] {'row'}, dimensions={0} | all-to-all | bytes 262144 | tf_op jit(solution)/shard_map/all_to_all | solution.py:292
  (30 shorter events, 5.0 us)
Async XLA Ops:
  0.0 18.5 %collective-permute-start.4 = (bf16[2,384,3072]{2,1,0:T(8,128)(2,1)}, bf16[2,384,3072]{2,1,0:T(8,128)(2,1)}, u32[]{:S(2)}, u32[]{:S(2)}) collective-permute-start(bf16[2,384,3072]{2,1,0:T(8,128)(2,1)} %own), channel_id=1, source_target_pairs={{0,8},{8,0},{16,24},{24,16},{32,40},{40,32},{48,56},{56,48},{64,72... | collective-permute-start | bytes 14155784 | tf_op jit(solution)/shard_map/ppermute | solution.py:50
  3.2 2.9 %collective-permute-start = (bf16[1,32,384]{2,1,0:T(8,128)(2,1)}, bf16[1,32,384]{2,1,0:T(8,128)(2,1)S(1)}, u32[]{:S(2)}, u32[]{:S(2)}) collective-permute-start(bf16[1,32,384]{2,1,0:T(8,128)(2,1)} %bitcast.16), channel_id=1, source_target_pairs={{0,16},{8,24},{16,0},{24,8},{32,48},{40,56},{48,32},{56,40},{64,80... | collective-permute-start | bytes 73736 | tf_op jit(solution)/shard_map/ppermute | solution.py:50
  6.9 9.0 %collective-permute-start.1 = (bf16[2,32,384]{2,1,0:T(8,128)(2,1)S(1)}, bf16[2,32,384]{2,1,0:T(8,128)(2,1)S(1)}, u32[]{:S(2)}, u32[]{:S(2)}) collective-permute-start(bf16[2,32,384]{2,1,0:T(8,128)(2,1)S(1)} %pad_maximum_fusion.1), channel_id=1, source_target_pairs={{0,32},{8,40},{16,48},{24,56},{32,64},{40,72},{48,80},{56,88},{64,... | collective-permute-start | bytes 147464 | tf_op jit(solution)/shard_map/ppermute | solution.py:50
  9.2 7.7 %collective-permute-start.2 = (bf16[2,32,384]{2,1,0:T(8,128)(2,1)S(1)}, bf16[2,32,384]{2,1,0:T(8,128)(2,1)S(1)}, u32[]{:S(2)}, u32[]{:S(2)}) collective-permute-start(bf16[2,32,384]{2,1,0:T(8,128)(2,1)S(1)} %pad_maximum_fusion.1), channel_id=1, source_target_pairs={{0,64},{8,72},{16,80},{24,88},{32,96},{40,104},{48,112},{56,120},{... | collective-permute-start | bytes 147464 | tf_op jit(solution)/shard_map/ppermute | solution.py:50
  13.5 5.1 %collective-permute-start.3 = (bf16[2,32,384]{2,1,0:T(8,128)(2,1)S(1)}, bf16[2,32,384]{2,1,0:T(8,128)(2,1)S(1)}, u32[]{:S(2)}, u32[]{:S(2)}) collective-permute-start(bf16[2,32,384]{2,1,0:T(8,128)(2,1)S(1)} %pad_maximum_fusion.1), channel_id=1, source_target_pairs={{0,96},{8,104},{16,112},{24,120},{32,0},{40,8},{48,16},{56,24},{64... | collective-permute-start | bytes 147464 | tf_op jit(solution)/shard_map/ppermute | solution.py:50
  18.6 6.4 %collective-permute-start.5 = (bf16[1,256,384]{2,1,0:T(8,128)(2,1)S(1)}, bf16[1,256,384]{2,1,0:T(8,128)(2,1)S(1)}, u32[]{:S(2)}, u32[]{:S(2)}) collective-permute-start(bf16[1,256,384]{2,1,0:T(8,128)(2,1)S(1)} %bitcast.10), channel_id=1, source_target_pairs={{0,2},{8,12},{16,18},{24,28},{32,34},{40,44},{48,50},{56,60},{64,6... | collective-permute-start | bytes 589832 | tf_op jit(solution)/shard_map/ppermute | solution.py:50
  21.6 5.9 %collective-permute-start.8 = (bf16[1,256,384]{2,1,0:T(8,128)(2,1)S(1)}, bf16[1,256,384]{2,1,0:T(8,128)(2,1)S(1)}, u32[]{:S(2)}, u32[]{:S(2)}) collective-permute-start(bf16[1,256,384]{2,1,0:T(8,128)(2,1)S(1)} %bitcast.11), channel_id=1, source_target_pairs={{0,3},{8,140},{16,19},{24,156},{32,35},{40,172},{48,51},{56,188},{... | collective-permute-start | bytes 589832 | tf_op jit(solution)/shard_map/ppermute | solution.py:50
  22.4 5.7 %collective-permute-start.7 = (bf16[1,256,384]{2,1,0:T(8,128)(2,1)S(1)}, bf16[1,256,384]{2,1,0:T(8,128)(2,1)S(1)}, u32[]{:S(2)}, u32[]{:S(2)}) collective-permute-start(bf16[1,256,384]{2,1,0:T(8,128)(2,1)S(1)} %bitcast.12), channel_id=1, source_target_pairs={{0,1},{8,136},{16,17},{24,152},{32,33},{40,168},{48,49},{56,184},{... | collective-permute-start | bytes 589832 | tf_op jit(solution)/shard_map/ppermute | solution.py:50
  25.0 9.9 %collective-permute-start.6 = (bf16[2,256,384]{2,1,0:T(8,128)(2,1)S(1)}, bf16[2,256,384]{2,1,0:T(8,128)(2,1)S(1)}, u32[]{:S(2)}, u32[]{:S(2)}) collective-permute-start(bf16[2,256,384]{2,1,0:T(8,128)(2,1)S(1)} %pad_maximum_fusion.p01), channel_id=1, source_target_pairs={{0,128},{8,9},{16,144},{24,25},{32,160},{40,41},{48,176},{56,57},{... | collective-permute-start | bytes 1179656 | tf_op jit(solution)/shard_map/ppermute | solution.py:50
  28.2 7.6 %collective-permute-start.9 = (bf16[2,256,384]{2,1,0:T(8,128)(2,1)S(1)}, bf16[2,256,384]{2,1,0:T(8,128)(2,1)S(1)}, u32[]{:S(2)}, u32[]{:S(2)}) collective-permute-start(bf16[2,256,384]{2,1,0:T(8,128)(2,1)S(1)} %constant_dynamic-update-slice_fusion.5.p23), channel_id=1, source_target_pairs={{0,132},{8,11},{16,148},{24,27},{32,164},{40,43},{48,180},{56,59},... | collective-permute-start | bytes 1179656 | tf_op jit(solution)/shard_map/ppermute | solution.py:50
  31.1 14.1 %collective-permute-start.10 = (bf16[2,256,384]{2,1,0:T(8,128)(2,1)S(1)}, bf16[2,256,384]{2,1,0:T(8,128)(2,1)S(1)}, u32[]{:S(2)}, u32[]{:S(2)}) collective-permute-start(bf16[2,256,384]{2,1,0:T(8,128)(2,1)S(1)} %constant_dynamic-update-slice_fusion.5.p23), channel_id=1, source_target_pairs={{0,128},{8,9},{16,144},{24,25},{32,160},{40,41},{48,176},{56,57},{... | collective-permute-start | bytes 1179656 | tf_op jit(solution)/shard_map/ppermute | solution.py:50
  31.1 19.2 %collective-permute-start.11 = (bf16[2,256,384]{2,1,0:T(8,128)(2,1)S(1)}, bf16[2,256,384]{2,1,0:T(8,128)(2,1)S(1)}, u32[]{:S(2)}, u32[]{:S(2)}) collective-permute-start(bf16[2,256,384]{2,1,0:T(8,128)(2,1)S(1)} %pad_maximum_fusion.p01), channel_id=1, source_target_pairs={{0,132},{8,11},{16,148},{24,27},{32,164},{40,43},{48,180},{56,59},... | collective-permute-start | bytes 1179656 | tf_op jit(solution)/shard_map/ppermute | solution.py:50
  35.0 15.8 %collective-permute-start.12 = (bf16[2,256,384]{2,1,0:T(8,128)(2,1)S(1)}, bf16[2,256,384]{2,1,0:T(8,128)(2,1)S(1)}, u32[]{:S(2)}, u32[]{:S(2)}) collective-permute-start(bf16[2,256,384]{2,1,0:T(8,128)(2,1)S(1)} %collective-permute-done.6.f0), channel_id=1, source_target_pairs={{0,128},{8,9},{16,144},{24,25},{32,160},{40,41},{48,176},{56,57},{... | collective-permute-start | bytes 1179656 | tf_op jit(solution)/shard_map/ppermute | solution.py:50
  35.8 15.0 %collective-permute-start.13 = (bf16[2,256,384]{2,1,0:T(8,128)(2,1)S(1)}, bf16[2,256,384]{2,1,0:T(8,128)(2,1)S(1)}, u32[]{:S(2)}, u32[]{:S(2)}) collective-permute-start(bf16[2,256,384]{2,1,0:T(8,128)(2,1)S(1)} %collective-permute-done.9.g1), channel_id=1, source_target_pairs={{0,132},{8,11},{16,148},{24,27},{32,164},{40,43},{48,180},{56,59},... | collective-permute-start | bytes 1179656 | tf_op jit(solution)/shard_map/ppermute | solution.py:50
  38.9 11.3 %collective-permute-start.14 = (bf16[1,256,384]{2,1,0:T(8,128)(2,1)S(1)}, bf16[1,256,384]{2,1,0:T(8,128)(2,1)S(1)}, u32[]{:S(2)}, u32[]{:S(2)}) collective-permute-start(bf16[1,256,384]{2,1,0:T(8,128)(2,1)S(1)} %bitcast.15), channel_id=1, source_target_pairs={{0,8},{8,0},{16,24},{24,16},{32,40},{40,32},{48,56},{56,48},{64,72... | collective-permute-start | bytes 589832 | tf_op jit(solution)/shard_map/ppermute | solution.py:50
  45.2 5.6 %collective-permute-start.15 = (bf16[1,256,384]{2,1,0:T(8,128)(2,1)S(1)}, bf16[1,256,384]{2,1,0:T(8,128)(2,1)S(1)}, u32[]{:S(2)}, u32[]{:S(2)}) collective-permute-start(bf16[1,256,384]{2,1,0:T(8,128)(2,1)S(1)} %get-tuple-element.28), channel_id=1, source_target_pairs={{0,136},{8,0},{16,152},{24,16},{32,168},{40,32},{48,184},{56,48},{... | collective-permute-start | bytes 589832 | tf_op jit(solution)/shard_map/ppermute | solution.py:50
  45.2 2.3 %copy-start = (bf16[2,384,3072]{2,1,0:T(8,128)(2,1)S(1)}, bf16[2,384,3072]{2,1,0:T(8,128)(2,1)}, u32[]{:S(2)}) copy-start(bf16[2,384,3072]{2,1,0:T(8,128)(2,1)} %own) | copy-start | bytes 14155780
  50.2 18.7 %copy-start.1 = (s32[64,64]{1,0:T(8,128)S(1)}, s32[64,64]{1,0:T(8,128)}, u32[]{:S(2)}) copy-start(s32[64,64]{1,0:T(8,128)} %q_index.1) | copy-start | bytes 49156

commit v17 on v16

--- a/solution.py
+++ b/solution.py
@@ -9,7 +9,7 @@
 NX, NY, NZ, NCORE = 4, 4, 8, 2
 FIRST = (0, 2, 1, -1)
 SECOND = (0, 2, 1, -1)
-ZSHIFTS = (0, 2, 4, -2)
+ZSHIFTS = (0, 4, 2, -2)
 MIB = 1024 * 1024
 
 
@@ -70,7 +70,8 @@
 def place_of(z_wanted):
     z = where_am_i()[3]
     side = (z ^ z_wanted) & 1
-    return (((z ^ side) - z_wanted) & 7) + side
+    away = ((z ^ side) - z_wanted) & 7
+    return 2 * ((away & 2) + (away >> 2)) + side
 
 
 def load_kernel(own, other, out, sems):
@@ -128,18 +129,19 @@
     twice = 2.0 * coulomb[...]
     for pair in range(4):
         columns = left_rows[128 * pair : 128 * pair + 128, :]
-        blocks = []
+        lefts, blocks = [], []
         for q in range(4):
-            left = []
             for i in range(8):
                 k = partner[q, 16 * pair + 8 * (i // 4) + 4 * (i // 2 % 2) + 2 * c + i % 2]
                 block = ((((k >> 1) & 1) ^ c) * 2 + (k >> 5)) * NZ + ((k >> 2) & 7)
                 start = pl.multiple_of(block * 32 + (k & 1) * 16, 16)
-                left.append(left_rows[pl.ds(start, 16), :])
-            left = jnp.concatenate(left, axis=0)
-            weighted = (left.astype(jnp.float32) * twice).astype(left.dtype)
-            met = contract(weighted, columns) - jnp.dot(
-                left,
+                lefts.append(left_rows[pl.ds(start, 16), :])
+        lefts = jnp.concatenate(lefts, axis=0)
+        weighted = (lefts.astype(jnp.float32) * twice).astype(lefts.dtype)
+        bare = contract(weighted, columns)
+        for q in range(4):
+            met = bare[128 * q : 128 * q + 128] - jnp.dot(
+                lefts[128 * q : 128 * q + 128],
                 image[q, :, 128 * pair : 128 * pair + 128],
                 preferred_element_type=jnp.float32,
             )

time: 87.8 us -> 87.2 us (level)
  starting transfers between devices: 32.6 us -> 33.8 us
  blocking collectives: 28.5 us -> 27.5 us
  waiting for transfers between devices: 9.76 us -> 8.77 us
    all_to_all x1, blocking collectives: 17.5 us -> 16 us  [local(): lax.all_to_all(placed, 'row', split_axis=0, concat_axis=0, tiled=True)]
    ppermute x16, starting transfers between devices: 32.6 us -> 33.8 us  [send(): return lax.ppermute(value, AXES, perm)]
    ppermute x16, waiting for transfers between devices: 9.76 us -> 8.77 us  [send(): return lax.ppermute(value, AXES, perm)]
  transfers between devices with their start and end apart: 16 -> 16, of which waited for: 9 -> 8; matrix products, arithmetic and copies ran while one was open for 4% -> 4% of each run, Pallas kernels for 3% -> 3%
where the time goes in v17:
time: 87.2 us; the launch traced here: 86.8 us
  starting transfers between devices  33.8 us (39%)
  blocking collectives  27.5 us (32%)
  Pallas kernels  10.9 us (12%)
  waiting for transfers between devices  8.77 us (10%)
  local copies, waits for them, and re-layouts  3.84 us (4%)
  other arithmetic  1.82 us (2%)
    ppermute x16, starting transfers between devices, send(): return lax.ppermute(value, AXES, perm)  33.8 us
    all_to_all x1, blocking collectives, local(): lax.all_to_all(placed, 'row', split_axis=0, concat_axis=0, tiled=True)  16 us
    all_to_all x1, blocking collectives, local(): lax.all_to_all(terms, 'col', split_axis=0, concat_axis=0, tiled=True)  11.6 us
    ppermute x16, waiting for transfers between devices, send(): return lax.ppermute(value, AXES, perm)  8.77 us
    pallas_call x1, Pallas kernels, solve(): pl.pallas_call(solve_kernel, in_specs=[pl.BlockSpec(memory_space=pltpu.SM...  7.28 us
    unnamed x8, local copies, waits for them, and re-layouts  3.12 us
    pallas_call x1, Pallas kernels, load(): pl.pallas_call(load_kernel, in_specs=[pl.BlockSpec(memory_space=pl.ANY)]...  2.72 us
  transfers between devices with their start and end apart: 16, of which 8 were waited for; matrix products, arithmetic and copies ran while one was open for 4% of the time, Pallas kernels for 3%

profile of v17, /device:TPU:1, one launch (start us, length us, event | category | flops | bytes accessed | tf_op | source)
XLA Modules:
  0.0 86.8 jit_solution(379783107568909089)
XLA Ops:
  0.0 3.2 %collective-permute-start.4 = (bf16[2,384,3072]{2,1,0:T(8,128)(2,1)}, bf16[2,384,3072]{2,1,0:T(8,128)(2,1)}, u32[]{:S(2)}, u32[]{:S(2)}) collective-permute-start(bf16[2,384,3072]{2,1,0:T(8,128)(2,1)} %own), channel_id=1, source_target_pairs={{0,8},{8,0},{16,24},{24,16},{32,40},{40,32},{48,56},{56,48},{64,72... | collective-permute-start | bytes 14155784 | tf_op jit(solution)/shard_map/ppermute | solution.py:50
  3.3 0.9 select_reduce_fusion.partner
  4.2 0.7 constant_dynamic-update-slice_fusion.4
  6.1 0.7 pad_maximum_fusion.1
  6.9 5.4 %collective-permute-start.1 = (bf16[2,32,384]{2,1,0:T(8,128)(2,1)S(1)}, bf16[2,32,384]{2,1,0:T(8,128)(2,1)S(1)}, u32[]{:S(2)}, u32[]{:S(2)}) collective-permute-start(bf16[2,32,384]{2,1,0:T(8,128)(2,1)S(1)} %pad_maximum_fusion.1), channel_id=1, source_target_pairs={{0,64},{8,72},{16,80},{24,88},{32,96},{40,104},{48,112},{56,120},{... | collective-permute-start | bytes 147464 | tf_op jit(solution)/shard_map/ppermute | solution.py:50
  12.3 1.2 %collective-permute-start.2 = (bf16[2,32,384]{2,1,0:T(8,128)(2,1)S(1)}, bf16[2,32,384]{2,1,0:T(8,128)(2,1)S(1)}, u32[]{:S(2)}, u32[]{:S(2)}) collective-permute-start(bf16[2,32,384]{2,1,0:T(8,128)(2,1)S(1)} %pad_maximum_fusion.1), channel_id=1, source_target_pairs={{0,32},{8,40},{16,48},{24,56},{32,64},{40,72},{48,80},{56,88},{64,... | collective-permute-start | bytes 147464 | tf_op jit(solution)/shard_map/ppermute | solution.py:50
  13.5 2.4 %collective-permute-start.3 = (bf16[2,32,384]{2,1,0:T(8,128)(2,1)S(1)}, bf16[2,32,384]{2,1,0:T(8,128)(2,1)S(1)}, u32[]{:S(2)}, u32[]{:S(2)}) collective-permute-start(bf16[2,32,384]{2,1,0:T(8,128)(2,1)S(1)} %pad_maximum_fusion.1), channel_id=1, source_target_pairs={{0,96},{8,104},{16,112},{24,120},{32,0},{40,8},{48,16},{56,24},{64... | collective-permute-start | bytes 147464 | tf_op jit(solution)/shard_map/ppermute | solution.py:50
  15.9 2.0 %collective-permute-done.2 = bf16[2,32,384]{2,1,0:T(8,128)(2,1)S(1)} collective-permute-done((bf16[2,32,384]{2,1,0:T(8,128)(2,1)S(1)}, bf16[2,32,384]{2,1,0:T(8,128)(2,1)S(1)}, u32[]{:S(2)}, u32[]{:S(2)}) %collective-permute-start.2) | collective-permute-done | bytes 49184 | tf_op jit(solution)/shard_map/ppermute | solution.py:50
  17.9 3.0 %collective-permute-start.5 = (bf16[1,256,384]{2,1,0:T(8,128)(2,1)S(1)}, bf16[1,256,384]{2,1,0:T(8,128)(2,1)S(1)}, u32[]{:S(2)}, u32[]{:S(2)}) collective-permute-start(bf16[1,256,384]{2,1,0:T(8,128)(2,1)S(1)} %bitcast.10), channel_id=1, source_target_pairs={{0,2},{8,12},{16,18},{24,28},{32,34},{40,44},{48,50},{56,60},{64,6... | collective-permute-start | bytes 589832 | tf_op jit(solution)/shard_map/ppermute | solution.py:50
  20.9 0.8 collective-permute-start.8
  22.4 1.6 %collective-permute-done.5 = bf16[1,256,384]{2,1,0:T(8,128)(2,1)S(1)} collective-permute-done((bf16[1,256,384]{2,1,0:T(8,128)(2,1)S(1)}, bf16[1,256,384]{2,1,0:T(8,128)(2,1)S(1)}, u32[]{:S(2)}, u32[]{:S(2)}) %collective-permute-start.5) | collective-permute-done | bytes 196640 | tf_op jit(solution)/shard_map/ppermute | solution.py:50
  24.1 1.3 %collective-permute-start.6 = (bf16[2,256,384]{2,1,0:T(8,128)(2,1)S(1)}, bf16[2,256,384]{2,1,0:T(8,128)(2,1)S(1)}, u32[]{:S(2)}, u32[]{:S(2)}) collective-permute-start(bf16[2,256,384]{2,1,0:T(8,128)(2,1)S(1)} %pad_maximum_fusion.p01), channel_id=1, source_target_pairs={{0,128},{8,9},{16,144},{24,25},{32,160},{40,41},{48,176},{56,57},{... | collective-permute-start | bytes 1179656 | tf_op jit(solution)/shard_map/ppermute | solution.py:50
  25.4 1.4 %collective-permute-done.8 = bf16[1,256,384]{2,1,0:T(8,128)(2,1)S(1)} collective-permute-done((bf16[1,256,384]{2,1,0:T(8,128)(2,1)S(1)}, bf16[1,256,384]{2,1,0:T(8,128)(2,1)S(1)}, u32[]{:S(2)}, u32[]{:S(2)}) %collective-permute-start.8) | collective-permute-done | bytes 196640 | tf_op jit(solution)/shard_map/ppermute | solution.py:50
  27.5 2.9 %collective-permute-start.9 = (bf16[2,256,384]{2,1,0:T(8,128)(2,1)S(1)}, bf16[2,256,384]{2,1,0:T(8,128)(2,1)S(1)}, u32[]{:S(2)}, u32[]{:S(2)}) collective-permute-start(bf16[2,256,384]{2,1,0:T(8,128)(2,1)S(1)} %constant_dynamic-update-slice_fusion.5.p23), channel_id=1, source_target_pairs={{0,132},{8,11},{16,148},{24,27},{32,164},{40,43},{48,180},{56,59},... | collective-permute-start | bytes 1179656 | tf_op jit(solution)/shard_map/ppermute | solution.py:50
  30.4 2.7 %collective-permute-start.11 = (bf16[2,256,384]{2,1,0:T(8,128)(2,1)S(1)}, bf16[2,256,384]{2,1,0:T(8,128)(2,1)S(1)}, u32[]{:S(2)}, u32[]{:S(2)}) collective-permute-start(bf16[2,256,384]{2,1,0:T(8,128)(2,1)S(1)} %pad_maximum_fusion.p01), channel_id=1, source_target_pairs={{0,132},{8,11},{16,148},{24,27},{32,164},{40,43},{48,180},{56,59},... | collective-permute-start | bytes 1179656 | tf_op jit(solution)/shard_map/ppermute | solution.py:50
  33.1 1.3 %collective-permute-done.6.f0 = bf16[2,256,384]{2,1,0:T(8,128)(2,1)S(1)} collective-permute-done((bf16[2,256,384]{2,1,0:T(8,128)(2,1)S(1)}, bf16[2,256,384]{2,1,0:T(8,128)(2,1)S(1)}, u32[]{:S(2)}, u32[]{:S(2)}) %collective-permute-start.6) | collective-permute-done | bytes 393248 | tf_op jit(solution)/shard_map/ppermute | solution.py:50
  35.1 3.4 %collective-permute-start.13 = (bf16[2,256,384]{2,1,0:T(8,128)(2,1)S(1)}, bf16[2,256,384]{2,1,0:T(8,128)(2,1)S(1)}, u32[]{:S(2)}, u32[]{:S(2)}) collective-permute-start(bf16[2,256,384]{2,1,0:T(8,128)(2,1)S(1)} %collective-permute-done.9.g1), channel_id=1, source_target_pairs={{0,132},{8,11},{16,148},{24,27},{32,164},{40,43},{48,180},{56,59},... | collective-permute-start | bytes 1179656 | tf_op jit(solution)/shard_map/ppermute | solution.py:50
  38.5 6.9 %collective-permute-start.14 = (bf16[1,256,384]{2,1,0:T(8,128)(2,1)S(1)}, bf16[1,256,384]{2,1,0:T(8,128)(2,1)S(1)}, u32[]{:S(2)}, u32[]{:S(2)}) collective-permute-start(bf16[1,256,384]{2,1,0:T(8,128)(2,1)S(1)} %bitcast.15), channel_id=1, source_target_pairs={{0,8},{8,0},{16,24},{24,16},{32,40},{40,32},{48,56},{56,48},{64,72... | collective-permute-start | bytes 589832 | tf_op jit(solution)/shard_map/ppermute | solution.py:50
  45.4 2.3 %copy-done = bf16[2,384,3072]{2,1,0:T(8,128)(2,1)S(1)} copy-done((bf16[2,384,3072]{2,1,0:T(8,128)(2,1)S(1)}, bf16[2,384,3072]{2,1,0:T(8,128)(2,1)}, u32[]{:S(2)}) %copy-start) | copy-done | bytes 4718616
  47.7 2.7 %load.1.w = bf16[4,384,3072]{2,1,0:T(8,128)(2,1)S(1)} custom-call(bf16[2,384,3072]{2,1,0:T(8,128)(2,1)S(1)} %copy-done, bf16[2,384,3072]{2,1,0:T(8,128)(2,1)} %collective-permute-done.4.other), custom_call_target="tpu_custom_call" | custom-call | bytes 18874368 | tf_op jit(solution)/shard_map/load/pallas_call | solution.py:91
  51.1 7.3 %solve.1 = f32[8,2,16,128]{3,2,1,0:T(8,128)S(1)} custom-call(s32[4,64]{1,0:T(4,128)S(1)} %select_reduce_fusion.partner, f32[1,384]{1,0:T(1,128)S(1)} %reshape.12.coulomb, bf16[4,384,3072]{2,1,0:T(8,128)(2,1)S(1)} %load.1.w, bf16[2,256,384]{2,1,0:T(8,128)(2,1)S(1)} %pad_maximum_fusion.p01, bf16[2,256,384]{2,1,0:T(8,128)(2,1)S(1)} %constant_dynamic-update-slice_fusion.5.p23, ...), custom_call_target="tpu_custom_call" | custom-call | flops 4831838208 | bytes 9437184 | tf_op jit(solution)/shard_map/solve/pallas_call | solution.py:162
  58.3 11.6 %all_to_all.10.terms = f32[8,2,16,128]{3,2,1,0:T(8,128)S(1)} all-to-all(f32[8,2,16,128]{3,2,1,0:T(8,128)S(1)} %solve.1), channel_id=1, replica_groups=mesh['row'=32,'col'=8] {'col'}, dimensions={0} | all-to-all | bytes 262144 | tf_op jit(solution)/shard_map/all_to_all | solution.py:292
  70.1 16.0 %all_to_all.11.arrived = bf16[32,16,128]{2,1,0:T(8,128)(2,1)S(1)} all-to-all(bf16[32,16,128]{2,1,0:T(8,128)(2,1)S(1)} %spread.1), channel_id=1, replica_groups=mesh['row'=32,'col'=8] {'row'}, dimensions={0} | all-to-all | bytes 262144 | tf_op jit(solution)/shard_map/all_to_all | solution.py:294
  86.1 0.7 settle.1
  (30 shorter events, 4.4 us)
Async XLA Ops:
  0.0 17.9 %collective-permute-start.4 = (bf16[2,384,3072]{2,1,0:T(8,128)(2,1)}, bf16[2,384,3072]{2,1,0:T(8,128)(2,1)}, u32[]{:S(2)}, u32[]{:S(2)}) collective-permute-start(bf16[2,384,3072]{2,1,0:T(8,128)(2,1)} %own), channel_id=1, source_target_pairs={{0,8},{8,0},{16,24},{24,16},{32,40},{40,32},{48,56},{56,48},{64,72... | collective-permute-start | bytes 14155784 | tf_op jit(solution)/shard_map/ppermute | solution.py:50
  3.2 2.9 %collective-permute-start = (bf16[1,32,384]{2,1,0:T(8,128)(2,1)}, bf16[1,32,384]{2,1,0:T(8,128)(2,1)S(1)}, u32[]{:S(2)}, u32[]{:S(2)}) collective-permute-start(bf16[1,32,384]{2,1,0:T(8,128)(2,1)} %bitcast.16), channel_id=1, source_target_pairs={{0,16},{8,24},{16,0},{24,8},{32,48},{40,56},{48,32},{56,40},{64,80... | collective-permute-start | bytes 73736 | tf_op jit(solution)/shard_map/ppermute | solution.py:50
  6.9 9.0 %collective-permute-start.1 = (bf16[2,32,384]{2,1,0:T(8,128)(2,1)S(1)}, bf16[2,32,384]{2,1,0:T(8,128)(2,1)S(1)}, u32[]{:S(2)}, u32[]{:S(2)}) collective-permute-start(bf16[2,32,384]{2,1,0:T(8,128)(2,1)S(1)} %pad_maximum_fusion.1), channel_id=1, source_target_pairs={{0,64},{8,72},{16,80},{24,88},{32,96},{40,104},{48,112},{56,120},{... | collective-permute-start | bytes 147464 | tf_op jit(solution)/shard_map/ppermute | solution.py:50
  12.3 5.6 %collective-permute-start.2 = (bf16[2,32,384]{2,1,0:T(8,128)(2,1)S(1)}, bf16[2,32,384]{2,1,0:T(8,128)(2,1)S(1)}, u32[]{:S(2)}, u32[]{:S(2)}) collective-permute-start(bf16[2,32,384]{2,1,0:T(8,128)(2,1)S(1)} %pad_maximum_fusion.1), channel_id=1, source_target_pairs={{0,32},{8,40},{16,48},{24,56},{32,64},{40,72},{48,80},{56,88},{64,... | collective-permute-start | bytes 147464 | tf_op jit(solution)/shard_map/ppermute | solution.py:50
  13.5 4.4 %collective-permute-start.3 = (bf16[2,32,384]{2,1,0:T(8,128)(2,1)S(1)}, bf16[2,32,384]{2,1,0:T(8,128)(2,1)S(1)}, u32[]{:S(2)}, u32[]{:S(2)}) collective-permute-start(bf16[2,32,384]{2,1,0:T(8,128)(2,1)S(1)} %pad_maximum_fusion.1), channel_id=1, source_target_pairs={{0,96},{8,104},{16,112},{24,120},{32,0},{40,8},{48,16},{56,24},{64... | collective-permute-start | bytes 147464 | tf_op jit(solution)/shard_map/ppermute | solution.py:50
  17.9 6.1 %collective-permute-start.5 = (bf16[1,256,384]{2,1,0:T(8,128)(2,1)S(1)}, bf16[1,256,384]{2,1,0:T(8,128)(2,1)S(1)}, u32[]{:S(2)}, u32[]{:S(2)}) collective-permute-start(bf16[1,256,384]{2,1,0:T(8,128)(2,1)S(1)} %bitcast.10), channel_id=1, source_target_pairs={{0,2},{8,12},{16,18},{24,28},{32,34},{40,44},{48,50},{56,60},{64,6... | collective-permute-start | bytes 589832 | tf_op jit(solution)/shard_map/ppermute | solution.py:50
  20.9 5.9 %collective-permute-start.8 = (bf16[1,256,384]{2,1,0:T(8,128)(2,1)S(1)}, bf16[1,256,384]{2,1,0:T(8,128)(2,1)S(1)}, u32[]{:S(2)}, u32[]{:S(2)}) collective-permute-start(bf16[1,256,384]{2,1,0:T(8,128)(2,1)S(1)} %bitcast.11), channel_id=1, source_target_pairs={{0,3},{8,140},{16,19},{24,156},{32,35},{40,172},{48,51},{56,188},{... | collective-permute-start | bytes 589832 | tf_op jit(solution)/shard_map/ppermute | solution.py:50
  21.7 5.7 %collective-permute-start.7 = (bf16[1,256,384]{2,1,0:T(8,128)(2,1)S(1)}, bf16[1,256,384]{2,1,0:T(8,128)(2,1)S(1)}, u32[]{:S(2)}, u32[]{:S(2)}) collective-permute-start(bf16[1,256,384]{2,1,0:T(8,128)(2,1)S(1)} %bitcast.12), channel_id=1, source_target_pairs={{0,1},{8,136},{16,17},{24,152},{32,33},{40,168},{48,49},{56,184},{... | collective-permute-start | bytes 589832 | tf_op jit(solution)/shard_map/ppermute | solution.py:50
  24.1 10.3 %collective-permute-start.6 = (bf16[2,256,384]{2,1,0:T(8,128)(2,1)S(1)}, bf16[2,256,384]{2,1,0:T(8,128)(2,1)S(1)}, u32[]{:S(2)}, u32[]{:S(2)}) collective-permute-start(bf16[2,256,384]{2,1,0:T(8,128)(2,1)S(1)} %pad_maximum_fusion.p01), channel_id=1, source_target_pairs={{0,128},{8,9},{16,144},{24,25},{32,160},{40,41},{48,176},{56,57},{... | collective-permute-start | bytes 1179656 | tf_op jit(solution)/shard_map/ppermute | solution.py:50
  27.5 7.6 %collective-permute-start.9 = (bf16[2,256,384]{2,1,0:T(8,128)(2,1)S(1)}, bf16[2,256,384]{2,1,0:T(8,128)(2,1)S(1)}, u32[]{:S(2)}, u32[]{:S(2)}) collective-permute-start(bf16[2,256,384]{2,1,0:T(8,128)(2,1)S(1)} %constant_dynamic-update-slice_fusion.5.p23), channel_id=1, source_target_pairs={{0,132},{8,11},{16,148},{24,27},{32,164},{40,43},{48,180},{56,59},... | collective-permute-start | bytes 1179656 | tf_op jit(solution)/shard_map/ppermute | solution.py:50
  30.4 15.0 %collective-permute-start.10 = (bf16[2,256,384]{2,1,0:T(8,128)(2,1)S(1)}, bf16[2,256,384]{2,1,0:T(8,128)(2,1)S(1)}, u32[]{:S(2)}, u32[]{:S(2)}) collective-permute-start(bf16[2,256,384]{2,1,0:T(8,128)(2,1)S(1)} %constant_dynamic-update-slice_fusion.5.p23), channel_id=1, source_target_pairs={{0,128},{8,9},{16,144},{24,25},{32,160},{40,41},{48,176},{56,57},{... | collective-permute-start | bytes 1179656 | tf_op jit(solution)/shard_map/ppermute | solution.py:50
  30.4 20.1 %collective-permute-start.11 = (bf16[2,256,384]{2,1,0:T(8,128)(2,1)S(1)}, bf16[2,256,384]{2,1,0:T(8,128)(2,1)S(1)}, u32[]{:S(2)}, u32[]{:S(2)}) collective-permute-start(bf16[2,256,384]{2,1,0:T(8,128)(2,1)S(1)} %pad_maximum_fusion.p01), channel_id=1, source_target_pairs={{0,132},{8,11},{16,148},{24,27},{32,164},{40,43},{48,180},{56,59},... | collective-permute-start | bytes 1179656 | tf_op jit(solution)/shard_map/ppermute | solution.py:50
  34.4 16.7 %collective-permute-start.12 = (bf16[2,256,384]{2,1,0:T(8,128)(2,1)S(1)}, bf16[2,256,384]{2,1,0:T(8,128)(2,1)S(1)}, u32[]{:S(2)}, u32[]{:S(2)}) collective-permute-start(bf16[2,256,384]{2,1,0:T(8,128)(2,1)S(1)} %collective-permute-done.6.f0), channel_id=1, source_target_pairs={{0,128},{8,9},{16,144},{24,25},{32,160},{40,41},{48,176},{56,57},{... | collective-permute-start | bytes 1179656 | tf_op jit(solution)/shard_map/ppermute | solution.py:50
  35.1 15.9 %collective-permute-start.13 = (bf16[2,256,384]{2,1,0:T(8,128)(2,1)S(1)}, bf16[2,256,384]{2,1,0:T(8,128)(2,1)S(1)}, u32[]{:S(2)}, u32[]{:S(2)}) collective-permute-start(bf16[2,256,384]{2,1,0:T(8,128)(2,1)S(1)} %collective-permute-done.9.g1), channel_id=1, source_target_pairs={{0,132},{8,11},{16,148},{24,27},{32,164},{40,43},{48,180},{56,59},... | collective-permute-start | bytes 1179656 | tf_op jit(solution)/shard_map/ppermute | solution.py:50
  38.5 12.0 %collective-permute-start.14 = (bf16[1,256,384]{2,1,0:T(8,128)(2,1)S(1)}, bf16[1,256,384]{2,1,0:T(8,128)(2,1)S(1)}, u32[]{:S(2)}, u32[]{:S(2)}) collective-permute-start(bf16[1,256,384]{2,1,0:T(8,128)(2,1)S(1)} %bitcast.15), channel_id=1, source_target_pairs={{0,8},{8,0},{16,24},{24,16},{32,40},{40,32},{48,56},{56,48},{64,72... | collective-permute-start | bytes 589832 | tf_op jit(solution)/shard_map/ppermute | solution.py:50
  45.4 5.7 %collective-permute-start.15 = (bf16[1,256,384]{2,1,0:T(8,128)(2,1)S(1)}, bf16[1,256,384]{2,1,0:T(8,128)(2,1)S(1)}, u32[]{:S(2)}, u32[]{:S(2)}) collective-permute-start(bf16[1,256,384]{2,1,0:T(8,128)(2,1)S(1)} %get-tuple-element.28), channel_id=1, source_target_pairs={{0,136},{8,0},{16,152},{24,16},{32,168},{40,32},{48,184},{56,48},{... | collective-permute-start | bytes 589832 | tf_op jit(solution)/shard_map/ppermute | solution.py:50
  45.4 2.3 %copy-start = (bf16[2,384,3072]{2,1,0:T(8,128)(2,1)S(1)}, bf16[2,384,3072]{2,1,0:T(8,128)(2,1)}, u32[]{:S(2)}) copy-start(bf16[2,384,3072]{2,1,0:T(8,128)(2,1)} %own) | copy-start | bytes 14155780
  50.5 19.4 %copy-start.1 = (s32[64,64]{1,0:T(8,128)S(1)}, s32[64,64]{1,0:T(8,128)}, u32[]{:S(2)}) copy-start(s32[64,64]{1,0:T(8,128)} %q_index.1) | copy-start | bytes 49156

commit v18 on v17

--- a/solution.py
+++ b/solution.py
@@ -122,33 +122,36 @@
         for z in range(NZ):
             to = pl.multiple_of((2 + low) * rows + z * 32, 32)
             left_rows[pl.ds(to, 32), :] = stack[0, pl.ds(starts[z], 32), :]
-    for q in range(4):
-        image[q] = contract(w[q], panel[...]).astype(image.dtype)
-
     lane = lax.broadcasted_iota(jnp.int32, (16, 128), 1)
     twice = 2.0 * coulomb[...]
+    lefts, bares = [], []
     for pair in range(4):
-        columns = left_rows[128 * pair : 128 * pair + 128, :]
-        lefts, blocks = [], []
+        found = []
         for q in range(4):
             for i in range(8):
                 k = partner[q, 16 * pair + 8 * (i // 4) + 4 * (i // 2 % 2) + 2 * c + i % 2]
                 block = ((((k >> 1) & 1) ^ c) * 2 + (k >> 5)) * NZ + ((k >> 2) & 7)
                 start = pl.multiple_of(block * 32 + (k & 1) * 16, 16)
-                lefts.append(left_rows[pl.ds(start, 16), :])
-        lefts = jnp.concatenate(lefts, axis=0)
-        weighted = (lefts.astype(jnp.float32) * twice).astype(lefts.dtype)
-        bare = contract(weighted, columns)
-        for q in range(4):
-            met = bare[128 * q : 128 * q + 128] - jnp.dot(
-                lefts[128 * q : 128 * q + 128],
+                found.append(left_rows[pl.ds(start, 16), :])
+        found = jnp.concatenate(found, axis=0)
+        weighted = (found.astype(jnp.float32) * twice).astype(found.dtype)
+        lefts.append(found)
+        bares.append(contract(weighted, left_rows[128 * pair : 128 * pair + 128, :]))
+    kept = [[None] * 4 for _ in range(4)]
+    for q in range(4):
+        image[q] = contract(w[q], panel[...]).astype(image.dtype)
+        for pair in range(4):
+            met = bares[pair][128 * q : 128 * q + 128] - jnp.dot(
+                lefts[pair][128 * q : 128 * q + 128],
                 image[q, :, 128 * pair : 128 * pair + 128],
                 preferred_element_type=jnp.float32,
             )
             block = jnp.zeros((16, 128), jnp.float32)
             for i in range(8):
                 block = jnp.where(lane // 16 == i, met[16 * i : 16 * i + 16], block)
-            blocks.append(block)
+            kept[pair][q] = block
+    for pair in range(4):
+        blocks = kept[pair]
         for two in range(2):
             even, odd = blocks[2 * two], blocks[2 * two + 1]
             out[2 * pair, two] = jnp.where(lane < 64, even, pltpu.roll(odd, 64, 1))

time: 87.2 us -> 88 us (level)
  no operation moved by 1% of the time
where the time goes in v18:
time: 88 us; the launch traced here: 87.6 us
  starting transfers between devices  33.8 us (38%)
  blocking collectives  27.6 us (31%)
  Pallas kernels  11.7 us (13%)
  waiting for transfers between devices  8.77 us (10%)
  local copies, waits for them, and re-layouts  3.84 us (4%)
  other arithmetic  1.82 us (2%)
    ppermute x16, starting transfers between devices, send(): return lax.ppermute(value, AXES, perm)  33.8 us
    all_to_all x1, blocking collectives, local(): lax.all_to_all(placed, 'row', split_axis=0, concat_axis=0, tiled=True)  16 us
    all_to_all x1, blocking collectives, local(): lax.all_to_all(terms, 'col', split_axis=0, concat_axis=0, tiled=True)  11.6 us
    ppermute x16, waiting for transfers between devices, send(): return lax.ppermute(value, AXES, perm)  8.77 us
    pallas_call x1, Pallas kernels, solve(): pl.pallas_call(solve_kernel, in_specs=[pl.BlockSpec(memory_space=pltpu.SM...  8.04 us
    unnamed x8, local copies, waits for them, and re-layouts  3.12 us
    pallas_call x1, Pallas kernels, load(): pl.pallas_call(load_kernel, in_specs=[pl.BlockSpec(memory_space=pl.ANY)]...  2.72 us
  transfers between devices with their start and end apart: 16, of which 8 were waited for; matrix products, arithmetic and copies ran while one was open for 4% of the time, Pallas kernels for 3%

profile of v18, /device:TPU:1, one launch (start us, length us, event | category | flops | bytes accessed | tf_op | source)
XLA Modules:
  0.0 87.6 jit_solution(11792270059510534615)
XLA Ops:
  0.0 3.2 %collective-permute-start.4 = (bf16[2,384,3072]{2,1,0:T(8,128)(2,1)}, bf16[2,384,3072]{2,1,0:T(8,128)(2,1)}, u32[]{:S(2)}, u32[]{:S(2)}) collective-permute-start(bf16[2,384,3072]{2,1,0:T(8,128)(2,1)} %own), channel_id=1, source_target_pairs={{0,8},{8,0},{16,24},{24,16},{32,40},{40,32},{48,56},{56,48},{64,72... | collective-permute-start | bytes 14155784 | tf_op jit(solution)/shard_map/ppermute | solution.py:50
  3.3 0.9 select_reduce_fusion.partner
  4.2 0.7 constant_dynamic-update-slice_fusion.4
  6.1 0.7 pad_maximum_fusion.1
  6.9 5.4 %collective-permute-start.1 = (bf16[2,32,384]{2,1,0:T(8,128)(2,1)S(1)}, bf16[2,32,384]{2,1,0:T(8,128)(2,1)S(1)}, u32[]{:S(2)}, u32[]{:S(2)}) collective-permute-start(bf16[2,32,384]{2,1,0:T(8,128)(2,1)S(1)} %pad_maximum_fusion.1), channel_id=1, source_target_pairs={{0,64},{8,72},{16,80},{24,88},{32,96},{40,104},{48,112},{56,120},{... | collective-permute-start | bytes 147464 | tf_op jit(solution)/shard_map/ppermute | solution.py:50
  12.3 1.2 %collective-permute-start.2 = (bf16[2,32,384]{2,1,0:T(8,128)(2,1)S(1)}, bf16[2,32,384]{2,1,0:T(8,128)(2,1)S(1)}, u32[]{:S(2)}, u32[]{:S(2)}) collective-permute-start(bf16[2,32,384]{2,1,0:T(8,128)(2,1)S(1)} %pad_maximum_fusion.1), channel_id=1, source_target_pairs={{0,32},{8,40},{16,48},{24,56},{32,64},{40,72},{48,80},{56,88},{64,... | collective-permute-start | bytes 147464 | tf_op jit(solution)/shard_map/ppermute | solution.py:50
  13.5 2.4 %collective-permute-start.3 = (bf16[2,32,384]{2,1,0:T(8,128)(2,1)S(1)}, bf16[2,32,384]{2,1,0:T(8,128)(2,1)S(1)}, u32[]{:S(2)}, u32[]{:S(2)}) collective-permute-start(bf16[2,32,384]{2,1,0:T(8,128)(2,1)S(1)} %pad_maximum_fusion.1), channel_id=1, source_target_pairs={{0,96},{8,104},{16,112},{24,120},{32,0},{40,8},{48,16},{56,24},{64... | collective-permute-start | bytes 147464 | tf_op jit(solution)/shard_map/ppermute | solution.py:50
  15.9 2.0 %collective-permute-done.2 = bf16[2,32,384]{2,1,0:T(8,128)(2,1)S(1)} collective-permute-done((bf16[2,32,384]{2,1,0:T(8,128)(2,1)S(1)}, bf16[2,32,384]{2,1,0:T(8,128)(2,1)S(1)}, u32[]{:S(2)}, u32[]{:S(2)}) %collective-permute-start.2) | collective-permute-done | bytes 49184 | tf_op jit(solution)/shard_map/ppermute | solution.py:50
  17.9 3.0 %collective-permute-start.5 = (bf16[1,256,384]{2,1,0:T(8,128)(2,1)S(1)}, bf16[1,256,384]{2,1,0:T(8,128)(2,1)S(1)}, u32[]{:S(2)}, u32[]{:S(2)}) collective-permute-start(bf16[1,256,384]{2,1,0:T(8,128)(2,1)S(1)} %bitcast.10), channel_id=1, source_target_pairs={{0,2},{8,12},{16,18},{24,28},{32,34},{40,44},{48,50},{56,60},{64,6... | collective-permute-start | bytes 589832 | tf_op jit(solution)/shard_map/ppermute | solution.py:50
  20.9 0.8 collective-permute-start.8
  22.4 1.6 %collective-permute-done.5 = bf16[1,256,384]{2,1,0:T(8,128)(2,1)S(1)} collective-permute-done((bf16[1,256,384]{2,1,0:T(8,128)(2,1)S(1)}, bf16[1,256,384]{2,1,0:T(8,128)(2,1)S(1)}, u32[]{:S(2)}, u32[]{:S(2)}) %collective-permute-start.5) | collective-permute-done | bytes 196640 | tf_op jit(solution)/shard_map/ppermute | solution.py:50
  24.1 1.3 %collective-permute-start.6 = (bf16[2,256,384]{2,1,0:T(8,128)(2,1)S(1)}, bf16[2,256,384]{2,1,0:T(8,128)(2,1)S(1)}, u32[]{:S(2)}, u32[]{:S(2)}) collective-permute-start(bf16[2,256,384]{2,1,0:T(8,128)(2,1)S(1)} %pad_maximum_fusion.p01), channel_id=1, source_target_pairs={{0,128},{8,9},{16,144},{24,25},{32,160},{40,41},{48,176},{56,57},{... | collective-permute-start | bytes 1179656 | tf_op jit(solution)/shard_map/ppermute | solution.py:50
  25.4 1.4 %collective-permute-done.8 = bf16[1,256,384]{2,1,0:T(8,128)(2,1)S(1)} collective-permute-done((bf16[1,256,384]{2,1,0:T(8,128)(2,1)S(1)}, bf16[1,256,384]{2,1,0:T(8,128)(2,1)S(1)}, u32[]{:S(2)}, u32[]{:S(2)}) %collective-permute-start.8) | collective-permute-done | bytes 196640 | tf_op jit(solution)/shard_map/ppermute | solution.py:50
  27.5 2.9 %collective-permute-start.9 = (bf16[2,256,384]{2,1,0:T(8,128)(2,1)S(1)}, bf16[2,256,384]{2,1,0:T(8,128)(2,1)S(1)}, u32[]{:S(2)}, u32[]{:S(2)}) collective-permute-start(bf16[2,256,384]{2,1,0:T(8,128)(2,1)S(1)} %constant_dynamic-update-slice_fusion.5.p23), channel_id=1, source_target_pairs={{0,132},{8,11},{16,148},{24,27},{32,164},{40,43},{48,180},{56,59},... | collective-permute-start | bytes 1179656 | tf_op jit(solution)/shard_map/ppermute | solution.py:50
  30.4 2.7 %collective-permute-start.11 = (bf16[2,256,384]{2,1,0:T(8,128)(2,1)S(1)}, bf16[2,256,384]{2,1,0:T(8,128)(2,1)S(1)}, u32[]{:S(2)}, u32[]{:S(2)}) collective-permute-start(bf16[2,256,384]{2,1,0:T(8,128)(2,1)S(1)} %pad_maximum_fusion.p01), channel_id=1, source_target_pairs={{0,132},{8,11},{16,148},{24,27},{32,164},{40,43},{48,180},{56,59},... | collective-permute-start | bytes 1179656 | tf_op jit(solution)/shard_map/ppermute | solution.py:50
  33.1 1.3 %collective-permute-done.6.f0 = bf16[2,256,384]{2,1,0:T(8,128)(2,1)S(1)} collective-permute-done((bf16[2,256,384]{2,1,0:T(8,128)(2,1)S(1)}, bf16[2,256,384]{2,1,0:T(8,128)(2,1)S(1)}, u32[]{:S(2)}, u32[]{:S(2)}) %collective-permute-start.6) | collective-permute-done | bytes 393248 | tf_op jit(solution)/shard_map/ppermute | solution.py:50
  35.1 3.4 %collective-permute-start.13 = (bf16[2,256,384]{2,1,0:T(8,128)(2,1)S(1)}, bf16[2,256,384]{2,1,0:T(8,128)(2,1)S(1)}, u32[]{:S(2)}, u32[]{:S(2)}) collective-permute-start(bf16[2,256,384]{2,1,0:T(8,128)(2,1)S(1)} %collective-permute-done.9.g1), channel_id=1, source_target_pairs={{0,132},{8,11},{16,148},{24,27},{32,164},{40,43},{48,180},{56,59},... | collective-permute-start | bytes 1179656 | tf_op jit(solution)/shard_map/ppermute | solution.py:50
  38.5 6.9 %collective-permute-start.14 = (bf16[1,256,384]{2,1,0:T(8,128)(2,1)S(1)}, bf16[1,256,384]{2,1,0:T(8,128)(2,1)S(1)}, u32[]{:S(2)}, u32[]{:S(2)}) collective-permute-start(bf16[1,256,384]{2,1,0:T(8,128)(2,1)S(1)} %bitcast.15), channel_id=1, source_target_pairs={{0,8},{8,0},{16,24},{24,16},{32,40},{40,32},{48,56},{56,48},{64,72... | collective-permute-start | bytes 589832 | tf_op jit(solution)/shard_map/ppermute | solution.py:50
  45.4 2.3 %copy-done = bf16[2,384,3072]{2,1,0:T(8,128)(2,1)S(1)} copy-done((bf16[2,384,3072]{2,1,0:T(8,128)(2,1)S(1)}, bf16[2,384,3072]{2,1,0:T(8,128)(2,1)}, u32[]{:S(2)}) %copy-start) | copy-done | bytes 4718616
  47.7 2.7 %load.1.w = bf16[4,384,3072]{2,1,0:T(8,128)(2,1)S(1)} custom-call(bf16[2,384,3072]{2,1,0:T(8,128)(2,1)S(1)} %copy-done, bf16[2,384,3072]{2,1,0:T(8,128)(2,1)} %collective-permute-done.4.other), custom_call_target="tpu_custom_call" | custom-call | bytes 18874368 | tf_op jit(solution)/shard_map/load/pallas_call | solution.py:91
  51.1 8.0 %solve.1 = f32[8,2,16,128]{3,2,1,0:T(8,128)S(1)} custom-call(s32[4,64]{1,0:T(4,128)S(1)} %select_reduce_fusion.partner, f32[1,384]{1,0:T(1,128)S(1)} %reshape.12.coulomb, bf16[4,384,3072]{2,1,0:T(8,128)(2,1)S(1)} %load.1.w, bf16[2,256,384]{2,1,0:T(8,128)(2,1)S(1)} %pad_maximum_fusion.p01, bf16[2,256,384]{2,1,0:T(8,128)(2,1)S(1)} %constant_dynamic-update-slice_fusion.5.p23, ...), custom_call_target="tpu_custom_call" | custom-call | flops 4831838208 | bytes 9437184 | tf_op jit(solution)/shard_map/solve/pallas_call | solution.py:165
  59.1 11.6 %all_to_all.10.terms = f32[8,2,16,128]{3,2,1,0:T(8,128)S(1)} all-to-all(f32[8,2,16,128]{3,2,1,0:T(8,128)S(1)} %solve.1), channel_id=1, replica_groups=mesh['row'=32,'col'=8] {'col'}, dimensions={0} | all-to-all | bytes 262144 | tf_op jit(solution)/shard_map/all_to_all | solution.py:295
  70.9 16.0 %all_to_all.11.arrived = bf16[32,16,128]{2,1,0:T(8,128)(2,1)S(1)} all-to-all(bf16[32,16,128]{2,1,0:T(8,128)(2,1)S(1)} %spread.1), channel_id=1, replica_groups=mesh['row'=32,'col'=8] {'row'}, dimensions={0} | all-to-all | bytes 262144 | tf_op jit(solution)/shard_map/all_to_all | solution.py:297
  86.9 0.7 settle.1
  (30 shorter events, 4.4 us)
Async XLA Ops:
  0.0 17.9 %collective-permute-start.4 = (bf16[2,384,3072]{2,1,0:T(8,128)(2,1)}, bf16[2,384,3072]{2,1,0:T(8,128)(2,1)}, u32[]{:S(2)}, u32[]{:S(2)}) collective-permute-start(bf16[2,384,3072]{2,1,0:T(8,128)(2,1)} %own), channel_id=1, source_target_pairs={{0,8},{8,0},{16,24},{24,16},{32,40},{40,32},{48,56},{56,48},{64,72... | collective-permute-start | bytes 14155784 | tf_op jit(solution)/shard_map/ppermute | solution.py:50
  3.2 2.9 %collective-permute-start = (bf16[1,32,384]{2,1,0:T(8,128)(2,1)}, bf16[1,32,384]{2,1,0:T(8,128)(2,1)S(1)}, u32[]{:S(2)}, u32[]{:S(2)}) collective-permute-start(bf16[1,32,384]{2,1,0:T(8,128)(2,1)} %bitcast.16), channel_id=1, source_target_pairs={{0,16},{8,24},{16,0},{24,8},{32,48},{40,56},{48,32},{56,40},{64,80... | collective-permute-start | bytes 73736 | tf_op jit(solution)/shard_map/ppermute | solution.py:50
  6.9 9.0 %collective-permute-start.1 = (bf16[2,32,384]{2,1,0:T(8,128)(2,1)S(1)}, bf16[2,32,384]{2,1,0:T(8,128)(2,1)S(1)}, u32[]{:S(2)}, u32[]{:S(2)}) collective-permute-start(bf16[2,32,384]{2,1,0:T(8,128)(2,1)S(1)} %pad_maximum_fusion.1), channel_id=1, source_target_pairs={{0,64},{8,72},{16,80},{24,88},{32,96},{40,104},{48,112},{56,120},{... | collective-permute-start | bytes 147464 | tf_op jit(solution)/shard_map/ppermute | solution.py:50
  12.3 5.6 %collective-permute-start.2 = (bf16[2,32,384]{2,1,0:T(8,128)(2,1)S(1)}, bf16[2,32,384]{2,1,0:T(8,128)(2,1)S(1)}, u32[]{:S(2)}, u32[]{:S(2)}) collective-permute-start(bf16[2,32,384]{2,1,0:T(8,128)(2,1)S(1)} %pad_maximum_fusion.1), channel_id=1, source_target_pairs={{0,32},{8,40},{16,48},{24,56},{32,64},{40,72},{48,80},{56,88},{64,... | collective-permute-start | bytes 147464 | tf_op jit(solution)/shard_map/ppermute | solution.py:50
  13.5 4.4 %collective-permute-start.3 = (bf16[2,32,384]{2,1,0:T(8,128)(2,1)S(1)}, bf16[2,32,384]{2,1,0:T(8,128)(2,1)S(1)}, u32[]{:S(2)}, u32[]{:S(2)}) collective-permute-start(bf16[2,32,384]{2,1,0:T(8,128)(2,1)S(1)} %pad_maximum_fusion.1), channel_id=1, source_target_pairs={{0,96},{8,104},{16,112},{24,120},{32,0},{40,8},{48,16},{56,24},{64... | collective-permute-start | bytes 147464 | tf_op jit(solution)/shard_map/ppermute | solution.py:50
  17.9 6.1 %collective-permute-start.5 = (bf16[1,256,384]{2,1,0:T(8,128)(2,1)S(1)}, bf16[1,256,384]{2,1,0:T(8,128)(2,1)S(1)}, u32[]{:S(2)}, u32[]{:S(2)}) collective-permute-start(bf16[1,256,384]{2,1,0:T(8,128)(2,1)S(1)} %bitcast.10), channel_id=1, source_target_pairs={{0,2},{8,12},{16,18},{24,28},{32,34},{40,44},{48,50},{56,60},{64,6... | collective-permute-start | bytes 589832 | tf_op jit(solution)/shard_map/ppermute | solution.py:50
  20.9 5.9 %collective-permute-start.8 = (bf16[1,256,384]{2,1,0:T(8,128)(2,1)S(1)}, bf16[1,256,384]{2,1,0:T(8,128)(2,1)S(1)}, u32[]{:S(2)}, u32[]{:S(2)}) collective-permute-start(bf16[1,256,384]{2,1,0:T(8,128)(2,1)S(1)} %bitcast.11), channel_id=1, source_target_pairs={{0,3},{8,140},{16,19},{24,156},{32,35},{40,172},{48,51},{56,188},{... | collective-permute-start | bytes 589832 | tf_op jit(solution)/shard_map/ppermute | solution.py:50
  21.7 5.7 %collective-permute-start.7 = (bf16[1,256,384]{2,1,0:T(8,128)(2,1)S(1)}, bf16[1,256,384]{2,1,0:T(8,128)(2,1)S(1)}, u32[]{:S(2)}, u32[]{:S(2)}) collective-permute-start(bf16[1,256,384]{2,1,0:T(8,128)(2,1)S(1)} %bitcast.12), channel_id=1, source_target_pairs={{0,1},{8,136},{16,17},{24,152},{32,33},{40,168},{48,49},{56,184},{... | collective-permute-start | bytes 589832 | tf_op jit(solution)/shard_map/ppermute | solution.py:50
  24.1 10.3 %collective-permute-start.6 = (bf16[2,256,384]{2,1,0:T(8,128)(2,1)S(1)}, bf16[2,256,384]{2,1,0:T(8,128)(2,1)S(1)}, u32[]{:S(2)}, u32[]{:S(2)}) collective-permute-start(bf16[2,256,384]{2,1,0:T(8,128)(2,1)S(1)} %pad_maximum_fusion.p01), channel_id=1, source_target_pairs={{0,128},{8,9},{16,144},{24,25},{32,160},{40,41},{48,176},{56,57},{... | collective-permute-start | bytes 1179656 | tf_op jit(solution)/shard_map/ppermute | solution.py:50
  27.5 7.6 %collective-permute-start.9 = (bf16[2,256,384]{2,1,0:T(8,128)(2,1)S(1)}, bf16[2,256,384]{2,1,0:T(8,128)(2,1)S(1)}, u32[]{:S(2)}, u32[]{:S(2)}) collective-permute-start(bf16[2,256,384]{2,1,0:T(8,128)(2,1)S(1)} %constant_dynamic-update-slice_fusion.5.p23), channel_id=1, source_target_pairs={{0,132},{8,11},{16,148},{24,27},{32,164},{40,43},{48,180},{56,59},... | collective-permute-start | bytes 1179656 | tf_op jit(solution)/shard_map/ppermute | solution.py:50
  30.4 15.0 %collective-permute-start.10 = (bf16[2,256,384]{2,1,0:T(8,128)(2,1)S(1)}, bf16[2,256,384]{2,1,0:T(8,128)(2,1)S(1)}, u32[]{:S(2)}, u32[]{:S(2)}) collective-permute-start(bf16[2,256,384]{2,1,0:T(8,128)(2,1)S(1)} %constant_dynamic-update-slice_fusion.5.p23), channel_id=1, source_target_pairs={{0,128},{8,9},{16,144},{24,25},{32,160},{40,41},{48,176},{56,57},{... | collective-permute-start | bytes 1179656 | tf_op jit(solution)/shard_map/ppermute | solution.py:50
  30.4 20.1 %collective-permute-start.11 = (bf16[2,256,384]{2,1,0:T(8,128)(2,1)S(1)}, bf16[2,256,384]{2,1,0:T(8,128)(2,1)S(1)}, u32[]{:S(2)}, u32[]{:S(2)}) collective-permute-start(bf16[2,256,384]{2,1,0:T(8,128)(2,1)S(1)} %pad_maximum_fusion.p01), channel_id=1, source_target_pairs={{0,132},{8,11},{16,148},{24,27},{32,164},{40,43},{48,180},{56,59},... | collective-permute-start | bytes 1179656 | tf_op jit(solution)/shard_map/ppermute | solution.py:50
  34.4 16.7 %collective-permute-start.12 = (bf16[2,256,384]{2,1,0:T(8,128)(2,1)S(1)}, bf16[2,256,384]{2,1,0:T(8,128)(2,1)S(1)}, u32[]{:S(2)}, u32[]{:S(2)}) collective-permute-start(bf16[2,256,384]{2,1,0:T(8,128)(2,1)S(1)} %collective-permute-done.6.f0), channel_id=1, source_target_pairs={{0,128},{8,9},{16,144},{24,25},{32,160},{40,41},{48,176},{56,57},{... | collective-permute-start | bytes 1179656 | tf_op jit(solution)/shard_map/ppermute | solution.py:50
  35.1 15.9 %collective-permute-start.13 = (bf16[2,256,384]{2,1,0:T(8,128)(2,1)S(1)}, bf16[2,256,384]{2,1,0:T(8,128)(2,1)S(1)}, u32[]{:S(2)}, u32[]{:S(2)}) collective-permute-start(bf16[2,256,384]{2,1,0:T(8,128)(2,1)S(1)} %collective-permute-done.9.g1), channel_id=1, source_target_pairs={{0,132},{8,11},{16,148},{24,27},{32,164},{40,43},{48,180},{56,59},... | collective-permute-start | bytes 1179656 | tf_op jit(solution)/shard_map/ppermute | solution.py:50
  38.5 12.0 %collective-permute-start.14 = (bf16[1,256,384]{2,1,0:T(8,128)(2,1)S(1)}, bf16[1,256,384]{2,1,0:T(8,128)(2,1)S(1)}, u32[]{:S(2)}, u32[]{:S(2)}) collective-permute-start(bf16[1,256,384]{2,1,0:T(8,128)(2,1)S(1)} %bitcast.15), channel_id=1, source_target_pairs={{0,8},{8,0},{16,24},{24,16},{32,40},{40,32},{48,56},{56,48},{64,72... | collective-permute-start | bytes 589832 | tf_op jit(solution)/shard_map/ppermute | solution.py:50
  45.4 5.7 %collective-permute-start.15 = (bf16[1,256,384]{2,1,0:T(8,128)(2,1)S(1)}, bf16[1,256,384]{2,1,0:T(8,128)(2,1)S(1)}, u32[]{:S(2)}, u32[]{:S(2)}) collective-permute-start(bf16[1,256,384]{2,1,0:T(8,128)(2,1)S(1)} %get-tuple-element.28), channel_id=1, source_target_pairs={{0,136},{8,0},{16,152},{24,16},{32,168},{40,32},{48,184},{56,48},{... | collective-permute-start | bytes 589832 | tf_op jit(solution)/shard_map/ppermute | solution.py:50
  45.4 2.3 %copy-start = (bf16[2,384,3072]{2,1,0:T(8,128)(2,1)S(1)}, bf16[2,384,3072]{2,1,0:T(8,128)(2,1)}, u32[]{:S(2)}) copy-start(bf16[2,384,3072]{2,1,0:T(8,128)(2,1)} %own) | copy-start | bytes 14155780
  50.5 20.2 %copy-start.1 = (s32[64,64]{1,0:T(8,128)S(1)}, s32[64,64]{1,0:T(8,128)}, u32[]{:S(2)}) copy-start(s32[64,64]{1,0:T(8,128)} %q_index.1) | copy-start | bytes 49156

commit v19 on v17

--- a/solution.py
+++ b/solution.py
@@ -7,7 +7,7 @@
 
 AXES = ("row", "col")
 NX, NY, NZ, NCORE = 4, 4, 8, 2
-FIRST = (0, 2, 1, -1)
+FIRST = (0, 1, 2, -1)
 SECOND = (0, 2, 1, -1)
 ZSHIFTS = (0, 4, 2, -2)
 MIB = 1024 * 1024
@@ -280,7 +280,7 @@
     gg1 = send(g1, second_plane(-1))
 
     core, low = r & 1, r >> 4
-    passed = jnp.where(core == 0, stack, jnp.where(low == 0, parts[2], parts[1]))
+    passed = jnp.where(core == 0, stack, jnp.where(low == 0, parts[2], parts[0]))
     w_own, w_other, f0, g1, passed, kept = lax.optimization_barrier(
         (screened, w_other, f0, g1, passed, stack)
     )

time: 87.2 us -> 86.5 us (level)
  waiting for transfers between devices: 8.77 us -> 7.72 us
    ppermute x16, waiting for transfers between devices: 8.77 us -> 7.72 us  [send(): return lax.ppermute(value, AXES, perm)]
    unnamed x8 -> x9, local copies, waits for them, and re-layouts: 3.12 us -> 3.14 us
  transfers between devices with their start and end apart: 16 -> 16, of which waited for: 8 -> 7; matrix products, arithmetic and copies ran while one was open for 4% -> 4% of each run, Pallas kernels for 3% -> 3%
where the time goes in v19:
time: 86.5 us; the launch traced here: 86.1 us
  starting transfers between devices  33.7 us (39%)
  blocking collectives  28 us (32%)
  Pallas kernels  10.9 us (13%)
  waiting for transfers between devices  7.72 us (9%)
  local copies, waits for them, and re-layouts  3.83 us (4%)
  other arithmetic  1.84 us (2%)
    ppermute x16, starting transfers between devices, send(): return lax.ppermute(value, AXES, perm)  33.7 us
    all_to_all x1, blocking collectives, local(): lax.all_to_all(placed, 'row', split_axis=0, concat_axis=0, tiled=True)  16.1 us
    all_to_all x1, blocking collectives, local(): lax.all_to_all(terms, 'col', split_axis=0, concat_axis=0, tiled=True)  11.9 us
    ppermute x16, waiting for transfers between devices, send(): return lax.ppermute(value, AXES, perm)  7.72 us
    pallas_call x1, Pallas kernels, solve(): pl.pallas_call(solve_kernel, in_specs=[pl.BlockSpec(memory_space=pltpu.SM...  7.28 us
    unnamed x9, local copies, waits for them, and re-layouts  3.14 us
    pallas_call x1, Pallas kernels, load(): pl.pallas_call(load_kernel, in_specs=[pl.BlockSpec(memory_space=pl.ANY)]...  2.72 us
  transfers between devices with their start and end apart: 16, of which 7 were waited for; matrix products, arithmetic and copies ran while one was open for 4% of the time, Pallas kernels for 3%

profile of v19, /device:TPU:1, one launch (start us, length us, event | category | flops | bytes accessed | tf_op | source)
XLA Modules:
  0.0 86.1 jit_solution(13613092274573374260)
XLA Ops:
  0.0 3.2 %collective-permute-start.4 = (bf16[2,384,3072]{2,1,0:T(8,128)(2,1)}, bf16[2,384,3072]{2,1,0:T(8,128)(2,1)}, u32[]{:S(2)}, u32[]{:S(2)}) collective-permute-start(bf16[2,384,3072]{2,1,0:T(8,128)(2,1)} %own), channel_id=1, source_target_pairs={{0,8},{8,0},{16,24},{24,16},{32,40},{40,32},{48,56},{56,48},{64,72... | collective-permute-start | bytes 14155784 | tf_op jit(solution)/shard_map/ppermute | solution.py:50
  3.3 0.9 %select_reduce_fusion.partner = s32[4,64]{1,0:T(4,128)S(1)} fusion(s32[64,64]{1,0:T(8,128)} %q_index.1, s32[4]{0:T(128)S(1)} %pad_add_fusion), kind=kLoop, calls=%fused_computation.2 | loop fusion | flops 48896 | bytes 17424 | tf_op jit(solution)/shard_map/reduce_sum | solution.py:264
  6.1 0.7 pad_maximum_fusion.1
  6.9 5.4 %collective-permute-start.1 = (bf16[2,32,384]{2,1,0:T(8,128)(2,1)S(1)}, bf16[2,32,384]{2,1,0:T(8,128)(2,1)S(1)}, u32[]{:S(2)}, u32[]{:S(2)}) collective-permute-start(bf16[2,32,384]{2,1,0:T(8,128)(2,1)S(1)} %pad_maximum_fusion.1), channel_id=1, source_target_pairs={{0,64},{8,72},{16,80},{24,88},{32,96},{40,104},{48,112},{56,120},{... | collective-permute-start | bytes 147464 | tf_op jit(solution)/shard_map/ppermute | solution.py:50
  12.3 1.2 %collective-permute-start.2 = (bf16[2,32,384]{2,1,0:T(8,128)(2,1)S(1)}, bf16[2,32,384]{2,1,0:T(8,128)(2,1)S(1)}, u32[]{:S(2)}, u32[]{:S(2)}) collective-permute-start(bf16[2,32,384]{2,1,0:T(8,128)(2,1)S(1)} %pad_maximum_fusion.1), channel_id=1, source_target_pairs={{0,32},{8,40},{16,48},{24,56},{32,64},{40,72},{48,80},{56,88},{64,... | collective-permute-start | bytes 147464 | tf_op jit(solution)/shard_map/ppermute | solution.py:50
  13.5 2.4 %collective-permute-start.3 = (bf16[2,32,384]{2,1,0:T(8,128)(2,1)S(1)}, bf16[2,32,384]{2,1,0:T(8,128)(2,1)S(1)}, u32[]{:S(2)}, u32[]{:S(2)}) collective-permute-start(bf16[2,32,384]{2,1,0:T(8,128)(2,1)S(1)} %pad_maximum_fusion.1), channel_id=1, source_target_pairs={{0,96},{8,104},{16,112},{24,120},{32,0},{40,8},{48,16},{56,24},{64... | collective-permute-start | bytes 147464 | tf_op jit(solution)/shard_map/ppermute | solution.py:50
  15.9 2.0 %collective-permute-done.2 = bf16[2,32,384]{2,1,0:T(8,128)(2,1)S(1)} collective-permute-done((bf16[2,32,384]{2,1,0:T(8,128)(2,1)S(1)}, bf16[2,32,384]{2,1,0:T(8,128)(2,1)S(1)}, u32[]{:S(2)}, u32[]{:S(2)}) %collective-permute-start.2) | collective-permute-done | bytes 49184 | tf_op jit(solution)/shard_map/ppermute | solution.py:50
  17.9 1.4 %collective-permute-start.5 = (bf16[1,256,384]{2,1,0:T(8,128)(2,1)S(1)}, bf16[1,256,384]{2,1,0:T(8,128)(2,1)S(1)}, u32[]{:S(2)}, u32[]{:S(2)}) collective-permute-start(bf16[1,256,384]{2,1,0:T(8,128)(2,1)S(1)} %bitcast.10), channel_id=1, source_target_pairs={{0,1},{8,136},{16,17},{24,152},{32,33},{40,168},{48,49},{56,184},{... | collective-permute-start | bytes 589832 | tf_op jit(solution)/shard_map/ppermute | solution.py:50
  19.3 2.6 %collective-permute-start.7 = (bf16[1,256,384]{2,1,0:T(8,128)(2,1)S(1)}, bf16[1,256,384]{2,1,0:T(8,128)(2,1)S(1)}, u32[]{:S(2)}, u32[]{:S(2)}) collective-permute-start(bf16[1,256,384]{2,1,0:T(8,128)(2,1)S(1)} %bitcast.11), channel_id=1, source_target_pairs={{0,2},{8,12},{16,18},{24,28},{32,34},{40,44},{48,50},{56,60},{64,6... | collective-permute-start | bytes 589832 | tf_op jit(solution)/shard_map/ppermute | solution.py:50
  21.9 1.1 %collective-permute-start.8 = (bf16[1,256,384]{2,1,0:T(8,128)(2,1)S(1)}, bf16[1,256,384]{2,1,0:T(8,128)(2,1)S(1)}, u32[]{:S(2)}, u32[]{:S(2)}) collective-permute-start(bf16[1,256,384]{2,1,0:T(8,128)(2,1)S(1)} %bitcast.12), channel_id=1, source_target_pairs={{0,3},{8,140},{16,19},{24,156},{32,35},{40,172},{48,51},{56,188},{... | collective-permute-start | bytes 589832 | tf_op jit(solution)/shard_map/ppermute | solution.py:50
  23.0 0.8 collective-permute-done.5
  23.8 1.3 %collective-permute-start.6 = (bf16[2,256,384]{2,1,0:T(8,128)(2,1)S(1)}, bf16[2,256,384]{2,1,0:T(8,128)(2,1)S(1)}, u32[]{:S(2)}, u32[]{:S(2)}) collective-permute-start(bf16[2,256,384]{2,1,0:T(8,128)(2,1)S(1)} %pad_maximum_fusion.p01), channel_id=1, source_target_pairs={{0,128},{8,9},{16,144},{24,25},{32,160},{40,41},{48,176},{56,57},{... | collective-permute-start | bytes 1179656 | tf_op jit(solution)/shard_map/ppermute | solution.py:50
  25.1 1.9 %collective-permute-done.7 = bf16[1,256,384]{2,1,0:T(8,128)(2,1)S(1)} collective-permute-done((bf16[1,256,384]{2,1,0:T(8,128)(2,1)S(1)}, bf16[1,256,384]{2,1,0:T(8,128)(2,1)S(1)}, u32[]{:S(2)}, u32[]{:S(2)}) %collective-permute-start.7) | collective-permute-done | bytes 196640 | tf_op jit(solution)/shard_map/ppermute | solution.py:50
  27.2 2.8 %collective-permute-start.9 = (bf16[2,256,384]{2,1,0:T(8,128)(2,1)S(1)}, bf16[2,256,384]{2,1,0:T(8,128)(2,1)S(1)}, u32[]{:S(2)}, u32[]{:S(2)}) collective-permute-start(bf16[2,256,384]{2,1,0:T(8,128)(2,1)S(1)} %get-tuple-element.30.p23), channel_id=1, source_target_pairs={{0,132},{8,11},{16,148},{24,27},{32,164},{40,43},{48,180},{56,59},... | collective-permute-start | bytes 1179656 | tf_op jit(solution)/shard_map/ppermute | solution.py:50
  30.1 2.7 %collective-permute-start.11 = (bf16[2,256,384]{2,1,0:T(8,128)(2,1)S(1)}, bf16[2,256,384]{2,1,0:T(8,128)(2,1)S(1)}, u32[]{:S(2)}, u32[]{:S(2)}) collective-permute-start(bf16[2,256,384]{2,1,0:T(8,128)(2,1)S(1)} %pad_maximum_fusion.p01), channel_id=1, source_target_pairs={{0,132},{8,11},{16,148},{24,27},{32,164},{40,43},{48,180},{56,59},... | collective-permute-start | bytes 1179656 | tf_op jit(solution)/shard_map/ppermute | solution.py:50
  32.7 1.2 %collective-permute-done.6.f0 = bf16[2,256,384]{2,1,0:T(8,128)(2,1)S(1)} collective-permute-done((bf16[2,256,384]{2,1,0:T(8,128)(2,1)S(1)}, bf16[2,256,384]{2,1,0:T(8,128)(2,1)S(1)}, u32[]{:S(2)}, u32[]{:S(2)}) %collective-permute-start.6) | collective-permute-done | bytes 393248 | tf_op jit(solution)/shard_map/ppermute | solution.py:50
  33.9 0.9 %collective-permute-done.9.g1 = bf16[2,256,384]{2,1,0:T(8,128)(2,1)S(1)} collective-permute-done((bf16[2,256,384]{2,1,0:T(8,128)(2,1)S(1)}, bf16[2,256,384]{2,1,0:T(8,128)(2,1)S(1)}, u32[]{:S(2)}, u32[]{:S(2)}) %collective-permute-start.9) | collective-permute-done | bytes 393248 | tf_op jit(solution)/shard_map/ppermute | solution.py:50
  34.8 3.1 %collective-permute-start.13 = (bf16[2,256,384]{2,1,0:T(8,128)(2,1)S(1)}, bf16[2,256,384]{2,1,0:T(8,128)(2,1)S(1)}, u32[]{:S(2)}, u32[]{:S(2)}) collective-permute-start(bf16[2,256,384]{2,1,0:T(8,128)(2,1)S(1)} %collective-permute-done.9.g1), channel_id=1, source_target_pairs={{0,132},{8,11},{16,148},{24,27},{32,164},{40,43},{48,180},{56,59},... | collective-permute-start | bytes 1179656 | tf_op jit(solution)/shard_map/ppermute | solution.py:50
  37.9 6.5 %collective-permute-start.14 = (bf16[1,256,384]{2,1,0:T(8,128)(2,1)S(1)}, bf16[1,256,384]{2,1,0:T(8,128)(2,1)S(1)}, u32[]{:S(2)}, u32[]{:S(2)}) collective-permute-start(bf16[1,256,384]{2,1,0:T(8,128)(2,1)S(1)} %bitcast.15), channel_id=1, source_target_pairs={{0,8},{8,0},{16,24},{24,16},{32,40},{40,32},{48,56},{56,48},{64,72... | collective-permute-start | bytes 589832 | tf_op jit(solution)/shard_map/ppermute | solution.py:50
  44.4 2.3 %copy-done = bf16[2,384,3072]{2,1,0:T(8,128)(2,1)S(1)} copy-done((bf16[2,384,3072]{2,1,0:T(8,128)(2,1)S(1)}, bf16[2,384,3072]{2,1,0:T(8,128)(2,1)}, u32[]{:S(2)}) %copy-start) | copy-done | bytes 4718616
  46.7 2.7 %load.1.w = bf16[4,384,3072]{2,1,0:T(8,128)(2,1)S(1)} custom-call(bf16[2,384,3072]{2,1,0:T(8,128)(2,1)S(1)} %copy-done, bf16[2,384,3072]{2,1,0:T(8,128)(2,1)} %collective-permute-done.4.other), custom_call_target="tpu_custom_call" | custom-call | bytes 18874368 | tf_op jit(solution)/shard_map/load/pallas_call | solution.py:91
  49.9 7.3 %solve.1 = f32[8,2,16,128]{3,2,1,0:T(8,128)S(1)} custom-call(s32[4,64]{1,0:T(4,128)S(1)} %select_reduce_fusion.partner, f32[1,384]{1,0:T(1,128)S(1)} %reshape.12.coulomb, bf16[4,384,3072]{2,1,0:T(8,128)(2,1)S(1)} %load.1.w, bf16[2,256,384]{2,1,0:T(8,128)(2,1)S(1)} %pad_maximum_fusion.p01, bf16[2,256,384]{2,1,0:T(8,128)(2,1)S(1)} %get-tuple-element.30.p23, ...), custom_call_target="tpu_custom_call" | custom-call | flops 4831838208 | bytes 9437184 | tf_op jit(solution)/shard_map/solve/pallas_call | solution.py:162
  57.1 11.9 %all_to_all.10.terms = f32[8,2,16,128]{3,2,1,0:T(8,128)S(1)} all-to-all(f32[8,2,16,128]{3,2,1,0:T(8,128)S(1)} %solve.1), channel_id=1, replica_groups=mesh['row'=32,'col'=8] {'col'}, dimensions={0} | all-to-all | bytes 262144 | tf_op jit(solution)/shard_map/all_to_all | solution.py:292
  69.3 16.1 %all_to_all.11.arrived = bf16[32,16,128]{2,1,0:T(8,128)(2,1)S(1)} all-to-all(bf16[32,16,128]{2,1,0:T(8,128)(2,1)S(1)} %spread.1), channel_id=1, replica_groups=mesh['row'=32,'col'=8] {'row'}, dimensions={0} | all-to-all | bytes 262144 | tf_op jit(solution)/shard_map/all_to_all | solution.py:294
  (30 shorter events, 3.6 us)
Async XLA Ops:
  0.0 17.9 %collective-permute-start.4 = (bf16[2,384,3072]{2,1,0:T(8,128)(2,1)}, bf16[2,384,3072]{2,1,0:T(8,128)(2,1)}, u32[]{:S(2)}, u32[]{:S(2)}) collective-permute-start(bf16[2,384,3072]{2,1,0:T(8,128)(2,1)} %own), channel_id=1, source_target_pairs={{0,8},{8,0},{16,24},{24,16},{32,40},{40,32},{48,56},{56,48},{64,72... | collective-permute-start | bytes 14155784 | tf_op jit(solution)/shard_map/ppermute | solution.py:50
  3.2 2.9 %collective-permute-start = (bf16[1,32,384]{2,1,0:T(8,128)(2,1)}, bf16[1,32,384]{2,1,0:T(8,128)(2,1)S(1)}, u32[]{:S(2)}, u32[]{:S(2)}) collective-permute-start(bf16[1,32,384]{2,1,0:T(8,128)(2,1)} %bitcast.16), channel_id=1, source_target_pairs={{0,16},{8,24},{16,0},{24,8},{32,48},{40,56},{48,32},{56,40},{64,80... | collective-permute-start | bytes 73736 | tf_op jit(solution)/shard_map/ppermute | solution.py:50
  6.9 9.0 %collective-permute-start.1 = (bf16[2,32,384]{2,1,0:T(8,128)(2,1)S(1)}, bf16[2,32,384]{2,1,0:T(8,128)(2,1)S(1)}, u32[]{:S(2)}, u32[]{:S(2)}) collective-permute-start(bf16[2,32,384]{2,1,0:T(8,128)(2,1)S(1)} %pad_maximum_fusion.1), channel_id=1, source_target_pairs={{0,64},{8,72},{16,80},{24,88},{32,96},{40,104},{48,112},{56,120},{... | collective-permute-start | bytes 147464 | tf_op jit(solution)/shard_map/ppermute | solution.py:50
  12.3 5.6 %collective-permute-start.2 = (bf16[2,32,384]{2,1,0:T(8,128)(2,1)S(1)}, bf16[2,32,384]{2,1,0:T(8,128)(2,1)S(1)}, u32[]{:S(2)}, u32[]{:S(2)}) collective-permute-start(bf16[2,32,384]{2,1,0:T(8,128)(2,1)S(1)} %pad_maximum_fusion.1), channel_id=1, source_target_pairs={{0,32},{8,40},{16,48},{24,56},{32,64},{40,72},{48,80},{56,88},{64,... | collective-permute-start | bytes 147464 | tf_op jit(solution)/shard_map/ppermute | solution.py:50
  13.5 4.4 %collective-permute-start.3 = (bf16[2,32,384]{2,1,0:T(8,128)(2,1)S(1)}, bf16[2,32,384]{2,1,0:T(8,128)(2,1)S(1)}, u32[]{:S(2)}, u32[]{:S(2)}) collective-permute-start(bf16[2,32,384]{2,1,0:T(8,128)(2,1)S(1)} %pad_maximum_fusion.1), channel_id=1, source_target_pairs={{0,96},{8,104},{16,112},{24,120},{32,0},{40,8},{48,16},{56,24},{64... | collective-permute-start | bytes 147464 | tf_op jit(solution)/shard_map/ppermute | solution.py:50
  17.9 5.9 %collective-permute-start.5 = (bf16[1,256,384]{2,1,0:T(8,128)(2,1)S(1)}, bf16[1,256,384]{2,1,0:T(8,128)(2,1)S(1)}, u32[]{:S(2)}, u32[]{:S(2)}) collective-permute-start(bf16[1,256,384]{2,1,0:T(8,128)(2,1)S(1)} %bitcast.10), channel_id=1, source_target_pairs={{0,1},{8,136},{16,17},{24,152},{32,33},{40,168},{48,49},{56,184},{... | collective-permute-start | bytes 589832 | tf_op jit(solution)/shard_map/ppermute | solution.py:50
  19.3 7.8 %collective-permute-start.7 = (bf16[1,256,384]{2,1,0:T(8,128)(2,1)S(1)}, bf16[1,256,384]{2,1,0:T(8,128)(2,1)S(1)}, u32[]{:S(2)}, u32[]{:S(2)}) collective-permute-start(bf16[1,256,384]{2,1,0:T(8,128)(2,1)S(1)} %bitcast.11), channel_id=1, source_target_pairs={{0,2},{8,12},{16,18},{24,28},{32,34},{40,44},{48,50},{56,60},{64,6... | collective-permute-start | bytes 589832 | tf_op jit(solution)/shard_map/ppermute | solution.py:50
  21.9 5.2 %collective-permute-start.8 = (bf16[1,256,384]{2,1,0:T(8,128)(2,1)S(1)}, bf16[1,256,384]{2,1,0:T(8,128)(2,1)S(1)}, u32[]{:S(2)}, u32[]{:S(2)}) collective-permute-start(bf16[1,256,384]{2,1,0:T(8,128)(2,1)S(1)} %bitcast.12), channel_id=1, source_target_pairs={{0,3},{8,140},{16,19},{24,156},{32,35},{40,172},{48,51},{56,188},{... | collective-permute-start | bytes 589832 | tf_op jit(solution)/shard_map/ppermute | solution.py:50
  23.8 10.1 %collective-permute-start.6 = (bf16[2,256,384]{2,1,0:T(8,128)(2,1)S(1)}, bf16[2,256,384]{2,1,0:T(8,128)(2,1)S(1)}, u32[]{:S(2)}, u32[]{:S(2)}) collective-permute-start(bf16[2,256,384]{2,1,0:T(8,128)(2,1)S(1)} %pad_maximum_fusion.p01), channel_id=1, source_target_pairs={{0,128},{8,9},{16,144},{24,25},{32,160},{40,41},{48,176},{56,57},{... | collective-permute-start | bytes 1179656 | tf_op jit(solution)/shard_map/ppermute | solution.py:50
  27.2 7.6 %collective-permute-start.9 = (bf16[2,256,384]{2,1,0:T(8,128)(2,1)S(1)}, bf16[2,256,384]{2,1,0:T(8,128)(2,1)S(1)}, u32[]{:S(2)}, u32[]{:S(2)}) collective-permute-start(bf16[2,256,384]{2,1,0:T(8,128)(2,1)S(1)} %get-tuple-element.30.p23), channel_id=1, source_target_pairs={{0,132},{8,11},{16,148},{24,27},{32,164},{40,43},{48,180},{56,59},... | collective-permute-start | bytes 1179656 | tf_op jit(solution)/shard_map/ppermute | solution.py:50
  30.0 14.3 %collective-permute-start.10 = (bf16[2,256,384]{2,1,0:T(8,128)(2,1)S(1)}, bf16[2,256,384]{2,1,0:T(8,128)(2,1)S(1)}, u32[]{:S(2)}, u32[]{:S(2)}) collective-permute-start(bf16[2,256,384]{2,1,0:T(8,128)(2,1)S(1)} %get-tuple-element.30.p23), channel_id=1, source_target_pairs={{0,128},{8,9},{16,144},{24,25},{32,160},{40,41},{48,176},{56,57},{... | collective-permute-start | bytes 1179656 | tf_op jit(solution)/shard_map/ppermute | solution.py:50
  30.1 19.4 %collective-permute-start.11 = (bf16[2,256,384]{2,1,0:T(8,128)(2,1)S(1)}, bf16[2,256,384]{2,1,0:T(8,128)(2,1)S(1)}, u32[]{:S(2)}, u32[]{:S(2)}) collective-permute-start(bf16[2,256,384]{2,1,0:T(8,128)(2,1)S(1)} %pad_maximum_fusion.p01), channel_id=1, source_target_pairs={{0,132},{8,11},{16,148},{24,27},{32,164},{40,43},{48,180},{56,59},... | collective-permute-start | bytes 1179656 | tf_op jit(solution)/shard_map/ppermute | solution.py:50
  33.9 16.0 %collective-permute-start.12 = (bf16[2,256,384]{2,1,0:T(8,128)(2,1)S(1)}, bf16[2,256,384]{2,1,0:T(8,128)(2,1)S(1)}, u32[]{:S(2)}, u32[]{:S(2)}) collective-permute-start(bf16[2,256,384]{2,1,0:T(8,128)(2,1)S(1)} %collective-permute-done.6.f0), channel_id=1, source_target_pairs={{0,128},{8,9},{16,144},{24,25},{32,160},{40,41},{48,176},{56,57},{... | collective-permute-start | bytes 1179656 | tf_op jit(solution)/shard_map/ppermute | solution.py:50
  34.8 15.1 %collective-permute-start.13 = (bf16[2,256,384]{2,1,0:T(8,128)(2,1)S(1)}, bf16[2,256,384]{2,1,0:T(8,128)(2,1)S(1)}, u32[]{:S(2)}, u32[]{:S(2)}) collective-permute-start(bf16[2,256,384]{2,1,0:T(8,128)(2,1)S(1)} %collective-permute-done.9.g1), channel_id=1, source_target_pairs={{0,132},{8,11},{16,148},{24,27},{32,164},{40,43},{48,180},{56,59},... | collective-permute-start | bytes 1179656 | tf_op jit(solution)/shard_map/ppermute | solution.py:50
  37.9 11.6 %collective-permute-start.14 = (bf16[1,256,384]{2,1,0:T(8,128)(2,1)S(1)}, bf16[1,256,384]{2,1,0:T(8,128)(2,1)S(1)}, u32[]{:S(2)}, u32[]{:S(2)}) collective-permute-start(bf16[1,256,384]{2,1,0:T(8,128)(2,1)S(1)} %bitcast.15), channel_id=1, source_target_pairs={{0,8},{8,0},{16,24},{24,16},{32,40},{40,32},{48,56},{56,48},{64,72... | collective-permute-start | bytes 589832 | tf_op jit(solution)/shard_map/ppermute | solution.py:50
  44.4 5.5 %collective-permute-start.15 = (bf16[1,256,384]{2,1,0:T(8,128)(2,1)S(1)}, bf16[1,256,384]{2,1,0:T(8,128)(2,1)S(1)}, u32[]{:S(2)}, u32[]{:S(2)}) collective-permute-start(bf16[1,256,384]{2,1,0:T(8,128)(2,1)S(1)} %get-tuple-element.28), channel_id=1, source_target_pairs={{0,136},{8,0},{16,152},{24,16},{32,168},{40,32},{48,184},{56,48},{... | collective-permute-start | bytes 589832 | tf_op jit(solution)/shard_map/ppermute | solution.py:50
  44.4 2.3 %copy-start = (bf16[2,384,3072]{2,1,0:T(8,128)(2,1)S(1)}, bf16[2,384,3072]{2,1,0:T(8,128)(2,1)}, u32[]{:S(2)}) copy-start(bf16[2,384,3072]{2,1,0:T(8,128)(2,1)} %own) | copy-start | bytes 14155780
  49.4 19.6 %copy-start.1 = (s32[64,64]{1,0:T(8,128)S(1)}, s32[64,64]{1,0:T(8,128)}, u32[]{:S(2)}) copy-start(s32[64,64]{1,0:T(8,128)} %q_index.1) | copy-start | bytes 49156
